TPU v7x, 32 devices: a whole 2x2x4 slice. The times are simulated.
32 devices in a mesh: rows: 8 (over y, x, core), seq: 4 (over z).
Axes of the slice: x: 2, y: 2, z: 4, core: 2. Of those that a mesh axis runs over, the one named last changes fastest.
Arguments:
- tokens_in: bfloat16 [8, 2048, 2048], P('rows', 'seq'), may hold values from -6 to 6
- corpus: int32 [8], P('rows'), may hold values from 0 to 7
- corpus_weight: int32 [8], replicated, may hold values from 16 to 64
- w_qkv: bfloat16 [2048, 1920], P(('rows', 'seq')), may hold values from -0.125 to 0.125
- w_out: bfloat16 [1280, 2048], P(None, ('rows', 'seq')), may hold values from -2 to 2
- w_gate: bfloat16 [2048, 4608], P(('rows', 'seq')), may hold values from -0.125 to 0.125
- w_up: bfloat16 [2048, 4608], P(('rows', 'seq')), may hold values from -0.125 to 0.125
- w_down: bfloat16 [4608, 2048], P(('rows', 'seq')), may hold values from -0.09375 to 0.09375
- attn_gain: bfloat16 [2048], P(('rows', 'seq')), may hold values from 0.5 to 1.5
- ffn_gain: bfloat16 [2048], P(('rows', 'seq')), may hold values from 0.5 to 1.5
- q_gain: bfloat16 [64], replicated, may hold values from 0.099609375 to 1.8984375
- k_gain: bfloat16 [64], replicated, may hold values from 0.099609375 to 1.8984375
- upstream: bfloat16 [8, 2048, 2048], P('rows', 'seq'), may hold values from -6 to 6
Outputs:
- output: bfloat16 [8, 2048, 2048], P('rows', 'seq')
- input_grad: bfloat16 [8, 2048, 2048], P('rows', 'seq')
- grad_qkv: float32 [2048, 1920], P(('rows', 'seq'))
- grad_out: float32 [1280, 2048], P(None, ('rows', 'seq'))
- grad_gate: float32 [2048, 4608], P(('rows', 'seq'))
- grad_up: float32 [2048, 4608], P(('rows', 'seq'))
- grad_down: float32 [4608, 2048], P(('rows', 'seq'))
- grad_attn_gain: float32 [2048], P(('rows', 'seq'))
- grad_ffn_gain: float32 [2048], P(('rows', 'seq'))
- grad_q_gain: float32 [64], replicated
- grad_k_gain: float32 [64], replicated
All inputs are finite; a program needn't handle non-finite values.
Results may differ from a plain program's by a relative error of at most 0.018.
Values may be sent and summed in bfloat16 or wider, within the bound.
No kernel may reach another device: no remote copies, remote signals or barrier semaphores. Data moves between devices by JAX's collectives and lax.ppermute only.
A program may use at most 320 MiB of HBM per device.

v0:
```python
from functools import partial

import jax
import jax.numpy as jnp
import numpy as np
from jax import lax
from jax.sharding import PartitionSpec as P

QUERY_HEADS = 20
KEY_VALUE_HEADS = 5
HEAD_SIZE = 64
CORPORA = 8
DENOM = 64


EPSILON = 1e-06
ROPE_BASE = 10000.0


def for_sending(shard):
    return jax.tree.map(lambda a: a.astype(jnp.bfloat16) if a.dtype == jnp.float32 else a, shard)


def rms_scale(values, gain_vector):
    mean_square = jnp.mean(values * values, axis=-1, keepdims=True)
    return values * lax.rsqrt(mean_square + EPSILON) * gain_vector


def rotate(values, position):
    half_width = values.shape[-1] // 2
    exponent = jnp.arange(half_width, dtype=jnp.float32) * (-2.0 / values.shape[-1])
    frequency = jnp.power(ROPE_BASE, exponent)
    angles = position[:, None] * frequency[None, :]
    cosine = jnp.cos(angles)[:, None, :]
    sine_part = jnp.sin(angles)[:, None, :]
    first_half = values[..., :half_width]
    second_half = values[..., half_width:]
    return jnp.concatenate(
        [
            first_half * cosine - second_half * sine_part,
            second_half * cosine + first_half * sine_part,
        ],
        axis=-1,
    )


def heads_piece(joint_query_key_value, q_gain, k_gain, position):
    leading_axis = joint_query_key_value.shape[:-1]
    query_column_width = QUERY_HEADS * HEAD_SIZE
    key_column_width = KEY_VALUE_HEADS * HEAD_SIZE
    queries = joint_query_key_value[..., :query_column_width].reshape(
        leading_axis + (QUERY_HEADS, HEAD_SIZE)
    )
    key_head_rows = joint_query_key_value[
        ..., query_column_width : query_column_width + key_column_width
    ].reshape(leading_axis + (KEY_VALUE_HEADS, HEAD_SIZE))
    value_head_rows = joint_query_key_value[..., query_column_width + key_column_width :].reshape(
        leading_axis + (KEY_VALUE_HEADS, HEAD_SIZE)
    )
    queries = rotate(rms_scale(queries, q_gain), position)
    key_head_rows = rotate(rms_scale(key_head_rows, k_gain), position)
    return (queries, key_head_rows, value_head_rows)


def activate(gate_values, up_values):
    return jax.nn.silu(gate_values) * up_values


def causal_mask(first_row, block_rows, reach_rows):
    key_place = jnp.arange(reach_rows, dtype=jnp.int32)
    query_place = first_row + jnp.arange(block_rows, dtype=jnp.int32)
    return key_place[None, None, :] <= query_place[None, :, None]


def split_item(item_rows, head_count):
    length = item_rows.shape[0]
    query_column_width = head_count * HEAD_SIZE
    queries = item_rows[:, :query_column_width].reshape(length, head_count, HEAD_SIZE)
    return (
        queries,
        item_rows[:, query_column_width : query_column_width + HEAD_SIZE],
        item_rows[:, query_column_width + HEAD_SIZE :],
    )


def attend_forward(item_rows, head_count):
    queries, key_rows, value_rows = split_item(item_rows, head_count)
    length = item_rows.shape[0]
    block_rows = min(512, length)
    score_scale = HEAD_SIZE ** (-0.5)
    outputs = []
    totals = []
    for first_row in range(0, length, block_rows):
        reach_rows = first_row + block_rows
        scores = (
            jnp.einsum(
                "qgd,kd->gqk",
                queries[first_row:reach_rows],
                key_rows[:reach_rows],
                preferred_element_type=jnp.float32,
            )
            * score_scale
        )
        scores = jnp.where(causal_mask(first_row, block_rows, reach_rows), scores, -jnp.inf)
        highest = jnp.max(scores, axis=-1, keepdims=True)
        weights = jnp.exp(scores - highest)
        norm_sum = jnp.sum(weights, axis=-1, keepdims=True)
        probability = (weights / norm_sum).astype(jnp.bfloat16)
        mixed_rows = jnp.einsum(
            "gqk,kd->qgd", probability, value_rows[:reach_rows], preferred_element_type=jnp.float32
        )
        outputs.append(mixed_rows.reshape(block_rows, head_count * HEAD_SIZE).astype(jnp.bfloat16))
        totals.append(jnp.transpose((highest + jnp.log(norm_sum))[:, :, 0]))
    return (jnp.concatenate(outputs, axis=0), jnp.concatenate(totals, axis=0))


def attend_backward(operands, head_count):
    item_rows, log_sums, grad_rows = operands
    queries, key_rows, value_rows = split_item(item_rows, head_count)
    length = item_rows.shape[0]
    block_rows = min(512, length)
    score_scale = HEAD_SIZE ** (-0.5)
    grad_queries = []
    grad_keys = jnp.zeros((length, head_count, HEAD_SIZE), jnp.float32)
    grad_values = jnp.zeros((length, head_count, HEAD_SIZE), jnp.float32)
    for first_row in range(0, length, block_rows):
        reach_rows = first_row + block_rows
        query_block = queries[first_row:reach_rows]
        grad_block = grad_rows[first_row:reach_rows].reshape(block_rows, head_count, HEAD_SIZE)
        scores = (
            jnp.einsum(
                "qgd,kd->gqk",
                query_block,
                key_rows[:reach_rows],
                preferred_element_type=jnp.float32,
            )
            * score_scale
        )
        shifted = scores - jnp.transpose(log_sums[first_row:reach_rows])[:, :, None]
        shifted = jnp.where(causal_mask(first_row, block_rows, reach_rows), shifted, -jnp.inf)
        probability = jnp.exp(shifted)
        grad_probability = jnp.einsum(
            "qgd,kd->gqk", grad_block, value_rows[:reach_rows], preferred_element_type=jnp.float32
        )
        row_inner = jnp.sum(probability * grad_probability, axis=-1, keepdims=True)
        grad_scores = (probability * (grad_probability - row_inner)).astype(jnp.bfloat16)
        query_part = (
            jnp.einsum(
                "gqk,kd->qgd",
                grad_scores,
                key_rows[:reach_rows],
                preferred_element_type=jnp.float32,
            )
            * score_scale
        )
        grad_queries.append(
            query_part.reshape(block_rows, head_count * HEAD_SIZE).astype(jnp.bfloat16)
        )
        grad_keys = grad_keys.at[:reach_rows].add(
            jnp.einsum("gqk,qgd->kgd", grad_scores, query_block, preferred_element_type=jnp.float32)
            * score_scale
        )
        grad_values = grad_values.at[:reach_rows].add(
            jnp.einsum(
                "gqk,qgd->kgd",
                probability.astype(jnp.bfloat16),
                grad_block,
                preferred_element_type=jnp.float32,
            )
        )
    return jnp.concatenate(
        [
            jnp.concatenate(grad_queries, axis=0),
            grad_keys.reshape(length, head_count * HEAD_SIZE).astype(jnp.bfloat16),
            grad_values.reshape(length, head_count * HEAD_SIZE).astype(jnp.bfloat16),
        ],
        axis=-1,
    )


def to_items(block_array):
    moved_axes = jnp.moveaxis(block_array, 3, 0)
    return moved_axes.reshape(
        (moved_axes.shape[0] * moved_axes.shape[1], moved_axes.shape[2], moved_axes.shape[4])
    )


def from_items(flat_items, slot_count):
    shaped = flat_items.reshape(
        (slot_count, flat_items.shape[0] // slot_count) + flat_items.shape[1:]
    )
    return jnp.moveaxis(shaped, 0, 2)[:, :, None]


def attend_items(received, head_count):
    slot_count = received.shape[3]
    mixed_rows, log_sums = lax.map(
        partial(attend_forward, head_count=head_count), to_items(received)
    )
    return (from_items(mixed_rows, slot_count), from_items(log_sums, slot_count), received)


def shards(
    tokens_in,
    corpus,
    corpus_weight,
    w_qkv,
    w_out,
    w_gate,
    w_up,
    w_down,
    attn_gain,
    ffn_gain,
    q_gain,
    k_gain,
    upstream,
):
    batch_row_list = tokens_in.shape[0]
    shard_length = tokens_in.shape[1]
    seq_devices = lax.axis_size("seq")
    heads_in_group = 2
    unit_count = QUERY_HEADS // heads_in_group
    capacity = -(-unit_count // seq_devices)
    slot_total = seq_devices * capacity
    unit_position_index = np.arange(unit_count)
    slot_place = unit_position_index % seq_devices * capacity + unit_position_index // seq_devices
    select_low = jnp.asarray(slot_place[:, None] == np.arange(slot_total)[None, :], jnp.bfloat16)
    kv_select = jnp.asarray(
        np.arange(KEY_VALUE_HEADS)[:, None]
        == (unit_position_index * heads_in_group // (QUERY_HEADS // KEY_VALUE_HEADS))[None, :],
        jnp.bfloat16,
    )
    unit_width = heads_in_group * HEAD_SIZE
    corpus_table = (corpus[:, None] == jnp.arange(CORPORA, dtype=jnp.int32)[None, :]).astype(
        jnp.float32
    )
    counts = lax.psum(jnp.sum(corpus_table, axis=0) * shard_length, ("rows", "seq"))
    weight_row = jnp.sum(corpus_table * corpus_weight.astype(jnp.float32)[None, :], axis=1)
    count_row = jnp.sum(corpus_table * counts[None, :], axis=1)
    all_count = jnp.sum(counts)
    factor = weight_row / DENOM * (all_count / (CORPORA * count_row))
    inputs = tokens_in.astype(jnp.float32)
    position = (
        lax.axis_index("seq") * shard_length + jnp.arange(shard_length, dtype=jnp.int32)
    ).astype(jnp.float32)
    gathered = (
        lax.all_gather(w_qkv, ("rows", "seq"), axis=0, tiled=True),
        lax.all_gather(w_out, ("rows", "seq"), axis=1, tiled=True),
        lax.all_gather(w_gate, ("rows", "seq"), axis=0, tiled=True),
        lax.all_gather(w_up, ("rows", "seq"), axis=0, tiled=True),
        lax.all_gather(w_down, ("rows", "seq"), axis=0, tiled=True),
        lax.all_gather(attn_gain, ("rows", "seq"), axis=0, tiled=True),
        lax.all_gather(ffn_gain, ("rows", "seq"), axis=0, tiled=True),
    )
    wqkv_full, wout_full, wgate_full, wup_full, wdown_full, attn_gain_full, ffn_gain_full = gathered
    normed_wide, norm_back = jax.vjp(rms_scale, inputs, attn_gain_full.astype(jnp.float32))
    normed = normed_wide.astype(jnp.bfloat16)
    joint_query_key_value = jnp.einsum(
        "btd,de->bte", normed, wqkv_full, preferred_element_type=jnp.float32
    )
    (queries, key_head_rows, value_head_rows), heads_back = jax.vjp(
        partial(heads_piece, position=position),
        joint_query_key_value,
        q_gain.astype(jnp.float32),
        k_gain.astype(jnp.float32),
    )
    query_units = queries.astype(jnp.bfloat16).reshape(
        batch_row_list, shard_length, unit_count, unit_width
    )
    key_units = jnp.einsum(
        "bthd,hu->btud",
        key_head_rows.astype(jnp.bfloat16),
        kv_select,
        preferred_element_type=jnp.float32,
    ).astype(jnp.bfloat16)
    value_units = jnp.einsum(
        "bthd,hu->btud",
        value_head_rows.astype(jnp.bfloat16),
        kv_select,
        preferred_element_type=jnp.float32,
    ).astype(jnp.bfloat16)
    payload = jnp.concatenate([query_units, key_units, value_units], axis=-1)
    outgoing = jnp.einsum(
        "btuc,us->btsc", payload, select_low, preferred_element_type=jnp.float32
    ).astype(jnp.bfloat16)
    outgoing = outgoing.reshape(
        batch_row_list, shard_length, seq_devices, capacity, payload.shape[-1]
    )
    mixed_slots, log_sums, kept_items = attend_items(
        lax.all_to_all(outgoing, "seq", split_axis=2, concat_axis=1, tiled=True),
        head_count=heads_in_group,
    )
    returned = lax.all_to_all(
        for_sending(mixed_slots), "seq", split_axis=1, concat_axis=2, tiled=True
    ).astype(mixed_slots.dtype)
    returned = returned.reshape(batch_row_list, shard_length, slot_total, unit_width)
    mixed_heads = jnp.einsum(
        "btsc,us->btuc", returned, select_low, preferred_element_type=jnp.float32
    ).astype(jnp.bfloat16)
    mixed_heads = mixed_heads.reshape(batch_row_list, shard_length, QUERY_HEADS * HEAD_SIZE)
    grad_full = upstream.astype(jnp.float32) * factor[:, None, None]
    grad_top = grad_full.astype(jnp.bfloat16)
    branch = jnp.einsum("btc,cd->btd", mixed_heads, wout_full, preferred_element_type=jnp.float32)
    middle = inputs + branch
    normed_ffn_wide, ffn_norm_back = jax.vjp(rms_scale, middle, ffn_gain_full.astype(jnp.float32))
    normed_ffn = normed_ffn_wide.astype(jnp.bfloat16)
    gate_values = jnp.einsum(
        "btd,df->btf", normed_ffn, wgate_full, preferred_element_type=jnp.float32
    )
    up_values = jnp.einsum("btd,df->btf", normed_ffn, wup_full, preferred_element_type=jnp.float32)
    hidden_wide, act_back = jax.vjp(activate, gate_values, up_values)
    hidden = hidden_wide.astype(jnp.bfloat16)
    ffn_values = jnp.einsum("btf,fd->btd", hidden, wdown_full, preferred_element_type=jnp.float32)
    output = (middle + ffn_values).astype(jnp.bfloat16)
    grad_wdown = jnp.einsum("btf,btd->fd", hidden, grad_top, preferred_element_type=jnp.float32)
    grad_hidden = jnp.einsum(
        "btd,fd->btf", grad_top, wdown_full, preferred_element_type=jnp.float32
    )
    gate_back, up_back = act_back(grad_hidden)
    gate_back = gate_back.astype(jnp.bfloat16)
    up_back = up_back.astype(jnp.bfloat16)
    grad_wgate = jnp.einsum(
        "btd,btf->df", normed_ffn, gate_back, preferred_element_type=jnp.float32
    )
    grad_wup = jnp.einsum("btd,btf->df", normed_ffn, up_back, preferred_element_type=jnp.float32)
    grad_normed_ffn = jnp.einsum(
        "btf,df->btd", gate_back, wgate_full, preferred_element_type=jnp.float32
    ) + jnp.einsum("btf,df->btd", up_back, wup_full, preferred_element_type=jnp.float32)
    grad_middle_part, grad_ffn_gain_local = ffn_norm_back(grad_normed_ffn)
    grad_middle = grad_full + grad_middle_part
    grad_branch = grad_middle.astype(jnp.bfloat16)
    grad_wout = jnp.einsum(
        "btc,btd->cd", mixed_heads, grad_branch, preferred_element_type=jnp.float32
    )
    grad_mixed = jnp.einsum(
        "btd,cd->btc", grad_branch, wout_full, preferred_element_type=jnp.float32
    ).astype(jnp.bfloat16)
    grad_units = grad_mixed.reshape(batch_row_list, shard_length, unit_count, unit_width)
    grad_outgoing = jnp.einsum(
        "btuc,us->btsc", grad_units, select_low, preferred_element_type=jnp.float32
    ).astype(jnp.bfloat16)
    grad_outgoing = grad_outgoing.reshape(
        batch_row_list, shard_length, seq_devices, capacity, unit_width
    )
    arrived = lax.all_to_all(grad_outgoing, "seq", split_axis=2, concat_axis=1, tiled=True)
    slot_grads = lax.map(
        partial(attend_backward, head_count=heads_in_group),
        (to_items(kept_items), to_items(log_sums), to_items(arrived)),
    )
    owner_grads = from_items(slot_grads, capacity)
    back_slots = lax.all_to_all(
        for_sending(owner_grads), "seq", split_axis=1, concat_axis=2, tiled=True
    ).astype(owner_grads.dtype)
    back_slots = back_slots.reshape(batch_row_list, shard_length, slot_total, 3 * unit_width)
    unit_gradient = jnp.einsum(
        "btsc,us->btuc", back_slots, select_low, preferred_element_type=jnp.float32
    )
    unit_gradient = unit_gradient.reshape(
        batch_row_list, shard_length, unit_count, 3, heads_in_group, HEAD_SIZE
    )
    grad_query = unit_gradient[:, :, :, 0].reshape(
        batch_row_list, shard_length, QUERY_HEADS, HEAD_SIZE
    )
    key_head_gradient = unit_gradient[:, :, :, 1].reshape(
        batch_row_list, shard_length, KEY_VALUE_HEADS, QUERY_HEADS // KEY_VALUE_HEADS, HEAD_SIZE
    )
    value_head_gradient = unit_gradient[:, :, :, 2].reshape(
        batch_row_list, shard_length, KEY_VALUE_HEADS, QUERY_HEADS // KEY_VALUE_HEADS, HEAD_SIZE
    )
    grad_key = jnp.sum(key_head_gradient, axis=3)
    grad_value = jnp.sum(value_head_gradient, axis=3)
    grad_joint, grad_q_local, grad_k_local = heads_back((grad_query, grad_key, grad_value))
    grad_joint = grad_joint.astype(jnp.bfloat16)
    grad_wqkv = jnp.einsum("btd,bte->de", normed, grad_joint, preferred_element_type=jnp.float32)
    grad_normed = jnp.einsum(
        "bte,de->btd", grad_joint, wqkv_full, preferred_element_type=jnp.float32
    )
    grad_input_part, grad_attn_gain_local = norm_back(grad_normed)
    input_grad = (grad_middle + grad_input_part).astype(jnp.bfloat16)
    summed = (
        lax.psum_scatter(grad_wqkv, ("rows", "seq"), scatter_dimension=0, tiled=True),
        lax.psum_scatter(grad_wout, ("rows", "seq"), scatter_dimension=1, tiled=True),
        lax.psum_scatter(grad_wgate, ("rows", "seq"), scatter_dimension=0, tiled=True),
        lax.psum_scatter(grad_wup, ("rows", "seq"), scatter_dimension=0, tiled=True),
        lax.psum_scatter(grad_wdown, ("rows", "seq"), scatter_dimension=0, tiled=True),
        lax.psum_scatter(grad_attn_gain_local, ("rows", "seq"), scatter_dimension=0, tiled=True),
        lax.psum_scatter(grad_ffn_gain_local, ("rows", "seq"), scatter_dimension=0, tiled=True),
    )
    gain_sums = lax.psum((grad_q_local, grad_k_local), ("rows", "seq"))
    return (
        output,
        input_grad,
        summed[0],
        summed[1],
        summed[2],
        summed[3],
        summed[4],
        summed[5],
        summed[6],
        gain_sums[0],
        gain_sums[1],
    )


def solution(mesh):
    return jax.shard_map(
        shards,
        mesh=mesh,
        in_specs=(
            P("rows", "seq", None),
            P("rows"),
            P(),
            P(("rows", "seq"), None),
            P(None, ("rows", "seq")),
            P(("rows", "seq"), None),
            P(("rows", "seq"), None),
            P(("rows", "seq"), None),
            P(("rows", "seq")),
            P(("rows", "seq")),
            P(),
            P(),
            P("rows", "seq", None),
        ),
        out_specs=(
            P("rows", "seq", None),
            P("rows", "seq", None),
            P(("rows", "seq"), None),
            P(None, ("rows", "seq")),
            P(("rows", "seq"), None),
            P(("rows", "seq"), None),
            P(("rows", "seq"), None),
            P(("rows", "seq")),
            P(("rows", "seq")),
            P(),
            P(),
        ),
        check_vma=False,
    )
```

profile of v0, /device:TPU:0, one launch (start us, length us, event | category | flops | bytes accessed | tf_op | source)
XLA Modules:
  0.0 2365.8 jit_solution(17439970237625097765)
XLA Ops:
  11.7 42.6 %all-reduce.14 = (bf16[2048]{0:T(1024)(128)(2,1)S(1)}, bf16[2048]{0:T(1024)(128)(2,1)}) all-reduce(bf16[2048]{0:T(1024)(128)(2,1)S(1)} %dynamic-update-slice.40, bf16[2048]{0:T(1024)(128)(2,1)S(1)} %dynamic-update-slice.41), channel_id=1, replica_groups=mesh['rows'=8,'seq'=4] {'rows','seq'}, use_global_device_ids=true, to_apply=%add.9 | all-reduce | flops 4096 | bytes 16384
  58.6 30.6 %all-gather.6.cloned.1.call-done = bf16[2048,1920]{1,0:T(8,128)(2,1)} async-done(((bf16[64,1920]{1,0:T(8,128)(2,1)}), bf16[2048,1920]{1,0:T(8,128)(2,1)}) %all-gather.6.cloned.1.call-update) | async-done | bytes 7864336 | tf_op jit(solution)/shard_map/all_gather | solution.py:247
  116.0 17.3 copy.162
  145.1 99.1 %all-to-all-done = bf16[1,512,4,3,256]{4,1,3,0,2:T(8,128)(2,1)S(1)} async-done(((bf16[1,512,4,3,256]{4,1,3,0,2:T(8,128)(2,1)}), bf16[1,512,4,3,256]{4,1,3,0,2:T(8,128)(2,1)S(1)}, u32[]{:S(2)}, u32[]{:S(2)}) %all-to-all-start) | async-done | bytes 3145760 | tf_op jit(solution)/shard_map/all_to_all | solution.py:290
  249.3 57.3 %while.35 = (s32[]{:T(128)}, bf16[3,2048,128]{1,2,0:T(8,128)(2,1)}, f32[3,2048,2]{1,2,0:T(2,128)S(1)}, bf16[3,2048,256]{1,2,0:T(8,128)(2,1)S(1)}, s32[]{:T(128)}) while((s32[]{:T(128)}, bf16[3,2048,128]{1,2,0:T(8,128)(2,1)}, f32[3,2048,2]{1,2,0:T(2,128)S(1)}, bf16[3,2048,256]{1,2,0:T(8,128)(2,1)S(1)}, s32[]{:T(128)}) %tuple.161), condition=%wide.region_12.13_spmd, body=%wide.region_3.12_spmd.sunk | while | flops 1407985152 | bytes 79606336 | solution.py:197
  316.3 81.5 %psum.21 = f32[8]{0:T(128)S(1)} all-reduce(f32[8]{0:T(128)S(1)} %fusion.170), channel_id=1, replica_groups=mesh['rows'=8,'seq'=4] {'rows','seq'}, use_global_device_ids=true, to_apply=%region_15.16 | all-reduce | flops 8 | bytes 64 | tf_op jit(solution)/shard_map/psum | solution.py:237
  434.0 37.4 %all-gather.12.cloned.1.call-done = bf16[2048,4608]{1,0:T(8,128)(2,1)} async-done(((bf16[64,4608]{1,0:T(8,128)(2,1)}), bf16[2048,4608]{1,0:T(8,128)(2,1)}) %all-gather.12.cloned.1.call-update) | async-done | bytes 18874384 | tf_op jit(solution)/shard_map/all_gather | solution.py:250
  471.4 16.5 fusion.180
  488.0 109.0 %all-gather.14.cloned.1.call-done = bf16[4608,2048]{1,0:T(8,128)(2,1)} async-done(((bf16[144,2048]{1,0:T(8,128)(2,1)}), bf16[4608,2048]{1,0:T(8,128)(2,1)}) %all-gather.14.cloned.1.call-update) | async-done | bytes 18874384 | tf_op jit(solution)/shard_map/all_gather | solution.py:251
  596.9 25.2 %multiply_convert_fusion = (bf16[512,4608]{1,0:T(8,128)(2,1)}, bf16[512,4608]{1,0:T(8,128)(2,1)}, bf16[512,4608]{1,0:T(8,128)(2,1)}) fusion(f32[512,4608]{1,0:T(8,128)} %fusion.179, f32[512,4608]{1,0:T(8,128)} %fusion.180, bf16[4608,2048]{1,0:T(8,128)(2,1)} %all-gather.14.cloned.1.call-done, bf16[1,512,2048]{2,1,0:T(8,128)(2,1)S(1)} %copy-done.34, ...), kind=kOutput, calls=%fused_computation.172 | convolution fusion | flops 9704570880 | bytes 54001668 | tf_op jit(solution)/shard_map/btd,fd->btf/dot_general | solution.py:316
  622.2 16.5 fusion.181
  638.6 19.8 fusion.130
  688.0 53.8 %all-to-all-done.2 = bf16[1,512,4,3,128]{4,1,3,0,2:T(8,128)(2,1)S(1)} async-done(((bf16[1,512,4,3,128]{4,1,3,0,2:T(8,128)(2,1)}), bf16[1,512,4,3,128]{4,1,3,0,2:T(8,128)(2,1)S(1)}, u32[]{:S(2)}, u32[]{:S(2)}) %all-to-all-start.2) | async-done | bytes 1572896 | tf_op jit(solution)/shard_map/all_to_all | solution.py:345
  743.1 184.4 %while.36 = (s32[]{:T(128)}, bf16[3,2048,384]{1,2,0:T(8,128)(2,1)}, bf16[3,2048,256]{1,2,0:T(8,128)(2,1)}, f32[3,2048,2]{1,2,0:T(2,128)}, bf16[3,2048,128]{2,1,0...) while((s32[]{:T(128)}, bf16[3,2048,384]{1,2,0:T(8,128)(2,1)}, ...), condition=%wide.region_24.25_spmd, body=%wide.region_19.24_spmd.sunk | while | flops 3436443136 | bytes 336573792 | solution.py:346
  937.8 139.5 %all_to_all.66 = bf16[1,2048,1,3,384]{4,3,2,0,1:T(4,128)(2,1)S(1)} all-to-all(bf16[1,2048,1,3,384]{4,3,2,0,1:T(4,128)(2,1)} %bitcast.771), channel_id=1, replica_groups=mesh['rows'=8,'seq'=4] {'seq'}, dimensions={1} | all-to-all | bytes 9437184 | tf_op jit(solution)/shard_map/all_to_all | solution.py:351
  1125.5 20.3 fusion.182
  1145.8 20.2 fusion.183
  1167.7 18.6 fusion.145
  1186.4 16.9 fusion.132
  1213.2 38.0 %all-reduce.13 = (f32[2048]{0:T(1024)S(1)}, f32[2048]{0:T(1024)S(1)}, f32[64]{0:T(128)}, f32[64]{0:T(128)}) all-reduce(f32[2048]{0:T(1024)S(1)} %get-tuple-element.265, f32[2048]{0:T(1024)S(1)} %copy-done.64, f32[64]{0:T(128)S(1)} %get-tuple-element.267, ...), channel_id=7, replica_groups=mesh['rows'=8,'seq'=4] {'rows','seq'}, use_global_device_ids=true, to_apply=%region_38.39.clone | all-reduce | flops 4224 | bytes 33792
  1258.4 34.8 %reduce-scatter.6.cloned.1.call-done = f32[64,1920]{1,0:T(8,128)} async-done(((f32[2048,1920]{1,0:T(8,128)}), f32[64,1920]{1,0:T(8,128)}) %reduce-scatter.6.cloned.1.call-update) | async-done | bytes 491536 | tf_op jit(solution)/shard_map/reduce_scatter | solution.py:381
  1293.2 354.8 %reduce-scatter.10.cloned.1.call-done = f32[64,4608]{1,0:T(8,128)} async-done(((f32[2048,4608]{1,0:T(8,128)}), f32[64,4608]{1,0:T(8,128)}) %reduce-scatter.10.cloned.1.call-update) | async-done | bytes 1179664 | tf_op jit(solution)/shard_map/reduce_scatter | solution.py:383
  1648.0 356.1 %reduce-scatter.12.cloned.1.call-done = f32[64,4608]{1,0:T(8,128)} async-done(((f32[2048,4608]{1,0:T(8,128)}), f32[64,4608]{1,0:T(8,128)}) %reduce-scatter.12.cloned.1.call-update) | async-done | bytes 1179664 | tf_op jit(solution)/shard_map/reduce_scatter | solution.py:384
  2004.1 354.7 %reduce-scatter.14.cloned.1.call-done = f32[144,2048]{1,0:T(8,128)} async-done(((f32[4608,2048]{1,0:T(8,128)}), f32[144,2048]{1,0:T(8,128)}) %reduce-scatter.14.cloned.1.call-update) | async-done | bytes 1179664 | tf_op jit(solution)/shard_map/reduce_scatter | solution.py:385
  (562 shorter events, 442.1 us)
Async XLA Ops:
  7.2 82.1 %all-gather.6.cloned.1.call-start = ((), (), s32[]{:S(2)}) async-start(), calls=%async_computation.9 | async-start | bytes 8110080 | tf_op jit(solution)/shard_map/all_gather | solution.py:247
  7.9 400.8 %all-gather.8.cloned.1.call-start = ((), (), s32[]{:S(2)}) async-start(), calls=%async_computation.10 | async-start | bytes 5406720 | tf_op jit(solution)/shard_map/all_gather | solution.py:248
  8.7 408.0 %all-gather.10.cloned.1.call-start = ((), (), s32[]{:S(2)}) async-start(), calls=%async_computation.11 | async-start | bytes 19464192 | tf_op jit(solution)/shard_map/all_gather | solution.py:249
  9.4 462.0 %all-gather.12.cloned.1.call-start = ((), (), s32[]{:S(2)}) async-start(), calls=%async_computation.12 | async-start | bytes 19464192 | tf_op jit(solution)/shard_map/all_gather | solution.py:250
  55.0 48.3 %copy-start.67 = (f32[64]{0:T(128)}, f32[64]{0:T(128)S(1)}, u32[]{:S(2)}) copy-start(f32[64]{0:T(128)S(1)} %convert_element_type.332) | copy-start | bytes 772
  55.6 53.4 %copy-start.65 = (f32[64]{0:T(128)}, f32[64]{0:T(128)S(1)}, u32[]{:S(2)}) copy-start(f32[64]{0:T(128)S(1)} %convert_element_type.335) | copy-start | bytes 772
  58.6 51.4 %copy-start.39 = (f32[512,32]{0,1:T(8,128)}, f32[512,32]{0,1:T(8,128)S(1)}, u32[]{:S(2)}) copy-start(f32[512,32]{0,1:T(8,128)S(1)} %get-tuple-element.345) | copy-start | bytes 196612
  58.6 51.4 %copy-start.41 = (f32[512,32]{0,1:T(8,128)}, f32[512,32]{0,1:T(8,128)S(1)}, u32[]{:S(2)}) copy-start(f32[512,32]{0,1:T(8,128)S(1)} %get-tuple-element.346) | copy-start | bytes 196612
  140.7 103.5 %all-to-all-start = ((bf16[1,512,4,3,256]{4,1,3,0,2:T(8,128)(2,1)}), bf16[1,512,4,3,256]{4,1,3,0,2:T(8,128)(2,1)S(1)}, u32[]{:S(2)}, u32[]{:S(2)}) async-start(bf16[1,512,4,3,256]{4,1,3,0,2:T(8,128)(2,1)} %bitcast.104), calls=%async_computation | async-start | bytes 6291456 | tf_op jit(solution)/shard_map/all_to_all | solution.py:290
  144.5 452.5 %all-gather.14.cloned.1.call-start = ((), (), s32[]{:S(2)}) async-start(), calls=%async_computation.13 | async-start | bytes 19464192 | tf_op jit(solution)/shard_map/all_gather | solution.py:251
  306.6 96.3 %copy-start.14 = (bf16[3,2048,256]{1,2,0:T(8,128)(2,1)}, bf16[3,2048,256]{1,2,0:T(8,128)(2,1)S(1)}, u32[]{:S(2)}) copy-start(bf16[3,2048,256]{1,2,0:T(8,128)(2,1)S(1)} %get-tuple-element.537) | copy-start | bytes 9437188
  306.6 96.3 %copy-start.53 = (f32[3,2048,2]{1,2,0:T(2,128)}, f32[3,2048,2]{1,2,0:T(2,128)S(1)}, u32[]{:S(2)}) copy-start(f32[3,2048,2]{1,2,0:T(2,128)S(1)} %get-tuple-element.497) | copy-start | bytes 147460
  306.6 91.2 %copy-start.69 = (bf16[2048]{0:T(1024)(128)(2,1)S(1)}, bf16[2048]{0:T(1024)(128)(2,1)}, u32[]{:S(2)}) copy-start(bf16[2048]{0:T(1024)(128)(2,1)} %get-tuple-element.296) | copy-start | bytes 12292
  306.6 93.1 %copy-start.70 = (s32[8]{0:T(128)S(1)}, s32[8]{0:T(128)}, u32[]{:S(2)}) copy-start(s32[8]{0:T(128)} %param.41) | copy-start | bytes 100
  311.2 89.8 %all-to-all-start.1 = ((bf16[1,2048,1,3,128]{4,3,2,0,1:T(4,128)(2,1)}), bf16[1,2048,1,3,128]{4,3,2,0,1:T(4,128)(2,1)}, u32[]{:S(2)}, u32[]{:S(2)}) async-start(bf16[1,2048,1,3,128]{4,3,2,0,1:T(4,128)(2,1)} %bitcast.789), calls=%async_computation.1 | async-start | bytes 4194304 | tf_op jit(solution)/shard_map/all_to_all | solution.py:293
  315.7 87.3 %copy-start.55 = (bf16[10,12,1]{0,1,2:T(8,128)(2,1)S(1)}, bf16[10,12,1]{0,1,2:T(8,128)(2,1)}, u32[]{:S(2)}) copy-start(bf16[10,12,1]{0,1,2:T(8,128)(2,1)} %constant.413) | copy-start | bytes 724
  434.0 162.9 %copy-start.34 = (bf16[1,512,2048]{2,1,0:T(8,128)(2,1)S(1)}, bf16[1,512,2048]{2,1,0:T(8,128)(2,1)}, u32[]{:S(2)}) copy-start(bf16[1,512,2048]{2,1,0:T(8,128)(2,1)} %param.51) | copy-start | bytes 6291460
  675.3 66.5 %all-to-all-start.2 = ((bf16[1,512,4,3,128]{4,1,3,0,2:T(8,128)(2,1)}), bf16[1,512,4,3,128]{4,1,3,0,2:T(8,128)(2,1)S(1)}, u32[]{:S(2)}, u32[]{:S(2)}) async-start(bf16[1,512,4,3,128]{4,1,3,0,2:T(8,128)(2,1)} %bitcast.144), calls=%async_computation.2 | async-start | bytes 3145728 | tf_op jit(solution)/shard_map/all_to_all | solution.py:345
  678.9 579.5 %reduce-scatter.8.cloned.1.call-start = ((), (), s32[]{:S(2)}) async-start(), calls=%async_computation.15 | async-start | bytes 10813440 | tf_op jit(solution)/shard_map/reduce_scatter | solution.py:382
  687.9 605.2 %reduce-scatter.6.cloned.1.call-start = ((), (), s32[]{:S(2)}) async-start(), calls=%async_computation.14 | async-start | bytes 16220160 | tf_op jit(solution)/shard_map/reduce_scatter | solution.py:381
  1123.9 524.1 %reduce-scatter.10.cloned.1.call-start = ((), (), s32[]{:S(2)}) async-start(), calls=%async_computation.16 | async-start | bytes 38928384 | tf_op jit(solution)/shard_map/reduce_scatter | solution.py:383
  1145.8 858.3 %reduce-scatter.12.cloned.1.call-start = ((), (), s32[]{:S(2)}) async-start(), calls=%async_computation.17 | async-start | bytes 38928384 | tf_op jit(solution)/shard_map/reduce_scatter | solution.py:384
  1166.0 1192.7 %reduce-scatter.14.cloned.1.call-start = ((), (), s32[]{:S(2)}) async-start(), calls=%async_computation.18 | async-start | bytes 38928384 | tf_op jit(solution)/shard_map/reduce_scatter | solution.py:385
  1203.3 49.1 %copy-start.60 = (f32[512]{0:T(512)S(1)}, f32[512]{0:T(512)}, u32[]{:S(2)}) copy-start(f32[512]{0:T(512)} %copy-done.59) | copy-start | bytes 6148
  (111 other events, 581.8 us)
Sparse Core Ops, SparseCore 0:
  10.8 78.3 all-gather.5
  92.1 83.9 all-gather.7
  178.8 155.2 all-gather.9
  336.8 134.5 all-gather.11
  474.1 122.8 all-gather.13
  688.0 245.6 reduce-scatter.7
  1124.0 169.0 reduce-scatter.5
  1300.2 347.8 reduce-scatter.9
  1656.1 347.8 reduce-scatter.11
  2010.9 347.8 reduce-scatter.13
where the time goes:
time: 2380 us; the launch traced here: 2370 us
  waiting for transfers between devices  1430 us (60%)
  matrix products  384 us (16%)
  blocking collectives  302 us (13%)
  local copies, waits for them, and re-layouts  122 us (5%)
  other arithmetic  92.4 us (4%)
    reduce_scatter x1, waiting for transfers between devices, shards(): lax.psum_scatter(grad_wup, ('rows', 'seq'), scatter_dimension=0, tiled=True)  356 us
    reduce_scatter x1, waiting for transfers between devices, shards(): lax.psum_scatter(grad_wgate, ('rows', 'seq'), scatter_dimension=0, tiled=...  355 us
    reduce_scatter x1, waiting for transfers between devices, shards(): lax.psum_scatter(grad_wdown, ('rows', 'seq'), scatter_dimension=0, tiled=...  355 us
    all_to_all x1, blocking collectives, shards(): lax.all_to_all(for_sending(owner_grads), 'seq', split_axis=1, concat_axis...  139 us
    all_gather x1, waiting for transfers between devices, shards(): lax.all_gather(w_down, ('rows', 'seq'), axis=0, tiled=True)  109 us
    all_to_all x1, waiting for transfers between devices, shards(): lax.all_to_all(outgoing, 'seq', split_axis=2, concat_axis=1, tiled=True)  99.1 us
    psum x1, blocking collectives, shards(): lax.psum(jnp.sum(corpus_table, axis=0) * shard_length, ('rows', 'seq'))  81.5 us
    unnamed x2, blocking collectives  80.6 us
  transfers between devices with their start and end apart: 13, of which 9 were waited for; matrix products, arithmetic and copies ran while one was open for 21% of the time, Pallas kernels for 0%

commit v1 on v0

v1 whole, which is shorter than its diff:
```python
from functools import partial

import jax
import jax.numpy as jnp
from jax import lax
from jax.experimental import pallas as pl
from jax.experimental.pallas import tpu as pltpu
from jax.sharding import PartitionSpec as P

QUERY_HEADS = 20
KEY_VALUE_HEADS = 5
HEAD_SIZE = 64
CORPORA = 8
DENOM = 64
EPSILON = 1e-06
ROPE_BASE = 10000.0
QUERY_COLUMNS = QUERY_HEADS * HEAD_SIZE
KEY_COLUMNS = KEY_VALUE_HEADS * HEAD_SIZE
LANES = 128
SCORE_EXPONENT = 1.4426950408889634 * HEAD_SIZE**-0.5
VMEM_LIMIT = 48 * 1024 * 1024

f32, bf16 = jnp.float32, jnp.bfloat16


def dot_nn(a, b):
    return lax.dot_general(a, b, (((1,), (0,)), ((), ())), preferred_element_type=f32)


def dot_nt(a, b):
    return lax.dot_general(a, b, (((1,), (1,)), ((), ())), preferred_element_type=f32)


def dot_tn(a, b):
    return lax.dot_general(a, b, (((0,), (0,)), ((), ())), preferred_element_type=f32)


def lanes_of(shape):
    return lax.broadcasted_iota(jnp.int32, shape, len(shape) - 1)


def head_sum(values):
    row = lax.broadcasted_iota(jnp.int32, (LANES, LANES), 0) // HEAD_SIZE
    column = lax.broadcasted_iota(jnp.int32, (LANES, LANES), 1) // HEAD_SIZE
    ones = jnp.where(row == column, 1.0, 0.0).astype(bf16)
    high = values.astype(bf16)
    low = (values - high.astype(f32)).astype(bf16)
    return dot_nn(high, ones) + dot_nn(low, ones)


def partner(values):
    first = lanes_of(values.shape) % HEAD_SIZE < HEAD_SIZE // 2
    return jnp.where(
        first,
        pltpu.roll(values, LANES - HEAD_SIZE // 2, 1),
        pltpu.roll(values, HEAD_SIZE // 2, 1),
    )


def heads_forward_kernel(norm_columns, joint_ref, gain_ref, cos_ref, sin_ref, out_ref):
    values = joint_ref[...]
    scale = lax.rsqrt(head_sum(values * values) * (1.0 / HEAD_SIZE) + EPSILON)
    normed = values * scale * gain_ref[0:1, :]
    turned = normed * cos_ref[...] + partner(normed) * sin_ref[...]
    place = pl.program_id(0) * LANES + lanes_of(values.shape)
    out_ref[...] = jnp.where(place < norm_columns, turned, values).astype(bf16)


def heads_forward(joint, gain, cos, sin, norm_columns):
    tokens, columns = joint.shape
    return pl.pallas_call(
        partial(heads_forward_kernel, norm_columns),
        grid=(columns // LANES,),
        in_specs=[
            pl.BlockSpec((tokens, LANES), lambda i: (0, i)),
            pl.BlockSpec((8, LANES), lambda i: (0, i)),
            pl.BlockSpec((tokens, LANES), lambda i: (0, 0)),
            pl.BlockSpec((tokens, LANES), lambda i: (0, 0)),
        ],
        out_specs=pl.BlockSpec((tokens, LANES), lambda i: (0, i)),
        out_shape=jax.ShapeDtypeStruct((tokens, columns), bf16),
        name="heads_forward",
        cost_estimate=pl.CostEstimate(
            flops=tokens * columns * 256, bytes_accessed=tokens * columns * 6, transcendentals=0
        ),
    )(joint, gain, cos, sin)


def heads_backward_kernel(
    norm_columns, grad_ref, joint_ref, gain_ref, cos_ref, sin_ref, out_ref, gain_out_ref
):
    grad = grad_ref[...].astype(f32)
    values = joint_ref[...]
    gain = gain_ref[0:1, :]
    turned = grad * cos_ref[...] - partner(grad) * sin_ref[...]
    scale = lax.rsqrt(head_sum(values * values) * (1.0 / HEAD_SIZE) + EPSILON)
    gained = turned * gain
    inner = head_sum(values * gained) * (1.0 / HEAD_SIZE)
    result = scale * gained - values * (scale * scale * scale) * inner
    place = pl.program_id(0) * LANES + lanes_of(values.shape)
    out_ref[...] = jnp.where(place < norm_columns, result, grad).astype(bf16)
    gain_out_ref[...] = jnp.broadcast_to(
        jnp.sum(turned * values * scale, axis=0, keepdims=True), gain_out_ref.shape
    )


def heads_backward(grad, joint, gain, cos, sin, norm_columns):
    tokens, columns = joint.shape
    return pl.pallas_call(
        partial(heads_backward_kernel, norm_columns),
        grid=(columns // LANES,),
        in_specs=[
            pl.BlockSpec((tokens, LANES), lambda i: (0, i)),
            pl.BlockSpec((tokens, LANES), lambda i: (0, i)),
            pl.BlockSpec((8, LANES), lambda i: (0, i)),
            pl.BlockSpec((tokens, LANES), lambda i: (0, 0)),
            pl.BlockSpec((tokens, LANES), lambda i: (0, 0)),
        ],
        out_specs=[
            pl.BlockSpec((tokens, LANES), lambda i: (0, i)),
            pl.BlockSpec((8, LANES), lambda i: (0, i)),
        ],
        out_shape=[
            jax.ShapeDtypeStruct((tokens, columns), bf16),
            jax.ShapeDtypeStruct((8, columns), f32),
        ],
        name="heads_backward",
        cost_estimate=pl.CostEstimate(
            flops=tokens * columns * 512, bytes_accessed=tokens * columns * 10, transcendentals=0
        ),
    )(grad, joint, gain, cos, sin)


def both_halves(pair, odd):
    wide = pair.astype(f32)
    first = lanes_of(wide.shape) < HEAD_SIZE
    keep = jnp.where(odd == 1, jnp.where(first, 0, 1), jnp.where(first, 1, 0)) == 1
    return jnp.where(keep, wide, pltpu.roll(wide, HEAD_SIZE, 1))


def attend_forward_kernel(place_ref, q_ref, k_ref, v_ref, out_ref, log_ref):
    group = pl.program_id(0) // 2
    place = place_ref[0]
    tokens = q_ref.shape[0]
    first = lanes_of((tokens, LANES)) < HEAD_SIZE
    pair = q_ref[...].astype(f32)
    queries = (jnp.where(first, pair, 0.0).astype(bf16), jnp.where(first, 0.0, pair).astype(bf16))

    def step(j, totals, diagonal):
        rows = pl.ds(pl.multiple_of(j * tokens, tokens), tokens)
        keys = both_halves(k_ref[rows, :], group % 2).astype(bf16)
        values = both_halves(v_ref[rows, :], (KEY_VALUE_HEADS + group) % 2)
        sides = (
            jnp.where(first, values, 1.0).astype(bf16),
            jnp.where(first, 1.0, values).astype(bf16),
        )
        result = []
        for head in range(2):
            weights = jnp.exp2(dot_nt(queries[head], keys) * SCORE_EXPONENT)
            if diagonal:
                row = lax.broadcasted_iota(jnp.int32, weights.shape, 0)
                weights = jnp.where(lanes_of(weights.shape) <= row, weights, 0.0)
            result.append(totals[head] + dot_nn(weights.astype(bf16), sides[head]))
        return tuple(result)

    zero = jnp.zeros((tokens, LANES), f32)
    totals = lax.fori_loop(0, place, lambda j, c: step(j, c, False), (zero, zero))
    totals = step(place, totals, True)
    numerator = jnp.where(first, totals[0], totals[1])
    swapped = jnp.where(first, totals[1], totals[0])
    out_ref[...] = (numerator / pltpu.roll(swapped, HEAD_SIZE, 1)).astype(bf16)
    log_ref[...] = jnp.log2(swapped)


def attend_forward(place, queries, keys_values):
    tokens = queries.shape[0]
    length = keys_values.shape[0]
    pairs = QUERY_COLUMNS // LANES
    return pl.pallas_call(
        attend_forward_kernel,
        grid_spec=pltpu.PrefetchScalarGridSpec(
            num_scalar_prefetch=1,
            grid=(pairs,),
            in_specs=[
                pl.BlockSpec((tokens, LANES), lambda i, s: (0, i)),
                pl.BlockSpec((length, LANES), lambda i, s: (0, (i // 2) // 2)),
                pl.BlockSpec((length, LANES), lambda i, s: (0, (KEY_VALUE_HEADS + i // 2) // 2)),
            ],
            out_specs=[
                pl.BlockSpec((tokens, LANES), lambda i, s: (0, i)),
                pl.BlockSpec((tokens, LANES), lambda i, s: (0, i)),
            ],
        ),
        out_shape=[
            jax.ShapeDtypeStruct((tokens, QUERY_COLUMNS), bf16),
            jax.ShapeDtypeStruct((tokens, QUERY_COLUMNS), f32),
        ],
        compiler_params=pltpu.CompilerParams(vmem_limit_bytes=VMEM_LIMIT),
        name="attend_forward",
        cost_estimate=pl.CostEstimate(
            flops=QUERY_HEADS * tokens * length * 800,
            bytes_accessed=tokens * QUERY_COLUMNS * 8 + length * 1280,
            transcendentals=QUERY_HEADS * tokens * length,
        ),
    )(place, queries, keys_values, keys_values)


def three_parts(values, lane):
    high = values.astype(bf16).astype(f32)
    rest = values - high
    middle = rest.astype(bf16).astype(f32)
    low = rest - middle
    return jnp.where(
        lane == 0, high, jnp.where(lane == 1, middle, jnp.where(lane == 2, low, 0.0))
    )


def attend_backward_kernel(
    place_ref, q_ref, k_ref, v_ref, out_ref, log_ref, grad_ref, dq_ref, dkv_ref, dk_sum, dv_sum
):
    pair_index = pl.program_id(0)
    group = pair_index // 2
    place = place_ref[0]
    tokens = q_ref.shape[0]
    lane = lanes_of((tokens, LANES))
    first = lane < HEAD_SIZE
    inside = lane % HEAD_SIZE
    pair = q_ref[...].astype(f32)
    grad = grad_ref[...].astype(f32)
    delta = pltpu.roll(head_sum(grad * out_ref[...].astype(f32)), HEAD_SIZE, 1)
    logs = three_parts(log_ref[...] * (1.0 / SCORE_EXPONENT), inside)
    deltas = three_parts(delta, inside)
    minus = jnp.where(inside < 3, -1.0, 0.0)

    def sides(own, other):
        return (
            jnp.where(first, own, other).astype(bf16),
            jnp.where(first, other, own).astype(bf16),
        )

    queries = sides(pair, 0.0)
    grads = sides(grad, 0.0)
    queries_log = sides(pair, logs)
    grads_delta = sides(grad, deltas)

    @pl.when(pair_index % 2 == 0)
    def _():
        dk_sum[...] = jnp.zeros_like(dk_sum)
        dv_sum[...] = jnp.zeros_like(dv_sum)

    def step(j, dq, diagonal):
        rows = pl.ds(pl.multiple_of(j * tokens, tokens), tokens)
        key_wide = both_halves(k_ref[rows, :], group % 2)
        value_wide = both_halves(v_ref[rows, :], (KEY_VALUE_HEADS + group) % 2)
        keys = sides(key_wide, 0.0)
        keys_log = sides(key_wide, minus)
        values_delta = sides(value_wide, minus)
        dk = dk_sum[rows, :]
        dv = dv_sum[rows, :]
        for head in range(2):
            weights = jnp.exp2(dot_nt(keys_log[head], queries_log[head]) * SCORE_EXPONENT)
            if diagonal:
                row = lax.broadcasted_iota(jnp.int32, weights.shape, 0)
                weights = jnp.where(row <= lanes_of(weights.shape), weights, 0.0)
            grad_weights = dot_nt(values_delta[head], grads_delta[head])
            grad_scores = (weights * grad_weights).astype(bf16)
            dv = dv + dot_nn(weights.astype(bf16), grads[head])
            dk = dk + dot_nn(grad_scores, queries[head])
            dq = dq + dot_tn(grad_scores, keys[head])
        dk_sum[rows, :] = dk
        dv_sum[rows, :] = dv
        return dq

    dq = lax.fori_loop(
        0, place, lambda j, c: step(j, c, False), jnp.zeros((tokens, LANES), f32)
    )
    dq = step(place, dq, True)
    dq_ref[...] = (dq * HEAD_SIZE**-0.5).astype(bf16)

    @pl.when(pair_index % 2 == 1)
    def _():
        wide_lane = lanes_of(dk_sum.shape)
        for total, slot, factor in (
            (dk_sum, group, HEAD_SIZE**-0.5),
            (dv_sum, KEY_VALUE_HEADS + group, 1.0),
        ):
            both = (total[...] + pltpu.roll(total[...], HEAD_SIZE, 1)) * factor
            columns = pl.ds(pl.multiple_of(slot // 2 * LANES, LANES), LANES)
            mine = wide_lane // HEAD_SIZE == slot % 2
            dkv_ref[:, columns] = jnp.where(
                mine, both, dkv_ref[:, columns].astype(f32)
            ).astype(bf16)


def attend_backward(place, queries, keys_values, mixed, logs, grad_mixed):
    tokens = queries.shape[0]
    length = keys_values.shape[0]
    pairs = QUERY_COLUMNS // LANES
    own = pl.BlockSpec((tokens, LANES), lambda i, s: (0, i))
    return pl.pallas_call(
        attend_backward_kernel,
        grid_spec=pltpu.PrefetchScalarGridSpec(
            num_scalar_prefetch=1,
            grid=(pairs,),
            in_specs=[
                own,
                pl.BlockSpec((length, LANES), lambda i, s: (0, (i // 2) // 2)),
                pl.BlockSpec((length, LANES), lambda i, s: (0, (KEY_VALUE_HEADS + i // 2) // 2)),
                own,
                own,
                own,
            ],
            out_specs=[
                own,
                pl.BlockSpec((length, 2 * KEY_COLUMNS), lambda i, s: (0, 0)),
            ],
            scratch_shapes=[pltpu.VMEM((length, LANES), f32), pltpu.VMEM((length, LANES), f32)],
        ),
        out_shape=[
            jax.ShapeDtypeStruct((tokens, QUERY_COLUMNS), bf16),
            jax.ShapeDtypeStruct((length, 2 * KEY_COLUMNS), bf16),
        ],
        compiler_params=pltpu.CompilerParams(vmem_limit_bytes=VMEM_LIMIT),
        name="attend_backward",
        cost_estimate=pl.CostEstimate(
            flops=QUERY_HEADS * tokens * length * 2000,
            bytes_accessed=tokens * QUERY_COLUMNS * 12 + length * 2560,
            transcendentals=QUERY_HEADS * tokens * length,
        ),
    )(place, queries, keys_values, keys_values, mixed, logs, grad_mixed)


def swap(values, bit):
    pairs = [(i, i ^ bit) for i in range(lax.axis_size("rows"))]
    return lax.ppermute(values, "rows", pairs)


def bit_of(bit):
    return (lax.axis_index("rows") // bit) % 2


def joined(own, other, side, axis):
    low = jnp.where(side == 0, own, other)
    high = jnp.where(side == 0, other, own)
    return jnp.stack([low, high], axis)


def gather_bit(values, bit, axis):
    return joined(values, swap(values, bit), bit_of(bit), axis)


def part(values, index, axis):
    return lax.dynamic_index_in_dim(values, index, axis, keepdims=False)


def reduce_bit(values, bit, axis):
    side = bit_of(bit)
    other = swap(part(values, 1 - side, axis), bit)
    return (part(values, side, axis).astype(f32) + other.astype(f32)).astype(bf16)


def outer_pairs(step, low, high):
    size = lax.axis_size("rows")
    return [
        (i, i + 4 * step)
        for i in range(size)
        if low <= i // 4 < high and 0 <= i // 4 + step < size // 4
    ]


def gather_outer(values, axis):
    count = lax.axis_size("rows") // 4
    if count == 1:
        return jnp.expand_dims(values, axis)
    if count == 2:
        return gather_bit(values, 4, axis)
    place = lax.axis_index("rows") // 4
    up, down = values, values
    ups, downs = [], []
    for t in range(1, count):
        up = lax.ppermute(up, "rows", outer_pairs(1, t - 1, count))
        down = lax.ppermute(down, "rows", outer_pairs(-1, 0, count - t + 1))
        ups.append(up)
        downs.append(down)
    line = jnp.stack(ups[::-1] + [values] + downs, axis)
    return lax.dynamic_slice_in_dim(line, count - 1 - place, count, axis)


def reduce_outer(values, axis):
    count = lax.axis_size("rows") // 4
    if count == 1:
        return jnp.squeeze(values, axis)
    if count == 2:
        return reduce_bit(values, 4, axis)
    place = lax.axis_index("rows") // 4

    def entry(index):
        return part(values, jnp.clip(index, 0, count - 1), axis)

    up, down = entry(place + count - 1), entry(place - count + 1)
    for t in range(1, count):
        up = lax.ppermute(up, "rows", outer_pairs(1, 0, t)).astype(f32)
        down = lax.ppermute(down, "rows", outer_pairs(-1, count - t, count)).astype(f32)
        if t < count - 1:
            up = (entry(place + count - 1 - t).astype(f32) + up).astype(bf16)
            down = (entry(place - count + 1 + t).astype(f32) + down).astype(bf16)
    return (entry(place).astype(f32) + up + down).astype(bf16)


def gather_seq(values):
    return lax.all_gather(values, "seq", axis=0, tiled=False)


def reduce_seq(values):
    return lax.psum_scatter(values, "seq", scatter_dimension=0, tiled=False)


def split_columns(columns):
    return columns // LANES // 2 * LANES


def gather_all(shard):
    columns = shard.shape[1]
    half = split_columns(columns)
    lines = gather_seq(shard)
    left = gather_bit(gather_outer(lines[..., :half], 0), 2, 1)
    right = gather_outer(gather_bit(lines[..., half:], 2, 0), 0)
    both = jnp.concatenate([left, right], axis=-1)
    return gather_bit(both, 1, 2).reshape(-1, columns)


def reduce_all(values, rows):
    columns = values.shape[1]
    half = split_columns(columns)
    seq = lax.axis_size("seq")
    blocks = values.reshape(-1, 2, 2, seq, rows, columns)
    blocks = reduce_bit(blocks, 1, 2)
    left = reduce_outer(reduce_bit(blocks[..., :half], 2, 1), 0)
    right = reduce_bit(reduce_outer(blocks[..., half:], 0), 2, 0)
    return reduce_seq(jnp.concatenate([left, right], axis=-1))


def gather_group(values):
    other = swap(values, 1)
    across = swap(values, 2)
    far = swap(across, 1)
    return jnp.concatenate([values, other, across, far], axis=0)


def reduce_group(values):
    tokens = values.shape[0] // 4
    parts = values.reshape(2, 2, tokens, values.shape[1])
    across = parts[1, 0] + swap(parts[1, 1].astype(bf16), 1).astype(f32)
    across = swap(across.astype(bf16), 2).astype(f32)
    own = parts[0, 0] + swap(parts[0, 1].astype(bf16), 1).astype(f32)
    return own + across


def mm(left, right):
    return jnp.einsum("ab,bc->ac", left, right, preferred_element_type=f32)


def mm_t(left, right):
    return jnp.einsum("ab,cb->ac", left, right, preferred_element_type=f32)


def t_mm(left, right):
    return jnp.einsum("ab,ac->bc", left, right, preferred_element_type=f32)


def norm_scale(values):
    return lax.rsqrt(jnp.mean(values * values, axis=-1, keepdims=True) + EPSILON)


def norm_backward(values, scale, gain, grad):
    gained = grad * gain
    inner = jnp.mean(values * gained, axis=-1, keepdims=True)
    result = scale * gained - values * (scale * scale * scale) * inner
    return result, jnp.sum(grad * values * scale, axis=0)


def shards(
    tokens_in,
    corpus,
    corpus_weight,
    w_qkv,
    w_out,
    w_gate,
    w_up,
    w_down,
    attn_gain,
    ffn_gain,
    q_gain,
    k_gain,
    upstream,
):
    shard_length, width = tokens_in.shape[1:]
    row_devices = lax.axis_size("rows")
    seq_devices = lax.axis_size("seq")
    outer = row_devices // 4
    d_rows = w_qkv.shape[0]
    f_rows = w_down.shape[0]
    place = lax.axis_index("seq").astype(jnp.int32)
    inputs = tokens_in[0].astype(f32)

    extra = jnp.stack(
        [
            attn_gain,
            ffn_gain,
            jnp.broadcast_to(corpus.astype(bf16), attn_gain.shape),
        ],
        axis=1,
    )
    extra = jnp.pad(extra, ((0, 0), (0, LANES - extra.shape[1])))
    kv_full = gather_all(jnp.concatenate([w_qkv[:, QUERY_COLUMNS:], extra], axis=1))
    wkv, extra_full = kv_full[:, : 2 * KEY_COLUMNS], kv_full[:, 2 * KEY_COLUMNS :]
    rows = dot_nt(jnp.eye(8, LANES, dtype=bf16), extra_full)
    attn_gain_full, ffn_gain_full, corpus_full = rows[0:1], rows[1:2], rows[2]
    query_out_full = gather_all(jnp.concatenate([w_qkv[:, :QUERY_COLUMNS], w_out.T], axis=1))
    wq, wout_t = query_out_full[:, :QUERY_COLUMNS], query_out_full[:, QUERY_COLUMNS:]

    def to_group(weight):
        blocks = weight.reshape(d_rows, outer, 4, seq_devices * f_rows)
        return jnp.moveaxis(blocks, 2, 0).reshape(2, 2, d_rows, outer * seq_devices * f_rows)

    gate_up = jnp.stack([to_group(w_gate), to_group(w_up)], axis=2)
    core, near = bit_of(1), bit_of(2)
    gate_up = joined(part(gate_up, core, 1), swap(part(gate_up, 1 - core, 1), 1), core, 1)
    gate_up = joined(part(gate_up, near, 0), swap(part(gate_up, 1 - near, 0), 2), near, 0)
    hidden_columns = gate_up.shape[-1]

    def gather_hidden(lines):
        full = gather_outer(gather_seq(lines), 0)
        return jnp.moveaxis(full, 1, 3).reshape(width, hidden_columns)

    wgate = gather_hidden(gate_up[:, :, 0])
    wup = gather_hidden(gate_up[:, :, 1])
    wdown = gather_outer(gather_seq(w_down), 0).reshape(hidden_columns, width)

    corpora = jnp.arange(CORPORA, dtype=jnp.int32)
    per_device = corpus_full.reshape(-1, d_rows)[:, 0].astype(jnp.int32)
    counts = (
        jnp.sum((per_device[:, None] == corpora[None, :]).astype(f32), axis=0) * shard_length
    )
    own_corpus = (corpus[0] == corpora).astype(f32)
    weight_row = jnp.sum(own_corpus * corpus_weight.astype(f32))
    count_row = jnp.sum(own_corpus * counts)
    factor = weight_row / DENOM * (jnp.sum(counts) / (CORPORA * count_row))
    grad_full = upstream[0].astype(f32) * factor
    grad_top = grad_full.astype(bf16)
    grad_top4 = gather_group(grad_top)

    position = (place * shard_length + jnp.arange(shard_length, dtype=jnp.int32)).astype(f32)
    half = HEAD_SIZE // 2
    exponent = jnp.arange(half, dtype=f32) * (-2.0 / HEAD_SIZE)
    angles = position[:, None] * jnp.power(ROPE_BASE, exponent)[None, :]
    cosine, sine = jnp.cos(angles), jnp.sin(angles)
    cos_table = jnp.concatenate([cosine] * 4, axis=1)
    sin_table = jnp.concatenate([-sine, sine] * 2, axis=1)
    wide_q = jnp.tile(q_gain.astype(f32), QUERY_HEADS)
    wide_k = jnp.concatenate(
        [jnp.tile(k_gain.astype(f32), KEY_VALUE_HEADS), jnp.ones((KEY_COLUMNS,), f32)]
    )
    wide_q = jnp.broadcast_to(wide_q[None, :], (8, QUERY_COLUMNS))
    wide_k = jnp.broadcast_to(wide_k[None, :], (8, 2 * KEY_COLUMNS))

    in_scale = norm_scale(inputs)
    normed = (inputs * in_scale * attn_gain_full).astype(bf16)
    joint_kv = mm(normed, wkv)
    keys_values = heads_forward(joint_kv, wide_k, cos_table, sin_table, KEY_COLUMNS)
    keys_values = gather_seq(keys_values).reshape(-1, 2 * KEY_COLUMNS)
    joint_q = mm(normed, wq)
    queries = heads_forward(joint_q, wide_q, cos_table, sin_table, QUERY_COLUMNS)
    place_array = place.reshape(1)
    mixed, logs = attend_forward(place_array, queries, keys_values)
    middle = inputs + mm_t(mixed, wout_t)

    ffn_scale = norm_scale(middle)
    normed_ffn = (middle * ffn_scale * ffn_gain_full).astype(bf16)
    normed4 = gather_group(normed_ffn)
    gate = mm(normed4, wgate)
    up = mm(normed4, wup)
    sigmoid = 1.0 / (1.0 + jnp.exp(-gate))
    silu = gate * sigmoid
    hidden = (silu * up).astype(bf16)
    grad_hidden = mm_t(grad_top4, wdown)
    gate_back = (grad_hidden * up * (sigmoid * (1.0 + gate * (1.0 - sigmoid)))).astype(bf16)
    up_back = (grad_hidden * silu).astype(bf16)
    grad_normed_ffn = reduce_group(mm_t(gate_back, wgate) + mm_t(up_back, wup))
    output = (middle + reduce_group(mm(hidden, wdown))).astype(bf16)

    def scatter_hidden(grad):
        blocks = grad.reshape(outer, 2, 2, seq_devices, d_rows, hidden_columns)
        return reduce_seq(jnp.moveaxis(reduce_outer(blocks, 0), 2, 0))

    grad_wdown = t_mm(hidden, grad_top4).astype(bf16)
    grad_wdown = reduce_seq(
        reduce_outer(grad_wdown.reshape(outer, seq_devices, f_rows, width), 0)
    ).astype(f32)
    grad_gate = scatter_hidden(t_mm(normed4, gate_back).astype(bf16))
    grad_up = scatter_hidden(t_mm(normed4, up_back).astype(bf16))
    grads = jnp.stack([grad_gate, grad_up], axis=2)
    grads = joined(part(grads, near, 0), swap(part(grads, 1 - near, 0), 2), near, 0)
    grads = joined(part(grads, core, 1), swap(part(grads, 1 - core, 1), 1), core, 1)

    def from_group(blocks):
        blocks = blocks.astype(f32).reshape(4, d_rows, outer, seq_devices * f_rows)
        return jnp.transpose(blocks, (1, 2, 0, 3)).reshape(d_rows, -1)

    grad_wgate, grad_wup = from_group(grads[:, :, 0]), from_group(grads[:, :, 1])

    grad_middle_part, grad_ffn_gain = norm_backward(
        middle, ffn_scale, ffn_gain_full, grad_normed_ffn
    )
    grad_middle = grad_full + grad_middle_part
    grad_branch = grad_middle.astype(bf16)
    grad_mixed = mm(grad_branch, wout_t).astype(bf16)
    grad_q, grad_kv = attend_backward(place_array, queries, keys_values, mixed, logs, grad_mixed)
    grad_kv = reduce_seq(grad_kv.reshape(seq_devices, shard_length, -1))
    joint_grad_q, gain_q = heads_backward(
        grad_q, joint_q, wide_q, cos_table, sin_table, QUERY_COLUMNS
    )
    grad_query_out = reduce_all(
        jnp.concatenate(
            [t_mm(normed, joint_grad_q).astype(bf16), t_mm(grad_branch, mixed).astype(bf16)],
            axis=1,
        ),
        d_rows,
    ).astype(f32)
    joint_grad_kv, gain_k = heads_backward(
        grad_kv, joint_kv, wide_k, cos_table, sin_table, KEY_COLUMNS
    )
    grad_wkv = reduce_all(t_mm(normed, joint_grad_kv).astype(bf16), d_rows).astype(f32)
    grad_normed = mm_t(joint_grad_q, wq) + mm_t(joint_grad_kv, wkv)
    grad_input_part, grad_attn_gain = norm_backward(
        inputs, in_scale, attn_gain_full, grad_normed
    )
    input_grad = (grad_middle + grad_input_part).astype(bf16)

    small = lax.psum(
        jnp.concatenate(
            [
                grad_attn_gain,
                grad_ffn_gain,
                jnp.sum(gain_q[0].reshape(-1, HEAD_SIZE), axis=0),
                jnp.sum(gain_k[0, :KEY_COLUMNS].reshape(-1, HEAD_SIZE), axis=0),
            ]
        ),
        ("rows", "seq"),
    )
    start = (lax.axis_index("rows") * seq_devices + place) * d_rows
    return (
        output[None],
        input_grad[None],
        jnp.concatenate([grad_query_out[:, :QUERY_COLUMNS], grad_wkv], axis=1),
        grad_query_out[:, QUERY_COLUMNS:].T,
        grad_wgate,
        grad_wup,
        grad_wdown,
        lax.dynamic_slice_in_dim(small[:width], start, d_rows),
        lax.dynamic_slice_in_dim(small[width : 2 * width], start, d_rows),
        small[2 * width : 2 * width + HEAD_SIZE],
        small[2 * width + HEAD_SIZE :],
    )


def solution(mesh):
    return jax.shard_map(
        shards,
        mesh=mesh,
        in_specs=(
            P("rows", "seq", None),
            P("rows"),
            P(),
            P(("rows", "seq"), None),
            P(None, ("rows", "seq")),
            P(("rows", "seq"), None),
            P(("rows", "seq"), None),
            P(("rows", "seq"), None),
            P(("rows", "seq")),
            P(("rows", "seq")),
            P(),
            P(),
            P("rows", "seq", None),
        ),
        out_specs=(
            P("rows", "seq", None),
            P("rows", "seq", None),
            P(("rows", "seq"), None),
            P(None, ("rows", "seq")),
            P(("rows", "seq"), None),
            P(("rows", "seq"), None),
            P(("rows", "seq"), None),
            P(("rows", "seq")),
            P(("rows", "seq")),
            P(),
            P(),
        ),
        check_vma=False,
    )
```

time: 2380 us -> 1010 us (0.42)
  waiting for transfers between devices: 1430 us -> 380 us
  blocking collectives: 302 us -> 71.3 us
  matrix products: 384 us -> 216 us
  Pallas kernels: 0 us -> 69.8 us
  local copies, waits for them, and re-layouts: 122 us -> 75.8 us
  other arithmetic: 92.4 us -> 127 us
  starting transfers between devices: 12.2 us -> 39 us
    reduce_scatter x5 -> x6, waiting for transfers between devices: 1100 us -> 59.9 us  [reduce_seq(): return lax.psum_scatter(values, 'seq', scatter_dimension=0, tiled=False)]
    ppermute x0 -> x42, waiting for transfers between devices: none -> 219 us  [swap(): return lax.ppermute(values, 'rows', pairs)]
    dot_general x105 -> x19, matrix products: 384 us -> 216 us  [the longest x6 84.5 us: mm_t(): return jnp.einsum('ab,cb->ac', left, right, preferred_element_type=f32)]
    all_to_all x3 -> x0, waiting for transfers between devices: 153 us -> none  [the longest x1 99.1 us: shards(): lax.all_to_all(outgoing, 'seq', split_axis=2, concat_axis=1, tiled=True)]
    all_to_all x1 -> x0, blocking collectives: 139 us -> none  [shards(): lax.all_to_all(for_sending(owner_grads), 'seq', split_axis=1, concat_axis...]
    unnamed x2 -> x0, blocking collectives: 80.6 us -> none
    all_gather x5, waiting for transfers between devices: 177 us -> 99.9 us  [gather_seq(): return lax.all_gather(values, 'seq', axis=0, tiled=False)]
    pallas_call x0 -> x6, Pallas kernels: none -> 69.8 us  [the longest x1 29.7 us: attend_backward(): pl.pallas_call(attend_backward_kernel, grid_spec=pltpu.PrefetchScalarGrid...]
  transfers between devices with their start and end apart: 13 -> 53, of which waited for: 9 -> 22; matrix products, arithmetic and copies ran while one was open for 21% -> 37% of each run, Pallas kernels for 0% -> 7%
where the time goes in v1:
time: 1010 us; the launch traced here: 997 us
  waiting for transfers between devices  380 us (38%)
  matrix products  216 us (21%)
  other arithmetic  127 us (13%)
  local copies, waits for them, and re-layouts  75.8 us (8%)
  blocking collectives  71.3 us (7%)
  Pallas kernels  69.8 us (7%)
  starting transfers between devices  39 us (4%)
  between operations  18.3 us (2%)
    ppermute x42, waiting for transfers between devices, swap(): return lax.ppermute(values, 'rows', pairs)  219 us
    all_gather x5, waiting for transfers between devices, gather_seq(): return lax.all_gather(values, 'seq', axis=0, tiled=False)  99.9 us
    dot_general x6, matrix products, mm_t(): return jnp.einsum('ab,cb->ac', left, right, preferred_element_type=f32)  84.5 us
    dot_general x6, matrix products, mm(): return jnp.einsum('ab,bc->ac', left, right, preferred_element_type=f32)  70 us
    dot_general x6, matrix products, t_mm(): return jnp.einsum('ab,ac->bc', left, right, preferred_element_type=f32)  61.3 us
    reduce_scatter x6, waiting for transfers between devices, reduce_seq(): return lax.psum_scatter(values, 'seq', scatter_dimension=0, tiled=False)  59.9 us
    psum x1, blocking collectives, shards(): lax.psum(jnp.concatenate([grad_attn_gain, grad_ffn_gain, jnp.sum(gain_q[0...  52.6 us
    ppermute x42, starting transfers between devices, swap(): return lax.ppermute(values, 'rows', pairs)  38 us
  transfers between devices with their start and end apart: 53, of which 22 were waited for; matrix products, arithmetic and copies ran while one was open for 37% of the time, Pallas kernels for 7%

profile of v1, /device:TPU:0, one launch (start us, length us, event | category | flops | bytes accessed | tf_op | source)
XLA Modules:
  0.0 997.0 jit_solution(1518251276934980441)
XLA Ops:
  21.9 23.7 %all-gather.12.cloned.1.call-done = bf16[256,2560]{1,0:T(8,128)(2,1)} async-done(((bf16[64,2560]{1,0:T(8,128)(2,1)}), bf16[256,2560]{1,0:T(8,128)(2,1)}) %all-gather.12.cloned.1.call-update) | async-done | bytes 1310736 | tf_op jit(solution)/shard_map/all_gather | solution.py:411
  69.9 18.6 %all-gather = bf16[256,768]{1,0:T(8,128)(2,1)S(1)} all-gather(bf16[64,768]{1,0:T(8,128)(2,1)S(1)} %fusion.82), channel_id=2, replica_groups=mesh['rows'=8,'seq'=4] {'seq'}, dimensions={0}, use_global_device_ids=true | all-gather | bytes 491520 | tf_op jit(solution)/shard_map/all_gather | solution.py:411
  155.2 49.3 %all-gather.16.cloned.1.call-done = bf16[8,2,1,64,1152]{4,3,2,1,0:T(8,128)(2,1)} async-done(((bf16[2,2,1,64,1152]{4,3,2,1,0:T(8,128)(2,1)}), bf16[8,2,1,64,1152]{4,3,2,1,0:T(8,128)(2,1)}) %all-gather.16.cloned.1.call-update) | async-done | bytes 2359312 | tf_op jit(solution)/shard_map/all_gather | solution.py:411
  239.3 20.8 %all-gather.14.cloned.1.call-done.k_ref.v_ref = bf16[2048,640]{1,0:T(8,128)(2,1)} async-done(((bf16[512,640]{1,0:T(8,128)(2,1)}), bf16[2048,640]{1,0:T(8,128)(2,1)}) %all-gather.14.cloned.1.call-update) | async-done | bytes 2621456 | tf_op jit(solution)/shard_map/all_gather | solution.py:411
  287.1 43.1 %collective-permute-done.11 = bf16[512,2048]{1,0:T(8,128)(2,1)} collective-permute-done((bf16[512,2048]{1,0:T(8,128)(2,1)}, bf16[512,2048]{1,0:T(8,128)(2,1)}, u32[]{:S(2)}, u32[]{:S(2)}) %collective-permute-start.11) | collective-permute-done | bytes 2097184 | tf_op jit(solution)/shard_map/ppermute | solution.py:335
  337.5 19.1 %fusion.92 = f32[2048,1152]{1,0:T(8,128)} fusion(bf16[2048,1152]{1,0:T(8,128)(2,1)S(1)} %bitcast.359, bf16[512,2048]{1,0:T(8,128)(2,1)} %collective-permute-done.12, bf16[512,2048]{1,0:T(8,128)(2,1)} %collective-permute-done.11, bf16[512,2048]{1,0:T(8,128)(2,1)} %collective-permute-done.10, bf16[512,2048]{1,0:T(8,128)(2,1)} %multiply_convert_fusion.3), kind=kOutput, calls=%fused_computation.254 | convolution fusion | flops 9697230848 | bytes 22544384 | tf_op jit(solution)/shard_map/ab,bc->ac/dot_general | solution.py:460
  356.7 20.4 %fusion.93 = f32[2048,1152]{1,0:T(8,128)} fusion(bf16[2048,1152]{1,0:T(8,128)(2,1)} %bitcast.361, bf16[512,2048]{1,0:T(8,128)(2,1)} %collective-permute-done.12, bf16[512,2048]{1,0:T(8,128)(2,1)} %collective-permute-done.11, bf16[512,2048]{1,0:T(8,128)(2,1)} %collective-permute-done.10, bf16[512,2048]{1,0:T(8,128)(2,1)} %multiply_convert_fusion.3), kind=kOutput, calls=%fused_computation.255 | convolution fusion | flops 9697230848 | bytes 22544384 | tf_op jit(solution)/shard_map/ab,bc->ac/dot_general | solution.py:460
  377.1 25.6 %multiply_convert_fusion = (bf16[2048,1152]{1,0:T(8,128)(2,1)}, bf16[2048,1152]{1,0:T(8,128)(2,1)}, bf16[2048,1152]{1,0:T(8,128)(2,1)}) fusion(f32[2048,1152]{1,0:T(8,128)} %fusion.93, f32[2048,1152]{1,0:T(8,128)} %fusion.92, bf16[1152,2048]{1,0:T(8,128)(2,1)S(1)} %bitcast.357, bf16[512,2048]{1,0:T(8,128)(2,1)} %collective-permute-done.23, ...), kind=kOutput, calls=%fused_computation.10 | convolution fusion | flops 9732620288 | bytes 46137344 | tf_op jit(solution)/shard_map/ab,cb->ac/dot_general | solution.py:464
  402.6 15.2 %convolution_convert_fusion.2 = bf16[2048,1152]{1,0:T(8,128)(2,1)S(1)} fusion(bf16[2048,1152]{1,0:T(8,128)(2,1)} %get-tuple-element.33, bf16[512,2048]{1,0:T(8,128)(2,1)} %collective-permute-done.12, bf16[512,2048]{1,0:T(8,128)(2,1)} %collective-permute-done.11, bf16[512,2048]{1,0:T(8,128)(2,1)} %collective-permute-done.10, ...), kind=kOutput, calls=%fused_computation.20 | convolution fusion | flops 9699590144 | bytes 17825792 | tf_op jit(solution)/shard_map/ab,ac->bc/dot_general | solution.py:468
  421.4 16.6 %convolution_convert_fusion.3 = bf16[2048,1152]{1,0:T(8,128)(2,1)} fusion(bf16[2048,1152]{1,0:T(8,128)(2,1)} %get-tuple-element.34, bf16[512,2048]{1,0:T(8,128)(2,1)} %collective-permute-done.12, bf16[512,2048]{1,0:T(8,128)(2,1)} %collective-permute-done.11, bf16[512,2048]{1,0:T(8,128)(2,1)} %collective-permute-done.10, ...), kind=kOutput, calls=%fused_computation.21 | convolution fusion | flops 9699590144 | bytes 17825792 | tf_op jit(solution)/shard_map/ab,ac->bc/dot_general | solution.py:468
  443.0 16.1 %fusion.100 = f32[2048,2048]{1,0:T(8,128)} fusion(bf16[2048,1152]{1,0:T(8,128)(2,1)} %get-tuple-element.34, bf16[2048,1152]{1,0:T(8,128)(2,1)S(1)} %bitcast.364), kind=kOutput, calls=%fused_computation.262 | convolution fusion | flops 9663676416 | bytes 26214400 | tf_op jit(solution)/shard_map/ab,cb->ac/dot_general | solution.py:464
  459.2 15.0 %collective-permute-done.38 = bf16[2,2,4,64,1152]{4,3,1,0,2:T(8,128)(2,1)S(1)} collective-permute-done((bf16[2,2,4,64,1152]{4,3,1,0,2:T(8,128)(2,1)}, bf16[2,2,4,64,1152]{4,3,1,0,2:T(8,128)(2,1)S(1)}, u32[]{:S(2)}, u32[]{:S(2)}) %collective-permute-start.38) | collective-permute-done | bytes 2359328 | tf_op jit(solution)/shard_map/ppermute | solution.py:335
  476.4 21.7 %bitcast_convert_fusion.4 = (bf16[2,2,512,2048]{3,2,1,0:T(8,128)(2,1)}, f32[2048,2048]{1,0:T(8,128)}) fusion(f32[2048,2048]{1,0:T(8,128)} %fusion.100, bf16[2048,1152]{1,0:T(8,128)(2,1)} %get-tuple-element.33, bf16[2048,1152]{1,0:T(8,128)(2,1)} %bitcast.360), kind=kOutput, calls=%fused_computation.253 | convolution fusion | flops 9672065024 | bytes 51380224 | tf_op jit(solution)/shard_map/ab,cb->ac/dot_general | solution.py:464
  502.8 17.6 %fusion.99 = (bf16[2,2,512,2048]{3,2,1,0:T(8,128)(2,1)S(1)}, f32[2,2,512,2048]{3,2,1,0:T(8,128)}) fusion(bf16[2,2,512,1152]{3,2,1,0:T(8,128)(2,1)} %bitcast.402, bf16[1152,2048,1,1]{1,0,3,2:T(8,128)(2,1)} %bitcast.358), kind=kOutput, calls=%fused_computation.261 | convolution fusion | flops 9667870720 | bytes 34603008 | tf_op jit(solution)/shard_map/ab,bc->ac/dot_general | solution.py:460
  528.3 14.3 %convolution_convert_fusion.4 = bf16[1152,2048]{1,0:T(8,128)(2,1)S(1)} fusion(bf16[2048,1152]{1,0:T(8,128)(2,1)} %get-tuple-element.35, bf16[512,2048]{1,0:T(8,128)(2,1)} %collective-permute-done.23, bf16[512,2048]{1,0:T(8,128)(2,1)} %collective-permute-done.22, bf16[512,2048]{1,0:T(8,128)(2,1)} %collective-permute-done.21, ...), kind=kOutput, calls=%fused_computation.22 | convolution fusion | flops 9699590144 | bytes 17825792 | tf_op jit(solution)/shard_map/ab,ac->bc/dot_general | solution.py:468
  556.5 39.3 %collective-permute-done.41 = bf16[4,144,2048]{2,1,0:T(8,128)(2,1)S(1)} collective-permute-done((bf16[4,144,2048]{2,1,0:T(8,128)(2,1)S(1)}, bf16[4,144,2048]{2,1,0:T(8,128)(2,1)S(1)}, u32[]{:S(2)}, u32[]{:S(2)}) %collective-permute-start.41) | collective-permute-done | bytes 2359328 | tf_op jit(solution)/shard_map/ppermute | solution.py:335
  604.2 38.5 %collective-permute-done.20 = bf16[512,2048]{1,0:T(8,128)(2,1)} collective-permute-done((bf16[512,2048]{1,0:T(8,128)(2,1)}, bf16[512,2048]{1,0:T(8,128)(2,1)}, u32[]{:S(2)}, u32[]{:S(2)}) %collective-permute-start.20) | collective-permute-done | bytes 2097184 | tf_op jit(solution)/shard_map/ppermute | solution.py:335
  654.7 29.7 %attend_backward.1 = (bf16[512,1280]{1,0:T(8,128)(2,1)S(1)}, bf16[2048,640]{1,0:T(8,128)(2,1)}) custom-call(s32[1]{0:T(128)} %bitcast.1.place_ref, bf16[512,1280]{1,0:T(8,128)(2,1)S(1)} %copy-done.1, bf16[2048,640]{1,0:T(8,128)(2,1)} %all-gather.14.cloned.1.call-done.k_ref.v_ref, bf16[2048,640]{1,0:T(8,128)(2,1)} %all-gather.14.cloned.1.call-done.k_ref.v_ref, ...), custom_call_target="tpu_custom_call" | custom-call | flops 41943040000 | bytes 13107200 | tf_op jit(solution)/shard_map/attend_backward/pallas_call | solution.py:300
  718.5 13.7 %copy.212 = bf16[2048,2560]{1,0:T(8,128)(2,1)} copy(bf16[2048,2560]{0,1:T(8,128)(2,1)} %pad_maximum_fusion.1) | data formatting | bytes 20971520 | tf_op jit(solution)/shard_map/concatenate | solution.py:624
  740.1 14.3 %collective-permute-done.39 = bf16[2,2,64,1152]{3,2,1,0:T(8,128)(2,1)S(1)} collective-permute-done((bf16[2,2,64,1152]{3,2,1,0:T(8,128)(2,1)S(1)}, bf16[2,2,64,1152]{3,2,1,0:T(8,128)(2,1)S(1)}, u32[]{:S(2)}, u32[]{:S(2)}) %collective-permute-start.39) | collective-permute-done | bytes 589856 | tf_op jit(solution)/shard_map/ppermute | solution.py:335
  769.2 59.8 %reduce-scatter.7.cloned.1.call-done = bf16[1,512,640]{2,1,0:T(8,128)(2,1)} async-done(((bf16[4,512,640]{2,1,0:T(8,128)(2,1)}), bf16[1,512,640]{2,1,0:T(8,128)(2,1)}) %reduce-scatter.7.cloned.1.call-update) | async-done | bytes 655376 | tf_op jit(solution)/shard_map/reduce_scatter | solution.py:415
  867.4 17.7 %collective-permute-done.30 = bf16[2,4,64,1280]{3,2,1,0:T(8,128)(2,1)} collective-permute-done((bf16[2,4,64,1280]{3,2,1,0:T(8,128)(2,1)}, bf16[2,4,64,1280]{3,2,1,0:T(8,128)(2,1)}, u32[]{:S(2)}, u32[]{:S(2)}) %collective-permute-start.30) | collective-permute-done | bytes 1310752 | tf_op jit(solution)/shard_map/ppermute | solution.py:335
  896.6 13.3 %collective-permute-done.34 = bf16[4,64,256]{2,1,0:T(8,128)(2,1)S(1)} collective-permute-done((bf16[4,64,256]{2,1,0:T(8,128)(2,1)S(1)}, bf16[4,64,256]{2,1,0:T(8,128)(2,1)S(1)}, u32[]{:S(2)}, u32[]{:S(2)}) %collective-permute-start.34) | collective-permute-done | bytes 131104 | tf_op jit(solution)/shard_map/ppermute | solution.py:335
  926.2 52.6 %psum.7 = f32[4224]{0:T(1024)S(1)} all-reduce(f32[4224]{0:T(1024)S(1)} %concatenate.55), channel_id=1, replica_groups=mesh['rows'=8,'seq'=4] {'rows','seq'}, use_global_device_ids=true, to_apply=%region_18.19 | all-reduce | flops 4224 | bytes 33792 | tf_op jit(solution)/shard_map/psum | solution.py:640
  (407 shorter events, 363.0 us)
Async XLA Ops:
  9.9 136.8 %all-gather.20.cloned.1.call-start = ((), (), s32[]{:S(2)}) async-start(), calls=%async_computation.16 | async-start | bytes 2949120 | tf_op jit(solution)/shard_map/all_gather | solution.py:411
  10.7 143.1 %all-gather.18.cloned.1.call-start = ((), (), s32[]{:S(2)}) async-start(), calls=%async_computation.15 | async-start | bytes 2949120 | tf_op jit(solution)/shard_map/all_gather | solution.py:411
  53.1 151.3 %all-gather.16.cloned.1.call-start = ((), (), s32[]{:S(2)}) async-start(), calls=%async_computation.14 | async-start | bytes 2949120 | tf_op jit(solution)/shard_map/all_gather | solution.py:411
  107.7 98.2 %collective-permute-start.9 = (bf16[2,2,4,64,2560]{4,3,2,1,0:T(8,128)(2,1)}, bf16[2,2,4,64,2560]{4,3,2,1,0:T(8,128)(2,1)}, u32[]{:S(2)}, u32[]{:S(2)}) collective-permute-start(bf16[2,2,4,64,2560]{4,3,2,1,0:T(8,128)(2,1)} %maximum_maximum_fusion), channel_id=1, source_target_pairs={{0,4},{4,0},{8,12},{12,8},{16,20},{20,16},{24,28},{28,24},{1,5},{5... | collective-permute-start | bytes 15728648 | tf_op jit(solution)/shard_map/ppermute | solution.py:335
  109.4 150.8 %all-gather.14.cloned.1.call-start = ((), (), s32[]{:S(2)}) async-start(), calls=%async_computation.13 | async-start | bytes 3276800 | tf_op jit(solution)/shard_map/all_gather | solution.py:411
  138.2 599.2 %reduce-scatter.15.cloned.1.call-start = ((), (), s32[]{:S(2)}) async-start(), calls=%async_computation.10 | async-start | bytes 2949120 | tf_op jit(solution)/shard_map/reduce_scatter | solution.py:415
  145.3 138.7 %collective-permute-start.22 = (bf16[512,2048]{1,0:T(8,128)(2,1)}, bf16[512,2048]{1,0:T(8,128)(2,1)}, u32[]{:S(2)}, u32[]{:S(2)}) collective-permute-start(bf16[512,2048]{1,0:T(8,128)(2,1)} %bitcast_convert_fusion), channel_id=1, source_target_pairs={{0,8},{4,12},{8,0},{12,4},{16,24},{20,28},{24,16},{28,20},{1,9},{5... | collective-permute-start | bytes 6291464 | tf_op jit(solution)/shard_map/ppermute | solution.py:335
  146.7 137.3 %collective-permute-start.17 = (bf16[4,144,2048]{2,1,0:T(8,128)(2,1)}, bf16[4,144,2048]{2,1,0:T(8,128)(2,1)}, u32[]{:S(2)}, u32[]{:S(2)}) collective-permute-start(bf16[4,144,2048]{2,1,0:T(8,128)(2,1)} %bitcast.377), channel_id=1, source_target_pairs={{0,16},{4,20},{8,24},{12,28},{16,0},{20,4},{24,8},{28,12},{1,17},{... | collective-permute-start | bytes 7077896 | tf_op jit(solution)/shard_map/ppermute | solution.py:335
  153.7 133.2 %collective-permute-start.16 = (bf16[4,2,2,64,1152]{4,3,2,1,0:T(8,128)(2,1)}, bf16[4,2,2,64,1152]{4,3,2,1,0:T(8,128)(2,1)}, u32[]{:S(2)}, u32[]{:S(2)}) collective-permute-start(bf16[4,2,2,64,1152]{4,3,2,1,0:T(8,128)(2,1)} %bitcast.379), channel_id=1, source_target_pairs={{0,16},{4,20},{8,24},{12,28},{16,0},{20,4},{24,8},{28,12},{1,17},{... | collective-permute-start | bytes 7077896 | tf_op jit(solution)/shard_map/ppermute | solution.py:335
  204.5 125.7 %collective-permute-start.15 = (bf16[4,2,2,64,1152]{4,3,2,1,0:T(8,128)(2,1)}, bf16[4,2,2,64,1152]{4,3,2,1,0:T(8,128)(2,1)}, u32[]{:S(2)}, u32[]{:S(2)}) collective-permute-start(bf16[4,2,2,64,1152]{4,3,2,1,0:T(8,128)(2,1)} %bitcast.381), channel_id=1, source_target_pairs={{0,16},{4,20},{8,24},{12,28},{16,0},{20,4},{24,8},{28,12},{1,17},{... | collective-permute-start | bytes 7077896 | tf_op jit(solution)/shard_map/ppermute | solution.py:335
  284.0 93.1 %collective-permute-start.21 = (bf16[512,2048]{1,0:T(8,128)(2,1)}, bf16[512,2048]{1,0:T(8,128)(2,1)}, u32[]{:S(2)}, u32[]{:S(2)}) collective-permute-start(bf16[512,2048]{1,0:T(8,128)(2,1)} %bitcast_convert_fusion), channel_id=1, source_target_pairs={{0,4},{4,0},{8,12},{12,8},{16,20},{20,16},{24,28},{28,24},{1,5},{5... | collective-permute-start | bytes 6291464 | tf_op jit(solution)/shard_map/ppermute | solution.py:335
  284.0 93.1 %collective-permute-start.23 = (bf16[512,2048]{1,0:T(8,128)(2,1)}, bf16[512,2048]{1,0:T(8,128)(2,1)}, u32[]{:S(2)}, u32[]{:S(2)}) collective-permute-start(bf16[512,2048]{1,0:T(8,128)(2,1)} %collective-permute-done.22), channel_id=1, source_target_pairs={{0,4},{4,0},{8,12},{12,8},{16,20},{20,16},{24,28},{28,24},{1,5},{5... | collective-permute-start | bytes 6291464 | tf_op jit(solution)/shard_map/ppermute | solution.py:335
  419.9 54.3 %collective-permute-start.38 = (bf16[2,2,4,64,1152]{4,3,1,0,2:T(8,128)(2,1)}, bf16[2,2,4,64,1152]{4,3,1,0,2:T(8,128)(2,1)S(1)}, u32[]{:S(2)}, u32[]{:S(2)}) collective-permute-start(bf16[2,2,4,64,1152]{4,3,1,0,2:T(8,128)(2,1)} %bitcast.329), channel_id=1, source_target_pairs={{0,16},{4,20},{8,24},{12,28},{16,0},{20,4},{24,8},{28,12},{1,17},{... | collective-permute-start | bytes 7077896 | tf_op jit(solution)/shard_map/ppermute | solution.py:335
  442.5 82.0 %collective-permute-start.37 = (bf16[2,2,4,64,1152]{4,3,1,0,2:T(8,128)(2,1)}, bf16[2,2,4,64,1152]{4,3,1,0,2:T(8,128)(2,1)}, u32[]{:S(2)}, u32[]{:S(2)}) collective-permute-start(bf16[2,2,4,64,1152]{4,3,1,0,2:T(8,128)(2,1)} %bitcast.330), channel_id=1, source_target_pairs={{0,16},{4,20},{8,24},{12,28},{16,0},{20,4},{24,8},{28,12},{1,17},{... | collective-permute-start | bytes 7077896 | tf_op jit(solution)/shard_map/ppermute | solution.py:335
  476.3 261.2 %reduce-scatter.13.cloned.1.call-start = ((), (), s32[]{:S(2)}) async-start(), calls=%async_computation.9 | async-start | bytes 2949120 | tf_op jit(solution)/shard_map/reduce_scatter | solution.py:415
  528.3 228.5 %reduce-scatter.17.cloned.1.call-start = ((), (), s32[]{:S(2)}) async-start(), calls=%async_computation.11 | async-start | bytes 2949120 | tf_op jit(solution)/shard_map/reduce_scatter | solution.py:415
  542.8 53.0 %collective-permute-start.41 = (bf16[4,144,2048]{2,1,0:T(8,128)(2,1)S(1)}, bf16[4,144,2048]{2,1,0:T(8,128)(2,1)S(1)}, u32[]{:S(2)}, u32[]{:S(2)}) collective-permute-start(bf16[4,144,2048]{2,1,0:T(8,128)(2,1)S(1)} %dynamic-slice_bitcast_fusion.1), channel_id=1, source_target_pairs={{0,16},{4,20},{8,24},{12,28},{16,0},{20,4},{24,8},{28,12},{1,17},{... | collective-permute-start | bytes 7077896 | tf_op jit(solution)/shard_map/ppermute | solution.py:335
  544.4 53.8 %collective-permute-start.24 = (bf16[512,2048]{1,0:T(8,128)(2,1)}, bf16[512,2048]{1,0:T(8,128)(2,1)}, u32[]{:S(2)}, u32[]{:S(2)}) collective-permute-start(bf16[512,2048]{1,0:T(8,128)(2,1)} %get-tuple-element.38), channel_id=1, source_target_pairs={{0,4},{4,0},{8,12},{12,8},{16,20},{20,16},{24,28},{28,24},{1,5},{5... | collective-permute-start | bytes 6291464 | tf_op jit(solution)/shard_map/ppermute | solution.py:335
  550.8 53.3 %collective-permute-start.18 = (bf16[512,2048]{1,0:T(8,128)(2,1)}, bf16[512,2048]{1,0:T(8,128)(2,1)}, u32[]{:S(2)}, u32[]{:S(2)}) collective-permute-start(bf16[512,2048]{1,0:T(8,128)(2,1)} %get-tuple-element.40), channel_id=1, source_target_pairs={{0,4},{4,0},{8,12},{12,8},{16,20},{20,16},{24,28},{28,24},{1,5},{5... | collective-permute-start | bytes 6291464 | tf_op jit(solution)/shard_map/ppermute | solution.py:335
  556.0 86.6 %collective-permute-start.20 = (bf16[512,2048]{1,0:T(8,128)(2,1)}, bf16[512,2048]{1,0:T(8,128)(2,1)}, u32[]{:S(2)}, u32[]{:S(2)}) collective-permute-start(bf16[512,2048]{1,0:T(8,128)(2,1)} %fusion.28), channel_id=1, source_target_pairs={{0,8},{4,12},{8,0},{12,4},{16,24},{20,28},{24,16},{28,20},{1,9},{5... | collective-permute-start | bytes 6291464 | tf_op jit(solution)/shard_map/ppermute | solution.py:335
  598.2 230.8 %reduce-scatter.7.cloned.1.call-start = ((), (), s32[]{:S(2)}) async-start(), calls=%async_computation.6 | async-start | bytes 3276800 | tf_op jit(solution)/shard_map/reduce_scatter | solution.py:415
  705.8 280.7 %reduce-scatter.11.cloned.1.call-start = ((), (), s32[]{:S(2)}) async-start(), calls=%async_computation.8 | async-start | bytes 409600 | tf_op jit(solution)/shard_map/reduce_scatter | solution.py:415
  737.5 103.7 %collective-permute-start.27 = (bf16[2,2,4,64,2560]{4,3,2,1,0:T(8,128)(2,1)}, bf16[2,2,4,64,2560]{4,3,2,1,0:T(8,128)(2,1)}, u32[]{:S(2)}, u32[]{:S(2)}) collective-permute-start(bf16[2,2,4,64,2560]{4,3,2,1,0:T(8,128)(2,1)} %dynamic-slice_bitcast_fusion), channel_id=1, source_target_pairs={{0,4},{4,0},{8,12},{12,8},{16,20},{20,16},{24,28},{28,24},{1,5},{5... | collective-permute-start | bytes 15728648 | tf_op jit(solution)/shard_map/ppermute | solution.py:335
  912.6 74.8 %reduce-scatter.9.cloned.1.call-start = ((), (), s32[]{:S(2)}) async-start(), calls=%async_computation.7 | async-start | bytes 1638400 | tf_op jit(solution)/shard_map/reduce_scatter | solution.py:415
  (101 other events, 2043.7 us)
Sparse Core Ops, SparseCore 0:
  10.2 35.3 all-gather.11
  47.2 55.5 all-gather.19
  104.4 49.3 all-gather.17
  155.1 49.2 all-gather.15
  206.5 53.6 all-gather.13
  476.4 71.7 reduce-scatter.14
  550.5 49.6 reduce-scatter.12
  602.5 67.4 reduce-scatter.16
  705.9 123.0 reduce-scatter.6
  912.8 31.3 reduce-scatter.10
  946.4 30.4 reduce-scatter.8

commit v2 on v1

--- a/solution.py
+++ b/solution.py
@@ -1,3 +1,4 @@
+import math
 from functools import partial
 
 import jax
@@ -21,6 +22,7 @@
 VMEM_LIMIT = 48 * 1024 * 1024
 
 f32, bf16 = jnp.float32, jnp.bfloat16
+LIGHT = pl.CostEstimate(flops=1000, bytes_accessed=1000, transcendentals=0)
 
 
 def dot_nn(a, b):
@@ -80,9 +82,7 @@
         out_specs=pl.BlockSpec((tokens, LANES), lambda i: (0, i)),
         out_shape=jax.ShapeDtypeStruct((tokens, columns), bf16),
         name="heads_forward",
-        cost_estimate=pl.CostEstimate(
-            flops=tokens * columns * 256, bytes_accessed=tokens * columns * 6, transcendentals=0
-        ),
+        cost_estimate=LIGHT,
     )(joint, gain, cos, sin)
 
 
@@ -125,9 +125,7 @@
             jax.ShapeDtypeStruct((8, columns), f32),
         ],
         name="heads_backward",
-        cost_estimate=pl.CostEstimate(
-            flops=tokens * columns * 512, bytes_accessed=tokens * columns * 10, transcendentals=0
-        ),
+        cost_estimate=LIGHT,
     )(grad, joint, gain, cos, sin)
 
 
@@ -197,11 +195,7 @@
         ],
         compiler_params=pltpu.CompilerParams(vmem_limit_bytes=VMEM_LIMIT),
         name="attend_forward",
-        cost_estimate=pl.CostEstimate(
-            flops=QUERY_HEADS * tokens * length * 800,
-            bytes_accessed=tokens * QUERY_COLUMNS * 8 + length * 1280,
-            transcendentals=QUERY_HEADS * tokens * length,
-        ),
+        cost_estimate=LIGHT,
     )(place, queries, keys_values, keys_values)
 
 
@@ -216,10 +210,11 @@
 
 
 def attend_backward_kernel(
-    place_ref, q_ref, k_ref, v_ref, out_ref, log_ref, grad_ref, dq_ref, dkv_ref, dk_sum, dv_sum
+    first_group, count, place_ref, q_ref, k_ref, v_ref, out_ref, log_ref, grad_ref, dq_ref, dkv_ref, dk_sum, dv_sum
 ):
     pair_index = pl.program_id(0)
-    group = pair_index // 2
+    local = pair_index // 2
+    group = first_group + local
     place = place_ref[0]
     tokens = q_ref.shape[0]
     lane = lanes_of((tokens, LANES))
@@ -281,8 +276,8 @@
     def _():
         wide_lane = lanes_of(dk_sum.shape)
         for total, slot, factor in (
-            (dk_sum, group, HEAD_SIZE**-0.5),
-            (dv_sum, KEY_VALUE_HEADS + group, 1.0),
+            (dk_sum, local, HEAD_SIZE**-0.5),
+            (dv_sum, count + local, 1.0),
         ):
             both = (total[...] + pltpu.roll(total[...], HEAD_SIZE, 1)) * factor
             columns = pl.ds(pl.multiple_of(slot // 2 * LANES, LANES), LANES)
@@ -292,42 +287,267 @@
             ).astype(bf16)
 
 
-def attend_backward(place, queries, keys_values, mixed, logs, grad_mixed):
+def attend_backward(first, count, place, queries, keys_values, mixed, logs, grad_mixed):
     tokens = queries.shape[0]
     length = keys_values.shape[0]
-    pairs = QUERY_COLUMNS // LANES
-    own = pl.BlockSpec((tokens, LANES), lambda i, s: (0, i))
+    group = QUERY_HEADS // KEY_VALUE_HEADS * HEAD_SIZE
+    own = pl.BlockSpec((tokens, LANES), lambda i, s: (0, 2 * first + i))
+    keys = pl.BlockSpec((length, LANES), lambda i, s: (0, (first + i // 2) // 2))
+    values = pl.BlockSpec(
+        (length, LANES), lambda i, s: (0, (KEY_VALUE_HEADS + first + i // 2) // 2)
+    )
+    columns = 2 * count * HEAD_SIZE
     return pl.pallas_call(
-        attend_backward_kernel,
+        partial(attend_backward_kernel, first, count),
         grid_spec=pltpu.PrefetchScalarGridSpec(
             num_scalar_prefetch=1,
-            grid=(pairs,),
-            in_specs=[
-                own,
-                pl.BlockSpec((length, LANES), lambda i, s: (0, (i // 2) // 2)),
-                pl.BlockSpec((length, LANES), lambda i, s: (0, (KEY_VALUE_HEADS + i // 2) // 2)),
-                own,
-                own,
-                own,
-            ],
+            grid=(2 * count,),
+            in_specs=[own, keys, values, own, own, own],
             out_specs=[
-                own,
-                pl.BlockSpec((length, 2 * KEY_COLUMNS), lambda i, s: (0, 0)),
+                pl.BlockSpec((tokens, LANES), lambda i, s: (0, i)),
+                pl.BlockSpec((length, columns), lambda i, s: (0, 0)),
             ],
             scratch_shapes=[pltpu.VMEM((length, LANES), f32), pltpu.VMEM((length, LANES), f32)],
         ),
         out_shape=[
-            jax.ShapeDtypeStruct((tokens, QUERY_COLUMNS), bf16),
-            jax.ShapeDtypeStruct((length, 2 * KEY_COLUMNS), bf16),
+            jax.ShapeDtypeStruct((tokens, count * group), bf16),
+            jax.ShapeDtypeStruct((length, columns), bf16),
         ],
         compiler_params=pltpu.CompilerParams(vmem_limit_bytes=VMEM_LIMIT),
         name="attend_backward",
-        cost_estimate=pl.CostEstimate(
-            flops=QUERY_HEADS * tokens * length * 2000,
-            bytes_accessed=tokens * QUERY_COLUMNS * 12 + length * 2560,
-            transcendentals=QUERY_HEADS * tokens * length,
+        cost_estimate=LIGHT,
+    )(place, queries, keys_values, keys_values, mixed, logs, grad_mixed)
+
+
+def hidden_kernel(n0_ref, n1_ref, wg_ref, wu_ref, hidden_ref, gate_ref, up_ref, n_all):
+    tokens = n0_ref.shape[0]
+
+    @pl.when(pl.program_id(0) == 0)
+    def _():
+        n_all[:tokens] = n0_ref[...]
+        n_all[tokens:] = n1_ref[...]
+
+    gate = dot_nn(n_all[...], wg_ref[...])
+    up = dot_nn(n_all[...], wu_ref[...])
+    hidden_ref[...] = (gate / (1.0 + jnp.exp(-gate)) * up).astype(bf16)
+    gate_ref[...] = gate.astype(bf16)
+    up_ref[...] = up.astype(bf16)
+
+
+def hidden_pass(normed, wgate, wup):
+    tokens, width = normed[0].shape
+    columns = wgate.shape[1]
+    tile = min(256, columns)
+    whole = pl.BlockSpec((tokens, width), lambda i: (0, 0))
+    down = pl.BlockSpec((width, tile), lambda i: (0, i))
+    out = pl.BlockSpec((2 * tokens, tile), lambda i: (0, i))
+    return pl.pallas_call(
+        hidden_kernel,
+        grid=(pl.cdiv(columns, tile),),
+        in_specs=[whole] * 2 + [down] * 2,
+        out_specs=[out] * 3,
+        out_shape=[jax.ShapeDtypeStruct((2 * tokens, columns), bf16)] * 3,
+        scratch_shapes=[pltpu.VMEM((2 * tokens, width), bf16)],
+        compiler_params=pltpu.CompilerParams(vmem_limit_bytes=VMEM_LIMIT),
+        name="hidden_pass",
+        cost_estimate=LIGHT,
+    )(*normed, wgate, wup)
+
+
+def gates_kernel(g0_ref, g1_ref, wd_ref, gate_ref, up_ref, gate_out_ref, up_out_ref, g_all):
+    tokens = g0_ref.shape[0]
+
+    @pl.when(pl.program_id(0) == 0)
+    def _():
+        g_all[:tokens] = g0_ref[...]
+        g_all[tokens:] = g1_ref[...]
+
+    grad = dot_nt(g_all[...], wd_ref[...])
+    gate = gate_ref[...].astype(f32)
+    up = up_ref[...].astype(f32)
+    sigmoid = 1.0 / (1.0 + jnp.exp(-gate))
+    gate_out_ref[...] = (grad * up * (sigmoid * (1.0 + gate * (1.0 - sigmoid)))).astype(bf16)
+    up_out_ref[...] = (grad * (gate * sigmoid)).astype(bf16)
+
+
+def gates_pass(grad_top, wdown, gate, up):
+    tokens, width = grad_top[0].shape
+    columns = gate.shape[1]
+    tile = min(256, columns)
+    whole = pl.BlockSpec((tokens, width), lambda i: (0, 0))
+    out = pl.BlockSpec((2 * tokens, tile), lambda i: (0, i))
+    return pl.pallas_call(
+        gates_kernel,
+        grid=(pl.cdiv(columns, tile),),
+        in_specs=[whole] * 2 + [pl.BlockSpec((tile, width), lambda i: (i, 0)), out, out],
+        out_specs=[out] * 2,
+        out_shape=[jax.ShapeDtypeStruct((2 * tokens, columns), bf16)] * 2,
+        scratch_shapes=[pltpu.VMEM((2 * tokens, width), bf16)],
+        compiler_params=pltpu.CompilerParams(vmem_limit_bytes=VMEM_LIMIT),
+        name="gates_pass",
+        cost_estimate=LIGHT,
+    )(*grad_top, wdown, gate, up)
+
+
+def back_kernel(count, transposed, *refs):
+    own_ref, send_ref = refs[-2:]
+    tokens = own_ref.shape[0]
+    dot = dot_nt if transposed else dot_nn
+
+    def total(start):
+        rows = pl.ds(start, tokens)
+        result = dot(refs[0][rows, :], refs[count][...])
+        for i in range(1, count):
+            result = result + dot(refs[i][rows, :], refs[count + i][...])
+        return result
+
+    own_ref[...] = total(0)
+    send_ref[...] = total(tokens).astype(bf16)
+
+
+def back_pass(lefts, weights, transposed):
+    tokens, depth = lefts[0].shape
+    width = weights[0].shape[0 if transposed else 1]
+    count = len(lefts)
+    tile = min(512, width)
+    if transposed:
+        weight_spec = pl.BlockSpec((tile, depth), lambda i: (i, 0))
+    else:
+        weight_spec = pl.BlockSpec((depth, tile), lambda i: (0, i))
+    out = pl.BlockSpec((tokens // 2, tile), lambda i: (0, i))
+    return pl.pallas_call(
+        partial(back_kernel, count, transposed),
+        grid=(width // tile,),
+        in_specs=[pl.BlockSpec((tokens, depth), lambda i: (0, 0))] * count
+        + [weight_spec] * count,
+        out_specs=[out, out],
+        out_shape=[
+            jax.ShapeDtypeStruct((tokens // 2, width), f32),
+            jax.ShapeDtypeStruct((tokens // 2, width), bf16),
+        ],
+        compiler_params=pltpu.CompilerParams(vmem_limit_bytes=VMEM_LIMIT),
+        name="back_pass",
+        cost_estimate=LIGHT,
+    )(*lefts, *weights)
+
+
+def weight_kernel(left_count, *refs):
+    lefts, rights, out_ref = refs[:left_count], refs[left_count:-1], refs[-1]
+    step = min(lefts[0].shape[0], rights[0].shape[0])
+
+    def piece(refs, start):
+        index, offset = divmod(start, refs[0].shape[0])
+        return refs[index][pl.ds(offset, step), :]
+
+    total = None
+    for start in range(0, left_count * lefts[0].shape[0], step):
+        term = dot_tn(piece(lefts, start), piece(rights, start))
+        total = term if total is None else total + term
+    out_ref[...] = total.astype(bf16)
+
+
+def weight_pass(lefts, rights):
+    rows, columns = lefts[0].shape[1], rights[0].shape[1]
+    tile = 512 if rows % 512 == 0 else 384 if rows % 384 == 0 else rows
+    return pl.pallas_call(
+        partial(weight_kernel, len(lefts)),
+        grid=(rows // tile,),
+        in_specs=[pl.BlockSpec((left.shape[0], tile), lambda i: (0, i)) for left in lefts]
+        + [pl.BlockSpec(right.shape, lambda i: (0, 0)) for right in rights],
+        out_specs=pl.BlockSpec((tile, columns), lambda i: (i, 0)),
+        out_shape=jax.ShapeDtypeStruct((rows, columns), bf16),
+        compiler_params=pltpu.CompilerParams(vmem_limit_bytes=VMEM_LIMIT),
+        name="weight_pass",
+        cost_estimate=LIGHT,
+    )(*lefts, *rights)
+
+
+def placed_kernel(side_ref, own_ref, other_ref, out_ref):
+    mine = pl.program_id(0) == side_ref[0]
+
+    @pl.when(mine)
+    def _():
+        out_ref[0, 0] = own_ref[:, 0]
+
+    @pl.when(jnp.logical_not(mine))
+    def _():
+        out_ref[0, 0] = other_ref[:, 0]
+
+
+def placed(own, other, side):
+    seq, group, rows, columns = own.shape
+
+    def entry(mine, e, g, s):
+        parked = jnp.where(e == 0, 0, group - 1)
+        return (0, jnp.where((e == s[0]) == mine, g, parked), 0, 0)
+
+    return pl.pallas_call(
+        placed_kernel,
+        grid_spec=pltpu.PrefetchScalarGridSpec(
+            num_scalar_prefetch=1,
+            grid=(2, group),
+            in_specs=[
+                pl.BlockSpec((seq, 1, rows, columns), partial(entry, True)),
+                pl.BlockSpec((seq, 1, rows, columns), partial(entry, False)),
+            ],
+            out_specs=pl.BlockSpec(
+                (1, 1, seq, rows, columns), lambda e, g, s: (e, g, 0, 0, 0)
+            ),
         ),
-    )(place, queries, keys_values, keys_values, mixed, logs, grad_mixed)
+        out_shape=jax.ShapeDtypeStruct((2, group, seq, rows, columns), own.dtype),
+        name="placed",
+        cost_estimate=LIGHT,
+    )(side.astype(jnp.int32).reshape(1), own, other)
+
+
+def joined_kernel(side_ref, own_ref, other_ref, out_ref):
+    mine = pl.program_id(1) == side_ref[0]
+
+    @pl.when(mine)
+    def _():
+        out_ref[:, 0] = own_ref[...]
+
+    @pl.when(jnp.logical_not(mine))
+    def _():
+        out_ref[:, 0] = other_ref[...]
+
+
+def joined(own, other, side, axis):
+    shape = own.shape[:axis] + (2,) + own.shape[axis:]
+    columns = own.shape[-1]
+    lead = math.prod(own.shape[:axis])
+    rows = math.prod(own.shape[axis:-1])
+    leads, chunks = lead, 1
+    while leads % 2 == 0 and leads * rows * columns > 800_000:
+        leads //= 2
+    while leads == 1 and rows % (32 * chunks) == 0 and rows // chunks * columns > 800_000:
+        chunks *= 2
+    block = rows // chunks
+
+    def entry(mine, p, e, i, s):
+        parked = jnp.where(e == 0, 0, chunks - 1)
+        return (p, jnp.where((e == s[0]) == mine, i, parked), 0)
+
+    return pl.pallas_call(
+        joined_kernel,
+        grid_spec=pltpu.PrefetchScalarGridSpec(
+            num_scalar_prefetch=1,
+            grid=(lead // leads, 2, chunks),
+            in_specs=[
+                pl.BlockSpec((leads, block, columns), partial(entry, True)),
+                pl.BlockSpec((leads, block, columns), partial(entry, False)),
+            ],
+            out_specs=pl.BlockSpec((leads, 1, block, columns), lambda p, e, i, s: (p, e, i, 0)),
+        ),
+        out_shape=jax.ShapeDtypeStruct((lead, 2, rows, columns), own.dtype),
+        compiler_params=pltpu.CompilerParams(vmem_limit_bytes=VMEM_LIMIT),
+        name="joined",
+        cost_estimate=LIGHT,
+    )(
+        side.astype(jnp.int32).reshape(1),
+        own.reshape(lead, rows, columns),
+        other.reshape(lead, rows, columns),
+    ).reshape(shape)
 
 
 def swap(values, bit):
@@ -339,12 +559,6 @@
     return (lax.axis_index("rows") // bit) % 2
 
 
-def joined(own, other, side, axis):
-    low = jnp.where(side == 0, own, other)
-    high = jnp.where(side == 0, other, own)
-    return jnp.stack([low, high], axis)
-
-
 def gather_bit(values, bit, axis):
     return joined(values, swap(values, bit), bit_of(bit), axis)
 
@@ -354,9 +568,7 @@
 
 
 def reduce_bit(values, bit, axis):
-    side = bit_of(bit)
-    other = swap(part(values, 1 - side, axis), bit)
-    return (part(values, side, axis).astype(f32) + other.astype(f32)).astype(bf16)
+    return add_bit(values, pass_bit(values, bit, axis), bit, axis)
 
 
 def outer_pairs(step, low, high):
@@ -368,13 +580,10 @@
     ]
 
 
-def gather_outer(values, axis):
+def send_outer(values):
     count = lax.axis_size("rows") // 4
-    if count == 1:
-        return jnp.expand_dims(values, axis)
     if count == 2:
-        return gather_bit(values, 4, axis)
-    place = lax.axis_index("rows") // 4
+        return (swap(values, 4),)
     up, down = values, values
     ups, downs = [], []
     for t in range(1, count):
@@ -382,29 +591,61 @@
         down = lax.ppermute(down, "rows", outer_pairs(-1, 0, count - t + 1))
         ups.append(up)
         downs.append(down)
-    line = jnp.stack(ups[::-1] + [values] + downs, axis)
+    return tuple(ups[::-1] + downs)
+
+
+def join_outer(values, received, axis):
+    count = lax.axis_size("rows") // 4
+    if count == 2:
+        return joined(values, received[0], bit_of(4), axis)
+    place = lax.axis_index("rows") // 4
+    line = jnp.stack([*received[: count - 1], values, *received[count - 1 :]], axis)
     return lax.dynamic_slice_in_dim(line, count - 1 - place, count, axis)
 
 
-def reduce_outer(values, axis):
+def gather_outer(values, axis):
+    return join_outer(values, send_outer(values), axis)
+
+
+def pass_outer(values, axis):
     count = lax.axis_size("rows") // 4
-    if count == 1:
-        return jnp.squeeze(values, axis)
-    if count == 2:
-        return reduce_bit(values, 4, axis)
     place = lax.axis_index("rows") // 4
 
     def entry(index):
         return part(values, jnp.clip(index, 0, count - 1), axis)
 
+    if count == 1:
+        return ()
+    if count == 2:
+        return (swap(entry(1 - place), 4),)
     up, down = entry(place + count - 1), entry(place - count + 1)
     for t in range(1, count):
-        up = lax.ppermute(up, "rows", outer_pairs(1, 0, t)).astype(f32)
-        down = lax.ppermute(down, "rows", outer_pairs(-1, count - t, count)).astype(f32)
+        up = lax.ppermute(up, "rows", outer_pairs(1, 0, t))
+        down = lax.ppermute(down, "rows", outer_pairs(-1, count - t, count))
         if t < count - 1:
-            up = (entry(place + count - 1 - t).astype(f32) + up).astype(bf16)
-            down = (entry(place - count + 1 + t).astype(f32) + down).astype(bf16)
-    return (entry(place).astype(f32) + up + down).astype(bf16)
+            up = (entry(place + count - 1 - t).astype(f32) + up.astype(f32)).astype(bf16)
+            down = (entry(place - count + 1 + t).astype(f32) + down.astype(f32)).astype(bf16)
+    return (up, down)
+
+
+def add_outer(values, received, axis):
+    total = part(values, lax.axis_index("rows") // 4, axis).astype(f32)
+    for term in received:
+        total = total + term.astype(f32)
+    return total.astype(bf16)
+
+
+def reduce_outer(values, axis):
+    return add_outer(values, pass_outer(values, axis), axis)
+
+
+def pass_bit(values, bit, axis):
+    return swap(part(values, 1 - bit_of(bit), axis), bit)
+
+
+def add_bit(values, received, bit, axis):
+    own = part(values, bit_of(bit), axis)
+    return (own.astype(f32) + received.astype(f32)).astype(bf16)
 
 
 def gather_seq(values):
@@ -415,45 +656,23 @@
     return lax.psum_scatter(values, "seq", scatter_dimension=0, tiled=False)
 
 
-def split_columns(columns):
-    return columns // LANES // 2 * LANES
-
-
-def gather_all(shard):
-    columns = shard.shape[1]
-    half = split_columns(columns)
-    lines = gather_seq(shard)
-    left = gather_bit(gather_outer(lines[..., :half], 0), 2, 1)
-    right = gather_outer(gather_bit(lines[..., half:], 2, 0), 0)
-    both = jnp.concatenate([left, right], axis=-1)
-    return gather_bit(both, 1, 2).reshape(-1, columns)
-
-
-def reduce_all(values, rows):
-    columns = values.shape[1]
-    half = split_columns(columns)
-    seq = lax.axis_size("seq")
-    blocks = values.reshape(-1, 2, 2, seq, rows, columns)
-    blocks = reduce_bit(blocks, 1, 2)
-    left = reduce_outer(reduce_bit(blocks[..., :half], 2, 1), 0)
-    right = reduce_bit(reduce_outer(blocks[..., half:], 0), 2, 0)
-    return reduce_seq(jnp.concatenate([left, right], axis=-1))
-
-
-def gather_group(values):
-    other = swap(values, 1)
-    across = swap(values, 2)
-    far = swap(across, 1)
-    return jnp.concatenate([values, other, across, far], axis=0)
-
-
-def reduce_group(values):
-    tokens = values.shape[0] // 4
-    parts = values.reshape(2, 2, tokens, values.shape[1])
-    across = parts[1, 0] + swap(parts[1, 1].astype(bf16), 1).astype(f32)
-    across = swap(across.astype(bf16), 2).astype(f32)
-    own = parts[0, 0] + swap(parts[0, 1].astype(bf16), 1).astype(f32)
-    return own + across
+def sum_all(values):
+    for axis in ("rows", "seq"):
+        size = lax.axis_size(axis)
+        bit = 1
+        while bit < size:
+            pairs = [(i, i ^ bit) for i in range(size)]
+            values = values + lax.ppermute(values, axis, pairs)
+            bit *= 2
+    return values
+
+
+def across_group(own, send):
+    return (own + swap(send, 1).astype(f32)).astype(bf16)
+
+
+def stage(*values):
+    return lax.optimization_barrier(values)
 
 
 def mm(left, right):
@@ -512,43 +731,51 @@
         axis=1,
     )
     extra = jnp.pad(extra, ((0, 0), (0, LANES - extra.shape[1])))
-    kv_full = gather_all(jnp.concatenate([w_qkv[:, QUERY_COLUMNS:], extra], axis=1))
-    wkv, extra_full = kv_full[:, : 2 * KEY_COLUMNS], kv_full[:, 2 * KEY_COLUMNS :]
-    rows = dot_nt(jnp.eye(8, LANES, dtype=bf16), extra_full)
+    kv_lines = gather_seq(jnp.concatenate([w_qkv[:, QUERY_COLUMNS:], extra], axis=1))
+    query_shard = jnp.concatenate([w_qkv[:, :QUERY_COLUMNS], w_out.T], axis=1)
+    query_shard, w_gate, w_up = stage(query_shard, w_gate, w_up)
+    query_lines = gather_seq(query_shard)
+
+    def to_group(weight):
+        blocks = weight.reshape(d_rows, outer, 4, seq_devices, f_rows)
+        blocks = jnp.transpose(blocks, (2, 0, 3, 1, 4))
+        return blocks.reshape(2, 2, d_rows, outer * seq_devices * f_rows)
+
+    def spread_hidden(lines, received):
+        if outer == 2:
+            lines = lines.reshape(seq_devices, 4, d_rows, hidden_columns)
+            other = received[0].reshape(lines.shape)
+            return placed(lines, other, bit_of(4)).reshape(width, hidden_columns)
+        full = join_outer(lines, received, 0)
+        return jnp.moveaxis(full, 1, 3).reshape(width, hidden_columns)
+
+    gate_up = jnp.stack([to_group(w_gate), to_group(w_up)], axis=2)
+    hidden_columns = gate_up.shape[-1]
+    core, near = bit_of(1), bit_of(2)
+    other, kv_lines, down_other, query_lines = stage(
+        swap(part(gate_up, 1 - core, 1), 1), kv_lines, send_outer(w_down), query_lines
+    )
+    gate_up = joined(part(gate_up, core, 1), other, core, 1)
+    down_pair = join_outer(w_down, down_other, 0)
+    left, right = kv_lines[..., : 3 * LANES], kv_lines[..., 3 * LANES :]
+    other, left_other, right_other = stage(
+        swap(part(gate_up, 1 - near, 0), 2), send_outer(left), swap(right, 2)
+    )
+    gate_up = joined(part(gate_up, near, 0), other, near, 0)
+    gate_lines = gather_seq(gate_up[:, :, 0])
+    left = join_outer(left, left_other, 0)
+    right = joined(right, right_other, near, 0)
+    left_other, right_other = stage(swap(left, 2), send_outer(right))
+    left = joined(left, left_other, near, 1)
+    right = join_outer(right, right_other, 0)
+    q_left, q_right = query_lines[..., :QUERY_COLUMNS], query_lines[..., QUERY_COLUMNS:]
+    q_left, q_right, left, right = stage(q_left, q_right, left, right)
+    q_left_other, q_right_other = send_outer(q_left), swap(q_right, 2)
+    left, right = gather_bit(left, 1, 2), gather_bit(right, 1, 2)
+    left, right = left.reshape(width, -1), right.reshape(width, -1)
+    wkv = jnp.concatenate([left, right[:, : 2 * LANES]], axis=1)
+    rows = dot_nt(jnp.eye(8, LANES, dtype=bf16), right[:, 2 * LANES :])
     attn_gain_full, ffn_gain_full, corpus_full = rows[0:1], rows[1:2], rows[2]
-    query_out_full = gather_all(jnp.concatenate([w_qkv[:, :QUERY_COLUMNS], w_out.T], axis=1))
-    wq, wout_t = query_out_full[:, :QUERY_COLUMNS], query_out_full[:, QUERY_COLUMNS:]
-
-    def to_group(weight):
-        blocks = weight.reshape(d_rows, outer, 4, seq_devices * f_rows)
-        return jnp.moveaxis(blocks, 2, 0).reshape(2, 2, d_rows, outer * seq_devices * f_rows)
-
-    gate_up = jnp.stack([to_group(w_gate), to_group(w_up)], axis=2)
-    core, near = bit_of(1), bit_of(2)
-    gate_up = joined(part(gate_up, core, 1), swap(part(gate_up, 1 - core, 1), 1), core, 1)
-    gate_up = joined(part(gate_up, near, 0), swap(part(gate_up, 1 - near, 0), 2), near, 0)
-    hidden_columns = gate_up.shape[-1]
-
-    def gather_hidden(lines):
-        full = gather_outer(gather_seq(lines), 0)
-        return jnp.moveaxis(full, 1, 3).reshape(width, hidden_columns)
-
-    wgate = gather_hidden(gate_up[:, :, 0])
-    wup = gather_hidden(gate_up[:, :, 1])
-    wdown = gather_outer(gather_seq(w_down), 0).reshape(hidden_columns, width)
-
-    corpora = jnp.arange(CORPORA, dtype=jnp.int32)
-    per_device = corpus_full.reshape(-1, d_rows)[:, 0].astype(jnp.int32)
-    counts = (
-        jnp.sum((per_device[:, None] == corpora[None, :]).astype(f32), axis=0) * shard_length
-    )
-    own_corpus = (corpus[0] == corpora).astype(f32)
-    weight_row = jnp.sum(own_corpus * corpus_weight.astype(f32))
-    count_row = jnp.sum(own_corpus * counts)
-    factor = weight_row / DENOM * (jnp.sum(counts) / (CORPORA * count_row))
-    grad_full = upstream[0].astype(f32) * factor
-    grad_top = grad_full.astype(bf16)
-    grad_top4 = gather_group(grad_top)
 
     position = (place * shard_length + jnp.arange(shard_length, dtype=jnp.int32)).astype(f32)
     half = HEAD_SIZE // 2
@@ -567,47 +794,85 @@
     in_scale = norm_scale(inputs)
     normed = (inputs * in_scale * attn_gain_full).astype(bf16)
     joint_kv = mm(normed, wkv)
-    keys_values = heads_forward(joint_kv, wide_k, cos_table, sin_table, KEY_COLUMNS)
-    keys_values = gather_seq(keys_values).reshape(-1, 2 * KEY_COLUMNS)
+    own_kv = heads_forward(joint_kv, wide_k, cos_table, sin_table, KEY_COLUMNS)
+    own_kv, q_left_other, q_right_other = stage(own_kv, q_left_other, q_right_other)
+    keys_values = gather_seq(own_kv).reshape(-1, 2 * KEY_COLUMNS)
+    q_left = join_outer(q_left, q_left_other, 0)
+    q_right = joined(q_right, q_right_other, near, 0)
+    left_other, right_other, gate_lines = stage(
+        swap(q_left, 2), send_outer(q_right), gate_lines
+    )
+    q_left = joined(q_left, left_other, near, 1)
+    q_right = join_outer(q_right, right_other, 0)
+    gate_other = send_outer(gate_lines)
+    wq = gather_bit(q_left, 1, 2).reshape(width, -1)
+
+    corpora = jnp.arange(CORPORA, dtype=jnp.int32)
+    per_device = corpus_full.reshape(-1, d_rows)[:, 0].astype(jnp.int32)
+    counts = (
+        jnp.sum((per_device[:, None] == corpora[None, :]).astype(f32), axis=0) * shard_length
+    )
+    own_corpus = (corpus[0] == corpora).astype(f32)
+    weight_row = jnp.sum(own_corpus * corpus_weight.astype(f32))
+    count_row = jnp.sum(own_corpus * counts)
+    factor = weight_row / DENOM * (jnp.sum(counts) / (CORPORA * count_row))
+    grad_full = upstream[0].astype(f32) * factor
+    grad_top, wq = stage(grad_full.astype(bf16), wq)
+
     joint_q = mm(normed, wq)
     queries = heads_forward(joint_q, wide_q, cos_table, sin_table, QUERY_COLUMNS)
     place_array = place.reshape(1)
+    keys_values, queries, up_in, down_in = stage(
+        keys_values, queries, gate_up[:, :, 1], down_pair
+    )
+    up_lines = gather_seq(up_in)
+    down_lines = gather_seq(down_in)
     mixed, logs = attend_forward(place_array, queries, keys_values)
+    mixed, grad_top1, grad_top2, gate_other, wout_other = stage(
+        mixed, swap(grad_top, 1), swap(grad_top, 2), gate_other, swap(q_right, 1)
+    )
+    wout_t = joined(q_right, wout_other, core, 2).reshape(width, -1)
     middle = inputs + mm_t(mixed, wout_t)
 
     ffn_scale = norm_scale(middle)
     normed_ffn = (middle * ffn_scale * ffn_gain_full).astype(bf16)
-    normed4 = gather_group(normed_ffn)
-    gate = mm(normed4, wgate)
-    up = mm(normed4, wup)
-    sigmoid = 1.0 / (1.0 + jnp.exp(-gate))
-    silu = gate * sigmoid
-    hidden = (silu * up).astype(bf16)
-    grad_hidden = mm_t(grad_top4, wdown)
-    gate_back = (grad_hidden * up * (sigmoid * (1.0 + gate * (1.0 - sigmoid)))).astype(bf16)
-    up_back = (grad_hidden * silu).astype(bf16)
-    grad_normed_ffn = reduce_group(mm_t(gate_back, wgate) + mm_t(up_back, wup))
-    output = (middle + reduce_group(mm(hidden, wdown))).astype(bf16)
-
-    def scatter_hidden(grad):
-        blocks = grad.reshape(outer, 2, 2, seq_devices, d_rows, hidden_columns)
-        return reduce_seq(jnp.moveaxis(reduce_outer(blocks, 0), 2, 0))
-
-    grad_wdown = t_mm(hidden, grad_top4).astype(bf16)
-    grad_wdown = reduce_seq(
-        reduce_outer(grad_wdown.reshape(outer, seq_devices, f_rows, width), 0)
-    ).astype(f32)
-    grad_gate = scatter_hidden(t_mm(normed4, gate_back).astype(bf16))
-    grad_up = scatter_hidden(t_mm(normed4, up_back).astype(bf16))
-    grads = jnp.stack([grad_gate, grad_up], axis=2)
-    grads = joined(part(grads, near, 0), swap(part(grads, 1 - near, 0), 2), near, 0)
-    grads = joined(part(grads, core, 1), swap(part(grads, 1 - core, 1), 1), core, 1)
-
-    def from_group(blocks):
-        blocks = blocks.astype(f32).reshape(4, d_rows, outer, seq_devices * f_rows)
-        return jnp.transpose(blocks, (1, 2, 0, 3)).reshape(d_rows, -1)
-
-    grad_wgate, grad_wup = from_group(grads[:, :, 0]), from_group(grads[:, :, 1])
+    normed1, up_other, wgate = stage(
+        swap(normed_ffn, 1), send_outer(up_lines), spread_hidden(gate_lines, gate_other)
+    )
+    wup = spread_hidden(up_lines, up_other)
+    hidden_near, gate_near, up_near = hidden_pass((normed_ffn, normed1), wgate, wup)
+    normed2, hidden_near, grad_top3 = stage(
+        swap(normed_ffn, 2), hidden_near, swap(grad_top2, 1)
+    )
+    normed3 = swap(normed2, 1)
+    hidden_far, gate_far, up_far = hidden_pass((normed2, normed3), wgate, wup)
+    normed4 = (normed_ffn, normed1, normed2, normed3)
+    grad_top4 = (grad_top, grad_top1, grad_top2, grad_top3)
+    grad_wdown = weight_pass((hidden_near, hidden_far), grad_top4)
+    grad_wdown, wdown = stage(grad_wdown, down_lines.reshape(hidden_columns, width))
+    gate_far, up_far = gates_pass((grad_top2, grad_top3), wdown, gate_far, up_far)
+    own, send = back_pass((gate_far, up_far), (wgate, wup), True)
+    across, wdown = stage(across_group(own, send), wdown)
+    gate_near, up_near = gates_pass((grad_top, grad_top1), wdown, gate_near, up_near)
+    own, send = back_pass((gate_near, up_near), (wgate, wup), True)
+
+    hidden_shape = (outer, 2, 2, seq_devices, d_rows, hidden_columns)
+    down_shape = (seq_devices, outer, f_rows, width)
+    grad_wdown = grad_wdown.reshape(down_shape)
+    grad_wgate = weight_pass(normed4, (gate_near, gate_far)).reshape(hidden_shape)
+    grad_wup = weight_pass(normed4, (up_near, up_far)).reshape(hidden_shape)
+    across, own, send, grad_wgate, grad_wup, down_other = stage(
+        swap(across, 2),
+        own,
+        swap(send, 1),
+        grad_wgate,
+        grad_wup,
+        pass_outer(grad_wdown, 1),
+    )
+    grad_wdown = add_outer(grad_wdown, down_other, 1)
+    own = own + send.astype(f32)
+    grad_normed_ffn = own + across.astype(f32)
+    grad_wdown = reduce_seq(grad_wdown)
 
     grad_middle_part, grad_ffn_gain = norm_backward(
         middle, ffn_scale, ffn_gain_full, grad_normed_ffn
@@ -615,52 +880,124 @@
     grad_middle = grad_full + grad_middle_part
     grad_branch = grad_middle.astype(bf16)
     grad_mixed = mm(grad_branch, wout_t).astype(bf16)
-    grad_q, grad_kv = attend_backward(place_array, queries, keys_values, mixed, logs, grad_mixed)
-    grad_kv = reduce_seq(grad_kv.reshape(seq_devices, shard_length, -1))
+    attend = (place_array, queries, keys_values, mixed, logs)
+    grad_q1, grad_kv1 = attend_backward(0, 3, *attend, grad_mixed)
+    grad_q1, grad_kv1, gate_other, grad_mixed, grad_wdown = stage(
+        grad_q1, grad_kv1, pass_outer(grad_wgate, 0), grad_mixed, grad_wdown
+    )
+    grad_kv1 = reduce_seq(grad_kv1.reshape(seq_devices, shard_length, -1))
+    grad_gate = jnp.moveaxis(add_outer(grad_wgate, gate_other, 0), 2, 0)
+    grad_q2, grad_kv2 = attend_backward(3, 2, *attend, grad_mixed)
+    shape = (outer, 2, 2, seq_devices, d_rows)
+    grad_wout = t_mm(grad_branch, mixed).astype(bf16).reshape(*shape, QUERY_COLUMNS)
+    grad_q2, grad_kv2, up_other, hidden_near, hidden_far, grad_kv1, wout_other = stage(
+        grad_q2,
+        grad_kv2,
+        pass_outer(grad_wup, 0),
+        hidden_near,
+        hidden_far,
+        grad_kv1,
+        pass_bit(grad_wout, 1, 2),
+    )
+    grad_kv2 = reduce_seq(grad_kv2.reshape(seq_devices, shard_length, -1))
+
+    grad_up = jnp.moveaxis(add_outer(grad_wup, up_other, 0), 2, 0)
+    grad_q = jnp.concatenate([grad_q1, grad_q2], axis=1)
     joint_grad_q, gain_q = heads_backward(
         grad_q, joint_q, wide_q, cos_table, sin_table, QUERY_COLUMNS
     )
-    grad_query_out = reduce_all(
-        jnp.concatenate(
-            [t_mm(normed, joint_grad_q).astype(bf16), t_mm(grad_branch, mixed).astype(bf16)],
-            axis=1,
-        ),
-        d_rows,
-    ).astype(f32)
+    grad_wq = t_mm(normed, joint_grad_q).astype(bf16).reshape(*shape, QUERY_COLUMNS)
+    grad_wout = add_bit(grad_wout, wout_other, 1, 2)
+    own_far, send_far = back_pass((hidden_far,), (wdown,), False)
+    own_near, send_near = back_pass((hidden_near,), (wdown,), False)
+    grad_kv2, wq_other, grad_up, grad_gate, own_far, send_far, send_near = stage(
+        grad_kv2, pass_bit(grad_wq, 1, 2), grad_up, grad_gate, own_far, send_far, send_near
+    )
+    gate_up = reduce_seq(jnp.stack([grad_gate, grad_up], axis=3))
+    grad_wq = add_bit(grad_wq, wq_other, 1, 2)
+    wq_other, wout_other = pass_bit(grad_wq, 2, 1), pass_outer(grad_wout, 0)
+
+    grad_kv1, grad_kv2 = (
+        part_.reshape(shard_length, 2, -1) for part_ in (grad_kv1, grad_kv2)
+    )
+    grad_kv = jnp.concatenate([grad_kv1, grad_kv2], axis=2).reshape(shard_length, -1)
     joint_grad_kv, gain_k = heads_backward(
         grad_kv, joint_kv, wide_k, cos_table, sin_table, KEY_COLUMNS
     )
-    grad_wkv = reduce_all(t_mm(normed, joint_grad_kv).astype(bf16), d_rows).astype(f32)
+    grad_wkv = t_mm(normed, joint_grad_kv).astype(bf16)
     grad_normed = mm_t(joint_grad_q, wq) + mm_t(joint_grad_kv, wkv)
     grad_input_part, grad_attn_gain = norm_backward(
         inputs, in_scale, attn_gain_full, grad_normed
     )
     input_grad = (grad_middle + grad_input_part).astype(bf16)
 
-    small = lax.psum(
+    gain_rows = jnp.stack([grad_attn_gain, grad_ffn_gain]).astype(bf16)
+    gain_columns = t_mm(gain_rows, jnp.eye(2, LANES, dtype=bf16)).astype(bf16)
+    left = grad_wkv[:, : 3 * LANES].reshape(*shape, -1)
+    right = jnp.concatenate([grad_wkv[:, 3 * LANES :], gain_columns], axis=1)
+    right = right.reshape(*shape, -1)
+    left, right, left_other, right_other, wq_other, wout_other = stage(
+        left, right, pass_bit(left, 1, 2), pass_bit(right, 1, 2), wq_other, wout_other
+    )
+    left = add_bit(left, left_other, 1, 2)
+    right = add_bit(right, right_other, 1, 2)
+    grad_wq = add_bit(grad_wq, wq_other, 2, 1)
+    grad_wout = add_outer(grad_wout, wout_other, 0)
+    left_other, right_other, wq_other, wout_other = stage(
+        pass_bit(left, 2, 1),
+        pass_outer(right, 0),
+        pass_outer(grad_wq, 0),
+        pass_bit(grad_wout, 2, 0),
+    )
+    left = add_bit(left, left_other, 2, 1)
+    right = add_outer(right, right_other, 0)
+    left_other, right_other = stage(pass_outer(left, 0), pass_bit(right, 2, 0))
+    sums = reduce_seq(
         jnp.concatenate(
             [
-                grad_attn_gain,
-                grad_ffn_gain,
+                add_outer(grad_wq, wq_other, 0),
+                add_outer(left, left_other, 0),
+                add_bit(right, right_other, 2, 0),
+                add_bit(grad_wout, wout_other, 2, 0),
+            ],
+            axis=-1,
+        )
+    )
+    own_near = own_near + swap(send_near, 1).astype(f32)
+    across = across_group(own_far, send_far)
+    output = (middle + own_near + swap(across, 2).astype(f32)).astype(bf16)
+    columns = QUERY_COLUMNS + 2 * KEY_COLUMNS
+    long_gains = sums[:, columns : columns + 2].astype(f32)
+    head_gains = sum_all(
+        jnp.concatenate(
+            [
                 jnp.sum(gain_q[0].reshape(-1, HEAD_SIZE), axis=0),
                 jnp.sum(gain_k[0, :KEY_COLUMNS].reshape(-1, HEAD_SIZE), axis=0),
             ]
-        ),
-        ("rows", "seq"),
-    )
-    start = (lax.axis_index("rows") * seq_devices + place) * d_rows
+        )[None]
+    )[0]
+
+    grads = gate_up
+    grads = joined(part(grads, near, 0), swap(part(grads, 1 - near, 0), 2), near, 0)
+    grads = joined(part(grads, core, 1), swap(part(grads, 1 - core, 1), 1), core, 1)
+
+    def from_group(blocks):
+        blocks = blocks.reshape(4, d_rows, seq_devices, outer, f_rows)
+        return jnp.transpose(blocks, (1, 3, 0, 2, 4)).reshape(d_rows, -1).astype(f32)
+
+    grad_wgate, grad_wup = from_group(grads[:, :, 0]), from_group(grads[:, :, 1])
     return (
         output[None],
         input_grad[None],
-        jnp.concatenate([grad_query_out[:, :QUERY_COLUMNS], grad_wkv], axis=1),
-        grad_query_out[:, QUERY_COLUMNS:].T,
+        sums[:, :columns].astype(f32),
+        sums[:, columns + LANES :].T.astype(f32),
         grad_wgate,
         grad_wup,
-        grad_wdown,
-        lax.dynamic_slice_in_dim(small[:width], start, d_rows),
-        lax.dynamic_slice_in_dim(small[width : 2 * width], start, d_rows),
-        small[2 * width : 2 * width + HEAD_SIZE],
-        small[2 * width + HEAD_SIZE :],
+        grad_wdown.astype(f32),
+        long_gains[:, 0],
+        long_gains[:, 1],
+        head_gains[:HEAD_SIZE],
+        head_gains[HEAD_SIZE:],
     )
 
 

time: 1010 us -> 857 us (0.85)
  Pallas kernels: 69.8 us -> 257 us
  matrix products: 216 us -> 43.2 us
  waiting for transfers between devices: 380 us -> 303 us
  blocking collectives: 71.3 us -> 19.9 us
  other arithmetic: 127 us -> 81.3 us
    pallas_call x1 -> x32, Pallas kernels: 29.7 us -> 218 us  [the longest x3 46.8 us: weight_pass(): pl.pallas_call(partial(weight_kernel, len(lefts)), grid=(rows // tile,),...]
    all_gather x5, waiting for transfers between devices: 99.9 us -> 11.2 us  [gather_seq(): return lax.all_gather(values, 'seq', axis=0, tiled=False)]
    dot_general x6 -> x3, matrix products: 84.5 us -> 16 us  [mm_t(): return jnp.einsum('ab,cb->ac', left, right, preferred_element_type=f32)]
    reduce_scatter x6 -> x5, waiting for transfers between devices: 59.9 us -> 1.1 us  [reduce_seq(): return lax.psum_scatter(values, 'seq', scatter_dimension=0, tiled=False)]
    dot_general x6 -> x3, matrix products: 70 us -> 12.8 us  [mm(): return jnp.einsum('ab,bc->ac', left, right, preferred_element_type=f32)]
    psum x1 -> x0, blocking collectives: 52.6 us -> none  [shards(): lax.psum(jnp.concatenate([grad_attn_gain, grad_ffn_gain, jnp.sum(gain_q[0...]
    dot_general x6 -> x4, matrix products: 61.3 us -> 14.1 us  [t_mm(): return jnp.einsum('ab,ac->bc', left, right, preferred_element_type=f32)]
    ppermute x0 -> x5, waiting for transfers between devices: none -> 45.6 us  [sum_all(): values = values + lax.ppermute(values, axis, pairs)]
  transfers between devices with their start and end apart: 53 -> 61, of which waited for: 22 -> 26; matrix products, arithmetic and copies ran while one was open for 37% -> 16% of each run, Pallas kernels for 7% -> 26%
where the time goes in v2:
time: 857 us; the launch traced here: 848 us
  waiting for transfers between devices  303 us (35%)
  Pallas kernels  257 us (30%)
  other arithmetic  81.3 us (9%)
  local copies, waits for them, and re-layouts  77.3 us (9%)
  starting transfers between devices  47.2 us (6%)
  matrix products  43.2 us (5%)
  blocking collectives  19.9 us (2%)
  between operations  18.5 us (2%)
    ppermute x46, waiting for transfers between devices, swap(): return lax.ppermute(values, 'rows', pairs)  245 us
    pallas_call x3, Pallas kernels, weight_pass(): pl.pallas_call(partial(weight_kernel, len(lefts)), grid=(rows // tile,),...  46.8 us
    pallas_call x4, Pallas kernels, back_pass(): pl.pallas_call(partial(back_kernel, count, transposed), grid=(width // ti...  46.2 us
    ppermute x5, waiting for transfers between devices, sum_all(): values = values + lax.ppermute(values, axis, pairs)  45.6 us
    ppermute x46, starting transfers between devices, swap(): return lax.ppermute(values, 'rows', pairs)  37.2 us
    pallas_call x2, Pallas kernels, attend_backward(): pl.pallas_call(partial(attend_backward_kernel, first, count), grid_spec=p...  32.2 us
    pallas_call x2, Pallas kernels, hidden_pass(): pl.pallas_call(hidden_kernel, grid=(pl.cdiv(columns, tile),), in_specs=[w...  32 us
    pallas_call x2, Pallas kernels, gates_pass(): pl.pallas_call(gates_kernel, grid=(pl.cdiv(columns, tile),), in_specs=[wh...  24.1 us
  transfers between devices with their start and end apart: 61, of which 26 were waited for; matrix products, arithmetic and copies ran while one was open for 16% of the time, Pallas kernels for 26%

profile of v2, /device:TPU:0, one launch (start us, length us, event | category | flops | bytes accessed | tf_op | source)
XLA Modules:
  0.0 847.5 jit_solution(11592019530611918743)
XLA Ops:
  27.7 19.9 %all-gather = bf16[256,768]{1,0:T(8,128)(2,1)S(1)} all-gather(bf16[64,768]{1,0:T(8,128)(2,1)S(1)} %fusion.35), channel_id=2, replica_groups=mesh['rows'=8,'seq'=4] {'seq'}, dimensions={0}, use_global_device_ids=true | all-gather | bytes 491520 | tf_op jit(solution)/shard_map/all_gather | solution.py:652
  59.6 11.3 %collective-permute-done.4 = bf16[4,64,384]{2,1,0:T(8,128)(2,1)S(1)} collective-permute-done((bf16[4,64,384]{2,1,0:T(8,128)(2,1)S(1)}, bf16[4,64,384]{2,1,0:T(8,128)(2,1)S(1)}, u32[]{:S(2)}, u32[]{:S(2)}) %collective-permute-start.4) | collective-permute-done | bytes 196640 | tf_op jit(solution)/shard_map/ppermute | solution.py:555
  110.1 26.8 %collective-permute-done.11 = bf16[2,4,64,1280]{3,2,1,0:T(8,128)(2,1)} collective-permute-done((bf16[2,4,64,1280]{3,2,1,0:T(8,128)(2,1)S(1)}, bf16[2,4,64,1280]{3,2,1,0:T(8,128)(2,1)}, u32[]{:S(2)}, u32[]{:S(2)}) %collective-permute-start.11) | collective-permute-done | bytes 1310752 | tf_op jit(solution)/shard_map/ppermute | solution.py:555
  186.5 11.9 %attend_forward.1 = (bf16[512,1280]{1,0:T(8,128)(2,1)S(1)}, f32[512,1280]{1,0:T(8,128)S(1)}) custom-call(s32[1]{0:T(128)} %bitcast.1.place_ref, bf16[512,1280]{1,0:T(8,128)(2,1)S(1)} %copy-done, bf16[2048,640]{1,0:T(8,128)(2,1)} %all-gather.14.cloned.1.call-done.k_ref.v_ref, bf16[2048,640]{1,0:T(8,128)(2,1)} %all-gather.14.cloned.1.call-done.k_ref.v_ref), custom_call_target="tpu_custom_call" | custom-call | flops 1000 | bytes 1000 | tf_op jit(solution)/shard_map/attend_forward/pallas_call | solution.py:177
  200.0 36.9 %collective-permute-done.16 = bf16[4,2,2,64,1152]{4,3,2,1,0:T(8,128)(2,1)} collective-permute-done((bf16[4,2,2,64,1152]{4,3,2,1,0:T(8,128)(2,1)}, bf16[4,2,2,64,1152]{4,3,2,1,0:T(8,128)(2,1)}, u32[]{:S(2)}, u32[]{:S(2)}) %collective-permute-start.16) | collective-permute-done | bytes 2359328 | tf_op jit(solution)/shard_map/ppermute | solution.py:555
  264.1 39.8 %collective-permute-done.20 = bf16[4,2,2,64,1152]{4,3,2,1,0:T(8,128)(2,1)} collective-permute-done((bf16[4,2,2,64,1152]{4,3,2,1,0:T(8,128)(2,1)}, bf16[4,2,2,64,1152]{4,3,2,1,0:T(8,128)(2,1)}, u32[]{:S(2)}, u32[]{:S(2)}) %collective-permute-start.20) | collective-permute-done | bytes 2359328 | tf_op jit(solution)/shard_map/ppermute | solution.py:555
  311.4 15.6 %hidden_pass.2 = (bf16[1024,1152]{1,0:T(8,128)(2,1)}, bf16[1024,1152]{1,0:T(8,128)(2,1)}, bf16[1024,1152]{1,0:T(8,128)(2,1)}) custom-call(bf16[512,2048]{1,0:T(8,128)(2,1)S(1)} %multiply_convert_fusion.n0_ref.refs_0_, bf16[512,2048]{1,0:T(8,128)(2,1)} %collective-permute-done.19.n1_ref.refs_1_, bf16[2048,1152]{1,0:T(8,128)(2,1)} %bitcast.290, ...), custom_call_target="tpu_custom_call" | custom-call | flops 1000 | bytes 1000 | tf_op jit(solution)/shard_map/hidden_pass/pallas_call | solution.py:344
  331.5 16.4 %hidden_pass.3 = (bf16[1024,1152]{1,0:T(8,128)(2,1)}, bf16[1024,1152]{1,0:T(8,128)(2,1)}, bf16[1024,1152]{1,0:T(8,128)(2,1)}) custom-call(bf16[512,2048]{1,0:T(8,128)(2,1)} %collective-permute-done.18.n0_ref.refs_2_, bf16[512,2048]{1,0:T(8,128)(2,1)S(1)} %collective-permute-done.22.n1_ref.refs_3_, bf16[2048,1152]{1,0:T(8,128)(2,1)} %bitcast.291, ...), custom_call_target="tpu_custom_call" | custom-call | flops 1000 | bytes 1000 | tf_op jit(solution)/shard_map/hidden_pass/pallas_call | solution.py:344
  347.9 14.9 %weight_pass.3 = bf16[1152,2048]{1,0:T(8,128)(2,1)} custom-call(bf16[1024,1152]{1,0:T(8,128)(2,1)} %get-tuple-element.190.refs_0_, bf16[1024,1152]{1,0:T(8,128)(2,1)} %get-tuple-element.198.refs_1_.refs_0_, bf16[512,2048]{1,0:T(8,128)(2,1)S(1)} %copy-done.3, bf16[512,2048]{1,0:T(8,128)(2,1)} %collective-permute-done.14.refs_3_.g1_ref, ...), custom_call_target="tpu_custom_call" | custom-call | flops 1000 | bytes 1000 | tf_op jit(solution)/shard_map/weight_pass/pallas_call | solution.py:452
  362.8 12.5 %gates_pass.2 = (bf16[1024,1152]{1,0:T(8,128)(2,1)}, bf16[1024,1152]{1,0:T(8,128)(2,1)}) custom-call(bf16[512,2048]{1,0:T(8,128)(2,1)} %collective-permute-done.15.refs_4_.g0_ref, bf16[512,2048]{1,0:T(8,128)(2,1)} %collective-permute-done.21.refs_5_.g1_ref, bf16[1152,2048]{1,0:T(8,128)(2,1)} %bitcast.298, bf16[1024,1152]{1,0:T(8,128)(2,1)} %get-tuple-element.163.gate_ref, ...), custom_call_target="tpu_custom_call" | custom-call | flops 1000 | bytes 1000 | tf_op jit(solution)/shard_map/gates_pass/pallas_call | solution.py:379
  377.0 14.9 %back_pass.4 = (f32[512,2048]{1,0:T(8,128)}, bf16[512,2048]{1,0:T(8,128)(2,1)}) custom-call(bf16[1024,1152]{1,0:T(8,128)(2,1)S(1)} %copy-done.8, bf16[1024,1152]{1,0:T(8,128)(2,1)} %get-tuple-element.166.refs_1_.refs_5_, bf16[2048,1152]{1,0:T(8,128)(2,1)} %bitcast.292, bf16[2048,1152]{1,0:T(8,128)(2,1)} %bitcast.296), custom_call_target="tpu_custom_call" | custom-call | flops 1000 | bytes 1000 | tf_op jit(solution)/shard_map/back_pass/pallas_call | solution.py:418
  402.3 11.7 %gates_pass.3 = (bf16[1024,1152]{1,0:T(8,128)(2,1)}, bf16[1024,1152]{1,0:T(8,128)(2,1)}) custom-call(bf16[512,2048]{1,0:T(8,128)(2,1)S(1)} %copy-done.4, bf16[512,2048]{1,0:T(8,128)(2,1)} %collective-permute-done.14.refs_3_.g1_ref, bf16[1152,2048]{1,0:T(8,128)(2,1)} %bitcast.299, bf16[1024,1152]{1,0:T(8,128)(2,1)} %get-tuple-element.171.gate_ref, ...), custom_call_target="tpu_custom_call" | custom-call | flops 1000 | bytes 1000 | tf_op jit(solution)/shard_map/gates_pass/pallas_call | solution.py:379
  415.7 14.9 %back_pass.5 = (f32[512,2048]{1,0:T(8,128)}, bf16[512,2048]{1,0:T(8,128)(2,1)}) custom-call(bf16[1024,1152]{1,0:T(8,128)(2,1)S(1)} %copy-done.9, bf16[1024,1152]{1,0:T(8,128)(2,1)} %get-tuple-element.174.refs_1_.refs_4_, bf16[2048,1152]{1,0:T(8,128)(2,1)} %bitcast.293, bf16[2048,1152]{1,0:T(8,128)(2,1)} %bitcast.297), custom_call_target="tpu_custom_call" | custom-call | flops 1000 | bytes 1000 | tf_op jit(solution)/shard_map/back_pass/pallas_call | solution.py:418
  430.5 16.0 %weight_pass.4 = bf16[2048,1152]{1,0:T(8,128)(2,1)} custom-call(bf16[512,2048]{1,0:T(8,128)(2,1)S(1)} %multiply_convert_fusion.n0_ref.refs_0_, bf16[512,2048]{1,0:T(8,128)(2,1)} %collective-permute-done.19.n1_ref.refs_1_, bf16[512,2048]{1,0:T(8,128)(2,1)} %collective-permute-done.18.n0_ref.refs_2_, bf16[512,2048]{1,0:T(8,128)(2,1)} %copy-done.1, ...), custom_call_target="tpu_custom_call" | custom-call | flops 1000 | bytes 1000 | tf_op jit(solution)/shard_map/weight_pass/pallas_call | solution.py:452
  446.5 15.9 %weight_pass.5 = bf16[2048,1152]{1,0:T(8,128)(2,1)} custom-call(bf16[512,2048]{1,0:T(8,128)(2,1)S(1)} %multiply_convert_fusion.n0_ref.refs_0_, bf16[512,2048]{1,0:T(8,128)(2,1)} %collective-permute-done.19.n1_ref.refs_1_, bf16[512,2048]{1,0:T(8,128)(2,1)} %collective-permute-done.18.n0_ref.refs_2_, bf16[512,2048]{1,0:T(8,128)(2,1)} %copy-done.1, ...), custom_call_target="tpu_custom_call" | custom-call | flops 1000 | bytes 1000 | tf_op jit(solution)/shard_map/weight_pass/pallas_call | solution.py:452
  481.8 18.9 %attend_backward.2 = (bf16[512,768]{1,0:T(8,128)(2,1)S(1)}, bf16[2048,384]{1,0:T(8,128)(2,1)}) custom-call(s32[1]{0:T(128)} %bitcast.1.place_ref, bf16[512,1280]{1,0:T(8,128)(2,1)S(1)} %copy-done, bf16[2048,640]{1,0:T(8,128)(2,1)} %all-gather.14.cloned.1.call-done.k_ref.v_ref, bf16[2048,640]{1,0:T(8,128)(2,1)} %all-gather.14.cloned.1.call-done.k_ref.v_ref, ...), custom_call_target="tpu_custom_call" | custom-call | flops 1000 | bytes 1000 | tf_op jit(solution)/shard_map/attend_backward/pallas_call | solution.py:300
  500.6 21.9 %collective-permute-done.27 = bf16[2,2,4,64,1152]{4,3,1,0,2:T(8,128)(2,1)} collective-permute-done((bf16[2,2,4,64,1152]{4,3,1,0,2:T(8,128)(2,1)S(1)}, bf16[2,2,4,64,1152]{4,3,1,0,2:T(8,128)(2,1)}, u32[]{:S(2)}, u32[]{:S(2)}) %collective-permute-start.27) | collective-permute-done | bytes 2359328 | tf_op jit(solution)/shard_map/ppermute | solution.py:555
  535.4 13.3 %attend_backward.3 = (bf16[512,512]{1,0:T(8,128)(2,1)S(1)}, bf16[2048,256]{1,0:T(8,128)(2,1)}) custom-call(s32[1]{0:T(128)} %bitcast.1.place_ref, bf16[512,1280]{1,0:T(8,128)(2,1)S(1)} %copy-done, bf16[2048,640]{1,0:T(8,128)(2,1)} %all-gather.14.cloned.1.call-done.k_ref.v_ref, bf16[2048,640]{1,0:T(8,128)(2,1)} %all-gather.14.cloned.1.call-done.k_ref.v_ref, ...), custom_call_target="tpu_custom_call" | custom-call | flops 1000 | bytes 1000 | tf_op jit(solution)/shard_map/attend_backward/pallas_call | solution.py:300
  549.5 38.9 %collective-permute-done.28 = bf16[2,2,4,64,1152]{4,3,1,0,2:T(8,128)(2,1)} collective-permute-done((bf16[2,2,4,64,1152]{4,3,1,0,2:T(8,128)(2,1)S(1)}, bf16[2,2,4,64,1152]{4,3,1,0,2:T(8,128)(2,1)}, u32[]{:S(2)}, u32[]{:S(2)}) %collective-permute-start.28) | collective-permute-done | bytes 2359328 | tf_op jit(solution)/shard_map/ppermute | solution.py:555
  590.6 8.9 %heads_backward.2 = (bf16[512,1280]{1,0:T(8,128)(2,1)}, f32[8,1280]{1,0:T(8,128)}) custom-call(bf16[512,1280]{1,0:T(8,128)(2,1)} %pad_maximum_fusion.6.grad_ref, f32[512,1280]{1,0:T(8,128)} %fusion.50.joint_ref, f32[8,1280]{1,0:T(8,128)} %broadcast_in_dim.14.gain_ref, f32[512,128]{1,0:T(8,128)} %get-tuple-element.268.cos_ref, ...), custom_call_target="tpu_custom_call" | custom-call | flops 1000 | bytes 1000 | tf_op jit(solution)/shard_map/heads_backward/pallas_call | solution.py:109
  613.6 8.4 back_pass.7
  683.0 14.9 %collective-permute-done.36 = bf16[2,4,64,1280]{3,2,1,0:T(8,128)(2,1)S(1)} collective-permute-done((bf16[2,4,64,1280]{3,2,1,0:T(8,128)(2,1)S(1)}, bf16[2,4,64,1280]{3,2,1,0:T(8,128)(2,1)S(1)}, u32[]{:S(2)}, u32[]{:S(2)}) %collective-permute-start.36) | collective-permute-done | bytes 1310752 | tf_op jit(solution)/shard_map/ppermute | solution.py:555
  710.4 13.8 %collective-permute-done.39 = bf16[2,4,64,384]{3,2,1,0:T(8,128)(2,1)S(1)} collective-permute-done((bf16[2,4,64,384]{3,2,1,0:T(8,128)(2,1)S(1)}, bf16[2,4,64,384]{3,2,1,0:T(8,128)(2,1)S(1)}, u32[]{:S(2)}, u32[]{:S(2)}) %collective-permute-start.39) | collective-permute-done | bytes 393248 | tf_op jit(solution)/shard_map/ppermute | solution.py:555
  742.0 40.0 %collective-permute-done.47 = f32[1,128]{1,0:T(1,128)S(1)} collective-permute-done((f32[1,128]{1,0:T(1,128)S(1)}, f32[1,128]{1,0:T(1,128)S(1)}, u32[]{:S(2)}, u32[]{:S(2)}) %collective-permute-start.47) | collective-permute-done | bytes 544 | tf_op jit(solution)/shard_map/ppermute | solution.py:665
  (423 shorter events, 370.7 us)
Async XLA Ops:
  7.2 44.7 %all-gather.12.cloned.1.call-start = ((), (), s32[]{:S(2)}) async-start(), calls=%async_computation.10 | async-start | bytes 1638400 | tf_op jit(solution)/shard_map/all_gather | solution.py:652
  9.8 128.6 %all-gather.16.cloned.1.call-start = ((), (), s32[]{:S(2)}) async-start(), calls=%async_computation.12 | async-start | bytes 2949120 | tf_op jit(solution)/shard_map/all_gather | solution.py:652
  72.2 106.3 %all-gather.14.cloned.1.call-start = ((), (), s32[]{:S(2)}) async-start(), calls=%async_computation.11 | async-start | bytes 3276800 | tf_op jit(solution)/shard_map/all_gather | solution.py:652
  110.1 140.5 %all-gather.18.cloned.1.call-start = ((), (), s32[]{:S(2)}) async-start(), calls=%async_computation.13 | async-start | bytes 2949120 | tf_op jit(solution)/shard_map/all_gather | solution.py:652
  178.5 184.3 %all-gather.20.cloned.1.call-start = ((), (), s32[]{:S(2)}) async-start(), calls=%async_computation.14 | async-start | bytes 5898240 | tf_op jit(solution)/shard_map/all_gather | solution.py:652
  182.9 54.0 %collective-permute-start.17 = (bf16[2,2,4,64,1280]{4,3,2,1,0:T(8,128)(2,1)}, bf16[2,2,4,64,1280]{4,3,2,1,0:T(8,128)(2,1)}, u32[]{:S(2)}, u32[]{:S(2)}) collective-permute-start(bf16[2,2,4,64,1280]{4,3,2,1,0:T(8,128)(2,1)} %bitcast.63), channel_id=1, source_target_pairs={{0,4},{4,0},{8,12},{12,8},{16,20},{20,16},{24,28},{28,24},{1,5},{5... | collective-permute-start | bytes 7864328 | tf_op jit(solution)/shard_map/ppermute | solution.py:555
  182.9 54.0 %collective-permute-start.16 = (bf16[4,2,2,64,1152]{4,3,2,1,0:T(8,128)(2,1)}, bf16[4,2,2,64,1152]{4,3,2,1,0:T(8,128)(2,1)}, u32[]{:S(2)}, u32[]{:S(2)}) collective-permute-start(bf16[4,2,2,64,1152]{4,3,2,1,0:T(8,128)(2,1)} %bitcast.51), channel_id=1, source_target_pairs={{0,16},{4,20},{8,24},{12,28},{16,0},{20,4},{24,8},{28,12},{1,17},{... | collective-permute-start | bytes 7077896 | tf_op jit(solution)/shard_map/ppermute | solution.py:555
  184.4 52.5 %collective-permute-start.14 = (bf16[512,2048]{1,0:T(8,128)(2,1)S(1)}, bf16[512,2048]{1,0:T(8,128)(2,1)}, u32[]{:S(2)}, u32[]{:S(2)}) collective-permute-start(bf16[512,2048]{1,0:T(8,128)(2,1)S(1)} %bitcast_convert_fusion.refs_2_.g0_ref), channel_id=1, source_target_pairs={{0,4},{4,0},{8,12},{12,8},{16,20},{20,16},{24,28},{28,24},{1,5},{5... | collective-permute-start | bytes 6291464 | tf_op jit(solution)/shard_map/ppermute | solution.py:555
  184.6 52.3 %collective-permute-start.15 = (bf16[512,2048]{1,0:T(8,128)(2,1)S(1)}, bf16[512,2048]{1,0:T(8,128)(2,1)}, u32[]{:S(2)}, u32[]{:S(2)}) collective-permute-start(bf16[512,2048]{1,0:T(8,128)(2,1)S(1)} %bitcast_convert_fusion.refs_2_.g0_ref), channel_id=1, source_target_pairs={{0,8},{4,12},{8,0},{12,4},{16,24},{20,28},{24,16},{28,20},{1,9},{5... | collective-permute-start | bytes 6291464 | tf_op jit(solution)/shard_map/ppermute | solution.py:555
  186.1 336.5 %reduce-scatter.6.cloned.1.call-start = ((), (), s32[]{:S(2)}) async-start(), calls=%async_computation.5 | async-start | bytes 2949120 | tf_op jit(solution)/shard_map/reduce_scatter | solution.py:656
  250.6 53.3 %collective-permute-start.20 = (bf16[4,2,2,64,1152]{4,3,2,1,0:T(8,128)(2,1)}, bf16[4,2,2,64,1152]{4,3,2,1,0:T(8,128)(2,1)}, u32[]{:S(2)}, u32[]{:S(2)}) collective-permute-start(bf16[4,2,2,64,1152]{4,3,2,1,0:T(8,128)(2,1)} %bitcast.336), channel_id=1, source_target_pairs={{0,16},{4,20},{8,24},{12,28},{16,0},{20,4},{24,8},{28,12},{1,17},{... | collective-permute-start | bytes 7077896 | tf_op jit(solution)/shard_map/ppermute | solution.py:555
  254.9 72.1 %collective-permute-start.18 = (bf16[512,2048]{1,0:T(8,128)(2,1)S(1)}, bf16[512,2048]{1,0:T(8,128)(2,1)}, u32[]{:S(2)}, u32[]{:S(2)}) collective-permute-start(bf16[512,2048]{1,0:T(8,128)(2,1)S(1)} %multiply_convert_fusion.n0_ref.refs_0_), channel_id=1, source_target_pairs={{0,8},{4,12},{8,0},{12,4},{16,24},{20,28},{24,16},{28,20},{1,9},{5... | collective-permute-start | bytes 6291464 | tf_op jit(solution)/shard_map/ppermute | solution.py:555
  256.5 70.6 %collective-permute-start.21 = (bf16[512,2048]{1,0:T(8,128)(2,1)}, bf16[512,2048]{1,0:T(8,128)(2,1)}, u32[]{:S(2)}, u32[]{:S(2)}) collective-permute-start(bf16[512,2048]{1,0:T(8,128)(2,1)} %collective-permute-done.15.refs_4_.g0_ref), channel_id=1, source_target_pairs={{0,4},{4,0},{8,12},{12,8},{16,20},{20,16},{24,28},{28,24},{1,5},{5... | collective-permute-start | bytes 6291464 | tf_op jit(solution)/shard_map/ppermute | solution.py:555
  395.6 66.8 %collective-permute-start.26 = (bf16[4,144,2048]{2,1,0:T(8,128)(2,1)}, bf16[4,144,2048]{2,1,0:T(8,128)(2,1)}, u32[]{:S(2)}, u32[]{:S(2)}) collective-permute-start(bf16[4,144,2048]{2,1,0:T(8,128)(2,1)} %dynamic-slice_bitcast_fusion.1), channel_id=1, source_target_pairs={{0,16},{4,20},{8,24},{12,28},{16,0},{20,4},{24,8},{28,12},{1,17},{... | collective-permute-start | bytes 7077896 | tf_op jit(solution)/shard_map/ppermute | solution.py:555
  400.9 61.5 %collective-permute-start.24 = (bf16[512,2048]{1,0:T(8,128)(2,1)}, bf16[512,2048]{1,0:T(8,128)(2,1)}, u32[]{:S(2)}, u32[]{:S(2)}) collective-permute-start(bf16[512,2048]{1,0:T(8,128)(2,1)} %add_convert_fusion.2), channel_id=1, source_target_pairs={{0,8},{4,12},{8,0},{12,4},{16,24},{20,28},{24,16},{28,20},{1,9},{5... | collective-permute-start | bytes 6291464 | tf_op jit(solution)/shard_map/ppermute | solution.py:555
  466.7 121.7 %reduce-scatter.8.cloned.1.call-start = ((), (), s32[]{:S(2)}) async-start(), calls=%async_computation.6 | async-start | bytes 1966080 | tf_op jit(solution)/shard_map/reduce_scatter | solution.py:656
  468.8 53.8 %collective-permute-start.27 = (bf16[2,2,4,64,1152]{4,3,1,0,2:T(8,128)(2,1)S(1)}, bf16[2,2,4,64,1152]{4,3,1,0,2:T(8,128)(2,1)}, u32[]{:S(2)}, u32[]{:S(2)}) collective-permute-start(bf16[2,2,4,64,1152]{4,3,1,0,2:T(8,128)(2,1)S(1)} %copy_bitcast_fusion.3), channel_id=1, source_target_pairs={{0,16},{4,20},{8,24},{12,28},{16,0},{20,4},{24,8},{28,12},{1,17},{... | collective-permute-start | bytes 7077896 | tf_op jit(solution)/shard_map/ppermute | solution.py:555
  525.2 118.5 %reduce-scatter.10.cloned.1.call-start = ((), (), s32[]{:S(2)}) async-start(), calls=%async_computation.7 | async-start | bytes 1310720 | tf_op jit(solution)/shard_map/reduce_scatter | solution.py:656
  532.6 55.7 %collective-permute-start.29 = (bf16[2,2,4,64,1280]{4,3,2,1,0:T(8,128)(2,1)S(1)}, bf16[2,2,4,64,1280]{4,3,2,1,0:T(8,128)(2,1)}, u32[]{:S(2)}, u32[]{:S(2)}) collective-permute-start(bf16[2,2,4,64,1280]{4,3,2,1,0:T(8,128)(2,1)S(1)} %dynamic-slice_bitcast_fusion), channel_id=1, source_target_pairs={{0,4},{4,0},{8,12},{12,8},{16,20},{20,16},{24,28},{28,24},{1,5},{5... | collective-permute-start | bytes 7864328 | tf_op jit(solution)/shard_map/ppermute | solution.py:555
  534.6 53.8 %collective-permute-start.28 = (bf16[2,2,4,64,1152]{4,3,1,0,2:T(8,128)(2,1)S(1)}, bf16[2,2,4,64,1152]{4,3,1,0,2:T(8,128)(2,1)}, u32[]{:S(2)}, u32[]{:S(2)}) collective-permute-start(bf16[2,2,4,64,1152]{4,3,1,0,2:T(8,128)(2,1)S(1)} %copy_bitcast_fusion.2), channel_id=1, source_target_pairs={{0,16},{4,20},{8,24},{12,28},{16,0},{20,4},{24,8},{28,12},{1,17},{... | collective-permute-start | bytes 7077896 | tf_op jit(solution)/shard_map/ppermute | solution.py:555
  611.8 190.5 %reduce-scatter.14.cloned.1.call-start = ((), (), s32[]{:S(2)}) async-start(), calls=%async_computation.9 | async-start | bytes 5898240 | tf_op jit(solution)/shard_map/reduce_scatter | solution.py:656
  648.8 164.7 %reduce-scatter.12.cloned.1.call-start = ((), (), s32[]{:S(2)}) async-start(), calls=%async_computation.8 | async-start | bytes 2129920 | tf_op jit(solution)/shard_map/reduce_scatter | solution.py:656
  710.4 95.7 %collective-permute-start.31 = (bf16[512,2048]{1,0:T(8,128)(2,1)S(1)}, bf16[512,2048]{1,0:T(8,128)(2,1)}, u32[]{:S(2)}, u32[]{:S(2)}) collective-permute-start(bf16[512,2048]{1,0:T(8,128)(2,1)S(1)} %copy-done.29), channel_id=1, source_target_pairs={{0,4},{4,0},{8,12},{12,8},{16,20},{20,16},{24,28},{28,24},{1,5},{5... | collective-permute-start | bytes 6291464 | tf_op jit(solution)/shard_map/ppermute | solution.py:555
  737.0 69.1 %collective-permute-start.33 = (bf16[512,2048]{1,0:T(8,128)(2,1)}, bf16[512,2048]{1,0:T(8,128)(2,1)}, u32[]{:S(2)}, u32[]{:S(2)}) collective-permute-start(bf16[512,2048]{1,0:T(8,128)(2,1)} %add_convert_fusion.1), channel_id=1, source_target_pairs={{0,8},{4,12},{8,0},{12,4},{16,24},{20,28},{24,16},{28,20},{1,9},{5... | collective-permute-start | bytes 6291464 | tf_op jit(solution)/shard_map/ppermute | solution.py:555
  (106 other events, 1697.3 us)
Sparse Core Ops, SparseCore 0:
  10.2 41.6 all-gather.11
  72.3 50.3 all-gather.15
  124.8 53.6 all-gather.13
  179.9 49.2 all-gather.17
  231.2 88.2 all-gather.19
  466.8 45.1 reduce-scatter.5
  525.3 39.7 reduce-scatter.7
  611.9 31.8 reduce-scatter.9
  649.0 88.7 reduce-scatter.13
  740.1 37.8 reduce-scatter.11

commit v3 on v2

--- a/solution.py
+++ b/solution.py
@@ -656,15 +656,9 @@
     return lax.psum_scatter(values, "seq", scatter_dimension=0, tiled=False)
 
 
-def sum_all(values):
-    for axis in ("rows", "seq"):
-        size = lax.axis_size(axis)
-        bit = 1
-        while bit < size:
-            pairs = [(i, i ^ bit) for i in range(size)]
-            values = values + lax.ppermute(values, axis, pairs)
-            bit *= 2
-    return values
+def exchange(values, axis, bit):
+    size = lax.axis_size(axis)
+    return lax.ppermute(values, axis, [(i, i ^ bit) for i in range(size)])
 
 
 def across_group(own, send):
@@ -731,7 +725,7 @@
         axis=1,
     )
     extra = jnp.pad(extra, ((0, 0), (0, LANES - extra.shape[1])))
-    kv_lines = gather_seq(jnp.concatenate([w_qkv[:, QUERY_COLUMNS:], extra], axis=1))
+    kv_shard = jnp.concatenate([w_qkv[:, QUERY_COLUMNS:], extra], axis=1)
     query_shard = jnp.concatenate([w_qkv[:, :QUERY_COLUMNS], w_out.T], axis=1)
     query_shard, w_gate, w_up = stage(query_shard, w_gate, w_up)
     query_lines = gather_seq(query_shard)
@@ -752,17 +746,17 @@
     gate_up = jnp.stack([to_group(w_gate), to_group(w_up)], axis=2)
     hidden_columns = gate_up.shape[-1]
     core, near = bit_of(1), bit_of(2)
-    other, kv_lines, down_other, query_lines = stage(
-        swap(part(gate_up, 1 - core, 1), 1), kv_lines, send_outer(w_down), query_lines
-    )
-    gate_up = joined(part(gate_up, core, 1), other, core, 1)
-    down_pair = join_outer(w_down, down_other, 0)
-    left, right = kv_lines[..., : 3 * LANES], kv_lines[..., 3 * LANES :]
-    other, left_other, right_other = stage(
-        swap(part(gate_up, 1 - near, 0), 2), send_outer(left), swap(right, 2)
+    gate_up = joined(
+        part(gate_up, core, 1), swap(part(gate_up, 1 - core, 1), 1), core, 1
+    )
+    gate_up, kv_shard = stage(gate_up, kv_shard)
+    other, kv_lines, query_lines = stage(
+        swap(part(gate_up, 1 - near, 0), 2), gather_seq(kv_shard), query_lines
     )
     gate_up = joined(part(gate_up, near, 0), other, near, 0)
     gate_lines = gather_seq(gate_up[:, :, 0])
+    left, right = kv_lines[..., : 3 * LANES], kv_lines[..., 3 * LANES :]
+    left_other, right_other = stage(send_outer(left), swap(right, 2))
     left = join_outer(left, left_other, 0)
     right = joined(right, right_other, near, 0)
     left_other, right_other = stage(swap(left, 2), send_outer(right))
@@ -795,7 +789,10 @@
     normed = (inputs * in_scale * attn_gain_full).astype(bf16)
     joint_kv = mm(normed, wkv)
     own_kv = heads_forward(joint_kv, wide_k, cos_table, sin_table, KEY_COLUMNS)
-    own_kv, q_left_other, q_right_other = stage(own_kv, q_left_other, q_right_other)
+    own_kv, q_left_other, q_right_other, down_other = stage(
+        own_kv, q_left_other, q_right_other, send_outer(w_down)
+    )
+    down_pair = join_outer(w_down, down_other, 0)
     keys_values = gather_seq(own_kv).reshape(-1, 2 * KEY_COLUMNS)
     q_left = join_outer(q_left, q_left_other, 0)
     q_right = joined(q_right, q_right_other, near, 0)
@@ -848,11 +845,12 @@
     hidden_far, gate_far, up_far = hidden_pass((normed2, normed3), wgate, wup)
     normed4 = (normed_ffn, normed1, normed2, normed3)
     grad_top4 = (grad_top, grad_top1, grad_top2, grad_top3)
-    grad_wdown = weight_pass((hidden_near, hidden_far), grad_top4)
-    grad_wdown, wdown = stage(grad_wdown, down_lines.reshape(hidden_columns, width))
+    wdown = down_lines.reshape(hidden_columns, width)
     gate_far, up_far = gates_pass((grad_top2, grad_top3), wdown, gate_far, up_far)
     own, send = back_pass((gate_far, up_far), (wgate, wup), True)
-    across, wdown = stage(across_group(own, send), wdown)
+    across, wdown, hidden_far = stage(across_group(own, send), wdown, hidden_far)
+    grad_wdown = weight_pass((hidden_near, hidden_far), grad_top4)
+    grad_wdown, wdown = stage(grad_wdown, wdown)
     gate_near, up_near = gates_pass((grad_top, grad_top1), wdown, gate_near, up_near)
     own, send = back_pass((gate_near, up_near), (wgate, wup), True)
 
@@ -881,39 +879,47 @@
     grad_branch = grad_middle.astype(bf16)
     grad_mixed = mm(grad_branch, wout_t).astype(bf16)
     attend = (place_array, queries, keys_values, mixed, logs)
-    grad_q1, grad_kv1 = attend_backward(0, 3, *attend, grad_mixed)
-    grad_q1, grad_kv1, gate_other, grad_mixed, grad_wdown = stage(
-        grad_q1, grad_kv1, pass_outer(grad_wgate, 0), grad_mixed, grad_wdown
+    grad_q1, grad_kv1 = attend_backward(0, 2, *attend, grad_mixed)
+    grad_q1, grad_kv1, gate_other, grad_mixed, grad_wdown, hidden_far = stage(
+        grad_q1, grad_kv1, pass_outer(grad_wgate, 0), grad_mixed, grad_wdown, hidden_far
     )
     grad_kv1 = reduce_seq(grad_kv1.reshape(seq_devices, shard_length, -1))
     grad_gate = jnp.moveaxis(add_outer(grad_wgate, gate_other, 0), 2, 0)
-    grad_q2, grad_kv2 = attend_backward(3, 2, *attend, grad_mixed)
     shape = (outer, 2, 2, seq_devices, d_rows)
-    grad_wout = t_mm(grad_branch, mixed).astype(bf16).reshape(*shape, QUERY_COLUMNS)
-    grad_q2, grad_kv2, up_other, hidden_near, hidden_far, grad_kv1, wout_other = stage(
+    own_far, send_far = back_pass((hidden_far,), (wdown,), False)
+    grad_wout, far_other, grad_mixed = stage(
+        t_mm(grad_branch, mixed).astype(bf16).reshape(*shape, QUERY_COLUMNS),
+        swap(send_far, 1),
+        grad_mixed,
+    )
+    across = (own_far + far_other.astype(f32)).astype(bf16)
+    across, grad_mixed = stage(across, grad_mixed)
+    grad_q2, grad_kv2 = attend_backward(2, 3, *attend, grad_mixed)
+    grad_q2, grad_kv2, hidden_near, grad_kv1, wout_other, up_other, across = stage(
         grad_q2,
         grad_kv2,
-        pass_outer(grad_wup, 0),
         hidden_near,
-        hidden_far,
         grad_kv1,
         pass_bit(grad_wout, 1, 2),
+        pass_outer(grad_wup, 0),
+        swap(across, 2),
     )
     grad_kv2 = reduce_seq(grad_kv2.reshape(seq_devices, shard_length, -1))
 
-    grad_up = jnp.moveaxis(add_outer(grad_wup, up_other, 0), 2, 0)
     grad_q = jnp.concatenate([grad_q1, grad_q2], axis=1)
     joint_grad_q, gain_q = heads_backward(
         grad_q, joint_q, wide_q, cos_table, sin_table, QUERY_COLUMNS
     )
     grad_wq = t_mm(normed, joint_grad_q).astype(bf16).reshape(*shape, QUERY_COLUMNS)
     grad_wout = add_bit(grad_wout, wout_other, 1, 2)
-    own_far, send_far = back_pass((hidden_far,), (wdown,), False)
     own_near, send_near = back_pass((hidden_near,), (wdown,), False)
-    grad_kv2, wq_other, grad_up, grad_gate, own_far, send_far, send_near = stage(
-        grad_kv2, pass_bit(grad_wq, 1, 2), grad_up, grad_gate, own_far, send_far, send_near
-    )
-    gate_up = reduce_seq(jnp.stack([grad_gate, grad_up], axis=3))
+    grad_up = jnp.moveaxis(add_outer(grad_wup, up_other, 0), 2, 0)
+    grad_gate_up = jnp.stack([grad_gate, grad_up], axis=3)
+    grad_kv2, wq_other, own_near, near_other, grad_gate_up = stage(
+        grad_kv2, pass_bit(grad_wq, 1, 2), own_near, swap(send_near, 1), grad_gate_up
+    )
+    output = (middle + own_near + near_other.astype(f32) + across.astype(f32)).astype(bf16)
+    gate_up = reduce_seq(grad_gate_up)
     grad_wq = add_bit(grad_wq, wq_other, 1, 2)
     wq_other, wout_other = pass_bit(grad_wq, 2, 1), pass_outer(grad_wout, 0)
 
@@ -936,22 +942,40 @@
     left = grad_wkv[:, : 3 * LANES].reshape(*shape, -1)
     right = jnp.concatenate([grad_wkv[:, 3 * LANES :], gain_columns], axis=1)
     right = right.reshape(*shape, -1)
-    left, right, left_other, right_other, wq_other, wout_other = stage(
-        left, right, pass_bit(left, 1, 2), pass_bit(right, 1, 2), wq_other, wout_other
-    )
+    head_gains = jnp.concatenate(
+        [
+            jnp.sum(gain_q[0].reshape(-1, HEAD_SIZE), axis=0),
+            jnp.sum(gain_k[0, :KEY_COLUMNS].reshape(-1, HEAD_SIZE), axis=0),
+        ]
+    )[None]
+    left, right, left_other, right_other, wq_other, wout_other, gains_other = stage(
+        left,
+        right,
+        pass_bit(left, 1, 2),
+        pass_bit(right, 1, 2),
+        wq_other,
+        wout_other,
+        exchange(head_gains, "rows", 1),
+    )
+    head_gains = head_gains + gains_other
     left = add_bit(left, left_other, 1, 2)
     right = add_bit(right, right_other, 1, 2)
     grad_wq = add_bit(grad_wq, wq_other, 2, 1)
     grad_wout = add_outer(grad_wout, wout_other, 0)
-    left_other, right_other, wq_other, wout_other = stage(
+    left_other, right_other, wq_other, wout_other, gains_other = stage(
         pass_bit(left, 2, 1),
         pass_outer(right, 0),
         pass_outer(grad_wq, 0),
         pass_bit(grad_wout, 2, 0),
-    )
+        exchange(head_gains, "seq", 1),
+    )
+    head_gains = head_gains + gains_other
     left = add_bit(left, left_other, 2, 1)
     right = add_outer(right, right_other, 0)
-    left_other, right_other = stage(pass_outer(left, 0), pass_bit(right, 2, 0))
+    left_other, right_other, gains_other = stage(
+        pass_outer(left, 0), pass_bit(right, 2, 0), exchange(head_gains, "rows", 2)
+    )
+    head_gains = head_gains + gains_other
     sums = reduce_seq(
         jnp.concatenate(
             [
@@ -963,29 +987,28 @@
             axis=-1,
         )
     )
-    own_near = own_near + swap(send_near, 1).astype(f32)
-    across = across_group(own_far, send_far)
-    output = (middle + own_near + swap(across, 2).astype(f32)).astype(bf16)
+    rest = [("rows", bit) for bit in (4, 8, 16) if bit < row_devices]
+    rest += [("seq", bit) for bit in (2, 4, 8) if bit < seq_devices]
+    other, gains_other = stage(
+        swap(part(gate_up, 1 - near, 0), 2), exchange(head_gains, *rest[0])
+    )
+    head_gains = head_gains + gains_other
+    grads = joined(part(gate_up, near, 0), other, near, 0)
+    for axis, bit in rest[1:]:
+        head_gains = head_gains + exchange(head_gains, axis, bit)
+    head_gains = head_gains[0]
+    grads = joined(part(grads, core, 1), swap(part(grads, 1 - core, 1), 1), core, 1)
+
+    def from_group(blocks):
+        blocks = blocks.reshape(4, d_rows, seq_devices, outer, f_rows)
+        return jnp.transpose(blocks, (1, 3, 0, 2, 4)).reshape(d_rows, -1)
+
+    grad_wgate, grad_wup = stage(from_group(grads[:, :, 0]), from_group(grads[:, :, 1]))
+    sums, grad_wgate, grad_wup, grad_wdown, output, input_grad = stage(
+        sums, grad_wgate.astype(f32), grad_wup.astype(f32), grad_wdown.astype(f32), output, input_grad
+    )
     columns = QUERY_COLUMNS + 2 * KEY_COLUMNS
     long_gains = sums[:, columns : columns + 2].astype(f32)
-    head_gains = sum_all(
-        jnp.concatenate(
-            [
-                jnp.sum(gain_q[0].reshape(-1, HEAD_SIZE), axis=0),
-                jnp.sum(gain_k[0, :KEY_COLUMNS].reshape(-1, HEAD_SIZE), axis=0),
-            ]
-        )[None]
-    )[0]
-
-    grads = gate_up
-    grads = joined(part(grads, near, 0), swap(part(grads, 1 - near, 0), 2), near, 0)
-    grads = joined(part(grads, core, 1), swap(part(grads, 1 - core, 1), 1), core, 1)
-
-    def from_group(blocks):
-        blocks = blocks.reshape(4, d_rows, seq_devices, outer, f_rows)
-        return jnp.transpose(blocks, (1, 3, 0, 2, 4)).reshape(d_rows, -1).astype(f32)
-
-    grad_wgate, grad_wup = from_group(grads[:, :, 0]), from_group(grads[:, :, 1])
     return (
         output[None],
         input_grad[None],
@@ -993,7 +1016,7 @@
         sums[:, columns + LANES :].T.astype(f32),
         grad_wgate,
         grad_wup,
-        grad_wdown.astype(f32),
+        grad_wdown,
         long_gains[:, 0],
         long_gains[:, 1],
         head_gains[:HEAD_SIZE],

time: 857 us -> 818 us (0.954)
  waiting for transfers between devices: 303 us -> 268 us
    ppermute x5, waiting for transfers between devices: 45.6 us -> 7.44 us  [exchange(): return lax.ppermute(values, axis, [(i, i ^ bit) for i in range(size)])]
    convert_element_type x6 -> x0, local copies, waits for them, and re-layouts: 20.1 us -> none  [from_group(): jnp.transpose(blocks, (1, 3, 0, 2, 4)).reshape(d_rows, -1).astype(f32)]
    convert_element_type x1 -> x5, other arithmetic: 1.19 us -> 16.3 us  [the longest x1 7.92 us: shards(): (middle + own_near + near_other.astype(f32) + across.astype(f32)).astype(...]
    broadcast_in_dim x2 -> x0, other arithmetic: 14 us -> none  [the longest x1 7.44 us: shards(): output[None]]
    unnamed x141 -> x143, local copies, waits for them, and re-layouts: 18.8 us -> 18.6 us
  transfers between devices with their start and end apart: 61 -> 61, of which waited for: 26 -> 27; matrix products, arithmetic and copies ran while one was open for 16% -> 18% of each run, Pallas kernels for 26% -> 25%
where the time goes in v3:
time: 818 us; the launch traced here: 808 us
  waiting for transfers between devices  268 us (33%)
  Pallas kernels  257 us (31%)
  other arithmetic  79.8 us (10%)
  local copies, waits for them, and re-layouts  73.4 us (9%)
  starting transfers between devices  46.6 us (6%)
  matrix products  44.2 us (5%)
  blocking collectives  19.9 us (2%)
  between operations  18.6 us (2%)
    ppermute x46, waiting for transfers between devices, swap(): return lax.ppermute(values, 'rows', pairs)  249 us
    pallas_call x3, Pallas kernels, weight_pass(): pl.pallas_call(partial(weight_kernel, len(lefts)), grid=(rows // tile,),...  47.1 us
    pallas_call x4, Pallas kernels, back_pass(): pl.pallas_call(partial(back_kernel, count, transposed), grid=(width // ti...  46.5 us
    ppermute x46, starting transfers between devices, swap(): return lax.ppermute(values, 'rows', pairs)  39.6 us
    pallas_call x2, Pallas kernels, hidden_pass(): pl.pallas_call(hidden_kernel, grid=(pl.cdiv(columns, tile),), in_specs=[w...  31.3 us
    pallas_call x2, Pallas kernels, attend_backward(): pl.pallas_call(partial(attend_backward_kernel, first, count), grid_spec=p...  31.1 us
    pallas_call x2, Pallas kernels, gates_pass(): pl.pallas_call(gates_kernel, grid=(pl.cdiv(columns, tile),), in_specs=[wh...  23.9 us
    pallas_call x17, Pallas kernels, joined(): pl.pallas_call(joined_kernel, grid_spec=pltpu.PrefetchScalarGridSpec(num_...  23 us
  transfers between devices with their start and end apart: 61, of which 27 were waited for; matrix products, arithmetic and copies ran while one was open for 18% of the time, Pallas kernels for 25%

profile of v3, /device:TPU:0, one launch (start us, length us, event | category | flops | bytes accessed | tf_op | source)
XLA Modules:
  0.0 807.8 jit_solution(5812509178944126376)
XLA Ops:
  28.3 19.9 %all-gather = bf16[256,768]{1,0:T(8,128)(2,1)S(1)} all-gather(bf16[64,768]{1,0:T(8,128)(2,1)S(1)} %fusion.33), channel_id=2, replica_groups=mesh['rows'=8,'seq'=4] {'seq'}, dimensions={0}, use_global_device_ids=true | all-gather | bytes 491520 | tf_op jit(solution)/shard_map/all_gather | solution.py:652
  60.9 11.2 %collective-permute-done.2 = bf16[4,64,384]{2,1,0:T(8,128)(2,1)S(1)} collective-permute-done((bf16[4,64,384]{2,1,0:T(8,128)(2,1)S(1)}, bf16[4,64,384]{2,1,0:T(8,128)(2,1)S(1)}, u32[]{:S(2)}, u32[]{:S(2)}) %collective-permute-start.2) | collective-permute-done | bytes 196640 | tf_op jit(solution)/shard_map/ppermute | solution.py:555
  110.6 25.6 %collective-permute-done.12 = bf16[2,4,64,1280]{3,2,1,0:T(8,128)(2,1)} collective-permute-done((bf16[2,4,64,1280]{3,2,1,0:T(8,128)(2,1)S(1)}, bf16[2,4,64,1280]{3,2,1,0:T(8,128)(2,1)}, u32[]{:S(2)}, u32[]{:S(2)}) %collective-permute-start.12) | collective-permute-done | bytes 1310752 | tf_op jit(solution)/shard_map/ppermute | solution.py:555
  179.3 11.8 %attend_forward.1 = (bf16[512,1280]{1,0:T(8,128)(2,1)S(1)}, f32[512,1280]{1,0:T(8,128)S(1)}) custom-call(s32[1]{0:T(128)} %bitcast.34.place_ref, bf16[512,1280]{1,0:T(8,128)(2,1)S(1)} %copy-done, bf16[2048,640]{1,0:T(8,128)(2,1)} %all-gather.14.cloned.1.call-done.k_ref.v_ref, bf16[2048,640]{1,0:T(8,128)(2,1)} %all-gather.14.cloned.1.call-done.k_ref.v_ref), custom_call_target="tpu_custom_call" | custom-call | flops 1000 | bytes 1000 | tf_op jit(solution)/shard_map/attend_forward/pallas_call | solution.py:177
  192.7 37.5 %collective-permute-done.16 = bf16[4,2,2,64,1152]{4,3,2,1,0:T(8,128)(2,1)} collective-permute-done((bf16[4,2,2,64,1152]{4,3,2,1,0:T(8,128)(2,1)}, bf16[4,2,2,64,1152]{4,3,2,1,0:T(8,128)(2,1)}, u32[]{:S(2)}, u32[]{:S(2)}) %collective-permute-start.16) | collective-permute-done | bytes 2359328 | tf_op jit(solution)/shard_map/ppermute | solution.py:555
  256.8 39.9 %collective-permute-done.20 = bf16[4,2,2,64,1152]{4,3,2,1,0:T(8,128)(2,1)} collective-permute-done((bf16[4,2,2,64,1152]{4,3,2,1,0:T(8,128)(2,1)}, bf16[4,2,2,64,1152]{4,3,2,1,0:T(8,128)(2,1)}, u32[]{:S(2)}, u32[]{:S(2)}) %collective-permute-start.20) | collective-permute-done | bytes 2359328 | tf_op jit(solution)/shard_map/ppermute | solution.py:555
  304.1 15.7 %hidden_pass.2 = (bf16[1024,1152]{1,0:T(8,128)(2,1)}, bf16[1024,1152]{1,0:T(8,128)(2,1)}, bf16[1024,1152]{1,0:T(8,128)(2,1)}) custom-call(bf16[512,2048]{1,0:T(8,128)(2,1)S(1)} %multiply_convert_fusion.n0_ref.refs_0_, bf16[512,2048]{1,0:T(8,128)(2,1)} %collective-permute-done.19.n1_ref.refs_1_, bf16[2048,1152]{1,0:T(8,128)(2,1)} %bitcast.288, ...), custom_call_target="tpu_custom_call" | custom-call | flops 1000 | bytes 1000 | tf_op jit(solution)/shard_map/hidden_pass/pallas_call | solution.py:344
  324.2 15.6 %hidden_pass.3 = (bf16[1024,1152]{1,0:T(8,128)(2,1)}, bf16[1024,1152]{1,0:T(8,128)(2,1)}, bf16[1024,1152]{1,0:T(8,128)(2,1)}) custom-call(bf16[512,2048]{1,0:T(8,128)(2,1)} %collective-permute-done.18.n0_ref.refs_2_, bf16[512,2048]{1,0:T(8,128)(2,1)S(1)} %collective-permute-done.22.n1_ref.refs_3_, bf16[2048,1152]{1,0:T(8,128)(2,1)} %bitcast.289, ...), custom_call_target="tpu_custom_call" | custom-call | flops 1000 | bytes 1000 | tf_op jit(solution)/shard_map/hidden_pass/pallas_call | solution.py:344
  341.2 12.3 %gates_pass.2 = (bf16[1024,1152]{1,0:T(8,128)(2,1)}, bf16[1024,1152]{1,0:T(8,128)(2,1)}) custom-call(bf16[512,2048]{1,0:T(8,128)(2,1)} %collective-permute-done.15.g0_ref.refs_4_, bf16[512,2048]{1,0:T(8,128)(2,1)} %collective-permute-done.21.g1_ref.refs_5_, bf16[1152,2048]{1,0:T(8,128)(2,1)} %bitcast.296, bf16[1024,1152]{1,0:T(8,128)(2,1)} %get-tuple-element.179.gate_ref, ...), custom_call_target="tpu_custom_call" | custom-call | flops 1000 | bytes 1000 | tf_op jit(solution)/shard_map/gates_pass/pallas_call | solution.py:379
  355.1 15.0 %back_pass.4 = (f32[512,2048]{1,0:T(8,128)}, bf16[512,2048]{1,0:T(8,128)(2,1)}) custom-call(bf16[1024,1152]{1,0:T(8,128)(2,1)S(1)} %copy-done.7, bf16[1024,1152]{1,0:T(8,128)(2,1)} %get-tuple-element.182.refs_1_.refs_5_, bf16[2048,1152]{1,0:T(8,128)(2,1)} %bitcast.290, bf16[2048,1152]{1,0:T(8,128)(2,1)} %bitcast.294), custom_call_target="tpu_custom_call" | custom-call | flops 1000 | bytes 1000 | tf_op jit(solution)/shard_map/back_pass/pallas_call | solution.py:418
  379.7 14.9 %weight_pass.3 = bf16[1152,2048]{1,0:T(8,128)(2,1)} custom-call(bf16[1024,1152]{1,0:T(8,128)(2,1)} %get-tuple-element.223.refs_0_, bf16[1024,1152]{1,0:T(8,128)(2,1)} %get-tuple-element.207.refs_1_.refs_0_, bf16[512,2048]{1,0:T(8,128)(2,1)S(1)} %copy-done.3, bf16[512,2048]{1,0:T(8,128)(2,1)} %collective-permute-done.14.refs_3_.g1_ref, ...), custom_call_target="tpu_custom_call" | custom-call | flops 1000 | bytes 1000 | tf_op jit(solution)/shard_map/weight_pass/pallas_call | solution.py:452
  398.6 11.7 %gates_pass.3 = (bf16[1024,1152]{1,0:T(8,128)(2,1)}, bf16[1024,1152]{1,0:T(8,128)(2,1)}) custom-call(bf16[512,2048]{1,0:T(8,128)(2,1)S(1)} %copy-done.3, bf16[512,2048]{1,0:T(8,128)(2,1)} %collective-permute-done.14.refs_3_.g1_ref, bf16[1152,2048]{1,0:T(8,128)(2,1)} %bitcast.297, bf16[1024,1152]{1,0:T(8,128)(2,1)} %get-tuple-element.192.gate_ref, ...), custom_call_target="tpu_custom_call" | custom-call | flops 1000 | bytes 1000 | tf_op jit(solution)/shard_map/gates_pass/pallas_call | solution.py:379
  411.9 14.9 %back_pass.5 = (f32[512,2048]{1,0:T(8,128)}, bf16[512,2048]{1,0:T(8,128)(2,1)}) custom-call(bf16[1024,1152]{1,0:T(8,128)(2,1)S(1)} %copy-done.8, bf16[1024,1152]{1,0:T(8,128)(2,1)} %get-tuple-element.195.refs_1_.refs_4_, bf16[2048,1152]{1,0:T(8,128)(2,1)} %bitcast.291, bf16[2048,1152]{1,0:T(8,128)(2,1)} %bitcast.295), custom_call_target="tpu_custom_call" | custom-call | flops 1000 | bytes 1000 | tf_op jit(solution)/shard_map/back_pass/pallas_call | solution.py:418
  428.3 15.9 %weight_pass.5 = bf16[2048,1152]{1,0:T(8,128)(2,1)} custom-call(bf16[512,2048]{1,0:T(8,128)(2,1)S(1)} %multiply_convert_fusion.n0_ref.refs_0_, bf16[512,2048]{1,0:T(8,128)(2,1)} %collective-permute-done.19.n1_ref.refs_1_, bf16[512,2048]{1,0:T(8,128)(2,1)} %collective-permute-done.18.n0_ref.refs_2_, bf16[512,2048]{1,0:T(8,128)(2,1)} %copy-done.1, ...), custom_call_target="tpu_custom_call" | custom-call | flops 1000 | bytes 1000 | tf_op jit(solution)/shard_map/weight_pass/pallas_call | solution.py:452
  444.2 16.3 %weight_pass.4 = bf16[2048,1152]{1,0:T(8,128)(2,1)} custom-call(bf16[512,2048]{1,0:T(8,128)(2,1)S(1)} %multiply_convert_fusion.n0_ref.refs_0_, bf16[512,2048]{1,0:T(8,128)(2,1)} %collective-permute-done.19.n1_ref.refs_1_, bf16[512,2048]{1,0:T(8,128)(2,1)} %collective-permute-done.18.n0_ref.refs_2_, bf16[512,2048]{1,0:T(8,128)(2,1)} %copy-done.1, ...), custom_call_target="tpu_custom_call" | custom-call | flops 1000 | bytes 1000 | tf_op jit(solution)/shard_map/weight_pass/pallas_call | solution.py:452
  460.5 14.7 %collective-permute-done.24 = bf16[512,2048]{1,0:T(8,128)(2,1)} collective-permute-done((bf16[512,2048]{1,0:T(8,128)(2,1)}, bf16[512,2048]{1,0:T(8,128)(2,1)}, u32[]{:S(2)}, u32[]{:S(2)}) %collective-permute-start.24) | collective-permute-done | bytes 2097184 | tf_op jit(solution)/shard_map/ppermute | solution.py:555
  495.3 12.4 %attend_backward.2 = (bf16[512,512]{1,0:T(8,128)(2,1)S(1)}, bf16[2048,256]{1,0:T(8,128)(2,1)S(1)}) custom-call(s32[1]{0:T(128)} %bitcast.34.place_ref, bf16[512,1280]{1,0:T(8,128)(2,1)S(1)} %copy-done, bf16[2048,640]{1,0:T(8,128)(2,1)} %all-gather.14.cloned.1.call-done.k_ref.v_ref, bf16[2048,640]{1,0:T(8,128)(2,1)} %all-gather.14.cloned.1.call-done.k_ref.v_ref, ...), custom_call_target="tpu_custom_call" | custom-call | flops 1000 | bytes 1000 | tf_op jit(solution)/shard_map/attend_backward/pallas_call | solution.py:300
  509.5 25.0 %collective-permute-done.27 = bf16[2,2,4,64,1152]{4,3,1,0,2:T(8,128)(2,1)} collective-permute-done((bf16[2,2,4,64,1152]{4,3,1,0,2:T(8,128)(2,1)S(1)}, bf16[2,2,4,64,1152]{4,3,1,0,2:T(8,128)(2,1)}, u32[]{:S(2)}, u32[]{:S(2)}) %collective-permute-start.27) | collective-permute-done | bytes 2359328 | tf_op jit(solution)/shard_map/ppermute | solution.py:555
  562.9 18.7 %attend_backward.3 = (bf16[512,768]{1,0:T(8,128)(2,1)S(1)}, bf16[2048,384]{1,0:T(8,128)(2,1)}) custom-call(s32[1]{0:T(128)} %bitcast.34.place_ref, bf16[512,1280]{1,0:T(8,128)(2,1)S(1)} %copy-done, bf16[2048,640]{1,0:T(8,128)(2,1)} %all-gather.14.cloned.1.call-done.k_ref.v_ref, bf16[2048,640]{1,0:T(8,128)(2,1)} %all-gather.14.cloned.1.call-done.k_ref.v_ref, ...), custom_call_target="tpu_custom_call" | custom-call | flops 1000 | bytes 1000 | tf_op jit(solution)/shard_map/attend_backward/pallas_call | solution.py:300
  581.6 20.0 %collective-permute-done.30 = bf16[2,2,4,64,1152]{4,3,1,0,2:T(8,128)(2,1)} collective-permute-done((bf16[2,2,4,64,1152]{4,3,1,0,2:T(8,128)(2,1)}, bf16[2,2,4,64,1152]{4,3,1,0,2:T(8,128)(2,1)}, u32[]{:S(2)}, u32[]{:S(2)}) %collective-permute-start.30) | collective-permute-done | bytes 2359328 | tf_op jit(solution)/shard_map/ppermute | solution.py:555
  616.5 8.7 %heads_backward.2 = (bf16[512,1280]{1,0:T(8,128)(2,1)}, f32[8,1280]{1,0:T(8,128)}) custom-call(bf16[512,1280]{1,0:T(8,128)(2,1)} %pad_maximum_fusion.6.grad_ref, f32[512,1280]{1,0:T(8,128)} %fusion.48.joint_ref, f32[8,1280]{1,0:T(8,128)} %broadcast_in_dim.14.gain_ref, f32[512,128]{1,0:T(8,128)} %get-tuple-element.306.cos_ref, ...), custom_call_target="tpu_custom_call" | custom-call | flops 1000 | bytes 1000 | tf_op jit(solution)/shard_map/heads_backward/pallas_call | solution.py:109
  628.1 8.4 %back_pass.7 = (f32[512,2048]{1,0:T(8,128)}, bf16[512,2048]{1,0:T(8,128)(2,1)}) custom-call(bf16[1024,1152]{1,0:T(8,128)(2,1)S(1)} %copy-done.5, bf16[1152,2048]{1,0:T(8,128)(2,1)} %bitcast.299), custom_call_target="tpu_custom_call" | custom-call | flops 1000 | bytes 1000 | tf_op jit(solution)/shard_map/back_pass/pallas_call | solution.py:418
  698.0 21.1 %collective-permute-done.36 = bf16[2,4,64,1280]{3,2,1,0:T(8,128)(2,1)} collective-permute-done((bf16[2,4,64,1280]{3,2,1,0:T(8,128)(2,1)}, bf16[2,4,64,1280]{3,2,1,0:T(8,128)(2,1)}, u32[]{:S(2)}, u32[]{:S(2)}) %collective-permute-start.36) | collective-permute-done | bytes 1310752 | tf_op jit(solution)/shard_map/ppermute | solution.py:555
  735.1 9.2 %collective-permute-done.39 = bf16[2,4,64,384]{3,2,1,0:T(8,128)(2,1)S(1)} collective-permute-done((bf16[2,4,64,384]{3,2,1,0:T(8,128)(2,1)S(1)}, bf16[2,4,64,384]{3,2,1,0:T(8,128)(2,1)S(1)}, u32[]{:S(2)}, u32[]{:S(2)}) %collective-permute-start.39) | collective-permute-done | bytes 393248 | tf_op jit(solution)/shard_map/ppermute | solution.py:555
  (427 shorter events, 372.9 us)
Async XLA Ops:
  7.2 44.7 %all-gather.12.cloned.1.call-start = ((), (), s32[]{:S(2)}) async-start(), calls=%async_computation.10 | async-start | bytes 1638400 | tf_op jit(solution)/shard_map/all_gather | solution.py:652
  9.8 128.8 %all-gather.16.cloned.1.call-start = ((), (), s32[]{:S(2)}) async-start(), calls=%async_computation.12 | async-start | bytes 2949120 | tf_op jit(solution)/shard_map/all_gather | solution.py:652
  53.1 118.7 %all-gather.14.cloned.1.call-start = ((), (), s32[]{:S(2)}) async-start(), calls=%async_computation.11 | async-start | bytes 3276800 | tf_op jit(solution)/shard_map/all_gather | solution.py:652
  53.4 45.4 %collective-permute-start.10 = (bf16[144,2048]{1,0:T(8,128)(2,1)S(1)}, bf16[144,2048]{1,0:T(8,128)(2,1)}, u32[]{:S(2)}, u32[]{:S(2)}) collective-permute-start(bf16[144,2048]{1,0:T(8,128)(2,1)S(1)} %copy-done.23), channel_id=1, source_target_pairs={{0,16},{4,20},{8,24},{12,28},{16,0},{20,4},{24,8},{28,12},{1,17},{... | collective-permute-start | bytes 1769480 | tf_op jit(solution)/shard_map/ppermute | solution.py:555
  110.6 133.3 %all-gather.18.cloned.1.call-start = ((), (), s32[]{:S(2)}) async-start(), calls=%async_computation.13 | async-start | bytes 2949120 | tf_op jit(solution)/shard_map/all_gather | solution.py:652
  171.9 169.3 %all-gather.20.cloned.1.call-start = ((), (), s32[]{:S(2)}) async-start(), calls=%async_computation.14 | async-start | bytes 5898240 | tf_op jit(solution)/shard_map/all_gather | solution.py:652
  176.2 54.0 %collective-permute-start.17 = (bf16[2,2,4,64,1280]{4,3,2,1,0:T(8,128)(2,1)}, bf16[2,2,4,64,1280]{4,3,2,1,0:T(8,128)(2,1)}, u32[]{:S(2)}, u32[]{:S(2)}) collective-permute-start(bf16[2,2,4,64,1280]{4,3,2,1,0:T(8,128)(2,1)} %bitcast.63), channel_id=1, source_target_pairs={{0,4},{4,0},{8,12},{12,8},{16,20},{20,16},{24,28},{28,24},{1,5},{5... | collective-permute-start | bytes 7864328 | tf_op jit(solution)/shard_map/ppermute | solution.py:555
  176.7 53.5 %collective-permute-start.16 = (bf16[4,2,2,64,1152]{4,3,2,1,0:T(8,128)(2,1)}, bf16[4,2,2,64,1152]{4,3,2,1,0:T(8,128)(2,1)}, u32[]{:S(2)}, u32[]{:S(2)}) collective-permute-start(bf16[4,2,2,64,1152]{4,3,2,1,0:T(8,128)(2,1)} %bitcast.51), channel_id=1, source_target_pairs={{0,16},{4,20},{8,24},{12,28},{16,0},{20,4},{24,8},{28,12},{1,17},{... | collective-permute-start | bytes 7077896 | tf_op jit(solution)/shard_map/ppermute | solution.py:555
  177.4 52.8 %collective-permute-start.15 = (bf16[512,2048]{1,0:T(8,128)(2,1)S(1)}, bf16[512,2048]{1,0:T(8,128)(2,1)}, u32[]{:S(2)}, u32[]{:S(2)}) collective-permute-start(bf16[512,2048]{1,0:T(8,128)(2,1)S(1)} %bitcast_convert_fusion.refs_2_.g0_ref), channel_id=1, source_target_pairs={{0,8},{4,12},{8,0},{12,4},{16,24},{20,28},{24,16},{28,20},{1,9},{5... | collective-permute-start | bytes 6291464 | tf_op jit(solution)/shard_map/ppermute | solution.py:555
  178.9 51.4 %collective-permute-start.14 = (bf16[512,2048]{1,0:T(8,128)(2,1)S(1)}, bf16[512,2048]{1,0:T(8,128)(2,1)}, u32[]{:S(2)}, u32[]{:S(2)}) collective-permute-start(bf16[512,2048]{1,0:T(8,128)(2,1)S(1)} %bitcast_convert_fusion.refs_2_.g0_ref), channel_id=1, source_target_pairs={{0,4},{4,0},{8,12},{12,8},{16,20},{20,16},{24,28},{28,24},{1,5},{5... | collective-permute-start | bytes 6291464 | tf_op jit(solution)/shard_map/ppermute | solution.py:555
  178.9 355.6 %reduce-scatter.6.cloned.1.call-start = ((), (), s32[]{:S(2)}) async-start(), calls=%async_computation.5 | async-start | bytes 2949120 | tf_op jit(solution)/shard_map/reduce_scatter | solution.py:656
  243.9 52.8 %collective-permute-start.20 = (bf16[4,2,2,64,1152]{4,3,2,1,0:T(8,128)(2,1)}, bf16[4,2,2,64,1152]{4,3,2,1,0:T(8,128)(2,1)}, u32[]{:S(2)}, u32[]{:S(2)}) collective-permute-start(bf16[4,2,2,64,1152]{4,3,2,1,0:T(8,128)(2,1)} %bitcast.328), channel_id=1, source_target_pairs={{0,16},{4,20},{8,24},{12,28},{16,0},{20,4},{24,8},{28,12},{1,17},{... | collective-permute-start | bytes 7077896 | tf_op jit(solution)/shard_map/ppermute | solution.py:555
  247.4 72.4 %collective-permute-start.21 = (bf16[512,2048]{1,0:T(8,128)(2,1)}, bf16[512,2048]{1,0:T(8,128)(2,1)}, u32[]{:S(2)}, u32[]{:S(2)}) collective-permute-start(bf16[512,2048]{1,0:T(8,128)(2,1)} %collective-permute-done.15.g0_ref.refs_4_), channel_id=1, source_target_pairs={{0,4},{4,0},{8,12},{12,8},{16,20},{20,16},{24,28},{28,24},{1,5},{5... | collective-permute-start | bytes 6291464 | tf_op jit(solution)/shard_map/ppermute | solution.py:555
  247.9 71.9 %collective-permute-start.18 = (bf16[512,2048]{1,0:T(8,128)(2,1)S(1)}, bf16[512,2048]{1,0:T(8,128)(2,1)}, u32[]{:S(2)}, u32[]{:S(2)}) collective-permute-start(bf16[512,2048]{1,0:T(8,128)(2,1)S(1)} %multiply_convert_fusion.n0_ref.refs_0_), channel_id=1, source_target_pairs={{0,8},{4,12},{8,0},{12,4},{16,24},{20,28},{24,16},{28,20},{1,9},{5... | collective-permute-start | bytes 6291464 | tf_op jit(solution)/shard_map/ppermute | solution.py:555
  398.1 77.1 %collective-permute-start.26 = (bf16[4,144,2048]{2,1,0:T(8,128)(2,1)}, bf16[4,144,2048]{2,1,0:T(8,128)(2,1)}, u32[]{:S(2)}, u32[]{:S(2)}) collective-permute-start(bf16[4,144,2048]{2,1,0:T(8,128)(2,1)} %dynamic-slice_bitcast_fusion.1), channel_id=1, source_target_pairs={{0,16},{4,20},{8,24},{12,28},{16,0},{20,4},{24,8},{28,12},{1,17},{... | collective-permute-start | bytes 7077896 | tf_op jit(solution)/shard_map/ppermute | solution.py:555
  426.8 48.4 %collective-permute-start.24 = (bf16[512,2048]{1,0:T(8,128)(2,1)}, bf16[512,2048]{1,0:T(8,128)(2,1)}, u32[]{:S(2)}, u32[]{:S(2)}) collective-permute-start(bf16[512,2048]{1,0:T(8,128)(2,1)} %add_convert_fusion.2), channel_id=1, source_target_pairs={{0,8},{4,12},{8,0},{12,4},{16,24},{20,28},{24,16},{28,20},{1,9},{5... | collective-permute-start | bytes 6291464 | tf_op jit(solution)/shard_map/ppermute | solution.py:555
  479.3 122.3 %reduce-scatter.8.cloned.1.call-start = ((), (), s32[]{:S(2)}) async-start(), calls=%async_computation.6 | async-start | bytes 1310720 | tf_op jit(solution)/shard_map/reduce_scatter | solution.py:656
  481.4 53.0 %collective-permute-start.27 = (bf16[2,2,4,64,1152]{4,3,1,0,2:T(8,128)(2,1)S(1)}, bf16[2,2,4,64,1152]{4,3,1,0,2:T(8,128)(2,1)}, u32[]{:S(2)}, u32[]{:S(2)}) collective-permute-start(bf16[2,2,4,64,1152]{4,3,1,0,2:T(8,128)(2,1)S(1)} %copy_bitcast_fusion.3), channel_id=1, source_target_pairs={{0,16},{4,20},{8,24},{12,28},{16,0},{20,4},{24,8},{28,12},{1,17},{... | collective-permute-start | bytes 7077896 | tf_op jit(solution)/shard_map/ppermute | solution.py:555
  547.7 53.8 %collective-permute-start.30 = (bf16[2,2,4,64,1152]{4,3,1,0,2:T(8,128)(2,1)}, bf16[2,2,4,64,1152]{4,3,1,0,2:T(8,128)(2,1)}, u32[]{:S(2)}, u32[]{:S(2)}) collective-permute-start(bf16[2,2,4,64,1152]{4,3,1,0,2:T(8,128)(2,1)} %copy_bitcast_fusion.2), channel_id=1, source_target_pairs={{0,16},{4,20},{8,24},{12,28},{16,0},{20,4},{24,8},{28,12},{1,17},{... | collective-permute-start | bytes 7077896 | tf_op jit(solution)/shard_map/ppermute | solution.py:555
  554.0 109.7 %reduce-scatter.10.cloned.1.call-start = ((), (), s32[]{:S(2)}) async-start(), calls=%async_computation.7 | async-start | bytes 1966080 | tf_op jit(solution)/shard_map/reduce_scatter | solution.py:656
  557.6 52.1 %collective-permute-start.29 = (bf16[2,2,4,64,1280]{4,3,2,1,0:T(8,128)(2,1)}, bf16[2,2,4,64,1280]{4,3,2,1,0:T(8,128)(2,1)}, u32[]{:S(2)}, u32[]{:S(2)}) collective-permute-start(bf16[2,2,4,64,1280]{4,3,2,1,0:T(8,128)(2,1)} %dynamic-slice_bitcast_fusion), channel_id=1, source_target_pairs={{0,4},{4,0},{8,12},{12,8},{16,20},{20,16},{24,28},{28,24},{1,5},{5... | collective-permute-start | bytes 7864328 | tf_op jit(solution)/shard_map/ppermute | solution.py:555
  561.5 48.3 %collective-permute-start.31 = (bf16[512,2048]{1,0:T(8,128)(2,1)}, bf16[512,2048]{1,0:T(8,128)(2,1)}, u32[]{:S(2)}, u32[]{:S(2)}) collective-permute-start(bf16[512,2048]{1,0:T(8,128)(2,1)} %add_convert_fusion.1), channel_id=1, source_target_pairs={{0,8},{4,12},{8,0},{12,4},{16,24},{20,28},{24,16},{28,20},{1,9},{5... | collective-permute-start | bytes 6291464 | tf_op jit(solution)/shard_map/ppermute | solution.py:555
  628.0 130.2 %reduce-scatter.14.cloned.1.call-start = ((), (), s32[]{:S(2)}) async-start(), calls=%async_computation.9 | async-start | bytes 5898240 | tf_op jit(solution)/shard_map/reduce_scatter | solution.py:656
  663.7 132.0 %reduce-scatter.12.cloned.1.call-start = ((), (), s32[]{:S(2)}) async-start(), calls=%async_computation.8 | async-start | bytes 2129920 | tf_op jit(solution)/shard_map/reduce_scatter | solution.py:656
  (109 other events, 1545.3 us)
Sparse Core Ops, SparseCore 0:
  10.2 41.6 all-gather.11
  54.0 49.5 all-gather.15
  110.7 53.7 all-gather.13
  172.0 50.4 all-gather.17
  224.4 88.2 all-gather.19
  479.4 48.7 reduce-scatter.5
  554.1 26.8 reduce-scatter.7
  628.1 35.0 reduce-scatter.9
  665.6 84.2 reduce-scatter.13
  757.2 38.4 reduce-scatter.11

commit v4 on v3

--- a/solution.py
+++ b/solution.py
@@ -789,9 +789,10 @@
     normed = (inputs * in_scale * attn_gain_full).astype(bf16)
     joint_kv = mm(normed, wkv)
     own_kv = heads_forward(joint_kv, wide_k, cos_table, sin_table, KEY_COLUMNS)
-    own_kv, q_left_other, q_right_other, down_other = stage(
-        own_kv, q_left_other, q_right_other, send_outer(w_down)
-    )
+    own_kv, q_left_other, q_right_other, down_other, up_in = stage(
+        own_kv, q_left_other, q_right_other, send_outer(w_down), gate_up[:, :, 1]
+    )
+    up_lines = gather_seq(up_in)
     down_pair = join_outer(w_down, down_other, 0)
     keys_values = gather_seq(own_kv).reshape(-1, 2 * KEY_COLUMNS)
     q_left = join_outer(q_left, q_left_other, 0)
@@ -819,54 +820,50 @@
     joint_q = mm(normed, wq)
     queries = heads_forward(joint_q, wide_q, cos_table, sin_table, QUERY_COLUMNS)
     place_array = place.reshape(1)
-    keys_values, queries, up_in, down_in = stage(
-        keys_values, queries, gate_up[:, :, 1], down_pair
-    )
-    up_lines = gather_seq(up_in)
+    keys_values, queries, down_in = stage(keys_values, queries, down_pair)
     down_lines = gather_seq(down_in)
     mixed, logs = attend_forward(place_array, queries, keys_values)
-    mixed, grad_top1, grad_top2, gate_other, wout_other = stage(
-        mixed, swap(grad_top, 1), swap(grad_top, 2), gate_other, swap(q_right, 1)
+    mixed, grad_top1, grad_top2, up_lines, wout_other = stage(
+        mixed, swap(grad_top, 1), swap(grad_top, 2), up_lines, swap(q_right, 1)
     )
     wout_t = joined(q_right, wout_other, core, 2).reshape(width, -1)
     middle = inputs + mm_t(mixed, wout_t)
 
     ffn_scale = norm_scale(middle)
     normed_ffn = (middle * ffn_scale * ffn_gain_full).astype(bf16)
-    normed1, up_other, wgate = stage(
-        swap(normed_ffn, 1), send_outer(up_lines), spread_hidden(gate_lines, gate_other)
+    up_other = send_outer(up_lines)
+    normed_ffn, gate_other = stage(normed_ffn, gate_other)
+    normed1, normed2, up_other, wgate = stage(
+        swap(normed_ffn, 1),
+        swap(normed_ffn, 2),
+        up_other,
+        spread_hidden(gate_lines, gate_other),
     )
     wup = spread_hidden(up_lines, up_other)
     hidden_near, gate_near, up_near = hidden_pass((normed_ffn, normed1), wgate, wup)
-    normed2, hidden_near, grad_top3 = stage(
-        swap(normed_ffn, 2), hidden_near, swap(grad_top2, 1)
-    )
-    normed3 = swap(normed2, 1)
+    normed3, hidden_near, grad_top3 = stage(
+        swap(normed2, 1), hidden_near, swap(grad_top2, 1)
+    )
     hidden_far, gate_far, up_far = hidden_pass((normed2, normed3), wgate, wup)
     normed4 = (normed_ffn, normed1, normed2, normed3)
     grad_top4 = (grad_top, grad_top1, grad_top2, grad_top3)
     wdown = down_lines.reshape(hidden_columns, width)
     gate_far, up_far = gates_pass((grad_top2, grad_top3), wdown, gate_far, up_far)
     own, send = back_pass((gate_far, up_far), (wgate, wup), True)
-    across, wdown, hidden_far = stage(across_group(own, send), wdown, hidden_far)
     grad_wdown = weight_pass((hidden_near, hidden_far), grad_top4)
-    grad_wdown, wdown = stage(grad_wdown, wdown)
+    own, send, grad_wdown, wdown = stage(own, swap(send, 1), grad_wdown, wdown)
+    across = (own + send.astype(f32)).astype(bf16)
+    across, wdown = stage(across, wdown)
     gate_near, up_near = gates_pass((grad_top, grad_top1), wdown, gate_near, up_near)
     own, send = back_pass((gate_near, up_near), (wgate, wup), True)
-
     hidden_shape = (outer, 2, 2, seq_devices, d_rows, hidden_columns)
-    down_shape = (seq_devices, outer, f_rows, width)
-    grad_wdown = grad_wdown.reshape(down_shape)
+    grad_wdown = grad_wdown.reshape(seq_devices, outer, f_rows, width)
     grad_wgate = weight_pass(normed4, (gate_near, gate_far)).reshape(hidden_shape)
+    across, own, send, grad_wgate, up_near = stage(
+        swap(across, 2), own, send, grad_wgate, up_near
+    )
     grad_wup = weight_pass(normed4, (up_near, up_far)).reshape(hidden_shape)
-    across, own, send, grad_wgate, grad_wup, down_other = stage(
-        swap(across, 2),
-        own,
-        swap(send, 1),
-        grad_wgate,
-        grad_wup,
-        pass_outer(grad_wdown, 1),
-    )
+    send, grad_wup, down_other = stage(swap(send, 1), grad_wup, pass_outer(grad_wdown, 1))
     grad_wdown = add_outer(grad_wdown, down_other, 1)
     own = own + send.astype(f32)
     grad_normed_ffn = own + across.astype(f32)
@@ -884,7 +881,7 @@
         grad_q1, grad_kv1, pass_outer(grad_wgate, 0), grad_mixed, grad_wdown, hidden_far
     )
     grad_kv1 = reduce_seq(grad_kv1.reshape(seq_devices, shard_length, -1))
-    grad_gate = jnp.moveaxis(add_outer(grad_wgate, gate_other, 0), 2, 0)
+    grad_gate = reduce_seq(jnp.moveaxis(add_outer(grad_wgate, gate_other, 0), 2, 0))
     shape = (outer, 2, 2, seq_devices, d_rows)
     own_far, send_far = back_pass((hidden_far,), (wdown,), False)
     grad_wout, far_other, grad_mixed = stage(
@@ -895,11 +892,12 @@
     across = (own_far + far_other.astype(f32)).astype(bf16)
     across, grad_mixed = stage(across, grad_mixed)
     grad_q2, grad_kv2 = attend_backward(2, 3, *attend, grad_mixed)
-    grad_q2, grad_kv2, hidden_near, grad_kv1, wout_other, up_other, across = stage(
+    grad_q2, grad_kv2, hidden_near, grad_kv1, grad_gate, wout_other, up_other, across = stage(
         grad_q2,
         grad_kv2,
         hidden_near,
         grad_kv1,
+        grad_gate,
         pass_bit(grad_wout, 1, 2),
         pass_outer(grad_wup, 0),
         swap(across, 2),
@@ -914,13 +912,14 @@
     grad_wout = add_bit(grad_wout, wout_other, 1, 2)
     own_near, send_near = back_pass((hidden_near,), (wdown,), False)
     grad_up = jnp.moveaxis(add_outer(grad_wup, up_other, 0), 2, 0)
-    grad_gate_up = jnp.stack([grad_gate, grad_up], axis=3)
-    grad_kv2, wq_other, own_near, near_other, grad_gate_up = stage(
-        grad_kv2, pass_bit(grad_wq, 1, 2), own_near, swap(send_near, 1), grad_gate_up
+    wq_other, own_near, near_other, grad_up = stage(
+        pass_bit(grad_wq, 1, 2), own_near, swap(send_near, 1), grad_up
+    )
+    grad_kv2, grad_wq, grad_wout, grad_up = stage(
+        grad_kv2, add_bit(grad_wq, wq_other, 1, 2), grad_wout, grad_up
     )
     output = (middle + own_near + near_other.astype(f32) + across.astype(f32)).astype(bf16)
-    gate_up = reduce_seq(grad_gate_up)
-    grad_wq = add_bit(grad_wq, wq_other, 1, 2)
+    grad_up = reduce_seq(grad_up)
     wq_other, wout_other = pass_bit(grad_wq, 2, 1), pass_outer(grad_wout, 0)
 
     grad_kv1, grad_kv2 = (
@@ -962,12 +961,13 @@
     right = add_bit(right, right_other, 1, 2)
     grad_wq = add_bit(grad_wq, wq_other, 2, 1)
     grad_wout = add_outer(grad_wout, wout_other, 0)
-    left_other, right_other, wq_other, wout_other, gains_other = stage(
+    left_other, right_other, wq_other, wout_other, gains_other, grad_up = stage(
         pass_bit(left, 2, 1),
         pass_outer(right, 0),
         pass_outer(grad_wq, 0),
         pass_bit(grad_wout, 2, 0),
         exchange(head_gains, "seq", 1),
+        grad_up,
     )
     head_gains = head_gains + gains_other
     left = add_bit(left, left_other, 2, 1)
@@ -989,6 +989,7 @@
     )
     rest = [("rows", bit) for bit in (4, 8, 16) if bit < row_devices]
     rest += [("seq", bit) for bit in (2, 4, 8) if bit < seq_devices]
+    gate_up = jnp.stack([grad_gate, grad_up], axis=2)
     other, gains_other = stage(
         swap(part(gate_up, 1 - near, 0), 2), exchange(head_gains, *rest[0])
     )

time: 818 us -> 788 us (0.963)
  waiting for transfers between devices: 268 us -> 250 us
    ppermute x46, waiting for transfers between devices: 249 us -> 199 us  [swap(): return lax.ppermute(values, 'rows', pairs)]
    all_gather x5, waiting for transfers between devices: 3.71 us -> 23.9 us  [gather_seq(): return lax.all_gather(values, 'seq', axis=0, tiled=False)]
    another operation x3 -> x0, other arithmetic: 12.9 us -> none  [shards(): grad_gate_up = jnp.stack([grad_gate, grad_up], axis=3)]
    reduce_scatter x5 -> x6, waiting for transfers between devices: 7.77 us -> 19.7 us  [reduce_seq(): return lax.psum_scatter(values, 'seq', scatter_dimension=0, tiled=False)]
    transpose x0 -> x2, other arithmetic: none -> 8.27 us  [the longest x1 4.48 us: shards(): jnp.moveaxis(add_outer(grad_wgate, gate_other, 0), 2, 0)]
    squeeze x16 -> x15, local copies, waits for them, and re-layouts: 18.7 us -> 14 us  [part(): return lax.dynamic_index_in_dim(values, index, axis, keepdims=False)]
    unnamed x143 -> x151, local copies, waits for them, and re-layouts: 18.6 us -> 17 us
  transfers between devices with their start and end apart: 61 -> 62, of which waited for: 27 -> 31; matrix products, arithmetic and copies ran while one was open for 18% -> 16% of each run, Pallas kernels for 25% -> 28%
where the time goes in v4:
time: 788 us; the launch traced here: 779 us
  Pallas kernels  259 us (33%)
  waiting for transfers between devices  250 us (32%)
  other arithmetic  76.5 us (10%)
  local copies, waits for them, and re-layouts  69.3 us (9%)
  starting transfers between devices  43.9 us (6%)
  matrix products  42.5 us (5%)
  blocking collectives  19.9 us (3%)
  between operations  18.3 us (2%)
    ppermute x46, waiting for transfers between devices, swap(): return lax.ppermute(values, 'rows', pairs)  199 us
    pallas_call x3, Pallas kernels, weight_pass(): pl.pallas_call(partial(weight_kernel, len(lefts)), grid=(rows // tile,),...  47.3 us
    pallas_call x4, Pallas kernels, back_pass(): pl.pallas_call(partial(back_kernel, count, transposed), grid=(width // ti...  46.6 us
    ppermute x46, starting transfers between devices, swap(): return lax.ppermute(values, 'rows', pairs)  38.2 us
    pallas_call x2, Pallas kernels, hidden_pass(): pl.pallas_call(hidden_kernel, grid=(pl.cdiv(columns, tile),), in_specs=[w...  31.9 us
    pallas_call x2, Pallas kernels, attend_backward(): pl.pallas_call(partial(attend_backward_kernel, first, count), grid_spec=p...  30.9 us
    pallas_call x2, Pallas kernels, gates_pass(): pl.pallas_call(gates_kernel, grid=(pl.cdiv(columns, tile),), in_specs=[wh...  24 us
    all_gather x5, waiting for transfers between devices, gather_seq(): return lax.all_gather(values, 'seq', axis=0, tiled=False)  23.9 us
  transfers between devices with their start and end apart: 62, of which 31 were waited for; matrix products, arithmetic and copies ran while one was open for 16% of the time, Pallas kernels for 28%

profile of v4, /device:TPU:0, one launch (start us, length us, event | category | flops | bytes accessed | tf_op | source)
XLA Modules:
  0.0 778.5 jit_solution(2945234093967474975)
XLA Ops:
  28.3 19.9 %all-gather = bf16[256,768]{1,0:T(8,128)(2,1)S(1)} all-gather(bf16[64,768]{1,0:T(8,128)(2,1)S(1)} %fusion.36), channel_id=2, replica_groups=mesh['rows'=8,'seq'=4] {'seq'}, dimensions={0}, use_global_device_ids=true | all-gather | bytes 491520 | tf_op jit(solution)/shard_map/all_gather | solution.py:652
  61.2 11.2 %collective-permute-done.2 = bf16[4,64,384]{2,1,0:T(8,128)(2,1)S(1)} collective-permute-done((bf16[4,64,384]{2,1,0:T(8,128)(2,1)S(1)}, bf16[4,64,384]{2,1,0:T(8,128)(2,1)S(1)}, u32[]{:S(2)}, u32[]{:S(2)}) %collective-permute-start.2) | collective-permute-done | bytes 196640 | tf_op jit(solution)/shard_map/ppermute | solution.py:555
  111.0 25.5 %collective-permute-done.12 = bf16[2,4,64,1280]{3,2,1,0:T(8,128)(2,1)} collective-permute-done((bf16[2,4,64,1280]{3,2,1,0:T(8,128)(2,1)S(1)}, bf16[2,4,64,1280]{3,2,1,0:T(8,128)(2,1)}, u32[]{:S(2)}, u32[]{:S(2)}) %collective-permute-start.12) | collective-permute-done | bytes 1310752 | tf_op jit(solution)/shard_map/ppermute | solution.py:555
  167.6 8.5 %heads_forward.3.q_ref = bf16[512,1280]{1,0:T(8,128)(2,1)} custom-call(f32[512,1280]{1,0:T(8,128)} %fusion.51.joint_ref, f32[8,1280]{1,0:T(8,128)} %broadcast_in_dim.14.gain_ref, f32[512,128]{1,0:T(8,128)} %get-tuple-element.328.cos_ref, f32[512,128]{1,0:T(8,128)} %get-tuple-element.329.sin_ref), custom_call_target="tpu_custom_call" | custom-call | flops 1000 | bytes 1000 | tf_op jit(solution)/shard_map/heads_forward/pallas_call | solution.py:73
  178.4 11.7 %attend_forward.1 = (bf16[512,1280]{1,0:T(8,128)(2,1)S(1)}, f32[512,1280]{1,0:T(8,128)S(1)}) custom-call(s32[1]{0:T(128)} %bitcast.place_ref, bf16[512,1280]{1,0:T(8,128)(2,1)S(1)} %copy-done, bf16[2048,640]{1,0:T(8,128)(2,1)} %all-gather.14.cloned.1.call-done.k_ref.v_ref, bf16[2048,640]{1,0:T(8,128)(2,1)} %all-gather.14.cloned.1.call-done.k_ref.v_ref), custom_call_target="tpu_custom_call" | custom-call | flops 1000 | bytes 1000 | tf_op jit(solution)/shard_map/attend_forward/pallas_call | solution.py:177
  191.6 20.2 %all-gather.18.cloned.1.call-done = bf16[8,2,64,1152]{3,2,1,0:T(8,128)(2,1)} async-done(((bf16[2,2,64,1152]{3,2,1,0:T(8,128)(2,1)}), bf16[8,2,64,1152]{3,2,1,0:T(8,128)(2,1)}) %all-gather.18.cloned.1.call-update) | async-done | bytes 2359312 | tf_op jit(solution)/shard_map/all_gather | solution.py:652
  239.4 38.5 %collective-permute-done.19.n0_ref.refs_2_ = bf16[512,2048]{1,0:T(8,128)(2,1)} collective-permute-done((bf16[512,2048]{1,0:T(8,128)(2,1)S(1)}, bf16[512,2048]{1,0:T(8,128)(2,1)}, u32[]{:S(2)}, u32[]{:S(2)}) %collective-permute-start.19) | collective-permute-done | bytes 2097184 | tf_op jit(solution)/shard_map/ppermute | solution.py:555
  288.5 15.6 %hidden_pass.2 = (bf16[1024,1152]{1,0:T(8,128)(2,1)}, bf16[1024,1152]{1,0:T(8,128)(2,1)}, bf16[1024,1152]{1,0:T(8,128)(2,1)}) custom-call(bf16[512,2048]{1,0:T(8,128)(2,1)S(1)} %multiply_convert_fusion.n0_ref.refs_0_, bf16[512,2048]{1,0:T(8,128)(2,1)} %collective-permute-done.18.n1_ref.refs_1_, bf16[2048,1152]{1,0:T(8,128)(2,1)} %bitcast.287, ...), custom_call_target="tpu_custom_call" | custom-call | flops 1000 | bytes 1000 | tf_op jit(solution)/shard_map/hidden_pass/pallas_call | solution.py:344
  304.1 16.3 %hidden_pass.3 = (bf16[1024,1152]{1,0:T(8,128)(2,1)}, bf16[1024,1152]{1,0:T(8,128)(2,1)}, bf16[1024,1152]{1,0:T(8,128)(2,1)}) custom-call(bf16[512,2048]{1,0:T(8,128)(2,1)} %collective-permute-done.19.n0_ref.refs_2_, bf16[512,2048]{1,0:T(8,128)(2,1)} %collective-permute-done.21.n1_ref.refs_3_, bf16[2048,1152]{1,0:T(8,128)(2,1)} %bitcast.288, ...), custom_call_target="tpu_custom_call" | custom-call | flops 1000 | bytes 1000 | tf_op jit(solution)/shard_map/hidden_pass/pallas_call | solution.py:344
  320.4 12.3 %gates_pass.2 = (bf16[1024,1152]{1,0:T(8,128)(2,1)}, bf16[1024,1152]{1,0:T(8,128)(2,1)}) custom-call(bf16[512,2048]{1,0:T(8,128)(2,1)} %collective-permute-done.15.g0_ref.refs_4_, bf16[512,2048]{1,0:T(8,128)(2,1)} %collective-permute-done.22.g1_ref.refs_5_, bf16[1152,2048]{1,0:T(8,128)(2,1)} %bitcast.295, bf16[1024,1152]{1,0:T(8,128)(2,1)} %get-tuple-element.193.gate_ref, ...), custom_call_target="tpu_custom_call" | custom-call | flops 1000 | bytes 1000 | tf_op jit(solution)/shard_map/gates_pass/pallas_call | solution.py:379
  334.4 15.0 %back_pass.4 = (f32[512,2048]{1,0:T(8,128)}, bf16[512,2048]{1,0:T(8,128)(2,1)S(1)}) custom-call(bf16[1024,1152]{1,0:T(8,128)(2,1)S(1)} %copy-done.8, bf16[1024,1152]{1,0:T(8,128)(2,1)} %get-tuple-element.196.refs_1_.refs_5_, bf16[2048,1152]{1,0:T(8,128)(2,1)} %bitcast.289, bf16[2048,1152]{1,0:T(8,128)(2,1)} %bitcast.293), custom_call_target="tpu_custom_call" | custom-call | flops 1000 | bytes 1000 | tf_op jit(solution)/shard_map/back_pass/pallas_call | solution.py:418
  349.8 15.3 %weight_pass.3 = bf16[1152,2048]{1,0:T(8,128)(2,1)} custom-call(bf16[1024,1152]{1,0:T(8,128)(2,1)} %get-tuple-element.241.refs_0_, bf16[1024,1152]{1,0:T(8,128)(2,1)} %get-tuple-element.223.refs_1_.refs_0_, bf16[512,2048]{1,0:T(8,128)(2,1)S(1)} %copy-done.3, bf16[512,2048]{1,0:T(8,128)(2,1)} %collective-permute-done.14.refs_3_.g1_ref, ...), custom_call_target="tpu_custom_call" | custom-call | flops 1000 | bytes 1000 | tf_op jit(solution)/shard_map/weight_pass/pallas_call | solution.py:452
  371.8 11.7 %gates_pass.3 = (bf16[1024,1152]{1,0:T(8,128)(2,1)}, bf16[1024,1152]{1,0:T(8,128)(2,1)}) custom-call(bf16[512,2048]{1,0:T(8,128)(2,1)S(1)} %copy-done.4, bf16[512,2048]{1,0:T(8,128)(2,1)} %collective-permute-done.14.refs_3_.g1_ref, bf16[1152,2048]{1,0:T(8,128)(2,1)} %bitcast.296, bf16[1024,1152]{1,0:T(8,128)(2,1)} %get-tuple-element.207.gate_ref, ...), custom_call_target="tpu_custom_call" | custom-call | flops 1000 | bytes 1000 | tf_op jit(solution)/shard_map/gates_pass/pallas_call | solution.py:379
  383.4 15.9 %weight_pass.4 = bf16[2048,1152]{1,0:T(8,128)(2,1)} custom-call(bf16[512,2048]{1,0:T(8,128)(2,1)S(1)} %multiply_convert_fusion.n0_ref.refs_0_, bf16[512,2048]{1,0:T(8,128)(2,1)} %collective-permute-done.18.n1_ref.refs_1_, bf16[512,2048]{1,0:T(8,128)(2,1)} %collective-permute-done.19.n0_ref.refs_2_, bf16[512,2048]{1,0:T(8,128)(2,1)} %collective-permute-done.21.n1_ref.refs_3_, ...), custom_call_target="tpu_custom_call" | custom-call | flops 1000 | bytes 1000 | tf_op jit(solution)/shard_map/weight_pass/pallas_call | solution.py:452
  399.3 14.9 %back_pass.5 = (f32[512,2048]{1,0:T(8,128)}, bf16[512,2048]{1,0:T(8,128)(2,1)}) custom-call(bf16[1024,1152]{1,0:T(8,128)(2,1)S(1)} %copy-done.9, bf16[1024,1152]{1,0:T(8,128)(2,1)} %get-tuple-element.215.refs_1_.refs_4_, bf16[2048,1152]{1,0:T(8,128)(2,1)} %bitcast.290, bf16[2048,1152]{1,0:T(8,128)(2,1)} %bitcast.294), custom_call_target="tpu_custom_call" | custom-call | flops 1000 | bytes 1000 | tf_op jit(solution)/shard_map/back_pass/pallas_call | solution.py:418
  415.0 16.2 %weight_pass.5 = bf16[2048,1152]{1,0:T(8,128)(2,1)} custom-call(bf16[512,2048]{1,0:T(8,128)(2,1)S(1)} %multiply_convert_fusion.n0_ref.refs_0_, bf16[512,2048]{1,0:T(8,128)(2,1)} %collective-permute-done.18.n1_ref.refs_1_, bf16[512,2048]{1,0:T(8,128)(2,1)} %collective-permute-done.19.n0_ref.refs_2_, bf16[512,2048]{1,0:T(8,128)(2,1)} %collective-permute-done.21.n1_ref.refs_3_, ...), custom_call_target="tpu_custom_call" | custom-call | flops 1000 | bytes 1000 | tf_op jit(solution)/shard_map/weight_pass/pallas_call | solution.py:452
  451.2 12.5 %attend_backward.2 = (bf16[512,512]{1,0:T(8,128)(2,1)S(1)}, bf16[2048,256]{1,0:T(8,128)(2,1)S(1)}) custom-call(s32[1]{0:T(128)} %bitcast.place_ref, bf16[512,1280]{1,0:T(8,128)(2,1)S(1)} %copy-done.1, bf16[2048,640]{1,0:T(8,128)(2,1)} %all-gather.14.cloned.1.call-done.k_ref.v_ref, bf16[2048,640]{1,0:T(8,128)(2,1)} %all-gather.14.cloned.1.call-done.k_ref.v_ref, ...), custom_call_target="tpu_custom_call" | custom-call | flops 1000 | bytes 1000 | tf_op jit(solution)/shard_map/attend_backward/pallas_call | solution.py:300
  464.6 27.4 %collective-permute-done.27 = bf16[2,2,4,64,1152]{4,3,1,0,2:T(8,128)(2,1)} collective-permute-done((bf16[2,2,4,64,1152]{4,3,1,0,2:T(8,128)(2,1)S(1)}, bf16[2,2,4,64,1152]{4,3,1,0,2:T(8,128)(2,1)}, u32[]{:S(2)}, u32[]{:S(2)}) %collective-permute-start.27) | collective-permute-done | bytes 2359328 | tf_op jit(solution)/shard_map/ppermute | solution.py:555
  523.0 18.4 %attend_backward.3 = (bf16[512,768]{1,0:T(8,128)(2,1)S(1)}, bf16[2048,384]{1,0:T(8,128)(2,1)}) custom-call(s32[1]{0:T(128)} %bitcast.place_ref, bf16[512,1280]{1,0:T(8,128)(2,1)S(1)} %copy-done.1, bf16[2048,640]{1,0:T(8,128)(2,1)} %all-gather.14.cloned.1.call-done.k_ref.v_ref, bf16[2048,640]{1,0:T(8,128)(2,1)} %all-gather.14.cloned.1.call-done.k_ref.v_ref, ...), custom_call_target="tpu_custom_call" | custom-call | flops 1000 | bytes 1000 | tf_op jit(solution)/shard_map/attend_backward/pallas_call | solution.py:300
  541.5 21.1 %collective-permute-done.30 = bf16[2,2,4,64,1152]{4,3,1,0,2:T(8,128)(2,1)} collective-permute-done((bf16[2,2,4,64,1152]{4,3,1,0,2:T(8,128)(2,1)S(1)}, bf16[2,2,4,64,1152]{4,3,1,0,2:T(8,128)(2,1)}, u32[]{:S(2)}, u32[]{:S(2)}) %collective-permute-start.30) | collective-permute-done | bytes 2359328 | tf_op jit(solution)/shard_map/ppermute | solution.py:555
  572.2 8.9 %heads_backward.2 = (bf16[512,1280]{1,0:T(8,128)(2,1)}, f32[8,1280]{1,0:T(8,128)}) custom-call(bf16[512,1280]{1,0:T(8,128)(2,1)} %pad_maximum_fusion.5.grad_ref, f32[512,1280]{1,0:T(8,128)} %fusion.51.joint_ref, f32[8,1280]{1,0:T(8,128)} %broadcast_in_dim.14.gain_ref, f32[512,128]{1,0:T(8,128)} %get-tuple-element.328.cos_ref, ...), custom_call_target="tpu_custom_call" | custom-call | flops 1000 | bytes 1000 | tf_op jit(solution)/shard_map/heads_backward/pallas_call | solution.py:109
  614.8 13.0 %reduce-scatter.13.cloned.1.call-done = bf16[1,512,384]{1,2,0:T(8,128)(2,1)} async-done(((bf16[4,512,384]{1,2,0:T(8,128)(2,1)}), bf16[1,512,384]{1,2,0:T(8,128)(2,1)}) %reduce-scatter.13.cloned.1.call-update) | async-done | bytes 393232 | tf_op jit(solution)/shard_map/reduce_scatter | solution.py:656
  665.6 20.2 %collective-permute-done.37 = bf16[2,4,64,1280]{3,2,1,0:T(8,128)(2,1)} collective-permute-done((bf16[2,4,64,1280]{3,2,1,0:T(8,128)(2,1)}, bf16[2,4,64,1280]{3,2,1,0:T(8,128)(2,1)}, u32[]{:S(2)}, u32[]{:S(2)}) %collective-permute-start.37) | collective-permute-done | bytes 1310752 | tf_op jit(solution)/shard_map/ppermute | solution.py:555
  703.5 11.1 %collective-permute-done.39 = bf16[2,4,64,384]{3,2,1,0:T(8,128)(2,1)S(1)} collective-permute-done((bf16[2,4,64,384]{3,2,1,0:T(8,128)(2,1)S(1)}, bf16[2,4,64,384]{3,2,1,0:T(8,128)(2,1)S(1)}, u32[]{:S(2)}, u32[]{:S(2)}) %collective-permute-start.39) | collective-permute-done | bytes 393248 | tf_op jit(solution)/shard_map/ppermute | solution.py:555
  (435 shorter events, 359.0 us)
Async XLA Ops:
  9.8 129.1 %all-gather.16.cloned.1.call-start = ((), (), s32[]{:S(2)}) async-start(), calls=%async_computation.14 | async-start | bytes 2949120 | tf_op jit(solution)/shard_map/all_gather | solution.py:652
  53.1 123.0 %all-gather.14.cloned.1.call-start = ((), (), s32[]{:S(2)}) async-start(), calls=%async_computation.13 | async-start | bytes 3276800 | tf_op jit(solution)/shard_map/all_gather | solution.py:652
  105.4 106.4 %all-gather.18.cloned.1.call-start = ((), (), s32[]{:S(2)}) async-start(), calls=%async_computation.15 | async-start | bytes 2949120 | tf_op jit(solution)/shard_map/all_gather | solution.py:652
  110.9 209.4 %all-gather.20.cloned.1.call-start = ((), (), s32[]{:S(2)}) async-start(), calls=%async_computation.16 | async-start | bytes 5898240 | tf_op jit(solution)/shard_map/all_gather | solution.py:652
  147.8 64.0 %collective-permute-start.16 = (bf16[2,2,4,64,1280]{4,3,2,1,0:T(8,128)(2,1)}, bf16[2,2,4,64,1280]{4,3,2,1,0:T(8,128)(2,1)}, u32[]{:S(2)}, u32[]{:S(2)}) collective-permute-start(bf16[2,2,4,64,1280]{4,3,2,1,0:T(8,128)(2,1)} %bitcast.64), channel_id=1, source_target_pairs={{0,4},{4,0},{8,12},{12,8},{16,20},{20,16},{24,28},{28,24},{1,5},{5... | collective-permute-start | bytes 7864328 | tf_op jit(solution)/shard_map/ppermute | solution.py:555
  155.8 56.0 %collective-permute-start.15 = (bf16[512,2048]{1,0:T(8,128)(2,1)S(1)}, bf16[512,2048]{1,0:T(8,128)(2,1)}, u32[]{:S(2)}, u32[]{:S(2)}) collective-permute-start(bf16[512,2048]{1,0:T(8,128)(2,1)S(1)} %bitcast_convert_fusion.refs_2_.g0_ref), channel_id=1, source_target_pairs={{0,8},{4,12},{8,0},{12,4},{16,24},{20,28},{24,16},{28,20},{1,9},{5... | collective-permute-start | bytes 6291464 | tf_op jit(solution)/shard_map/ppermute | solution.py:555
  157.2 54.6 %collective-permute-start.14 = (bf16[512,2048]{1,0:T(8,128)(2,1)S(1)}, bf16[512,2048]{1,0:T(8,128)(2,1)}, u32[]{:S(2)}, u32[]{:S(2)}) collective-permute-start(bf16[512,2048]{1,0:T(8,128)(2,1)S(1)} %bitcast_convert_fusion.refs_2_.g0_ref), channel_id=1, source_target_pairs={{0,4},{4,0},{8,12},{12,8},{16,20},{20,16},{24,28},{28,24},{1,5},{5... | collective-permute-start | bytes 6291464 | tf_op jit(solution)/shard_map/ppermute | solution.py:555
  176.2 315.8 %reduce-scatter.7.cloned.1.call-start = ((), (), s32[]{:S(2)}) async-start(), calls=%async_computation.6 | async-start | bytes 2949120 | tf_op jit(solution)/shard_map/reduce_scatter | solution.py:656
  176.4 54.4 %collective-permute-start.17 = (bf16[4,2,2,64,1152]{4,3,2,1,0:T(8,128)(2,1)}, bf16[4,2,2,64,1152]{4,3,2,1,0:T(8,128)(2,1)}, u32[]{:S(2)}, u32[]{:S(2)}) collective-permute-start(bf16[4,2,2,64,1152]{4,3,2,1,0:T(8,128)(2,1)} %bitcast.325), channel_id=1, source_target_pairs={{0,16},{4,20},{8,24},{12,28},{16,0},{20,4},{24,8},{28,12},{1,17},{... | collective-permute-start | bytes 7077896 | tf_op jit(solution)/shard_map/ppermute | solution.py:555
  211.8 69.2 %collective-permute-start.20 = (bf16[4,2,2,64,1152]{4,3,2,1,0:T(8,128)(2,1)}, bf16[4,2,2,64,1152]{4,3,2,1,0:T(8,128)(2,1)}, u32[]{:S(2)}, u32[]{:S(2)}) collective-permute-start(bf16[4,2,2,64,1152]{4,3,2,1,0:T(8,128)(2,1)} %bitcast.327), channel_id=1, source_target_pairs={{0,16},{4,20},{8,24},{12,28},{16,0},{20,4},{24,8},{28,12},{1,17},{... | collective-permute-start | bytes 7077896 | tf_op jit(solution)/shard_map/ppermute | solution.py:555
  230.8 47.0 %collective-permute-start.19 = (bf16[512,2048]{1,0:T(8,128)(2,1)S(1)}, bf16[512,2048]{1,0:T(8,128)(2,1)}, u32[]{:S(2)}, u32[]{:S(2)}) collective-permute-start(bf16[512,2048]{1,0:T(8,128)(2,1)S(1)} %multiply_convert_fusion.n0_ref.refs_0_), channel_id=1, source_target_pairs={{0,8},{4,12},{8,0},{12,4},{16,24},{20,28},{24,16},{28,20},{1,9},{5... | collective-permute-start | bytes 6291464 | tf_op jit(solution)/shard_map/ppermute | solution.py:555
  231.4 46.5 %collective-permute-start.18 = (bf16[512,2048]{1,0:T(8,128)(2,1)S(1)}, bf16[512,2048]{1,0:T(8,128)(2,1)}, u32[]{:S(2)}, u32[]{:S(2)}) collective-permute-start(bf16[512,2048]{1,0:T(8,128)(2,1)S(1)} %multiply_convert_fusion.n0_ref.refs_0_), channel_id=1, source_target_pairs={{0,4},{4,0},{8,12},{12,8},{16,20},{20,16},{24,28},{28,24},{1,5},{5... | collective-permute-start | bytes 6291464 | tf_op jit(solution)/shard_map/ppermute | solution.py:555
  231.4 72.7 %collective-permute-start.22 = (bf16[512,2048]{1,0:T(8,128)(2,1)}, bf16[512,2048]{1,0:T(8,128)(2,1)}, u32[]{:S(2)}, u32[]{:S(2)}) collective-permute-start(bf16[512,2048]{1,0:T(8,128)(2,1)} %collective-permute-done.15.g0_ref.refs_4_), channel_id=1, source_target_pairs={{0,4},{4,0},{8,12},{12,8},{16,20},{20,16},{24,28},{28,24},{1,5},{5... | collective-permute-start | bytes 6291464 | tf_op jit(solution)/shard_map/ppermute | solution.py:555
  367.1 47.9 %collective-permute-start.24 = (bf16[512,2048]{1,0:T(8,128)(2,1)}, bf16[512,2048]{1,0:T(8,128)(2,1)}, u32[]{:S(2)}, u32[]{:S(2)}) collective-permute-start(bf16[512,2048]{1,0:T(8,128)(2,1)} %add_convert_fusion.2), channel_id=1, source_target_pairs={{0,8},{4,12},{8,0},{12,4},{16,24},{20,28},{24,16},{28,20},{1,9},{5... | collective-permute-start | bytes 6291464 | tf_op jit(solution)/shard_map/ppermute | solution.py:555
  371.2 60.0 %collective-permute-start.26 = (bf16[4,144,2048]{2,1,0:T(8,128)(2,1)}, bf16[4,144,2048]{2,1,0:T(8,128)(2,1)}, u32[]{:S(2)}, u32[]{:S(2)}) collective-permute-start(bf16[4,144,2048]{2,1,0:T(8,128)(2,1)} %dynamic-slice_bitcast_fusion.1), channel_id=1, source_target_pairs={{0,16},{4,20},{8,24},{12,28},{16,0},{20,4},{24,8},{28,12},{1,17},{... | collective-permute-start | bytes 7077896 | tf_op jit(solution)/shard_map/ppermute | solution.py:555
  436.1 126.5 %reduce-scatter.9.cloned.1.call-start = ((), (), s32[]{:S(2)}) async-start(), calls=%async_computation.7 | async-start | bytes 1310720 | tf_op jit(solution)/shard_map/reduce_scatter | solution.py:656
  438.2 53.8 %collective-permute-start.27 = (bf16[2,2,4,64,1152]{4,3,1,0,2:T(8,128)(2,1)S(1)}, bf16[2,2,4,64,1152]{4,3,1,0,2:T(8,128)(2,1)}, u32[]{:S(2)}, u32[]{:S(2)}) collective-permute-start(bf16[2,2,4,64,1152]{4,3,1,0,2:T(8,128)(2,1)S(1)} %copy_bitcast_fusion.3), channel_id=1, source_target_pairs={{0,16},{4,20},{8,24},{12,28},{16,0},{20,4},{24,8},{28,12},{1,17},{... | collective-permute-start | bytes 7077896 | tf_op jit(solution)/shard_map/ppermute | solution.py:555
  492.1 78.0 %reduce-scatter.11.cloned.1.call-start = ((), (), s32[]{:S(2)}) async-start(), calls=%async_computation.8 | async-start | bytes 2949120 | tf_op jit(solution)/shard_map/reduce_scatter | solution.py:656
  506.6 121.2 %reduce-scatter.13.cloned.1.call-start = ((), (), s32[]{:S(2)}) async-start(), calls=%async_computation.9 | async-start | bytes 1966080 | tf_op jit(solution)/shard_map/reduce_scatter | solution.py:656
  508.7 53.9 %collective-permute-start.30 = (bf16[2,2,4,64,1152]{4,3,1,0,2:T(8,128)(2,1)S(1)}, bf16[2,2,4,64,1152]{4,3,1,0,2:T(8,128)(2,1)}, u32[]{:S(2)}, u32[]{:S(2)}) collective-permute-start(bf16[2,2,4,64,1152]{4,3,1,0,2:T(8,128)(2,1)S(1)} %copy_bitcast_fusion.2), channel_id=1, source_target_pairs={{0,16},{4,20},{8,24},{12,28},{16,0},{20,4},{24,8},{28,12},{1,17},{... | collective-permute-start | bytes 7077896 | tf_op jit(solution)/shard_map/ppermute | solution.py:555
  516.8 53.3 %collective-permute-start.29 = (bf16[2,2,4,64,1280]{4,3,2,1,0:T(8,128)(2,1)}, bf16[2,2,4,64,1280]{4,3,2,1,0:T(8,128)(2,1)}, u32[]{:S(2)}, u32[]{:S(2)}) collective-permute-start(bf16[2,2,4,64,1280]{4,3,2,1,0:T(8,128)(2,1)} %dynamic-slice_bitcast_fusion), channel_id=1, source_target_pairs={{0,4},{4,0},{8,12},{12,8},{16,20},{20,16},{24,28},{28,24},{1,5},{5... | collective-permute-start | bytes 7864328 | tf_op jit(solution)/shard_map/ppermute | solution.py:555
  521.6 48.4 %collective-permute-start.31 = (bf16[512,2048]{1,0:T(8,128)(2,1)}, bf16[512,2048]{1,0:T(8,128)(2,1)}, u32[]{:S(2)}, u32[]{:S(2)}) collective-permute-start(bf16[512,2048]{1,0:T(8,128)(2,1)} %add_convert_fusion.1), channel_id=1, source_target_pairs={{0,8},{4,12},{8,0},{12,4},{16,24},{20,28},{24,16},{28,20},{1,9},{5... | collective-permute-start | bytes 6291464 | tf_op jit(solution)/shard_map/ppermute | solution.py:555
  592.2 126.1 %reduce-scatter.15.cloned.1.call-start = ((), (), s32[]{:S(2)}) async-start(), calls=%async_computation.10 | async-start | bytes 2949120 | tf_op jit(solution)/shard_map/reduce_scatter | solution.py:656
  653.6 113.1 %reduce-scatter.17.cloned.1.call-start = ((), (), s32[]{:S(2)}) async-start(), calls=%async_computation.11 | async-start | bytes 2129920 | tf_op jit(solution)/shard_map/reduce_scatter | solution.py:656
  (113 other events, 1032.6 us)
Sparse Core Ops, SparseCore 0:
  10.2 41.6 all-gather.11
  54.0 49.5 all-gather.15
  105.7 55.3 all-gather.13
  162.5 49.2 all-gather.17
  213.8 88.2 all-gather.19
  436.2 48.0 reduce-scatter.6
  492.2 27.0 reduce-scatter.8
  521.7 46.6 reduce-scatter.10
  592.3 35.4 reduce-scatter.12
  653.7 46.9 reduce-scatter.14
  730.5 36.0 reduce-scatter.16

commit v5 on v4

--- a/solution.py
+++ b/solution.py
@@ -19,6 +19,7 @@
 KEY_COLUMNS = KEY_VALUE_HEADS * HEAD_SIZE
 LANES = 128
 SCORE_EXPONENT = 1.4426950408889634 * HEAD_SIZE**-0.5
+SPLIT = 2
 VMEM_LIMIT = 48 * 1024 * 1024
 
 f32, bf16 = jnp.float32, jnp.bfloat16
@@ -59,31 +60,47 @@
     )
 
 
-def heads_forward_kernel(norm_columns, joint_ref, gain_ref, cos_ref, sin_ref, out_ref):
-    values = joint_ref[...]
-    scale = lax.rsqrt(head_sum(values * values) * (1.0 / HEAD_SIZE) + EPSILON)
-    normed = values * scale * gain_ref[0:1, :]
-    turned = normed * cos_ref[...] + partner(normed) * sin_ref[...]
-    place = pl.program_id(0) * LANES + lanes_of(values.shape)
-    out_ref[...] = jnp.where(place < norm_columns, turned, values).astype(bf16)
-
-
-def heads_forward(joint, gain, cos, sin, norm_columns):
-    tokens, columns = joint.shape
+def heads_forward_kernel(
+    norm_columns, normed_ref, weight_ref, gain_ref, cos_ref, sin_ref, joint_ref, out_ref
+):
+    joint = dot_nn(normed_ref[...], weight_ref[...])
+    joint_ref[...] = joint
+    columns = joint.shape[1]
+    for start in range(0, columns, LANES):
+        chunk = slice(start, start + LANES)
+        values = joint[:, chunk]
+        scale = lax.rsqrt(head_sum(values * values) * (1.0 / HEAD_SIZE) + EPSILON)
+        normed = values * scale * gain_ref[0:1, chunk]
+        turned = normed * cos_ref[...] + partner(normed) * sin_ref[...]
+        place = pl.program_id(0) * columns + start + lanes_of(values.shape)
+        out_ref[:, chunk] = jnp.where(place < norm_columns, turned, values).astype(bf16)
+
+
+def heads_forward(normed, weight, gain, cos, sin, norm_columns):
+    tokens, width = normed.shape
+    columns = weight.shape[1]
+    tile = 2 * LANES if columns % (2 * LANES) == 0 else LANES
+    out = pl.BlockSpec((tokens, tile), lambda i: (0, i))
+    table = pl.BlockSpec((tokens, LANES), lambda i: (0, 0))
     return pl.pallas_call(
         partial(heads_forward_kernel, norm_columns),
-        grid=(columns // LANES,),
+        grid=(columns // tile,),
         in_specs=[
-            pl.BlockSpec((tokens, LANES), lambda i: (0, i)),
-            pl.BlockSpec((8, LANES), lambda i: (0, i)),
-            pl.BlockSpec((tokens, LANES), lambda i: (0, 0)),
-            pl.BlockSpec((tokens, LANES), lambda i: (0, 0)),
+            pl.BlockSpec((tokens, width), lambda i: (0, 0)),
+            pl.BlockSpec((width, tile), lambda i: (0, i)),
+            pl.BlockSpec((8, tile), lambda i: (0, i)),
+            table,
+            table,
         ],
-        out_specs=pl.BlockSpec((tokens, LANES), lambda i: (0, i)),
-        out_shape=jax.ShapeDtypeStruct((tokens, columns), bf16),
+        out_specs=[out, out],
+        out_shape=[
+            jax.ShapeDtypeStruct((tokens, columns), f32),
+            jax.ShapeDtypeStruct((tokens, columns), bf16),
+        ],
+        compiler_params=pltpu.CompilerParams(vmem_limit_bytes=VMEM_LIMIT),
         name="heads_forward",
         cost_estimate=LIGHT,
-    )(joint, gain, cos, sin)
+    )(normed, weight, gain, cos, sin)
 
 
 def heads_backward_kernel(
@@ -235,8 +252,11 @@
 
     queries = sides(pair, 0.0)
     grads = sides(grad, 0.0)
-    queries_log = sides(pair, logs)
-    grads_delta = sides(grad, deltas)
+    def turned(values):
+        return jnp.transpose(values.astype(f32)).astype(bf16)
+
+    queries_log = tuple(turned(v) for v in sides(pair, logs))
+    grads_delta = tuple(turned(v) for v in sides(grad, deltas))
 
     @pl.when(pair_index % 2 == 0)
     def _():
@@ -247,29 +267,40 @@
         rows = pl.ds(pl.multiple_of(j * tokens, tokens), tokens)
         key_wide = both_halves(k_ref[rows, :], group % 2)
         value_wide = both_halves(v_ref[rows, :], (KEY_VALUE_HEADS + group) % 2)
-        keys = sides(key_wide, 0.0)
+        keys_turned = jnp.transpose(key_wide)[:HEAD_SIZE].astype(bf16)
         keys_log = sides(key_wide, minus)
         values_delta = sides(value_wide, minus)
         dk = dk_sum[rows, :]
         dv = dv_sum[rows, :]
-        for head in range(2):
-            weights = jnp.exp2(dot_nt(keys_log[head], queries_log[head]) * SCORE_EXPONENT)
-            if diagonal:
-                row = lax.broadcasted_iota(jnp.int32, weights.shape, 0)
-                weights = jnp.where(row <= lanes_of(weights.shape), weights, 0.0)
-            grad_weights = dot_nt(values_delta[head], grads_delta[head])
-            grad_scores = (weights * grad_weights).astype(bf16)
-            dv = dv + dot_nn(weights.astype(bf16), grads[head])
-            dk = dk + dot_nn(grad_scores, queries[head])
-            dq = dq + dot_tn(grad_scores, keys[head])
-        dk_sum[rows, :] = dk
-        dv_sum[rows, :] = dv
-        return dq
-
-    dq = lax.fori_loop(
-        0, place, lambda j, c: step(j, c, False), jnp.zeros((tokens, LANES), f32)
-    )
-    dq = step(place, dq, True)
+        parts = list(dq)
+        block = tokens // SPLIT
+        for sub in range(SPLIT):
+            keep = slice(sub * block, (sub + 1) * block)
+            dk_part, dv_part = dk[keep], dv[keep]
+            start = sub * block if diagonal else 0
+            for head in range(2):
+                weights = jnp.exp2(
+                    dot_nn(keys_log[head][keep], queries_log[head][:, start:]) * SCORE_EXPONENT
+                )
+                if diagonal:
+                    row = lax.broadcasted_iota(jnp.int32, weights.shape, 0)
+                    weights = jnp.where(row <= lanes_of(weights.shape), weights, 0.0)
+                grad_weights = dot_nn(values_delta[head][keep], grads_delta[head][:, start:])
+                grad_scores = (weights * grad_weights).astype(bf16)
+                dv_part = dv_part + dot_nn(weights.astype(bf16), grads[head][start:])
+                dk_part = dk_part + dot_nn(grad_scores, queries[head][start:])
+                term = dot_nn(keys_turned[:, keep], grad_scores)
+                if start:
+                    term = jnp.concatenate([jnp.zeros((HEAD_SIZE, start), f32), term], axis=1)
+                parts[head] = parts[head] + term
+            target = pl.ds(pl.multiple_of(j * tokens + sub * block, block), block)
+            dk_sum[target, :] = dk_part
+            dv_sum[target, :] = dv_part
+        return tuple(parts)
+
+    zero = jnp.zeros((HEAD_SIZE, tokens), f32)
+    dq = lax.fori_loop(0, place, lambda j, c: step(j, c, False), (zero, zero))
+    dq = jnp.transpose(jnp.concatenate(step(place, dq, True), axis=0))
     dq_ref[...] = (dq * HEAD_SIZE**-0.5).astype(bf16)
 
     @pl.when(pair_index % 2 == 1)
@@ -787,13 +818,13 @@
 
     in_scale = norm_scale(inputs)
     normed = (inputs * in_scale * attn_gain_full).astype(bf16)
-    joint_kv = mm(normed, wkv)
-    own_kv = heads_forward(joint_kv, wide_k, cos_table, sin_table, KEY_COLUMNS)
+    joint_kv, own_kv = heads_forward(
+        normed, wkv, wide_k, cos_table, sin_table, KEY_COLUMNS
+    )
     own_kv, q_left_other, q_right_other, down_other, up_in = stage(
         own_kv, q_left_other, q_right_other, send_outer(w_down), gate_up[:, :, 1]
     )
     up_lines = gather_seq(up_in)
-    down_pair = join_outer(w_down, down_other, 0)
     keys_values = gather_seq(own_kv).reshape(-1, 2 * KEY_COLUMNS)
     q_left = join_outer(q_left, q_left_other, 0)
     q_right = joined(q_right, q_right_other, near, 0)
@@ -801,7 +832,6 @@
         swap(q_left, 2), send_outer(q_right), gate_lines
     )
     q_left = joined(q_left, left_other, near, 1)
-    q_right = join_outer(q_right, right_other, 0)
     gate_other = send_outer(gate_lines)
     wq = gather_bit(q_left, 1, 2).reshape(width, -1)
 
@@ -817,8 +847,12 @@
     grad_full = upstream[0].astype(f32) * factor
     grad_top, wq = stage(grad_full.astype(bf16), wq)
 
-    joint_q = mm(normed, wq)
-    queries = heads_forward(joint_q, wide_q, cos_table, sin_table, QUERY_COLUMNS)
+    joint_q, queries = heads_forward(
+        normed, wq, wide_q, cos_table, sin_table, QUERY_COLUMNS
+    )
+    queries, q_right, right_other, down_other = stage(queries, q_right, right_other, down_other)
+    q_right = join_outer(q_right, right_other, 0)
+    down_pair = join_outer(w_down, down_other, 0)
     place_array = place.reshape(1)
     keys_values, queries, down_in = stage(keys_values, queries, down_pair)
     down_lines = gather_seq(down_in)
@@ -912,15 +946,11 @@
     grad_wout = add_bit(grad_wout, wout_other, 1, 2)
     own_near, send_near = back_pass((hidden_near,), (wdown,), False)
     grad_up = jnp.moveaxis(add_outer(grad_wup, up_other, 0), 2, 0)
-    wq_other, own_near, near_other, grad_up = stage(
-        pass_bit(grad_wq, 1, 2), own_near, swap(send_near, 1), grad_up
-    )
-    grad_kv2, grad_wq, grad_wout, grad_up = stage(
-        grad_kv2, add_bit(grad_wq, wq_other, 1, 2), grad_wout, grad_up
-    )
-    output = (middle + own_near + near_other.astype(f32) + across.astype(f32)).astype(bf16)
+    grad_kv2, joint_grad_q, grad_wq, grad_wout, own_near, send_near, grad_up = stage(
+        grad_kv2, joint_grad_q, grad_wq, grad_wout, own_near, send_near, grad_up
+    )
     grad_up = reduce_seq(grad_up)
-    wq_other, wout_other = pass_bit(grad_wq, 2, 1), pass_outer(grad_wout, 0)
+
 
     grad_kv1, grad_kv2 = (
         part_.reshape(shard_length, 2, -1) for part_ in (grad_kv1, grad_kv2)
@@ -929,7 +959,14 @@
     joint_grad_kv, gain_k = heads_backward(
         grad_kv, joint_kv, wide_k, cos_table, sin_table, KEY_COLUMNS
     )
-    grad_wkv = t_mm(normed, joint_grad_kv).astype(bf16)
+    wq_other, near_other, joint_grad_kv = stage(
+        pass_bit(grad_wq, 1, 2), swap(send_near, 1), joint_grad_kv
+    )
+    grad_wkv, grad_wq, grad_wout = stage(
+        t_mm(normed, joint_grad_kv).astype(bf16), add_bit(grad_wq, wq_other, 1, 2), grad_wout
+    )
+    wq_other, wout_other = pass_bit(grad_wq, 2, 1), pass_outer(grad_wout, 0)
+    output = (middle + own_near + near_other.astype(f32) + across.astype(f32)).astype(bf16)
     grad_normed = mm_t(joint_grad_q, wq) + mm_t(joint_grad_kv, wkv)
     grad_input_part, grad_attn_gain = norm_backward(
         inputs, in_scale, attn_gain_full, grad_normed

time: 788 us -> 767 us (0.973)
  waiting for transfers between devices: 250 us -> 232 us
  matrix products: 42.5 us -> 28.7 us
  local copies, waits for them, and re-layouts: 69.3 us -> 77.4 us
    reduce_scatter x6, waiting for transfers between devices: 19.7 us -> 6.41 us  [reduce_seq(): return lax.psum_scatter(values, 'seq', scatter_dimension=0, tiled=False)]
    unnamed x151 -> x179, local copies, waits for them, and re-layouts: 17 us -> 29.9 us
    dot_general x3 -> x1, matrix products: 13.5 us -> 2.87 us  [mm(): return jnp.einsum('ab,bc->ac', left, right, preferred_element_type=f32)]
    ppermute x46, waiting for transfers between devices: 199 us -> 190 us  [swap(): return lax.ppermute(values, 'rows', pairs)]
    squeeze x15 -> x16, local copies, waits for them, and re-layouts: 14 us -> 17.7 us  [part(): return lax.dynamic_index_in_dim(values, index, axis, keepdims=False)]
  transfers between devices with their start and end apart: 62 -> 62, of which waited for: 31 -> 27; matrix products, arithmetic and copies ran while one was open for 16% -> 17% of each run, Pallas kernels for 28% -> 30%
where the time goes in v5:
time: 767 us; the launch traced here: 757 us
  Pallas kernels  254 us (33%)
  waiting for transfers between devices  232 us (30%)
  other arithmetic  81.7 us (11%)
  local copies, waits for them, and re-layouts  77.4 us (10%)
  starting transfers between devices  45 us (6%)
  matrix products  28.7 us (4%)
  blocking collectives  19.9 us (3%)
  between operations  18.5 us (2%)
    ppermute x46, waiting for transfers between devices, swap(): return lax.ppermute(values, 'rows', pairs)  190 us
    pallas_call x3, Pallas kernels, weight_pass(): pl.pallas_call(partial(weight_kernel, len(lefts)), grid=(rows // tile,),...  47.4 us
    pallas_call x4, Pallas kernels, back_pass(): pl.pallas_call(partial(back_kernel, count, transposed), grid=(width // ti...  46.4 us
    ppermute x46, starting transfers between devices, swap(): return lax.ppermute(values, 'rows', pairs)  39.4 us
    pallas_call x2, Pallas kernels, hidden_pass(): pl.pallas_call(hidden_kernel, grid=(pl.cdiv(columns, tile),), in_specs=[w...  31.9 us
    unnamed x179, local copies, waits for them, and re-layouts  29.9 us
    pallas_call x2, Pallas kernels, attend_backward(): pl.pallas_call(partial(attend_backward_kernel, first, count), grid_spec=p...  28.3 us
    all_gather x5, waiting for transfers between devices, gather_seq(): return lax.all_gather(values, 'seq', axis=0, tiled=False)  28.3 us
  transfers between devices with their start and end apart: 62, of which 27 were waited for; matrix products, arithmetic and copies ran while one was open for 17% of the time, Pallas kernels for 30%

profile of v5, /device:TPU:0, one launch (start us, length us, event | category | flops | bytes accessed | tf_op | source)
XLA Modules:
  0.0 757.4 jit_solution(5438098148075516722)
XLA Ops:
  28.3 19.9 %all-gather = bf16[256,768]{1,0:T(8,128)(2,1)S(1)} all-gather(bf16[64,768]{1,0:T(8,128)(2,1)S(1)} %fusion.35), channel_id=2, replica_groups=mesh['rows'=8,'seq'=4] {'seq'}, dimensions={0}, use_global_device_ids=true | all-gather | bytes 491520 | tf_op jit(solution)/shard_map/all_gather | solution.py:683
  61.1 11.5 %collective-permute-done.2 = bf16[4,64,384]{2,1,0:T(8,128)(2,1)S(1)} collective-permute-done((bf16[4,64,384]{2,1,0:T(8,128)(2,1)S(1)}, bf16[4,64,384]{2,1,0:T(8,128)(2,1)S(1)}, u32[]{:S(2)}, u32[]{:S(2)}) %collective-permute-start.2) | collective-permute-done | bytes 196640 | tf_op jit(solution)/shard_map/ppermute | solution.py:586
  111.5 25.3 %collective-permute-done.12 = bf16[2,4,64,1280]{3,2,1,0:T(8,128)(2,1)S(1)} collective-permute-done((bf16[2,4,64,1280]{3,2,1,0:T(8,128)(2,1)S(1)}, bf16[2,4,64,1280]{3,2,1,0:T(8,128)(2,1)S(1)}, u32[]{:S(2)}, u32[]{:S(2)}) %collective-permute-start.12) | collective-permute-done | bytes 1310752 | tf_op jit(solution)/shard_map/ppermute | solution.py:586
  156.1 8.5 %heads_forward.3 = (f32[512,1280]{1,0:T(8,128)}, bf16[512,1280]{1,0:T(8,128)(2,1)S(1)}) custom-call(bf16[512,2048]{1,0:T(8,128)(2,1)S(1)} %fusion.7.normed_ref, bf16[2048,1280]{1,0:T(8,128)(2,1)} %bitcast.295, f32[8,1280]{1,0:T(8,128)S(1)} %broadcast_in_dim.14.gain_ref, f32[512,128]{1,0:T(8,128)S(1)} %copy-done.11, f32[512,128]{1,0:T(8,128)S(1)} %copy-done.13), custom_call_target="tpu_custom_call" | custom-call | flops 1000 | bytes 1000 | tf_op jit(solution)/shard_map/heads_forward/pallas_call | solution.py:85
  172.4 11.7 %attend_forward.1 = (bf16[512,1280]{1,0:T(8,128)(2,1)S(1)}, f32[512,1280]{1,0:T(8,128)S(1)}) custom-call(s32[1]{0:T(128)} %bitcast.34.place_ref, bf16[512,1280]{1,0:T(8,128)(2,1)S(1)} %get-tuple-element.189.q_ref, bf16[2048,640]{1,0:T(8,128)(2,1)} %all-gather.14.cloned.1.call-done.k_ref.v_ref, bf16[2048,640]{1,0:T(8,128)(2,1)} %all-gather.14.cloned.1.call-done.k_ref.v_ref), custom_call_target="tpu_custom_call" | custom-call | flops 1000 | bytes 1000 | tf_op jit(solution)/shard_map/attend_forward/pallas_call | solution.py:194
  186.6 24.5 %all-gather.18.cloned.1.call-done = bf16[8,2,64,1152]{3,2,1,0:T(8,128)(2,1)} async-done(((bf16[2,2,64,1152]{3,2,1,0:T(8,128)(2,1)}), bf16[8,2,64,1152]{3,2,1,0:T(8,128)(2,1)}) %all-gather.18.cloned.1.call-update) | async-done | bytes 2359312 | tf_op jit(solution)/shard_map/all_gather | solution.py:683
  239.1 37.2 %collective-permute-done.19.n0_ref.refs_2_ = bf16[512,2048]{1,0:T(8,128)(2,1)} collective-permute-done((bf16[512,2048]{1,0:T(8,128)(2,1)S(1)}, bf16[512,2048]{1,0:T(8,128)(2,1)}, u32[]{:S(2)}, u32[]{:S(2)}) %collective-permute-start.19) | collective-permute-done | bytes 2097184 | tf_op jit(solution)/shard_map/ppermute | solution.py:586
  283.7 15.6 %hidden_pass.2 = (bf16[1024,1152]{1,0:T(8,128)(2,1)}, bf16[1024,1152]{1,0:T(8,128)(2,1)}, bf16[1024,1152]{1,0:T(8,128)(2,1)}) custom-call(bf16[512,2048]{1,0:T(8,128)(2,1)S(1)} %multiply_convert_fusion.n0_ref.refs_0_, bf16[512,2048]{1,0:T(8,128)(2,1)} %collective-permute-done.18.n1_ref.refs_1_, bf16[2048,1152]{1,0:T(8,128)(2,1)} %bitcast.283, ...), custom_call_target="tpu_custom_call" | custom-call | flops 1000 | bytes 1000 | tf_op jit(solution)/shard_map/hidden_pass/pallas_call | solution.py:375
  299.3 16.3 %hidden_pass.3 = (bf16[1024,1152]{1,0:T(8,128)(2,1)}, bf16[1024,1152]{1,0:T(8,128)(2,1)}, bf16[1024,1152]{1,0:T(8,128)(2,1)}) custom-call(bf16[512,2048]{1,0:T(8,128)(2,1)} %collective-permute-done.19.n0_ref.refs_2_, bf16[512,2048]{1,0:T(8,128)(2,1)} %collective-permute-done.21.n1_ref.refs_3_, bf16[2048,1152]{1,0:T(8,128)(2,1)} %bitcast.284, ...), custom_call_target="tpu_custom_call" | custom-call | flops 1000 | bytes 1000 | tf_op jit(solution)/shard_map/hidden_pass/pallas_call | solution.py:375
  315.7 12.3 %gates_pass.2 = (bf16[1024,1152]{1,0:T(8,128)(2,1)}, bf16[1024,1152]{1,0:T(8,128)(2,1)}) custom-call(bf16[512,2048]{1,0:T(8,128)(2,1)} %collective-permute-done.15.g0_ref.refs_4_, bf16[512,2048]{1,0:T(8,128)(2,1)} %collective-permute-done.22.g1_ref.refs_5_, bf16[1152,2048]{1,0:T(8,128)(2,1)} %bitcast.291, bf16[1024,1152]{1,0:T(8,128)(2,1)} %get-tuple-element.212.gate_ref, ...), custom_call_target="tpu_custom_call" | custom-call | flops 1000 | bytes 1000 | tf_op jit(solution)/shard_map/gates_pass/pallas_call | solution.py:410
  329.6 14.9 %back_pass.4 = (f32[512,2048]{1,0:T(8,128)}, bf16[512,2048]{1,0:T(8,128)(2,1)S(1)}) custom-call(bf16[1024,1152]{1,0:T(8,128)(2,1)S(1)} %copy-done.5, bf16[1024,1152]{1,0:T(8,128)(2,1)} %get-tuple-element.215.refs_1_.refs_5_, bf16[2048,1152]{1,0:T(8,128)(2,1)} %bitcast.285, bf16[2048,1152]{1,0:T(8,128)(2,1)} %bitcast.289), custom_call_target="tpu_custom_call" | custom-call | flops 1000 | bytes 1000 | tf_op jit(solution)/shard_map/back_pass/pallas_call | solution.py:449
  345.0 15.3 %weight_pass.3 = bf16[1152,2048]{1,0:T(8,128)(2,1)} custom-call(bf16[1024,1152]{1,0:T(8,128)(2,1)} %get-tuple-element.262.refs_0_, bf16[1024,1152]{1,0:T(8,128)(2,1)} %get-tuple-element.242.refs_1_.refs_0_, bf16[512,2048]{1,0:T(8,128)(2,1)} %bitcast_convert_fusion.refs_2_.g0_ref, bf16[512,2048]{1,0:T(8,128)(2,1)S(1)} %copy-done.8, ...), custom_call_target="tpu_custom_call" | custom-call | flops 1000 | bytes 1000 | tf_op jit(solution)/shard_map/weight_pass/pallas_call | solution.py:483
  368.0 11.7 %gates_pass.3 = (bf16[1024,1152]{1,0:T(8,128)(2,1)}, bf16[1024,1152]{1,0:T(8,128)(2,1)}) custom-call(bf16[512,2048]{1,0:T(8,128)(2,1)} %bitcast_convert_fusion.refs_2_.g0_ref, bf16[512,2048]{1,0:T(8,128)(2,1)S(1)} %copy-done.9, bf16[1152,2048]{1,0:T(8,128)(2,1)} %bitcast.292, bf16[1024,1152]{1,0:T(8,128)(2,1)} %get-tuple-element.226.gate_ref, ...), custom_call_target="tpu_custom_call" | custom-call | flops 1000 | bytes 1000 | tf_op jit(solution)/shard_map/gates_pass/pallas_call | solution.py:410
  379.7 15.9 %weight_pass.4 = bf16[2048,1152]{1,0:T(8,128)(2,1)} custom-call(bf16[512,2048]{1,0:T(8,128)(2,1)S(1)} %multiply_convert_fusion.n0_ref.refs_0_, bf16[512,2048]{1,0:T(8,128)(2,1)} %collective-permute-done.18.n1_ref.refs_1_, bf16[512,2048]{1,0:T(8,128)(2,1)} %collective-permute-done.19.n0_ref.refs_2_, bf16[512,2048]{1,0:T(8,128)(2,1)} %collective-permute-done.21.n1_ref.refs_3_, ...), custom_call_target="tpu_custom_call" | custom-call | flops 1000 | bytes 1000 | tf_op jit(solution)/shard_map/weight_pass/pallas_call | solution.py:483
  395.6 14.9 %back_pass.5 = (f32[512,2048]{1,0:T(8,128)}, bf16[512,2048]{1,0:T(8,128)(2,1)}) custom-call(bf16[1024,1152]{1,0:T(8,128)(2,1)S(1)} %copy-done.6, bf16[1024,1152]{1,0:T(8,128)(2,1)} %get-tuple-element.234.refs_1_.refs_4_, bf16[2048,1152]{1,0:T(8,128)(2,1)} %bitcast.286, bf16[2048,1152]{1,0:T(8,128)(2,1)} %bitcast.290), custom_call_target="tpu_custom_call" | custom-call | flops 1000 | bytes 1000 | tf_op jit(solution)/shard_map/back_pass/pallas_call | solution.py:449
  410.5 16.2 %weight_pass.5 = bf16[2048,1152]{1,0:T(8,128)(2,1)} custom-call(bf16[512,2048]{1,0:T(8,128)(2,1)S(1)} %multiply_convert_fusion.n0_ref.refs_0_, bf16[512,2048]{1,0:T(8,128)(2,1)} %collective-permute-done.18.n1_ref.refs_1_, bf16[512,2048]{1,0:T(8,128)(2,1)} %collective-permute-done.19.n0_ref.refs_2_, bf16[512,2048]{1,0:T(8,128)(2,1)} %collective-permute-done.21.n1_ref.refs_3_, ...), custom_call_target="tpu_custom_call" | custom-call | flops 1000 | bytes 1000 | tf_op jit(solution)/shard_map/weight_pass/pallas_call | solution.py:483
  447.5 11.4 %attend_backward.2 = (bf16[512,512]{1,0:T(8,128)(2,1)S(1)}, bf16[2048,256]{1,0:T(8,128)(2,1)S(1)}) custom-call(s32[1]{0:T(128)} %bitcast.34.place_ref, bf16[512,1280]{1,0:T(8,128)(2,1)S(1)} %get-tuple-element.189.q_ref, bf16[2048,640]{1,0:T(8,128)(2,1)} %all-gather.14.cloned.1.call-done.k_ref.v_ref, ...), custom_call_target="tpu_custom_call" | custom-call | flops 1000 | bytes 1000 | tf_op jit(solution)/shard_map/attend_backward/pallas_call | solution.py:331
  460.7 26.9 %collective-permute-done.27 = bf16[2,2,4,64,1152]{4,3,1,0,2:T(8,128)(2,1)} collective-permute-done((bf16[2,2,4,64,1152]{4,3,1,0,2:T(8,128)(2,1)S(1)}, bf16[2,2,4,64,1152]{4,3,1,0,2:T(8,128)(2,1)}, u32[]{:S(2)}, u32[]{:S(2)}) %collective-permute-start.27) | collective-permute-done | bytes 2359328 | tf_op jit(solution)/shard_map/ppermute | solution.py:586
  518.4 16.9 %attend_backward.3 = (bf16[512,768]{1,0:T(8,128)(2,1)S(1)}, bf16[2048,384]{1,0:T(8,128)(2,1)}) custom-call(s32[1]{0:T(128)} %bitcast.34.place_ref, bf16[512,1280]{1,0:T(8,128)(2,1)S(1)} %get-tuple-element.189.q_ref, bf16[2048,640]{1,0:T(8,128)(2,1)} %all-gather.14.cloned.1.call-done.k_ref.v_ref, bf16[2048,640]{1,0:T(8,128)(2,1)} %all-gather.14.cloned.1.call-done.k_ref.v_ref, ...), custom_call_target="tpu_custom_call" | custom-call | flops 1000 | bytes 1000 | tf_op jit(solution)/shard_map/attend_backward/pallas_call | solution.py:331
  535.3 22.8 %collective-permute-done.30 = bf16[2,2,4,64,1152]{4,3,1,0,2:T(8,128)(2,1)} collective-permute-done((bf16[2,2,4,64,1152]{4,3,1,0,2:T(8,128)(2,1)S(1)}, bf16[2,2,4,64,1152]{4,3,1,0,2:T(8,128)(2,1)}, u32[]{:S(2)}, u32[]{:S(2)}) %collective-permute-start.30) | collective-permute-done | bytes 2359328 | tf_op jit(solution)/shard_map/ppermute | solution.py:586
  568.5 8.4 %back_pass.7 = (f32[512,2048]{1,0:T(8,128)}, bf16[512,2048]{1,0:T(8,128)(2,1)}) custom-call(bf16[1024,1152]{1,0:T(8,128)(2,1)S(1)} %copy-done.3, bf16[1152,2048]{1,0:T(8,128)(2,1)} %bitcast.294), custom_call_target="tpu_custom_call" | custom-call | flops 1000 | bytes 1000 | tf_op jit(solution)/shard_map/back_pass/pallas_call | solution.py:449
  578.0 8.9 %heads_backward.2 = (bf16[512,1280]{1,0:T(8,128)(2,1)}, f32[8,1280]{1,0:T(8,128)}) custom-call(bf16[512,1280]{1,0:T(8,128)(2,1)} %pad_maximum_fusion.3.grad_ref, f32[512,1280]{1,0:T(8,128)} %get-tuple-element.259.joint_ref, f32[8,1280]{1,0:T(8,128)} %copy-done.39, f32[512,128]{1,0:T(8,128)} %copy-done.10, f32[512,128]{1,0:T(8,128)} %copy-done.12), custom_call_target="tpu_custom_call" | custom-call | flops 1000 | bytes 1000 | tf_op jit(solution)/shard_map/heads_backward/pallas_call | solution.py:126
  643.8 20.6 %collective-permute-done.37 = bf16[2,4,64,1280]{3,2,1,0:T(8,128)(2,1)} collective-permute-done((bf16[2,4,64,1280]{3,2,1,0:T(8,128)(2,1)}, bf16[2,4,64,1280]{3,2,1,0:T(8,128)(2,1)}, u32[]{:S(2)}, u32[]{:S(2)}) %collective-permute-start.37) | collective-permute-done | bytes 1310752 | tf_op jit(solution)/shard_map/ppermute | solution.py:586
  683.6 10.7 %collective-permute-done.39 = bf16[2,4,64,384]{3,2,1,0:T(8,128)(2,1)S(1)} collective-permute-done((bf16[2,4,64,384]{3,2,1,0:T(8,128)(2,1)S(1)}, bf16[2,4,64,384]{3,2,1,0:T(8,128)(2,1)S(1)}, u32[]{:S(2)}, u32[]{:S(2)}) %collective-permute-start.39) | collective-permute-done | bytes 393248 | tf_op jit(solution)/shard_map/ppermute | solution.py:586
  (462 shorter events, 340.8 us)
Async XLA Ops:
  9.8 130.6 %all-gather.16.cloned.1.call-start = ((), (), s32[]{:S(2)}) async-start(), calls=%async_computation.14 | async-start | bytes 2949120 | tf_op jit(solution)/shard_map/all_gather | solution.py:683
  53.1 117.5 %all-gather.14.cloned.1.call-start = ((), (), s32[]{:S(2)}) async-start(), calls=%async_computation.13 | async-start | bytes 3276800 | tf_op jit(solution)/shard_map/all_gather | solution.py:683
  53.6 48.4 %collective-permute-start.10 = (bf16[144,2048]{1,0:T(8,128)(2,1)}, bf16[144,2048]{1,0:T(8,128)(2,1)}, u32[]{:S(2)}, u32[]{:S(2)}) collective-permute-start(bf16[144,2048]{1,0:T(8,128)(2,1)} %param.20), channel_id=1, source_target_pairs={{0,16},{4,20},{8,24},{12,28},{16,0},{20,4},{24,8},{28,12},{1,17},{... | collective-permute-start | bytes 1769480 | tf_op jit(solution)/shard_map/ppermute | solution.py:586
  105.3 105.8 %all-gather.18.cloned.1.call-start = ((), (), s32[]{:S(2)}) async-start(), calls=%async_computation.15 | async-start | bytes 2949120 | tf_op jit(solution)/shard_map/all_gather | solution.py:683
  143.4 172.3 %all-gather.20.cloned.1.call-start = ((), (), s32[]{:S(2)}) async-start(), calls=%async_computation.16 | async-start | bytes 5898240 | tf_op jit(solution)/shard_map/all_gather | solution.py:683
  166.2 48.4 %collective-permute-start.16 = (bf16[2,2,4,64,1280]{4,3,2,1,0:T(8,128)(2,1)}, bf16[2,2,4,64,1280]{4,3,2,1,0:T(8,128)(2,1)}, u32[]{:S(2)}, u32[]{:S(2)}) collective-permute-start(bf16[2,2,4,64,1280]{4,3,2,1,0:T(8,128)(2,1)} %bitcast.64), channel_id=1, source_target_pairs={{0,4},{4,0},{8,12},{12,8},{16,20},{20,16},{24,28},{28,24},{1,5},{5... | collective-permute-start | bytes 7864328 | tf_op jit(solution)/shard_map/ppermute | solution.py:586
  166.7 47.9 %collective-permute-start.15 = (bf16[512,2048]{1,0:T(8,128)(2,1)}, bf16[512,2048]{1,0:T(8,128)(2,1)}, u32[]{:S(2)}, u32[]{:S(2)}) collective-permute-start(bf16[512,2048]{1,0:T(8,128)(2,1)} %bitcast_convert_fusion.refs_2_.g0_ref), channel_id=1, source_target_pairs={{0,8},{4,12},{8,0},{12,4},{16,24},{20,28},{24,16},{28,20},{1,9},{5... | collective-permute-start | bytes 6291464 | tf_op jit(solution)/shard_map/ppermute | solution.py:586
  168.2 46.4 %collective-permute-start.14 = (bf16[512,2048]{1,0:T(8,128)(2,1)}, bf16[512,2048]{1,0:T(8,128)(2,1)S(1)}, u32[]{:S(2)}, u32[]{:S(2)}) collective-permute-start(bf16[512,2048]{1,0:T(8,128)(2,1)} %bitcast_convert_fusion.refs_2_.g0_ref), channel_id=1, source_target_pairs={{0,4},{4,0},{8,12},{12,8},{16,20},{20,16},{24,28},{28,24},{1,5},{5... | collective-permute-start | bytes 6291464 | tf_op jit(solution)/shard_map/ppermute | solution.py:586
  170.6 316.9 %reduce-scatter.7.cloned.1.call-start = ((), (), s32[]{:S(2)}) async-start(), calls=%async_computation.6 | async-start | bytes 2949120 | tf_op jit(solution)/shard_map/reduce_scatter | solution.py:687
  170.9 58.7 %collective-permute-start.17 = (bf16[4,2,2,64,1152]{4,3,2,1,0:T(8,128)(2,1)}, bf16[4,2,2,64,1152]{4,3,2,1,0:T(8,128)(2,1)}, u32[]{:S(2)}, u32[]{:S(2)}) collective-permute-start(bf16[4,2,2,64,1152]{4,3,2,1,0:T(8,128)(2,1)} %bitcast.320), channel_id=1, source_target_pairs={{0,16},{4,20},{8,24},{12,28},{16,0},{20,4},{24,8},{28,12},{1,17},{... | collective-permute-start | bytes 7077896 | tf_op jit(solution)/shard_map/ppermute | solution.py:586
  214.6 61.6 %collective-permute-start.20 = (bf16[4,2,2,64,1152]{4,3,2,1,0:T(8,128)(2,1)}, bf16[4,2,2,64,1152]{4,3,2,1,0:T(8,128)(2,1)}, u32[]{:S(2)}, u32[]{:S(2)}) collective-permute-start(bf16[4,2,2,64,1152]{4,3,2,1,0:T(8,128)(2,1)} %bitcast.322), channel_id=1, source_target_pairs={{0,16},{4,20},{8,24},{12,28},{16,0},{20,4},{24,8},{28,12},{1,17},{... | collective-permute-start | bytes 7077896 | tf_op jit(solution)/shard_map/ppermute | solution.py:586
  229.6 46.7 %collective-permute-start.19 = (bf16[512,2048]{1,0:T(8,128)(2,1)S(1)}, bf16[512,2048]{1,0:T(8,128)(2,1)}, u32[]{:S(2)}, u32[]{:S(2)}) collective-permute-start(bf16[512,2048]{1,0:T(8,128)(2,1)S(1)} %multiply_convert_fusion.n0_ref.refs_0_), channel_id=1, source_target_pairs={{0,8},{4,12},{8,0},{12,4},{16,24},{20,28},{24,16},{28,20},{1,9},{5... | collective-permute-start | bytes 6291464 | tf_op jit(solution)/shard_map/ppermute | solution.py:586
  231.1 68.2 %collective-permute-start.22 = (bf16[512,2048]{1,0:T(8,128)(2,1)}, bf16[512,2048]{1,0:T(8,128)(2,1)}, u32[]{:S(2)}, u32[]{:S(2)}) collective-permute-start(bf16[512,2048]{1,0:T(8,128)(2,1)} %collective-permute-done.15.g0_ref.refs_4_), channel_id=1, source_target_pairs={{0,4},{4,0},{8,12},{12,8},{16,20},{20,16},{24,28},{28,24},{1,5},{5... | collective-permute-start | bytes 6291464 | tf_op jit(solution)/shard_map/ppermute | solution.py:586
  362.3 48.1 %collective-permute-start.24 = (bf16[512,2048]{1,0:T(8,128)(2,1)}, bf16[512,2048]{1,0:T(8,128)(2,1)}, u32[]{:S(2)}, u32[]{:S(2)}) collective-permute-start(bf16[512,2048]{1,0:T(8,128)(2,1)} %add_convert_fusion.2), channel_id=1, source_target_pairs={{0,8},{4,12},{8,0},{12,4},{16,24},{20,28},{24,16},{28,20},{1,9},{5... | collective-permute-start | bytes 6291464 | tf_op jit(solution)/shard_map/ppermute | solution.py:586
  367.3 59.4 %collective-permute-start.26 = (bf16[4,144,2048]{2,1,0:T(8,128)(2,1)}, bf16[4,144,2048]{2,1,0:T(8,128)(2,1)}, u32[]{:S(2)}, u32[]{:S(2)}) collective-permute-start(bf16[4,144,2048]{2,1,0:T(8,128)(2,1)} %dynamic-slice_bitcast_fusion.1), channel_id=1, source_target_pairs={{0,16},{4,20},{8,24},{12,28},{16,0},{20,4},{24,8},{28,12},{1,17},{... | collective-permute-start | bytes 7077896 | tf_op jit(solution)/shard_map/ppermute | solution.py:586
  431.6 126.5 %reduce-scatter.9.cloned.1.call-start = ((), (), s32[]{:S(2)}) async-start(), calls=%async_computation.7 | async-start | bytes 1310720 | tf_op jit(solution)/shard_map/reduce_scatter | solution.py:687
  433.8 53.8 %collective-permute-start.27 = (bf16[2,2,4,64,1152]{4,3,1,0,2:T(8,128)(2,1)S(1)}, bf16[2,2,4,64,1152]{4,3,1,0,2:T(8,128)(2,1)}, u32[]{:S(2)}, u32[]{:S(2)}) collective-permute-start(bf16[2,2,4,64,1152]{4,3,1,0,2:T(8,128)(2,1)S(1)} %copy_bitcast_fusion.2), channel_id=1, source_target_pairs={{0,16},{4,20},{8,24},{12,28},{16,0},{20,4},{24,8},{28,12},{1,17},{... | collective-permute-start | bytes 7077896 | tf_op jit(solution)/shard_map/ppermute | solution.py:586
  487.6 78.3 %reduce-scatter.11.cloned.1.call-start = ((), (), s32[]{:S(2)}) async-start(), calls=%async_computation.8 | async-start | bytes 2949120 | tf_op jit(solution)/shard_map/reduce_scatter | solution.py:687
  502.1 101.3 %reduce-scatter.13.cloned.1.call-start = ((), (), s32[]{:S(2)}) async-start(), calls=%async_computation.9 | async-start | bytes 1966080 | tf_op jit(solution)/shard_map/reduce_scatter | solution.py:687
  504.4 53.8 %collective-permute-start.30 = (bf16[2,2,4,64,1152]{4,3,1,0,2:T(8,128)(2,1)S(1)}, bf16[2,2,4,64,1152]{4,3,1,0,2:T(8,128)(2,1)}, u32[]{:S(2)}, u32[]{:S(2)}) collective-permute-start(bf16[2,2,4,64,1152]{4,3,1,0,2:T(8,128)(2,1)S(1)} %copy_bitcast_fusion.1), channel_id=1, source_target_pairs={{0,16},{4,20},{8,24},{12,28},{16,0},{20,4},{24,8},{28,12},{1,17},{... | collective-permute-start | bytes 7077896 | tf_op jit(solution)/shard_map/ppermute | solution.py:586
  512.9 53.0 %collective-permute-start.29 = (bf16[2,2,4,64,1280]{4,3,2,1,0:T(8,128)(2,1)}, bf16[2,2,4,64,1280]{4,3,2,1,0:T(8,128)(2,1)}, u32[]{:S(2)}, u32[]{:S(2)}) collective-permute-start(bf16[2,2,4,64,1280]{4,3,2,1,0:T(8,128)(2,1)} %dynamic-slice_bitcast_fusion), channel_id=1, source_target_pairs={{0,4},{4,0},{8,12},{12,8},{16,20},{20,16},{24,28},{28,24},{1,5},{5... | collective-permute-start | bytes 7864328 | tf_op jit(solution)/shard_map/ppermute | solution.py:586
  517.8 48.1 %collective-permute-start.31 = (bf16[512,2048]{1,0:T(8,128)(2,1)}, bf16[512,2048]{1,0:T(8,128)(2,1)}, u32[]{:S(2)}, u32[]{:S(2)}) collective-permute-start(bf16[512,2048]{1,0:T(8,128)(2,1)} %add_convert_fusion.1), channel_id=1, source_target_pairs={{0,8},{4,12},{8,0},{12,4},{16,24},{20,28},{24,16},{28,20},{1,9},{5... | collective-permute-start | bytes 6291464 | tf_op jit(solution)/shard_map/ppermute | solution.py:586
  568.5 129.6 %reduce-scatter.15.cloned.1.call-start = ((), (), s32[]{:S(2)}) async-start(), calls=%async_computation.10 | async-start | bytes 2949120 | tf_op jit(solution)/shard_map/reduce_scatter | solution.py:687
  608.8 136.7 %reduce-scatter.17.cloned.1.call-start = ((), (), s32[]{:S(2)}) async-start(), calls=%async_computation.11 | async-start | bytes 2129920 | tf_op jit(solution)/shard_map/reduce_scatter | solution.py:687
  (128 other events, 1090.5 us)
Sparse Core Ops, SparseCore 0:
  10.2 41.6 all-gather.11
  53.4 49.5 all-gather.15
  105.5 54.9 all-gather.13
  161.9 49.2 all-gather.17
  213.2 88.2 all-gather.19
  431.8 47.7 reduce-scatter.6
  487.7 26.7 reduce-scatter.8
  516.9 46.6 reduce-scatter.10
  568.6 34.7 reduce-scatter.12
  608.9 47.0 reduce-scatter.14
  710.6 34.9 reduce-scatter.16

commit v6 on v5

--- a/solution.py
+++ b/solution.py
@@ -852,14 +852,13 @@
     )
     queries, q_right, right_other, down_other = stage(queries, q_right, right_other, down_other)
     q_right = join_outer(q_right, right_other, 0)
-    down_pair = join_outer(w_down, down_other, 0)
     place_array = place.reshape(1)
-    keys_values, queries, down_in = stage(keys_values, queries, down_pair)
-    down_lines = gather_seq(down_in)
+    keys_values, queries = stage(keys_values, queries)
     mixed, logs = attend_forward(place_array, queries, keys_values)
-    mixed, grad_top1, grad_top2, up_lines, wout_other = stage(
-        mixed, swap(grad_top, 1), swap(grad_top, 2), up_lines, swap(q_right, 1)
-    )
+    mixed, grad_top1, grad_top2, up_lines, wout_other, down_other = stage(
+        mixed, swap(grad_top, 1), swap(grad_top, 2), up_lines, swap(q_right, 1), down_other
+    )
+    down_lines = gather_seq(join_outer(w_down, down_other, 0))
     wout_t = joined(q_right, wout_other, core, 2).reshape(width, -1)
     middle = inputs + mm_t(mixed, wout_t)
 
@@ -911,18 +910,20 @@
     grad_mixed = mm(grad_branch, wout_t).astype(bf16)
     attend = (place_array, queries, keys_values, mixed, logs)
     grad_q1, grad_kv1 = attend_backward(0, 2, *attend, grad_mixed)
-    grad_q1, grad_kv1, gate_other, grad_mixed, grad_wdown, hidden_far = stage(
-        grad_q1, grad_kv1, pass_outer(grad_wgate, 0), grad_mixed, grad_wdown, hidden_far
+    gate_other = pass_outer(grad_wgate, 0)
+    grad_q1, grad_kv1, grad_mixed, grad_wdown, hidden_far = stage(
+        grad_q1, grad_kv1, grad_mixed, grad_wdown, hidden_far
     )
     grad_kv1 = reduce_seq(grad_kv1.reshape(seq_devices, shard_length, -1))
-    grad_gate = reduce_seq(jnp.moveaxis(add_outer(grad_wgate, gate_other, 0), 2, 0))
     shape = (outer, 2, 2, seq_devices, d_rows)
     own_far, send_far = back_pass((hidden_far,), (wdown,), False)
-    grad_wout, far_other, grad_mixed = stage(
+    grad_wout, far_other, gate_other, grad_mixed = stage(
         t_mm(grad_branch, mixed).astype(bf16).reshape(*shape, QUERY_COLUMNS),
         swap(send_far, 1),
+        gate_other,
         grad_mixed,
     )
+    grad_gate = reduce_seq(jnp.moveaxis(add_outer(grad_wgate, gate_other, 0), 2, 0))
     across = (own_far + far_other.astype(f32)).astype(bf16)
     across, grad_mixed = stage(across, grad_mixed)
     grad_q2, grad_kv2 = attend_backward(2, 3, *attend, grad_mixed)
@@ -962,11 +963,10 @@
     wq_other, near_other, joint_grad_kv = stage(
         pass_bit(grad_wq, 1, 2), swap(send_near, 1), joint_grad_kv
     )
-    grad_wkv, grad_wq, grad_wout = stage(
-        t_mm(normed, joint_grad_kv).astype(bf16), add_bit(grad_wq, wq_other, 1, 2), grad_wout
-    )
+    grad_wq = add_bit(grad_wq, wq_other, 1, 2)
     wq_other, wout_other = pass_bit(grad_wq, 2, 1), pass_outer(grad_wout, 0)
     output = (middle + own_near + near_other.astype(f32) + across.astype(f32)).astype(bf16)
+    grad_wkv = t_mm(normed, joint_grad_kv).astype(bf16)
     grad_normed = mm_t(joint_grad_q, wq) + mm_t(joint_grad_kv, wkv)
     grad_input_part, grad_attn_gain = norm_backward(
         inputs, in_scale, attn_gain_full, grad_normed
@@ -975,6 +975,12 @@
 
     gain_rows = jnp.stack([grad_attn_gain, grad_ffn_gain]).astype(bf16)
     gain_columns = t_mm(gain_rows, jnp.eye(2, LANES, dtype=bf16)).astype(bf16)
+    grad_wkv, gain_columns, wq_other, wout_other = stage(
+        grad_wkv, gain_columns, wq_other, wout_other
+    )
+    grad_wq = add_bit(grad_wq, wq_other, 2, 1)
+    grad_wout = add_outer(grad_wout, wout_other, 0)
+    wq_other, wout_other = pass_outer(grad_wq, 0), pass_bit(grad_wout, 2, 0)
     left = grad_wkv[:, : 3 * LANES].reshape(*shape, -1)
     right = jnp.concatenate([grad_wkv[:, 3 * LANES :], gain_columns], axis=1)
     right = right.reshape(*shape, -1)
@@ -984,25 +990,21 @@
             jnp.sum(gain_k[0, :KEY_COLUMNS].reshape(-1, HEAD_SIZE), axis=0),
         ]
     )[None]
-    left, right, left_other, right_other, wq_other, wout_other, gains_other = stage(
+    left, right, left_other, right_other, gains_other = stage(
         left,
         right,
         pass_bit(left, 1, 2),
         pass_bit(right, 1, 2),
-        wq_other,
-        wout_other,
         exchange(head_gains, "rows", 1),
     )
     head_gains = head_gains + gains_other
     left = add_bit(left, left_other, 1, 2)
     right = add_bit(right, right_other, 1, 2)
-    grad_wq = add_bit(grad_wq, wq_other, 2, 1)
-    grad_wout = add_outer(grad_wout, wout_other, 0)
     left_other, right_other, wq_other, wout_other, gains_other, grad_up = stage(
         pass_bit(left, 2, 1),
         pass_outer(right, 0),
-        pass_outer(grad_wq, 0),
-        pass_bit(grad_wout, 2, 0),
+        wq_other,
+        wout_other,
         exchange(head_gains, "seq", 1),
         grad_up,
     )

time: 767 us -> 808 us (1.053)
  waiting for transfers between devices: 232 us -> 267 us
  matrix products: 28.7 us -> 38.7 us
    reduce_scatter x6, waiting for transfers between devices: 6.41 us -> 29.4 us  [reduce_seq(): return lax.psum_scatter(values, 'seq', scatter_dimension=0, tiled=False)]
    ppermute x46, waiting for transfers between devices: 190 us -> 202 us  [swap(): return lax.ppermute(values, 'rows', pairs)]
    unnamed x179 -> x153, local copies, waits for them, and re-layouts: 29.9 us -> 26.8 us
  transfers between devices with their start and end apart: 62 -> 62, of which waited for: 27 -> 29; matrix products, arithmetic and copies ran while one was open for 17% -> 18% of each run, Pallas kernels for 30% -> 28%
where the time goes in v6:
time: 808 us; the launch traced here: 799 us
  waiting for transfers between devices  267 us (33%)
  Pallas kernels  254 us (31%)
  other arithmetic  78.6 us (10%)
  local copies, waits for them, and re-layouts  78.5 us (10%)
  starting transfers between devices  43.7 us (5%)
  matrix products  38.7 us (5%)
  blocking collectives  19.9 us (2%)
  between operations  18.3 us (2%)
    ppermute x46, waiting for transfers between devices, swap(): return lax.ppermute(values, 'rows', pairs)  202 us
    pallas_call x3, Pallas kernels, weight_pass(): pl.pallas_call(partial(weight_kernel, len(lefts)), grid=(rows // tile,),...  47.1 us
    pallas_call x4, Pallas kernels, back_pass(): pl.pallas_call(partial(back_kernel, count, transposed), grid=(width // ti...  46.3 us
    ppermute x46, starting transfers between devices, swap(): return lax.ppermute(values, 'rows', pairs)  39.3 us
    all_gather x5, waiting for transfers between devices, gather_seq(): return lax.all_gather(values, 'seq', axis=0, tiled=False)  32.4 us
    pallas_call x2, Pallas kernels, hidden_pass(): pl.pallas_call(hidden_kernel, grid=(pl.cdiv(columns, tile),), in_specs=[w...  32 us
    reduce_scatter x6, waiting for transfers between devices, reduce_seq(): return lax.psum_scatter(values, 'seq', scatter_dimension=0, tiled=False)  29.4 us
    pallas_call x2, Pallas kernels, attend_backward(): pl.pallas_call(partial(attend_backward_kernel, first, count), grid_spec=p...  27.9 us
  transfers between devices with their start and end apart: 62, of which 29 were waited for; matrix products, arithmetic and copies ran while one was open for 18% of the time, Pallas kernels for 28%

profile of v6, /device:TPU:0, one launch (start us, length us, event | category | flops | bytes accessed | tf_op | source)
XLA Modules:
  0.0 798.7 jit_solution(490573936162864482)
XLA Ops:
  28.3 19.9 %all-gather = bf16[256,768]{1,0:T(8,128)(2,1)S(1)} all-gather(bf16[64,768]{1,0:T(8,128)(2,1)S(1)} %fusion.35), channel_id=2, replica_groups=mesh['rows'=8,'seq'=4] {'seq'}, dimensions={0}, use_global_device_ids=true | all-gather | bytes 491520 | tf_op jit(solution)/shard_map/all_gather | solution.py:683
  61.1 11.4 %collective-permute-done.2 = bf16[4,64,384]{2,1,0:T(8,128)(2,1)S(1)} collective-permute-done((bf16[4,64,384]{2,1,0:T(8,128)(2,1)S(1)}, bf16[4,64,384]{2,1,0:T(8,128)(2,1)S(1)}, u32[]{:S(2)}, u32[]{:S(2)}) %collective-permute-start.2) | collective-permute-done | bytes 196640 | tf_op jit(solution)/shard_map/ppermute | solution.py:586
  111.5 25.2 %collective-permute-done.12 = bf16[2,4,64,1280]{3,2,1,0:T(8,128)(2,1)S(1)} collective-permute-done((bf16[2,4,64,1280]{3,2,1,0:T(8,128)(2,1)S(1)}, bf16[2,4,64,1280]{3,2,1,0:T(8,128)(2,1)S(1)}, u32[]{:S(2)}, u32[]{:S(2)}) %collective-permute-start.12) | collective-permute-done | bytes 1310752 | tf_op jit(solution)/shard_map/ppermute | solution.py:586
  156.2 8.4 %heads_forward.3 = (f32[512,1280]{1,0:T(8,128)}, bf16[512,1280]{1,0:T(8,128)(2,1)S(1)}) custom-call(bf16[512,2048]{1,0:T(8,128)(2,1)S(1)} %fusion.7.normed_ref, bf16[2048,1280]{1,0:T(8,128)(2,1)} %bitcast.293, f32[8,1280]{1,0:T(8,128)S(1)} %broadcast_in_dim.14.gain_ref, f32[512,128]{1,0:T(8,128)S(1)} %copy-done.11, f32[512,128]{1,0:T(8,128)S(1)} %copy-done.13), custom_call_target="tpu_custom_call" | custom-call | flops 1000 | bytes 1000 | tf_op jit(solution)/shard_map/heads_forward/pallas_call | solution.py:85
  168.2 11.7 %attend_forward.1 = (bf16[512,1280]{1,0:T(8,128)(2,1)S(1)}, f32[512,1280]{1,0:T(8,128)S(1)}) custom-call(s32[1]{0:T(128)} %bitcast.place_ref, bf16[512,1280]{1,0:T(8,128)(2,1)S(1)} %get-tuple-element.187.q_ref, bf16[2048,640]{1,0:T(8,128)(2,1)} %all-gather.15.cloned.1.call-done.k_ref.v_ref, bf16[2048,640]{1,0:T(8,128)(2,1)} %all-gather.15.cloned.1.call-done.k_ref.v_ref), custom_call_target="tpu_custom_call" | custom-call | flops 1000 | bytes 1000 | tf_op jit(solution)/shard_map/attend_forward/pallas_call | solution.py:194
  182.5 28.7 %all-gather.19.cloned.1.call-done = bf16[8,2,64,1152]{3,2,1,0:T(8,128)(2,1)} async-done(((bf16[2,2,64,1152]{3,2,1,0:T(8,128)(2,1)}), bf16[8,2,64,1152]{3,2,1,0:T(8,128)(2,1)}) %all-gather.19.cloned.1.call-update) | async-done | bytes 2359312 | tf_op jit(solution)/shard_map/all_gather | solution.py:683
  233.6 38.7 %collective-permute-done.17 = bf16[4,2,2,64,1152]{4,3,2,1,0:T(8,128)(2,1)S(1)} collective-permute-done((bf16[4,2,2,64,1152]{4,3,2,1,0:T(8,128)(2,1)}, bf16[4,2,2,64,1152]{4,3,2,1,0:T(8,128)(2,1)S(1)}, u32[]{:S(2)}, u32[]{:S(2)}) %collective-permute-start.17) | collective-permute-done | bytes 2359328 | tf_op jit(solution)/shard_map/ppermute | solution.py:586
  283.2 34.7 %collective-permute-done.19.n0_ref.refs_2_ = bf16[512,2048]{1,0:T(8,128)(2,1)} collective-permute-done((bf16[512,2048]{1,0:T(8,128)(2,1)S(1)}, bf16[512,2048]{1,0:T(8,128)(2,1)}, u32[]{:S(2)}, u32[]{:S(2)}) %collective-permute-start.19) | collective-permute-done | bytes 2097184 | tf_op jit(solution)/shard_map/ppermute | solution.py:586
  328.6 15.6 %hidden_pass.2 = (bf16[1024,1152]{1,0:T(8,128)(2,1)}, bf16[1024,1152]{1,0:T(8,128)(2,1)}, bf16[1024,1152]{1,0:T(8,128)(2,1)}) custom-call(bf16[512,2048]{1,0:T(8,128)(2,1)S(1)} %multiply_convert_fusion.n0_ref.refs_0_, bf16[512,2048]{1,0:T(8,128)(2,1)} %collective-permute-done.18.n1_ref.refs_1_, bf16[2048,1152]{1,0:T(8,128)(2,1)} %bitcast.281, ...), custom_call_target="tpu_custom_call" | custom-call | flops 1000 | bytes 1000 | tf_op jit(solution)/shard_map/hidden_pass/pallas_call | solution.py:375
  344.2 16.3 %hidden_pass.3 = (bf16[1024,1152]{1,0:T(8,128)(2,1)}, bf16[1024,1152]{1,0:T(8,128)(2,1)}, bf16[1024,1152]{1,0:T(8,128)(2,1)}) custom-call(bf16[512,2048]{1,0:T(8,128)(2,1)} %collective-permute-done.19.n0_ref.refs_2_, bf16[512,2048]{1,0:T(8,128)(2,1)} %collective-permute-done.21.n1_ref.refs_3_, bf16[2048,1152]{1,0:T(8,128)(2,1)} %bitcast.282, ...), custom_call_target="tpu_custom_call" | custom-call | flops 1000 | bytes 1000 | tf_op jit(solution)/shard_map/hidden_pass/pallas_call | solution.py:375
  360.5 12.3 %gates_pass.2 = (bf16[1024,1152]{1,0:T(8,128)(2,1)}, bf16[1024,1152]{1,0:T(8,128)(2,1)}) custom-call(bf16[512,2048]{1,0:T(8,128)(2,1)} %collective-permute-done.15.g0_ref.refs_4_, bf16[512,2048]{1,0:T(8,128)(2,1)} %collective-permute-done.22.g1_ref.refs_5_, bf16[1152,2048]{1,0:T(8,128)(2,1)} %bitcast.289, bf16[1024,1152]{1,0:T(8,128)(2,1)} %get-tuple-element.211.gate_ref, ...), custom_call_target="tpu_custom_call" | custom-call | flops 1000 | bytes 1000 | tf_op jit(solution)/shard_map/gates_pass/pallas_call | solution.py:410
  374.5 14.9 %back_pass.4 = (f32[512,2048]{1,0:T(8,128)}, bf16[512,2048]{1,0:T(8,128)(2,1)S(1)}) custom-call(bf16[1024,1152]{1,0:T(8,128)(2,1)S(1)} %copy-done.5, bf16[1024,1152]{1,0:T(8,128)(2,1)} %get-tuple-element.214.refs_1_.refs_5_, bf16[2048,1152]{1,0:T(8,128)(2,1)} %bitcast.283, bf16[2048,1152]{1,0:T(8,128)(2,1)} %bitcast.287), custom_call_target="tpu_custom_call" | custom-call | flops 1000 | bytes 1000 | tf_op jit(solution)/shard_map/back_pass/pallas_call | solution.py:449
  389.9 15.3 %weight_pass.3 = bf16[1152,2048]{1,0:T(8,128)(2,1)} custom-call(bf16[1024,1152]{1,0:T(8,128)(2,1)} %get-tuple-element.261.refs_0_, bf16[1024,1152]{1,0:T(8,128)(2,1)} %get-tuple-element.240.refs_1_.refs_0_, bf16[512,2048]{1,0:T(8,128)(2,1)} %bitcast_convert_fusion.refs_2_.g0_ref, bf16[512,2048]{1,0:T(8,128)(2,1)S(1)} %copy-done.8, ...), custom_call_target="tpu_custom_call" | custom-call | flops 1000 | bytes 1000 | tf_op jit(solution)/shard_map/weight_pass/pallas_call | solution.py:483
  413.6 11.7 %gates_pass.3 = (bf16[1024,1152]{1,0:T(8,128)(2,1)}, bf16[1024,1152]{1,0:T(8,128)(2,1)}) custom-call(bf16[512,2048]{1,0:T(8,128)(2,1)} %bitcast_convert_fusion.refs_2_.g0_ref, bf16[512,2048]{1,0:T(8,128)(2,1)S(1)} %copy-done.9, bf16[1152,2048]{1,0:T(8,128)(2,1)} %bitcast.290, bf16[1024,1152]{1,0:T(8,128)(2,1)} %get-tuple-element.225.gate_ref, ...), custom_call_target="tpu_custom_call" | custom-call | flops 1000 | bytes 1000 | tf_op jit(solution)/shard_map/gates_pass/pallas_call | solution.py:410
  425.3 15.9 %weight_pass.4 = bf16[2048,1152]{1,0:T(8,128)(2,1)} custom-call(bf16[512,2048]{1,0:T(8,128)(2,1)S(1)} %multiply_convert_fusion.n0_ref.refs_0_, bf16[512,2048]{1,0:T(8,128)(2,1)} %collective-permute-done.18.n1_ref.refs_1_, bf16[512,2048]{1,0:T(8,128)(2,1)} %collective-permute-done.19.n0_ref.refs_2_, bf16[512,2048]{1,0:T(8,128)(2,1)} %collective-permute-done.21.n1_ref.refs_3_, ...), custom_call_target="tpu_custom_call" | custom-call | flops 1000 | bytes 1000 | tf_op jit(solution)/shard_map/weight_pass/pallas_call | solution.py:483
  441.2 14.9 %back_pass.5 = (f32[512,2048]{1,0:T(8,128)}, bf16[512,2048]{1,0:T(8,128)(2,1)}) custom-call(bf16[1024,1152]{1,0:T(8,128)(2,1)S(1)} %copy-done.6, bf16[1024,1152]{1,0:T(8,128)(2,1)} %get-tuple-element.233.refs_1_.refs_4_, bf16[2048,1152]{1,0:T(8,128)(2,1)} %bitcast.284, bf16[2048,1152]{1,0:T(8,128)(2,1)} %bitcast.288), custom_call_target="tpu_custom_call" | custom-call | flops 1000 | bytes 1000 | tf_op jit(solution)/shard_map/back_pass/pallas_call | solution.py:449
  456.2 15.8 %weight_pass.5 = bf16[2048,1152]{1,0:T(8,128)(2,1)} custom-call(bf16[512,2048]{1,0:T(8,128)(2,1)S(1)} %multiply_convert_fusion.n0_ref.refs_0_, bf16[512,2048]{1,0:T(8,128)(2,1)} %collective-permute-done.18.n1_ref.refs_1_, bf16[512,2048]{1,0:T(8,128)(2,1)} %collective-permute-done.19.n0_ref.refs_2_, bf16[512,2048]{1,0:T(8,128)(2,1)} %collective-permute-done.21.n1_ref.refs_3_, ...), custom_call_target="tpu_custom_call" | custom-call | flops 1000 | bytes 1000 | tf_op jit(solution)/shard_map/weight_pass/pallas_call | solution.py:483
  493.8 11.0 %attend_backward.2 = (bf16[512,512]{1,0:T(8,128)(2,1)S(1)}, bf16[2048,256]{1,0:T(8,128)(2,1)S(1)}) custom-call(s32[1]{0:T(128)} %bitcast.place_ref, bf16[512,1280]{1,0:T(8,128)(2,1)S(1)} %get-tuple-element.187.q_ref, bf16[2048,640]{1,0:T(8,128)(2,1)} %all-gather.15.cloned.1.call-done.k_ref.v_ref, ...), custom_call_target="tpu_custom_call" | custom-call | flops 1000 | bytes 1000 | tf_op jit(solution)/shard_map/attend_backward/pallas_call | solution.py:331
  507.6 17.1 %reduce-scatter.7.cloned.1.call-done = bf16[1,144,2048]{2,1,0:T(8,128)(2,1)} async-done(((bf16[4,144,2048]{2,1,0:T(8,128)(2,1)}), bf16[1,144,2048]{2,1,0:T(8,128)(2,1)}) %reduce-scatter.7.cloned.1.call-update) | async-done | bytes 589840 | tf_op jit(solution)/shard_map/reduce_scatter | solution.py:687
  559.2 16.9 %attend_backward.3 = (bf16[512,768]{1,0:T(8,128)(2,1)S(1)}, bf16[2048,384]{1,0:T(8,128)(2,1)}) custom-call(s32[1]{0:T(128)} %bitcast.place_ref, bf16[512,1280]{1,0:T(8,128)(2,1)S(1)} %get-tuple-element.187.q_ref, bf16[2048,640]{1,0:T(8,128)(2,1)} %all-gather.15.cloned.1.call-done.k_ref.v_ref, bf16[2048,640]{1,0:T(8,128)(2,1)} %all-gather.15.cloned.1.call-done.k_ref.v_ref, ...), custom_call_target="tpu_custom_call" | custom-call | flops 1000 | bytes 1000 | tf_op jit(solution)/shard_map/attend_backward/pallas_call | solution.py:331
  576.1 26.3 %collective-permute-done.30 = bf16[2,2,4,64,1152]{4,3,1,0,2:T(8,128)(2,1)} collective-permute-done((bf16[2,2,4,64,1152]{4,3,1,0,2:T(8,128)(2,1)S(1)}, bf16[2,2,4,64,1152]{4,3,1,0,2:T(8,128)(2,1)}, u32[]{:S(2)}, u32[]{:S(2)}) %collective-permute-start.30) | collective-permute-done | bytes 2359328 | tf_op jit(solution)/shard_map/ppermute | solution.py:586
  622.9 8.9 %heads_backward.2 = (bf16[512,1280]{1,0:T(8,128)(2,1)}, f32[8,1280]{1,0:T(8,128)}) custom-call(bf16[512,1280]{1,0:T(8,128)(2,1)} %pad_maximum_fusion.3.grad_ref, f32[512,1280]{1,0:T(8,128)} %get-tuple-element.258.joint_ref, f32[8,1280]{1,0:T(8,128)} %copy-done.38, f32[512,128]{1,0:T(8,128)} %copy-done.10, f32[512,128]{1,0:T(8,128)} %copy-done.12), custom_call_target="tpu_custom_call" | custom-call | flops 1000 | bytes 1000 | tf_op jit(solution)/shard_map/heads_backward/pallas_call | solution.py:126
  689.6 18.2 %collective-permute-done.34 = bf16[2,4,64,1280]{3,2,1,0:T(8,128)(2,1)} collective-permute-done((bf16[2,4,64,1280]{3,2,1,0:T(8,128)(2,1)}, bf16[2,4,64,1280]{3,2,1,0:T(8,128)(2,1)}, u32[]{:S(2)}, u32[]{:S(2)}) %collective-permute-start.34) | collective-permute-done | bytes 1310752 | tf_op jit(solution)/shard_map/ppermute | solution.py:586
  720.8 10.3 %collective-permute-done.42 = bf16[4,64,1280]{2,1,0:T(8,128)(2,1)} collective-permute-done((bf16[4,64,1280]{2,1,0:T(8,128)(2,1)S(1)}, bf16[4,64,1280]{2,1,0:T(8,128)(2,1)}, u32[]{:S(2)}, u32[]{:S(2)}) %collective-permute-start.42) | collective-permute-done | bytes 655392 | tf_op jit(solution)/shard_map/ppermute | solution.py:586
  (435 shorter events, 360.1 us)
Async XLA Ops:
  7.2 44.7 %all-gather.13.cloned.1.call-start = ((), (), s32[]{:S(2)}) async-start(), calls=%async_computation.13 | async-start | bytes 1638400 | tf_op jit(solution)/shard_map/all_gather | solution.py:683
  9.8 130.6 %all-gather.17.cloned.1.call-start = ((), (), s32[]{:S(2)}) async-start(), calls=%async_computation.15 | async-start | bytes 2949120 | tf_op jit(solution)/shard_map/all_gather | solution.py:683
  53.2 115.0 %all-gather.15.cloned.1.call-start = ((), (), s32[]{:S(2)}) async-start(), calls=%async_computation.14 | async-start | bytes 3276800 | tf_op jit(solution)/shard_map/all_gather | solution.py:683
  53.7 48.4 %collective-permute-start.10 = (bf16[144,2048]{1,0:T(8,128)(2,1)}, bf16[144,2048]{1,0:T(8,128)(2,1)}, u32[]{:S(2)}, u32[]{:S(2)}) collective-permute-start(bf16[144,2048]{1,0:T(8,128)(2,1)} %param.20), channel_id=1, source_target_pairs={{0,16},{4,20},{8,24},{12,28},{16,0},{20,4},{24,8},{28,12},{1,17},{... | collective-permute-start | bytes 1769480 | tf_op jit(solution)/shard_map/ppermute | solution.py:586
  105.4 105.8 %all-gather.19.cloned.1.call-start = ((), (), s32[]{:S(2)}) async-start(), calls=%async_computation.16 | async-start | bytes 2949120 | tf_op jit(solution)/shard_map/all_gather | solution.py:683
  143.6 216.9 %all-gather.11.cloned.1.call-start = ((), (), s32[]{:S(2)}) async-start(), calls=%async_computation.6 | async-start | bytes 5898240 | tf_op jit(solution)/shard_map/all_gather | solution.py:683
  166.2 48.4 %collective-permute-start.16 = (bf16[2,2,4,64,1280]{4,3,2,1,0:T(8,128)(2,1)}, bf16[2,2,4,64,1280]{4,3,2,1,0:T(8,128)(2,1)}, u32[]{:S(2)}, u32[]{:S(2)}) collective-permute-start(bf16[2,2,4,64,1280]{4,3,2,1,0:T(8,128)(2,1)} %bitcast.61), channel_id=1, source_target_pairs={{0,4},{4,0},{8,12},{12,8},{16,20},{20,16},{24,28},{28,24},{1,5},{5... | collective-permute-start | bytes 7864328 | tf_op jit(solution)/shard_map/ppermute | solution.py:586
  166.7 47.9 %collective-permute-start.15 = (bf16[512,2048]{1,0:T(8,128)(2,1)}, bf16[512,2048]{1,0:T(8,128)(2,1)}, u32[]{:S(2)}, u32[]{:S(2)}) collective-permute-start(bf16[512,2048]{1,0:T(8,128)(2,1)} %bitcast_convert_fusion.refs_2_.g0_ref), channel_id=1, source_target_pairs={{0,8},{4,12},{8,0},{12,4},{16,24},{20,28},{24,16},{28,20},{1,9},{5... | collective-permute-start | bytes 6291464 | tf_op jit(solution)/shard_map/ppermute | solution.py:586
  168.2 46.4 %collective-permute-start.14 = (bf16[512,2048]{1,0:T(8,128)(2,1)}, bf16[512,2048]{1,0:T(8,128)(2,1)S(1)}, u32[]{:S(2)}, u32[]{:S(2)}) collective-permute-start(bf16[512,2048]{1,0:T(8,128)(2,1)} %bitcast_convert_fusion.refs_2_.g0_ref), channel_id=1, source_target_pairs={{0,4},{4,0},{8,12},{12,8},{16,20},{20,16},{24,28},{28,24},{1,5},{5... | collective-permute-start | bytes 6291464 | tf_op jit(solution)/shard_map/ppermute | solution.py:586
  217.8 306.9 %reduce-scatter.7.cloned.1.call-start = ((), (), s32[]{:S(2)}) async-start(), calls=%async_computation.7 | async-start | bytes 2949120 | tf_op jit(solution)/shard_map/reduce_scatter | solution.py:687
  217.8 54.5 %collective-permute-start.17 = (bf16[4,2,2,64,1152]{4,3,2,1,0:T(8,128)(2,1)}, bf16[4,2,2,64,1152]{4,3,2,1,0:T(8,128)(2,1)S(1)}, u32[]{:S(2)}, u32[]{:S(2)}) collective-permute-start(bf16[4,2,2,64,1152]{4,3,2,1,0:T(8,128)(2,1)} %bitcast.318), channel_id=1, source_target_pairs={{0,16},{4,20},{8,24},{12,28},{16,0},{20,4},{24,8},{28,12},{1,17},{... | collective-permute-start | bytes 7077896 | tf_op jit(solution)/shard_map/ppermute | solution.py:586
  219.3 101.8 %collective-permute-start.20 = (bf16[4,2,2,64,1152]{4,3,2,1,0:T(8,128)(2,1)}, bf16[4,2,2,64,1152]{4,3,2,1,0:T(8,128)(2,1)}, u32[]{:S(2)}, u32[]{:S(2)}) collective-permute-start(bf16[4,2,2,64,1152]{4,3,2,1,0:T(8,128)(2,1)} %bitcast.320), channel_id=1, source_target_pairs={{0,16},{4,20},{8,24},{12,28},{16,0},{20,4},{24,8},{28,12},{1,17},{... | collective-permute-start | bytes 7077896 | tf_op jit(solution)/shard_map/ppermute | solution.py:586
  275.2 69.0 %collective-permute-start.22 = (bf16[512,2048]{1,0:T(8,128)(2,1)}, bf16[512,2048]{1,0:T(8,128)(2,1)}, u32[]{:S(2)}, u32[]{:S(2)}) collective-permute-start(bf16[512,2048]{1,0:T(8,128)(2,1)} %collective-permute-done.15.g0_ref.refs_4_), channel_id=1, source_target_pairs={{0,4},{4,0},{8,12},{12,8},{16,20},{20,16},{24,28},{28,24},{1,5},{5... | collective-permute-start | bytes 6291464 | tf_op jit(solution)/shard_map/ppermute | solution.py:586
  407.2 48.9 %collective-permute-start.24 = (bf16[512,2048]{1,0:T(8,128)(2,1)}, bf16[512,2048]{1,0:T(8,128)(2,1)}, u32[]{:S(2)}, u32[]{:S(2)}) collective-permute-start(bf16[512,2048]{1,0:T(8,128)(2,1)} %add_convert_fusion.2), channel_id=1, source_target_pairs={{0,8},{4,12},{8,0},{12,4},{16,24},{20,28},{24,16},{28,20},{1,9},{5... | collective-permute-start | bytes 6291464 | tf_op jit(solution)/shard_map/ppermute | solution.py:586
  412.3 59.8 %collective-permute-start.26 = (bf16[4,144,2048]{2,1,0:T(8,128)(2,1)}, bf16[4,144,2048]{2,1,0:T(8,128)(2,1)}, u32[]{:S(2)}, u32[]{:S(2)}) collective-permute-start(bf16[4,144,2048]{2,1,0:T(8,128)(2,1)} %dynamic-slice_bitcast_fusion.1), channel_id=1, source_target_pairs={{0,16},{4,20},{8,24},{12,28},{16,0},{20,4},{24,8},{28,12},{1,17},{... | collective-permute-start | bytes 7077896 | tf_op jit(solution)/shard_map/ppermute | solution.py:586
  476.9 125.5 %reduce-scatter.9.cloned.1.call-start = ((), (), s32[]{:S(2)}) async-start(), calls=%async_computation.8 | async-start | bytes 1310720 | tf_op jit(solution)/shard_map/reduce_scatter | solution.py:687
  480.4 61.6 %collective-permute-start.28 = (bf16[2,2,4,64,1152]{4,3,1,0,2:T(8,128)(2,1)}, bf16[2,2,4,64,1152]{4,3,1,0,2:T(8,128)(2,1)}, u32[]{:S(2)}, u32[]{:S(2)}) collective-permute-start(bf16[2,2,4,64,1152]{4,3,1,0,2:T(8,128)(2,1)} %copy_bitcast_fusion.2), channel_id=1, source_target_pairs={{0,16},{4,20},{8,24},{12,28},{16,0},{20,4},{24,8},{28,12},{1,17},{... | collective-permute-start | bytes 7077896 | tf_op jit(solution)/shard_map/ppermute | solution.py:586
  534.6 76.1 %reduce-scatter.11.cloned.1.call-start = ((), (), s32[]{:S(2)}) async-start(), calls=%async_computation.9 | async-start | bytes 2949120 | tf_op jit(solution)/shard_map/reduce_scatter | solution.py:687
  546.5 101.8 %reduce-scatter.13.cloned.1.call-start = ((), (), s32[]{:S(2)}) async-start(), calls=%async_computation.10 | async-start | bytes 1966080 | tf_op jit(solution)/shard_map/reduce_scatter | solution.py:687
  548.6 53.8 %collective-permute-start.30 = (bf16[2,2,4,64,1152]{4,3,1,0,2:T(8,128)(2,1)S(1)}, bf16[2,2,4,64,1152]{4,3,1,0,2:T(8,128)(2,1)}, u32[]{:S(2)}, u32[]{:S(2)}) collective-permute-start(bf16[2,2,4,64,1152]{4,3,1,0,2:T(8,128)(2,1)S(1)} %copy_bitcast_fusion.1), channel_id=1, source_target_pairs={{0,16},{4,20},{8,24},{12,28},{16,0},{20,4},{24,8},{28,12},{1,17},{... | collective-permute-start | bytes 7077896 | tf_op jit(solution)/shard_map/ppermute | solution.py:586
  553.7 52.1 %collective-permute-start.29 = (bf16[2,2,4,64,1280]{4,3,2,1,0:T(8,128)(2,1)}, bf16[2,2,4,64,1280]{4,3,2,1,0:T(8,128)(2,1)}, u32[]{:S(2)}, u32[]{:S(2)}) collective-permute-start(bf16[2,2,4,64,1280]{4,3,2,1,0:T(8,128)(2,1)} %dynamic-slice_bitcast_fusion), channel_id=1, source_target_pairs={{0,4},{4,0},{8,12},{12,8},{16,20},{20,16},{24,28},{28,24},{1,5},{5... | collective-permute-start | bytes 7864328 | tf_op jit(solution)/shard_map/ppermute | solution.py:586
  557.7 48.1 %collective-permute-start.31 = (bf16[512,2048]{1,0:T(8,128)(2,1)}, bf16[512,2048]{1,0:T(8,128)(2,1)}, u32[]{:S(2)}, u32[]{:S(2)}) collective-permute-start(bf16[512,2048]{1,0:T(8,128)(2,1)} %add_convert_fusion.1), channel_id=1, source_target_pairs={{0,8},{4,12},{8,0},{12,4},{16,24},{20,28},{24,16},{28,20},{1,9},{5... | collective-permute-start | bytes 6291464 | tf_op jit(solution)/shard_map/ppermute | solution.py:586
  613.3 119.2 %reduce-scatter.15.cloned.1.call-start = ((), (), s32[]{:S(2)}) async-start(), calls=%async_computation.11 | async-start | bytes 2949120 | tf_op jit(solution)/shard_map/reduce_scatter | solution.py:687
  654.5 132.4 %reduce-scatter.17.cloned.1.call-start = ((), (), s32[]{:S(2)}) async-start(), calls=%async_computation.12 | async-start | bytes 2129920 | tf_op jit(solution)/shard_map/reduce_scatter | solution.py:687
  (114 other events, 1067.4 us)
Sparse Core Ops, SparseCore 0:
  10.2 41.6 all-gather.12
  53.4 49.5 all-gather.16
  105.5 54.9 all-gather.14
  161.9 49.2 all-gather.18
  217.9 89.9 all-gather.10
  477.1 47.6 reduce-scatter.6
  534.7 26.7 reduce-scatter.8
  564.0 46.7 reduce-scatter.10
  613.4 34.7 reduce-scatter.12
  654.6 47.0 reduce-scatter.14
  752.3 34.5 reduce-scatter.16

commit v7 on v6

--- a/solution.py
+++ b/solution.py
@@ -852,13 +852,14 @@
     )
     queries, q_right, right_other, down_other = stage(queries, q_right, right_other, down_other)
     q_right = join_outer(q_right, right_other, 0)
+    down_pair = join_outer(w_down, down_other, 0)
     place_array = place.reshape(1)
-    keys_values, queries = stage(keys_values, queries)
+    keys_values, queries, down_in = stage(keys_values, queries, down_pair)
+    down_lines = gather_seq(down_in)
     mixed, logs = attend_forward(place_array, queries, keys_values)
-    mixed, grad_top1, grad_top2, up_lines, wout_other, down_other = stage(
-        mixed, swap(grad_top, 1), swap(grad_top, 2), up_lines, swap(q_right, 1), down_other
-    )
-    down_lines = gather_seq(join_outer(w_down, down_other, 0))
+    mixed, grad_top1, grad_top2, up_lines, wout_other = stage(
+        mixed, swap(grad_top, 1), swap(grad_top, 2), up_lines, swap(q_right, 1)
+    )
     wout_t = joined(q_right, wout_other, core, 2).reshape(width, -1)
     middle = inputs + mm_t(mixed, wout_t)
 
@@ -945,12 +946,17 @@
     )
     grad_wq = t_mm(normed, joint_grad_q).astype(bf16).reshape(*shape, QUERY_COLUMNS)
     grad_wout = add_bit(grad_wout, wout_other, 1, 2)
+    grad_up = jnp.moveaxis(add_outer(grad_wup, up_other, 0), 2, 0)
+    grad_kv2, joint_grad_q, grad_wq, grad_wout, grad_up = stage(
+        grad_kv2, joint_grad_q, grad_wq, grad_wout, grad_up
+    )
+    grad_up = reduce_seq(grad_up)
     own_near, send_near = back_pass((hidden_near,), (wdown,), False)
-    grad_up = jnp.moveaxis(add_outer(grad_wup, up_other, 0), 2, 0)
-    grad_kv2, joint_grad_q, grad_wq, grad_wout, own_near, send_near, grad_up = stage(
-        grad_kv2, joint_grad_q, grad_wq, grad_wout, own_near, send_near, grad_up
-    )
-    grad_up = reduce_seq(grad_up)
+    wq_other, grad_kv2, own_near, send_near = stage(
+        pass_bit(grad_wq, 1, 2), grad_kv2, own_near, send_near
+    )
+    grad_wq, grad_kv2 = stage(add_bit(grad_wq, wq_other, 1, 2), grad_kv2)
+    wq_other, wout_other = pass_bit(grad_wq, 2, 1), pass_outer(grad_wout, 0)
 
 
     grad_kv1, grad_kv2 = (
@@ -960,12 +966,6 @@
     joint_grad_kv, gain_k = heads_backward(
         grad_kv, joint_kv, wide_k, cos_table, sin_table, KEY_COLUMNS
     )
-    wq_other, near_other, joint_grad_kv = stage(
-        pass_bit(grad_wq, 1, 2), swap(send_near, 1), joint_grad_kv
-    )
-    grad_wq = add_bit(grad_wq, wq_other, 1, 2)
-    wq_other, wout_other = pass_bit(grad_wq, 2, 1), pass_outer(grad_wout, 0)
-    output = (middle + own_near + near_other.astype(f32) + across.astype(f32)).astype(bf16)
     grad_wkv = t_mm(normed, joint_grad_kv).astype(bf16)
     grad_normed = mm_t(joint_grad_q, wq) + mm_t(joint_grad_kv, wkv)
     grad_input_part, grad_attn_gain = norm_backward(
@@ -975,9 +975,10 @@
 
     gain_rows = jnp.stack([grad_attn_gain, grad_ffn_gain]).astype(bf16)
     gain_columns = t_mm(gain_rows, jnp.eye(2, LANES, dtype=bf16)).astype(bf16)
-    grad_wkv, gain_columns, wq_other, wout_other = stage(
-        grad_wkv, gain_columns, wq_other, wout_other
-    )
+    grad_wkv, gain_columns, wq_other, wout_other, near_other = stage(
+        grad_wkv, gain_columns, wq_other, wout_other, swap(send_near, 1)
+    )
+    output = (middle + own_near + near_other.astype(f32) + across.astype(f32)).astype(bf16)
     grad_wq = add_bit(grad_wq, wq_other, 2, 1)
     grad_wout = add_outer(grad_wout, wout_other, 0)
     wq_other, wout_other = pass_outer(grad_wq, 0), pass_bit(grad_wout, 2, 0)

time: 808 us -> 770 us (0.953)
  waiting for transfers between devices: 267 us -> 226 us
    ppermute x46, waiting for transfers between devices: 202 us -> 164 us  [swap(): return lax.ppermute(values, 'rows', pairs)]
    unnamed x153 -> x149, local copies, waits for them, and re-layouts: 26.8 us -> 23.7 us
  transfers between devices with their start and end apart: 62 -> 62, of which waited for: 29 -> 26; matrix products, arithmetic and copies ran while one was open for 18% -> 20% of each run, Pallas kernels for 28% -> 30%
where the time goes in v7:
time: 770 us; the launch traced here: 760 us
  Pallas kernels  253 us (33%)
  waiting for transfers between devices  226 us (29%)
  other arithmetic  80.8 us (10%)
  local copies, waits for them, and re-layouts  78.7 us (10%)
  starting transfers between devices  43.7 us (6%)
  matrix products  39.8 us (5%)
  blocking collectives  19.9 us (3%)
  between operations  18.2 us (2%)
    ppermute x46, waiting for transfers between devices, swap(): return lax.ppermute(values, 'rows', pairs)  164 us
    pallas_call x3, Pallas kernels, weight_pass(): pl.pallas_call(partial(weight_kernel, len(lefts)), grid=(rows // tile,),...  47.2 us
    pallas_call x4, Pallas kernels, back_pass(): pl.pallas_call(partial(back_kernel, count, transposed), grid=(width // ti...  46.2 us
    ppermute x46, starting transfers between devices, swap(): return lax.ppermute(values, 'rows', pairs)  39.8 us
    reduce_scatter x6, waiting for transfers between devices, reduce_seq(): return lax.psum_scatter(values, 'seq', scatter_dimension=0, tiled=False)  33.3 us
    pallas_call x2, Pallas kernels, hidden_pass(): pl.pallas_call(hidden_kernel, grid=(pl.cdiv(columns, tile),), in_specs=[w...  31.9 us
    all_gather x5, waiting for transfers between devices, gather_seq(): return lax.all_gather(values, 'seq', axis=0, tiled=False)  28 us
    pallas_call x2, Pallas kernels, attend_backward(): pl.pallas_call(partial(attend_backward_kernel, first, count), grid_spec=p...  27.9 us
  transfers between devices with their start and end apart: 62, of which 26 were waited for; matrix products, arithmetic and copies ran while one was open for 20% of the time, Pallas kernels for 30%

profile of v7, /device:TPU:0, one launch (start us, length us, event | category | flops | bytes accessed | tf_op | source)
XLA Modules:
  0.0 760.2 jit_solution(5170514428538758533)
XLA Ops:
  28.3 19.9 %all-gather = bf16[256,768]{1,0:T(8,128)(2,1)S(1)} all-gather(bf16[64,768]{1,0:T(8,128)(2,1)S(1)} %fusion.35), channel_id=2, replica_groups=mesh['rows'=8,'seq'=4] {'seq'}, dimensions={0}, use_global_device_ids=true | all-gather | bytes 491520 | tf_op jit(solution)/shard_map/all_gather | solution.py:683
  60.9 11.4 %collective-permute-done.2 = bf16[4,64,384]{2,1,0:T(8,128)(2,1)S(1)} collective-permute-done((bf16[4,64,384]{2,1,0:T(8,128)(2,1)S(1)}, bf16[4,64,384]{2,1,0:T(8,128)(2,1)S(1)}, u32[]{:S(2)}, u32[]{:S(2)}) %collective-permute-start.2) | collective-permute-done | bytes 196640 | tf_op jit(solution)/shard_map/ppermute | solution.py:586
  111.2 25.3 %collective-permute-done.12 = bf16[2,4,64,1280]{3,2,1,0:T(8,128)(2,1)S(1)} collective-permute-done((bf16[2,4,64,1280]{3,2,1,0:T(8,128)(2,1)S(1)}, bf16[2,4,64,1280]{3,2,1,0:T(8,128)(2,1)S(1)}, u32[]{:S(2)}, u32[]{:S(2)}) %collective-permute-start.12) | collective-permute-done | bytes 1310752 | tf_op jit(solution)/shard_map/ppermute | solution.py:586
  156.0 8.4 %heads_forward.3 = (f32[512,1280]{1,0:T(8,128)}, bf16[512,1280]{1,0:T(8,128)(2,1)S(1)}) custom-call(bf16[512,2048]{1,0:T(8,128)(2,1)S(1)} %fusion.7.normed_ref, bf16[2048,1280]{1,0:T(8,128)(2,1)} %bitcast.295, f32[8,1280]{1,0:T(8,128)S(1)} %broadcast_in_dim.14.gain_ref, f32[512,128]{1,0:T(8,128)S(1)} %copy-done.11, f32[512,128]{1,0:T(8,128)S(1)} %copy-done.13), custom_call_target="tpu_custom_call" | custom-call | flops 1000 | bytes 1000 | tf_op jit(solution)/shard_map/heads_forward/pallas_call | solution.py:85
  172.4 11.7 %attend_forward.1 = (bf16[512,1280]{1,0:T(8,128)(2,1)S(1)}, f32[512,1280]{1,0:T(8,128)S(1)}) custom-call(s32[1]{0:T(128)} %bitcast.place_ref, bf16[512,1280]{1,0:T(8,128)(2,1)S(1)} %get-tuple-element.190.q_ref, bf16[2048,640]{1,0:T(8,128)(2,1)} %all-gather.14.cloned.1.call-done.k_ref.v_ref, bf16[2048,640]{1,0:T(8,128)(2,1)} %all-gather.14.cloned.1.call-done.k_ref.v_ref), custom_call_target="tpu_custom_call" | custom-call | flops 1000 | bytes 1000 | tf_op jit(solution)/shard_map/attend_forward/pallas_call | solution.py:194
  186.7 24.3 %all-gather.18.cloned.1.call-done = bf16[8,2,64,1152]{3,2,1,0:T(8,128)(2,1)} async-done(((bf16[2,2,64,1152]{3,2,1,0:T(8,128)(2,1)}), bf16[8,2,64,1152]{3,2,1,0:T(8,128)(2,1)}) %all-gather.18.cloned.1.call-update) | async-done | bytes 2359312 | tf_op jit(solution)/shard_map/all_gather | solution.py:683
  238.9 37.2 %collective-permute-done.19.n0_ref.refs_2_ = bf16[512,2048]{1,0:T(8,128)(2,1)} collective-permute-done((bf16[512,2048]{1,0:T(8,128)(2,1)S(1)}, bf16[512,2048]{1,0:T(8,128)(2,1)}, u32[]{:S(2)}, u32[]{:S(2)}) %collective-permute-start.19) | collective-permute-done | bytes 2097184 | tf_op jit(solution)/shard_map/ppermute | solution.py:586
  283.7 15.6 %hidden_pass.2 = (bf16[1024,1152]{1,0:T(8,128)(2,1)}, bf16[1024,1152]{1,0:T(8,128)(2,1)}, bf16[1024,1152]{1,0:T(8,128)(2,1)}) custom-call(bf16[512,2048]{1,0:T(8,128)(2,1)S(1)} %multiply_convert_fusion.n0_ref.refs_0_, bf16[512,2048]{1,0:T(8,128)(2,1)} %collective-permute-done.18.n1_ref.refs_1_, bf16[2048,1152]{1,0:T(8,128)(2,1)} %bitcast.283, ...), custom_call_target="tpu_custom_call" | custom-call | flops 1000 | bytes 1000 | tf_op jit(solution)/shard_map/hidden_pass/pallas_call | solution.py:375
  299.3 16.3 %hidden_pass.3 = (bf16[1024,1152]{1,0:T(8,128)(2,1)}, bf16[1024,1152]{1,0:T(8,128)(2,1)}, bf16[1024,1152]{1,0:T(8,128)(2,1)}) custom-call(bf16[512,2048]{1,0:T(8,128)(2,1)} %collective-permute-done.19.n0_ref.refs_2_, bf16[512,2048]{1,0:T(8,128)(2,1)} %collective-permute-done.21.n1_ref.refs_3_, bf16[2048,1152]{1,0:T(8,128)(2,1)} %bitcast.284, ...), custom_call_target="tpu_custom_call" | custom-call | flops 1000 | bytes 1000 | tf_op jit(solution)/shard_map/hidden_pass/pallas_call | solution.py:375
  315.6 12.3 %gates_pass.2 = (bf16[1024,1152]{1,0:T(8,128)(2,1)}, bf16[1024,1152]{1,0:T(8,128)(2,1)}) custom-call(bf16[512,2048]{1,0:T(8,128)(2,1)} %collective-permute-done.15.g0_ref.refs_4_, bf16[512,2048]{1,0:T(8,128)(2,1)} %collective-permute-done.22.g1_ref.refs_5_, bf16[1152,2048]{1,0:T(8,128)(2,1)} %bitcast.291, bf16[1024,1152]{1,0:T(8,128)(2,1)} %get-tuple-element.213.gate_ref, ...), custom_call_target="tpu_custom_call" | custom-call | flops 1000 | bytes 1000 | tf_op jit(solution)/shard_map/gates_pass/pallas_call | solution.py:410
  329.6 14.9 %back_pass.4 = (f32[512,2048]{1,0:T(8,128)}, bf16[512,2048]{1,0:T(8,128)(2,1)S(1)}) custom-call(bf16[1024,1152]{1,0:T(8,128)(2,1)S(1)} %copy-done.5, bf16[1024,1152]{1,0:T(8,128)(2,1)} %get-tuple-element.216.refs_1_.refs_5_, bf16[2048,1152]{1,0:T(8,128)(2,1)} %bitcast.285, bf16[2048,1152]{1,0:T(8,128)(2,1)} %bitcast.289), custom_call_target="tpu_custom_call" | custom-call | flops 1000 | bytes 1000 | tf_op jit(solution)/shard_map/back_pass/pallas_call | solution.py:449
  344.9 15.2 %weight_pass.3 = bf16[1152,2048]{1,0:T(8,128)(2,1)} custom-call(bf16[1024,1152]{1,0:T(8,128)(2,1)} %get-tuple-element.266.refs_0_, bf16[1024,1152]{1,0:T(8,128)(2,1)} %get-tuple-element.242.refs_1_.refs_0_, bf16[512,2048]{1,0:T(8,128)(2,1)} %bitcast_convert_fusion.refs_2_.g0_ref, bf16[512,2048]{1,0:T(8,128)(2,1)S(1)} %copy-done.8, ...), custom_call_target="tpu_custom_call" | custom-call | flops 1000 | bytes 1000 | tf_op jit(solution)/shard_map/weight_pass/pallas_call | solution.py:483
  367.8 11.6 %gates_pass.3 = (bf16[1024,1152]{1,0:T(8,128)(2,1)}, bf16[1024,1152]{1,0:T(8,128)(2,1)}) custom-call(bf16[512,2048]{1,0:T(8,128)(2,1)} %bitcast_convert_fusion.refs_2_.g0_ref, bf16[512,2048]{1,0:T(8,128)(2,1)S(1)} %copy-done.9, bf16[1152,2048]{1,0:T(8,128)(2,1)} %bitcast.292, bf16[1024,1152]{1,0:T(8,128)(2,1)} %get-tuple-element.227.gate_ref, ...), custom_call_target="tpu_custom_call" | custom-call | flops 1000 | bytes 1000 | tf_op jit(solution)/shard_map/gates_pass/pallas_call | solution.py:410
  379.4 15.9 %weight_pass.4 = bf16[2048,1152]{1,0:T(8,128)(2,1)} custom-call(bf16[512,2048]{1,0:T(8,128)(2,1)S(1)} %multiply_convert_fusion.n0_ref.refs_0_, bf16[512,2048]{1,0:T(8,128)(2,1)} %collective-permute-done.18.n1_ref.refs_1_, bf16[512,2048]{1,0:T(8,128)(2,1)} %collective-permute-done.19.n0_ref.refs_2_, bf16[512,2048]{1,0:T(8,128)(2,1)} %collective-permute-done.21.n1_ref.refs_3_, ...), custom_call_target="tpu_custom_call" | custom-call | flops 1000 | bytes 1000 | tf_op jit(solution)/shard_map/weight_pass/pallas_call | solution.py:483
  395.3 14.9 %back_pass.5 = (f32[512,2048]{1,0:T(8,128)}, bf16[512,2048]{1,0:T(8,128)(2,1)}) custom-call(bf16[1024,1152]{1,0:T(8,128)(2,1)S(1)} %copy-done.6, bf16[1024,1152]{1,0:T(8,128)(2,1)} %get-tuple-element.235.refs_1_.refs_4_, bf16[2048,1152]{1,0:T(8,128)(2,1)} %bitcast.286, bf16[2048,1152]{1,0:T(8,128)(2,1)} %bitcast.290), custom_call_target="tpu_custom_call" | custom-call | flops 1000 | bytes 1000 | tf_op jit(solution)/shard_map/back_pass/pallas_call | solution.py:449
  410.3 16.0 %weight_pass.5 = bf16[2048,1152]{1,0:T(8,128)(2,1)} custom-call(bf16[512,2048]{1,0:T(8,128)(2,1)S(1)} %multiply_convert_fusion.n0_ref.refs_0_, bf16[512,2048]{1,0:T(8,128)(2,1)} %collective-permute-done.18.n1_ref.refs_1_, bf16[512,2048]{1,0:T(8,128)(2,1)} %collective-permute-done.19.n0_ref.refs_2_, bf16[512,2048]{1,0:T(8,128)(2,1)} %collective-permute-done.21.n1_ref.refs_3_, ...), custom_call_target="tpu_custom_call" | custom-call | flops 1000 | bytes 1000 | tf_op jit(solution)/shard_map/weight_pass/pallas_call | solution.py:483
  448.3 11.0 %attend_backward.2 = (bf16[512,512]{1,0:T(8,128)(2,1)S(1)}, bf16[2048,256]{1,0:T(8,128)(2,1)S(1)}) custom-call(s32[1]{0:T(128)} %bitcast.place_ref, bf16[512,1280]{1,0:T(8,128)(2,1)S(1)} %get-tuple-element.190.q_ref, bf16[2048,640]{1,0:T(8,128)(2,1)} %all-gather.14.cloned.1.call-done.k_ref.v_ref, ...), custom_call_target="tpu_custom_call" | custom-call | flops 1000 | bytes 1000 | tf_op jit(solution)/shard_map/attend_backward/pallas_call | solution.py:331
  462.2 16.8 %reduce-scatter.7.cloned.1.call-done = bf16[1,144,2048]{2,1,0:T(8,128)(2,1)} async-done(((bf16[4,144,2048]{2,1,0:T(8,128)(2,1)}), bf16[1,144,2048]{2,1,0:T(8,128)(2,1)}) %reduce-scatter.7.cloned.1.call-update) | async-done | bytes 589840 | tf_op jit(solution)/shard_map/reduce_scatter | solution.py:687
  513.8 16.9 %attend_backward.3 = (bf16[512,768]{1,0:T(8,128)(2,1)S(1)}, bf16[2048,384]{1,0:T(8,128)(2,1)}) custom-call(s32[1]{0:T(128)} %bitcast.place_ref, bf16[512,1280]{1,0:T(8,128)(2,1)S(1)} %get-tuple-element.190.q_ref, bf16[2048,640]{1,0:T(8,128)(2,1)} %all-gather.14.cloned.1.call-done.k_ref.v_ref, bf16[2048,640]{1,0:T(8,128)(2,1)} %all-gather.14.cloned.1.call-done.k_ref.v_ref, ...), custom_call_target="tpu_custom_call" | custom-call | flops 1000 | bytes 1000 | tf_op jit(solution)/shard_map/attend_backward/pallas_call | solution.py:331
  530.7 26.3 %collective-permute-done.30 = bf16[2,2,4,64,1152]{4,3,1,0,2:T(8,128)(2,1)} collective-permute-done((bf16[2,2,4,64,1152]{4,3,1,0,2:T(8,128)(2,1)S(1)}, bf16[2,2,4,64,1152]{4,3,1,0,2:T(8,128)(2,1)}, u32[]{:S(2)}, u32[]{:S(2)}) %collective-permute-start.30) | collective-permute-done | bytes 2359328 | tf_op jit(solution)/shard_map/ppermute | solution.py:586
  569.0 8.9 %heads_backward.2 = (bf16[512,1280]{1,0:T(8,128)(2,1)}, f32[8,1280]{1,0:T(8,128)}) custom-call(bf16[512,1280]{1,0:T(8,128)(2,1)} %pad_maximum_fusion.3.grad_ref, f32[512,1280]{1,0:T(8,128)} %get-tuple-element.260.joint_ref, f32[8,1280]{1,0:T(8,128)} %copy-done.38, f32[512,128]{1,0:T(8,128)} %copy-done.10, f32[512,128]{1,0:T(8,128)} %copy-done.12), custom_call_target="tpu_custom_call" | custom-call | flops 1000 | bytes 1000 | tf_op jit(solution)/shard_map/heads_backward/pallas_call | solution.py:126
  593.3 9.5 %reduce-scatter.13.cloned.1.call-done = bf16[1,512,384]{1,2,0:T(8,128)(2,1)} async-done(((bf16[4,512,384]{1,2,0:T(8,128)(2,1)}), bf16[1,512,384]{1,2,0:T(8,128)(2,1)}) %reduce-scatter.13.cloned.1.call-update) | async-done | bytes 393232 | tf_op jit(solution)/shard_map/reduce_scatter | solution.py:687
  654.1 13.4 %collective-permute-done.33 = bf16[2,4,64,1280]{3,2,1,0:T(8,128)(2,1)} collective-permute-done((bf16[2,4,64,1280]{3,2,1,0:T(8,128)(2,1)}, bf16[2,4,64,1280]{3,2,1,0:T(8,128)(2,1)}, u32[]{:S(2)}, u32[]{:S(2)}) %collective-permute-start.33) | collective-permute-done | bytes 1310752 | tf_op jit(solution)/shard_map/ppermute | solution.py:586
  681.9 10.7 %collective-permute-done.42 = bf16[4,64,1280]{2,1,0:T(8,128)(2,1)} collective-permute-done((bf16[4,64,1280]{2,1,0:T(8,128)(2,1)}, bf16[4,64,1280]{2,1,0:T(8,128)(2,1)}, u32[]{:S(2)}, u32[]{:S(2)}) %collective-permute-start.42) | collective-permute-done | bytes 655392 | tf_op jit(solution)/shard_map/ppermute | solution.py:586
  (432 shorter events, 357.2 us)
Async XLA Ops:
  9.8 130.4 %all-gather.16.cloned.1.call-start = ((), (), s32[]{:S(2)}) async-start(), calls=%async_computation.14 | async-start | bytes 2949120 | tf_op jit(solution)/shard_map/all_gather | solution.py:683
  53.2 117.2 %all-gather.14.cloned.1.call-start = ((), (), s32[]{:S(2)}) async-start(), calls=%async_computation.13 | async-start | bytes 3276800 | tf_op jit(solution)/shard_map/all_gather | solution.py:683
  53.4 48.2 %collective-permute-start.10 = (bf16[144,2048]{1,0:T(8,128)(2,1)}, bf16[144,2048]{1,0:T(8,128)(2,1)}, u32[]{:S(2)}, u32[]{:S(2)}) collective-permute-start(bf16[144,2048]{1,0:T(8,128)(2,1)} %param.20), channel_id=1, source_target_pairs={{0,16},{4,20},{8,24},{12,28},{16,0},{20,4},{24,8},{28,12},{1,17},{... | collective-permute-start | bytes 1769480 | tf_op jit(solution)/shard_map/ppermute | solution.py:586
  105.1 105.8 %all-gather.18.cloned.1.call-start = ((), (), s32[]{:S(2)}) async-start(), calls=%async_computation.15 | async-start | bytes 2949120 | tf_op jit(solution)/shard_map/all_gather | solution.py:683
  143.2 172.4 %all-gather.20.cloned.1.call-start = ((), (), s32[]{:S(2)}) async-start(), calls=%async_computation.16 | async-start | bytes 5898240 | tf_op jit(solution)/shard_map/all_gather | solution.py:683
  166.0 48.4 %collective-permute-start.16 = (bf16[2,2,4,64,1280]{4,3,2,1,0:T(8,128)(2,1)}, bf16[2,2,4,64,1280]{4,3,2,1,0:T(8,128)(2,1)}, u32[]{:S(2)}, u32[]{:S(2)}) collective-permute-start(bf16[2,2,4,64,1280]{4,3,2,1,0:T(8,128)(2,1)} %bitcast.64), channel_id=1, source_target_pairs={{0,4},{4,0},{8,12},{12,8},{16,20},{20,16},{24,28},{28,24},{1,5},{5... | collective-permute-start | bytes 7864328 | tf_op jit(solution)/shard_map/ppermute | solution.py:586
  166.5 47.9 %collective-permute-start.15 = (bf16[512,2048]{1,0:T(8,128)(2,1)}, bf16[512,2048]{1,0:T(8,128)(2,1)}, u32[]{:S(2)}, u32[]{:S(2)}) collective-permute-start(bf16[512,2048]{1,0:T(8,128)(2,1)} %bitcast_convert_fusion.refs_2_.g0_ref), channel_id=1, source_target_pairs={{0,8},{4,12},{8,0},{12,4},{16,24},{20,28},{24,16},{28,20},{1,9},{5... | collective-permute-start | bytes 6291464 | tf_op jit(solution)/shard_map/ppermute | solution.py:586
  167.9 46.4 %collective-permute-start.14 = (bf16[512,2048]{1,0:T(8,128)(2,1)}, bf16[512,2048]{1,0:T(8,128)(2,1)S(1)}, u32[]{:S(2)}, u32[]{:S(2)}) collective-permute-start(bf16[512,2048]{1,0:T(8,128)(2,1)} %bitcast_convert_fusion.refs_2_.g0_ref), channel_id=1, source_target_pairs={{0,4},{4,0},{8,12},{12,8},{16,20},{20,16},{24,28},{28,24},{1,5},{5... | collective-permute-start | bytes 6291464 | tf_op jit(solution)/shard_map/ppermute | solution.py:586
  170.4 308.6 %reduce-scatter.7.cloned.1.call-start = ((), (), s32[]{:S(2)}) async-start(), calls=%async_computation.6 | async-start | bytes 2949120 | tf_op jit(solution)/shard_map/reduce_scatter | solution.py:687
  170.8 58.6 %collective-permute-start.17 = (bf16[4,2,2,64,1152]{4,3,2,1,0:T(8,128)(2,1)}, bf16[4,2,2,64,1152]{4,3,2,1,0:T(8,128)(2,1)}, u32[]{:S(2)}, u32[]{:S(2)}) collective-permute-start(bf16[4,2,2,64,1152]{4,3,2,1,0:T(8,128)(2,1)} %bitcast.322), channel_id=1, source_target_pairs={{0,16},{4,20},{8,24},{12,28},{16,0},{20,4},{24,8},{28,12},{1,17},{... | collective-permute-start | bytes 7077896 | tf_op jit(solution)/shard_map/ppermute | solution.py:586
  214.4 61.8 %collective-permute-start.20 = (bf16[4,2,2,64,1152]{4,3,2,1,0:T(8,128)(2,1)}, bf16[4,2,2,64,1152]{4,3,2,1,0:T(8,128)(2,1)}, u32[]{:S(2)}, u32[]{:S(2)}) collective-permute-start(bf16[4,2,2,64,1152]{4,3,2,1,0:T(8,128)(2,1)} %bitcast.324), channel_id=1, source_target_pairs={{0,16},{4,20},{8,24},{12,28},{16,0},{20,4},{24,8},{28,12},{1,17},{... | collective-permute-start | bytes 7077896 | tf_op jit(solution)/shard_map/ppermute | solution.py:586
  229.5 46.6 %collective-permute-start.19 = (bf16[512,2048]{1,0:T(8,128)(2,1)S(1)}, bf16[512,2048]{1,0:T(8,128)(2,1)}, u32[]{:S(2)}, u32[]{:S(2)}) collective-permute-start(bf16[512,2048]{1,0:T(8,128)(2,1)S(1)} %multiply_convert_fusion.n0_ref.refs_0_), channel_id=1, source_target_pairs={{0,8},{4,12},{8,0},{12,4},{16,24},{20,28},{24,16},{28,20},{1,9},{5... | collective-permute-start | bytes 6291464 | tf_op jit(solution)/shard_map/ppermute | solution.py:586
  231.0 68.3 %collective-permute-start.22 = (bf16[512,2048]{1,0:T(8,128)(2,1)}, bf16[512,2048]{1,0:T(8,128)(2,1)}, u32[]{:S(2)}, u32[]{:S(2)}) collective-permute-start(bf16[512,2048]{1,0:T(8,128)(2,1)} %collective-permute-done.15.g0_ref.refs_4_), channel_id=1, source_target_pairs={{0,4},{4,0},{8,12},{12,8},{16,20},{20,16},{24,28},{28,24},{1,5},{5... | collective-permute-start | bytes 6291464 | tf_op jit(solution)/shard_map/ppermute | solution.py:586
  362.2 48.1 %collective-permute-start.24 = (bf16[512,2048]{1,0:T(8,128)(2,1)}, bf16[512,2048]{1,0:T(8,128)(2,1)}, u32[]{:S(2)}, u32[]{:S(2)}) collective-permute-start(bf16[512,2048]{1,0:T(8,128)(2,1)} %add_convert_fusion.2), channel_id=1, source_target_pairs={{0,8},{4,12},{8,0},{12,4},{16,24},{20,28},{24,16},{28,20},{1,9},{5... | collective-permute-start | bytes 6291464 | tf_op jit(solution)/shard_map/ppermute | solution.py:586
  367.1 59.2 %collective-permute-start.26 = (bf16[4,144,2048]{2,1,0:T(8,128)(2,1)}, bf16[4,144,2048]{2,1,0:T(8,128)(2,1)}, u32[]{:S(2)}, u32[]{:S(2)}) collective-permute-start(bf16[4,144,2048]{2,1,0:T(8,128)(2,1)} %dynamic-slice_bitcast_fusion.1), channel_id=1, source_target_pairs={{0,16},{4,20},{8,24},{12,28},{16,0},{20,4},{24,8},{28,12},{1,17},{... | collective-permute-start | bytes 7077896 | tf_op jit(solution)/shard_map/ppermute | solution.py:586
  431.1 125.9 %reduce-scatter.9.cloned.1.call-start = ((), (), s32[]{:S(2)}) async-start(), calls=%async_computation.7 | async-start | bytes 1310720 | tf_op jit(solution)/shard_map/reduce_scatter | solution.py:687
  434.7 62.0 %collective-permute-start.28 = (bf16[2,2,4,64,1152]{4,3,1,0,2:T(8,128)(2,1)}, bf16[2,2,4,64,1152]{4,3,1,0,2:T(8,128)(2,1)}, u32[]{:S(2)}, u32[]{:S(2)}) collective-permute-start(bf16[2,2,4,64,1152]{4,3,1,0,2:T(8,128)(2,1)} %copy_bitcast_fusion.2), channel_id=1, source_target_pairs={{0,16},{4,20},{8,24},{12,28},{16,0},{20,4},{24,8},{28,12},{1,17},{... | collective-permute-start | bytes 7077896 | tf_op jit(solution)/shard_map/ppermute | solution.py:586
  488.9 76.1 %reduce-scatter.11.cloned.1.call-start = ((), (), s32[]{:S(2)}) async-start(), calls=%async_computation.8 | async-start | bytes 2949120 | tf_op jit(solution)/shard_map/reduce_scatter | solution.py:687
  501.3 101.5 %reduce-scatter.13.cloned.1.call-start = ((), (), s32[]{:S(2)}) async-start(), calls=%async_computation.9 | async-start | bytes 1966080 | tf_op jit(solution)/shard_map/reduce_scatter | solution.py:687
  503.3 53.8 %collective-permute-start.30 = (bf16[2,2,4,64,1152]{4,3,1,0,2:T(8,128)(2,1)S(1)}, bf16[2,2,4,64,1152]{4,3,1,0,2:T(8,128)(2,1)}, u32[]{:S(2)}, u32[]{:S(2)}) collective-permute-start(bf16[2,2,4,64,1152]{4,3,1,0,2:T(8,128)(2,1)S(1)} %copy_bitcast_fusion.1), channel_id=1, source_target_pairs={{0,16},{4,20},{8,24},{12,28},{16,0},{20,4},{24,8},{28,12},{1,17},{... | collective-permute-start | bytes 7077896 | tf_op jit(solution)/shard_map/ppermute | solution.py:586
  508.4 52.1 %collective-permute-start.29 = (bf16[2,2,4,64,1280]{4,3,2,1,0:T(8,128)(2,1)}, bf16[2,2,4,64,1280]{4,3,2,1,0:T(8,128)(2,1)}, u32[]{:S(2)}, u32[]{:S(2)}) collective-permute-start(bf16[2,2,4,64,1280]{4,3,2,1,0:T(8,128)(2,1)} %dynamic-slice_bitcast_fusion), channel_id=1, source_target_pairs={{0,4},{4,0},{8,12},{12,8},{16,20},{20,16},{24,28},{28,24},{1,5},{5... | collective-permute-start | bytes 7864328 | tf_op jit(solution)/shard_map/ppermute | solution.py:586
  512.3 48.1 %collective-permute-start.31 = (bf16[512,2048]{1,0:T(8,128)(2,1)}, bf16[512,2048]{1,0:T(8,128)(2,1)}, u32[]{:S(2)}, u32[]{:S(2)}) collective-permute-start(bf16[512,2048]{1,0:T(8,128)(2,1)} %add_convert_fusion.1), channel_id=1, source_target_pairs={{0,8},{4,12},{8,0},{12,4},{16,24},{20,28},{24,16},{28,20},{1,9},{5... | collective-permute-start | bytes 6291464 | tf_op jit(solution)/shard_map/ppermute | solution.py:586
  567.6 114.4 %reduce-scatter.15.cloned.1.call-start = ((), (), s32[]{:S(2)}) async-start(), calls=%async_computation.10 | async-start | bytes 2949120 | tf_op jit(solution)/shard_map/reduce_scatter | solution.py:687
  615.8 132.6 %reduce-scatter.17.cloned.1.call-start = ((), (), s32[]{:S(2)}) async-start(), calls=%async_computation.11 | async-start | bytes 2129920 | tf_op jit(solution)/shard_map/reduce_scatter | solution.py:687
  (112 other events, 1095.2 us)
Sparse Core Ops, SparseCore 0:
  10.2 41.6 all-gather.11
  53.4 49.5 all-gather.15
  105.2 54.9 all-gather.13
  161.7 49.2 all-gather.17
  212.9 88.2 all-gather.19
  431.3 47.6 reduce-scatter.6
  489.0 26.7 reduce-scatter.8
  518.3 46.6 reduce-scatter.10
  568.0 34.7 reduce-scatter.12
  615.9 47.1 reduce-scatter.14
  714.0 34.3 reduce-scatter.16

commit v8 on v7

--- a/solution.py
+++ b/solution.py
@@ -101,6 +101,38 @@
         name="heads_forward",
         cost_estimate=LIGHT,
     )(normed, weight, gain, cos, sin)
+
+
+def project_kernel(side_ref, mixed_ref, own_ref, other_ref, inputs_ref, out_ref):
+    mine = pl.program_id(0) % 2 == side_ref[0]
+
+    @pl.when(mine)
+    def _():
+        out_ref[...] = inputs_ref[...].astype(f32) + dot_nt(mixed_ref[...], own_ref[0])
+
+    @pl.when(jnp.logical_not(mine))
+    def _():
+        out_ref[...] = inputs_ref[...].astype(f32) + dot_nt(mixed_ref[...], other_ref[0])
+
+
+def project(mixed, own, other, inputs, side):
+    tokens, depth = mixed.shape
+    count, block, _ = own.shape
+    weight = pl.BlockSpec((1, block, depth), lambda i, s: (i // 2, 0, 0))
+    out = pl.BlockSpec((tokens, block), lambda i, s: (0, i))
+    return pl.pallas_call(
+        project_kernel,
+        grid_spec=pltpu.PrefetchScalarGridSpec(
+            num_scalar_prefetch=1,
+            grid=(2 * count,),
+            in_specs=[pl.BlockSpec((tokens, depth), lambda i, s: (0, 0)), weight, weight, out],
+            out_specs=out,
+        ),
+        out_shape=jax.ShapeDtypeStruct((tokens, 2 * count * block), f32),
+        compiler_params=pltpu.CompilerParams(vmem_limit_bytes=VMEM_LIMIT),
+        name="project",
+        cost_estimate=LIGHT,
+    )(side.astype(jnp.int32).reshape(1), mixed, own, other, inputs)
 
 
 def heads_backward_kernel(
@@ -860,13 +892,18 @@
     mixed, grad_top1, grad_top2, up_lines, wout_other = stage(
         mixed, swap(grad_top, 1), swap(grad_top, 2), up_lines, swap(q_right, 1)
     )
-    wout_t = joined(q_right, wout_other, core, 2).reshape(width, -1)
-    middle = inputs + mm_t(mixed, wout_t)
+    half_rows = (2 * outer, seq_devices * d_rows, QUERY_COLUMNS)
+    middle = project(
+        mixed, q_right.reshape(half_rows), wout_other.reshape(half_rows), tokens_in[0], core
+    )
 
     ffn_scale = norm_scale(middle)
     normed_ffn = (middle * ffn_scale * ffn_gain_full).astype(bf16)
     up_other = send_outer(up_lines)
-    normed_ffn, gate_other = stage(normed_ffn, gate_other)
+    normed_ffn, gate_other, q_right, wout_other = stage(
+        normed_ffn, gate_other, q_right, wout_other
+    )
+    wout_t = joined(q_right, wout_other, core, 2).reshape(width, -1)
     normed1, normed2, up_other, wgate = stage(
         swap(normed_ffn, 1),
         swap(normed_ffn, 2),
@@ -947,15 +984,11 @@
     grad_wq = t_mm(normed, joint_grad_q).astype(bf16).reshape(*shape, QUERY_COLUMNS)
     grad_wout = add_bit(grad_wout, wout_other, 1, 2)
     grad_up = jnp.moveaxis(add_outer(grad_wup, up_other, 0), 2, 0)
-    grad_kv2, joint_grad_q, grad_wq, grad_wout, grad_up = stage(
-        grad_kv2, joint_grad_q, grad_wq, grad_wout, grad_up
+    grad_kv2, grad_normed, grad_wq, grad_wout, grad_up = stage(
+        grad_kv2, mm_t(joint_grad_q, wq), grad_wq, grad_wout, grad_up
     )
     grad_up = reduce_seq(grad_up)
-    own_near, send_near = back_pass((hidden_near,), (wdown,), False)
-    wq_other, grad_kv2, own_near, send_near = stage(
-        pass_bit(grad_wq, 1, 2), grad_kv2, own_near, send_near
-    )
-    grad_wq, grad_kv2 = stage(add_bit(grad_wq, wq_other, 1, 2), grad_kv2)
+    grad_wq, grad_kv2 = stage(reduce_bit(grad_wq, 1, 2), grad_kv2)
     wq_other, wout_other = pass_bit(grad_wq, 2, 1), pass_outer(grad_wout, 0)
 
 
@@ -967,7 +1000,7 @@
         grad_kv, joint_kv, wide_k, cos_table, sin_table, KEY_COLUMNS
     )
     grad_wkv = t_mm(normed, joint_grad_kv).astype(bf16)
-    grad_normed = mm_t(joint_grad_q, wq) + mm_t(joint_grad_kv, wkv)
+    grad_normed = grad_normed + mm_t(joint_grad_kv, wkv)
     grad_input_part, grad_attn_gain = norm_backward(
         inputs, in_scale, attn_gain_full, grad_normed
     )
@@ -975,10 +1008,10 @@
 
     gain_rows = jnp.stack([grad_attn_gain, grad_ffn_gain]).astype(bf16)
     gain_columns = t_mm(gain_rows, jnp.eye(2, LANES, dtype=bf16)).astype(bf16)
-    grad_wkv, gain_columns, wq_other, wout_other, near_other = stage(
-        grad_wkv, gain_columns, wq_other, wout_other, swap(send_near, 1)
-    )
-    output = (middle + own_near + near_other.astype(f32) + across.astype(f32)).astype(bf16)
+    grad_wkv, gain_columns, wq_other, wout_other, hidden_near = stage(
+        grad_wkv, gain_columns, wq_other, wout_other, hidden_near
+    )
+    own_near, send_near = back_pass((hidden_near,), (wdown,), False)
     grad_wq = add_bit(grad_wq, wq_other, 2, 1)
     grad_wout = add_outer(grad_wout, wout_other, 0)
     wq_other, wout_other = pass_outer(grad_wq, 0), pass_bit(grad_wout, 2, 0)
@@ -1012,9 +1045,13 @@
     head_gains = head_gains + gains_other
     left = add_bit(left, left_other, 2, 1)
     right = add_outer(right, right_other, 0)
-    left_other, right_other, gains_other = stage(
-        pass_outer(left, 0), pass_bit(right, 2, 0), exchange(head_gains, "rows", 2)
-    )
+    left_other, right_other, gains_other, near_other = stage(
+        pass_outer(left, 0),
+        pass_bit(right, 2, 0),
+        exchange(head_gains, "rows", 2),
+        swap(send_near, 1),
+    )
+    output = (middle + own_near + near_other.astype(f32) + across.astype(f32)).astype(bf16)
     head_gains = head_gains + gains_other
     sums = reduce_seq(
         jnp.concatenate(

time: 770 us -> 760 us (0.987)
  Pallas kernels: 253 us -> 271 us
  waiting for transfers between devices: 226 us -> 213 us
  local copies, waits for them, and re-layouts: 78.7 us -> 68.3 us
    pallas_call x0 -> x1, Pallas kernels: none -> 9.85 us  [project(): pl.pallas_call(project_kernel, grid_spec=pltpu.PrefetchScalarGridSpec(num...]
    ppermute x46, waiting for transfers between devices: 164 us -> 155 us  [swap(): return lax.ppermute(values, 'rows', pairs)]
    dot_general x3 -> x2, matrix products: 21.1 us -> 14.4 us  [mm_t(): return jnp.einsum('ab,cb->ac', left, right, preferred_element_type=f32)]
    unnamed x149 -> x139, local copies, waits for them, and re-layouts: 23.7 us -> 17.2 us
  transfers between devices with their start and end apart: 62 -> 62, of which waited for: 26 -> 28; matrix products, arithmetic and copies ran while one was open for 20% -> 19% of each run, Pallas kernels for 30% -> 32%
where the time goes in v8:
time: 760 us; the launch traced here: 750 us
  Pallas kernels  271 us (36%)
  waiting for transfers between devices  213 us (28%)
  other arithmetic  82.4 us (11%)
  local copies, waits for them, and re-layouts  68.3 us (9%)
  starting transfers between devices  44.5 us (6%)
  matrix products  33.4 us (4%)
  blocking collectives  19.9 us (3%)
  between operations  18.1 us (2%)
    ppermute x46, waiting for transfers between devices, swap(): return lax.ppermute(values, 'rows', pairs)  155 us
    pallas_call x3, Pallas kernels, weight_pass(): pl.pallas_call(partial(weight_kernel, len(lefts)), grid=(rows // tile,),...  48 us
    pallas_call x4, Pallas kernels, back_pass(): pl.pallas_call(partial(back_kernel, count, transposed), grid=(width // ti...  46 us
    ppermute x46, starting transfers between devices, swap(): return lax.ppermute(values, 'rows', pairs)  40.3 us
    pallas_call x2, Pallas kernels, hidden_pass(): pl.pallas_call(hidden_kernel, grid=(pl.cdiv(columns, tile),), in_specs=[w...  31.9 us
    reduce_scatter x6, waiting for transfers between devices, reduce_seq(): return lax.psum_scatter(values, 'seq', scatter_dimension=0, tiled=False)  30.2 us
    pallas_call x2, Pallas kernels, attend_backward(): pl.pallas_call(partial(attend_backward_kernel, first, count), grid_spec=p...  28 us
    pallas_call x17, Pallas kernels, joined(): pl.pallas_call(joined_kernel, grid_spec=pltpu.PrefetchScalarGridSpec(num_...  25.9 us
  transfers between devices with their start and end apart: 62, of which 28 were waited for; matrix products, arithmetic and copies ran while one was open for 19% of the time, Pallas kernels for 32%

profile of v8, /device:TPU:0, one launch (start us, length us, event | category | flops | bytes accessed | tf_op | source)
XLA Modules:
  0.0 750.4 jit_solution(12352108240640633974)
XLA Ops:
  28.3 19.9 %all-gather = bf16[256,768]{1,0:T(8,128)(2,1)S(1)} all-gather(bf16[64,768]{1,0:T(8,128)(2,1)S(1)} %fusion.35), channel_id=2, replica_groups=mesh['rows'=8,'seq'=4] {'seq'}, dimensions={0}, use_global_device_ids=true | all-gather | bytes 491520 | tf_op jit(solution)/shard_map/all_gather | solution.py:715
  60.9 11.4 %collective-permute-done.2 = bf16[4,64,384]{2,1,0:T(8,128)(2,1)S(1)} collective-permute-done((bf16[4,64,384]{2,1,0:T(8,128)(2,1)S(1)}, bf16[4,64,384]{2,1,0:T(8,128)(2,1)S(1)}, u32[]{:S(2)}, u32[]{:S(2)}) %collective-permute-start.2) | collective-permute-done | bytes 196640 | tf_op jit(solution)/shard_map/ppermute | solution.py:618
  112.0 26.8 %collective-permute-done.12 = bf16[2,4,64,1280]{3,2,1,0:T(8,128)(2,1)} collective-permute-done((bf16[2,4,64,1280]{3,2,1,0:T(8,128)(2,1)}, bf16[2,4,64,1280]{3,2,1,0:T(8,128)(2,1)}, u32[]{:S(2)}, u32[]{:S(2)}) %collective-permute-start.12) | collective-permute-done | bytes 1310752 | tf_op jit(solution)/shard_map/ppermute | solution.py:618
  156.1 8.3 %heads_forward.3 = (f32[512,1280]{1,0:T(8,128)}, bf16[512,1280]{1,0:T(8,128)(2,1)S(1)}) custom-call(bf16[512,2048]{1,0:T(8,128)(2,1)S(1)} %copy-done.3, bf16[2048,1280]{1,0:T(8,128)(2,1)} %bitcast.287, f32[8,1280]{1,0:T(8,128)S(1)} %broadcast_in_dim.14.gain_ref, f32[512,128]{1,0:T(8,128)S(1)} %get-tuple-element.350.cos_ref, ...), custom_call_target="tpu_custom_call" | custom-call | flops 1000 | bytes 1000 | tf_op jit(solution)/shard_map/heads_forward/pallas_call | solution.py:85
  176.4 11.7 %attend_forward.1 = (bf16[512,1280]{1,0:T(8,128)(2,1)S(1)}, f32[512,1280]{1,0:T(8,128)S(1)}) custom-call(s32[1]{0:T(128)} %bitcast.place_ref, bf16[512,1280]{1,0:T(8,128)(2,1)S(1)} %copy-done.7, bf16[2048,640]{1,0:T(8,128)(2,1)} %all-gather.14.cloned.1.call-done.k_ref.v_ref, bf16[2048,640]{1,0:T(8,128)(2,1)} %all-gather.14.cloned.1.call-done.k_ref.v_ref), custom_call_target="tpu_custom_call" | custom-call | flops 1000 | bytes 1000 | tf_op jit(solution)/shard_map/attend_forward/pallas_call | solution.py:226
  189.6 21.4 %all-gather.18.cloned.1.call-done = bf16[8,2,64,1152]{3,2,1,0:T(8,128)(2,1)} async-done(((bf16[2,2,64,1152]{3,2,1,0:T(8,128)(2,1)}), bf16[8,2,64,1152]{3,2,1,0:T(8,128)(2,1)}) %all-gather.18.cloned.1.call-update) | async-done | bytes 2359312 | tf_op jit(solution)/shard_map/all_gather | solution.py:715
  218.6 9.8 %project.1 = f32[512,2048]{1,0:T(8,128)} custom-call(s32[1]{0:T(128)} %bitcast.2.side_ref, bf16[512,1280]{1,0:T(8,128)(2,1)S(1)} %get-tuple-element.196.mixed_ref.out_ref, bf16[4,256,1280]{2,1,0:T(8,128)(2,1)} %bitcast.64.own_ref, bf16[4,256,1280]{2,1,0:T(8,128)(2,1)} %bitcast.65.other_ref, bf16[512,2048]{1,0:T(8,128)(2,1)S(1)} %bitcast.237), custom_call_target="tpu_custom_call" | custom-call | flops 1000 | bytes 1000 | tf_op jit(solution)/shard_map/project/pallas_call | solution.py:123
  241.7 37.6 %collective-permute-done.19.n0_ref.refs_2_ = bf16[512,2048]{1,0:T(8,128)(2,1)} collective-permute-done((bf16[512,2048]{1,0:T(8,128)(2,1)S(1)}, bf16[512,2048]{1,0:T(8,128)(2,1)}, u32[]{:S(2)}, u32[]{:S(2)}) %collective-permute-start.19) | collective-permute-done | bytes 2097184 | tf_op jit(solution)/shard_map/ppermute | solution.py:618
  286.7 15.6 %hidden_pass.2 = (bf16[1024,1152]{1,0:T(8,128)(2,1)}, bf16[1024,1152]{1,0:T(8,128)(2,1)}, bf16[1024,1152]{1,0:T(8,128)(2,1)}) custom-call(bf16[512,2048]{1,0:T(8,128)(2,1)S(1)} %multiply_convert_fusion.n0_ref.refs_0_, bf16[512,2048]{1,0:T(8,128)(2,1)} %collective-permute-done.18.n1_ref.refs_1_, bf16[2048,1152]{1,0:T(8,128)(2,1)} %bitcast.275, ...), custom_call_target="tpu_custom_call" | custom-call | flops 1000 | bytes 1000 | tf_op jit(solution)/shard_map/hidden_pass/pallas_call | solution.py:407
  302.4 16.3 %hidden_pass.3 = (bf16[1024,1152]{1,0:T(8,128)(2,1)}, bf16[1024,1152]{1,0:T(8,128)(2,1)}, bf16[1024,1152]{1,0:T(8,128)(2,1)}) custom-call(bf16[512,2048]{1,0:T(8,128)(2,1)} %collective-permute-done.19.n0_ref.refs_2_, bf16[512,2048]{1,0:T(8,128)(2,1)} %collective-permute-done.21.n1_ref.refs_3_, bf16[2048,1152]{1,0:T(8,128)(2,1)} %bitcast.276, ...), custom_call_target="tpu_custom_call" | custom-call | flops 1000 | bytes 1000 | tf_op jit(solution)/shard_map/hidden_pass/pallas_call | solution.py:407
  318.7 12.4 %gates_pass.2 = (bf16[1024,1152]{1,0:T(8,128)(2,1)}, bf16[1024,1152]{1,0:T(8,128)(2,1)}) custom-call(bf16[512,2048]{1,0:T(8,128)(2,1)} %collective-permute-done.15.g0_ref.refs_4_, bf16[512,2048]{1,0:T(8,128)(2,1)} %collective-permute-done.22.g1_ref.refs_5_, bf16[1152,2048]{1,0:T(8,128)(2,1)} %bitcast.283, bf16[1024,1152]{1,0:T(8,128)(2,1)} %get-tuple-element.212.gate_ref, ...), custom_call_target="tpu_custom_call" | custom-call | flops 1000 | bytes 1000 | tf_op jit(solution)/shard_map/gates_pass/pallas_call | solution.py:442
  332.7 14.7 %back_pass.4 = (f32[512,2048]{1,0:T(8,128)}, bf16[512,2048]{1,0:T(8,128)(2,1)S(1)}) custom-call(bf16[1024,1152]{1,0:T(8,128)(2,1)S(1)} %copy-done.12, bf16[1024,1152]{1,0:T(8,128)(2,1)} %get-tuple-element.215.refs_1_.refs_5_, bf16[2048,1152]{1,0:T(8,128)(2,1)} %bitcast.277, bf16[2048,1152]{1,0:T(8,128)(2,1)} %bitcast.281), custom_call_target="tpu_custom_call" | custom-call | flops 1000 | bytes 1000 | tf_op jit(solution)/shard_map/back_pass/pallas_call | solution.py:481
  347.9 15.8 %weight_pass.3 = bf16[1152,2048]{1,0:T(8,128)(2,1)} custom-call(bf16[1024,1152]{1,0:T(8,128)(2,1)} %get-tuple-element.291.refs_0_, bf16[1024,1152]{1,0:T(8,128)(2,1)} %get-tuple-element.243.refs_1_.refs_0_, bf16[512,2048]{1,0:T(8,128)(2,1)} %bitcast_convert_fusion.refs_2_.g0_ref, bf16[512,2048]{1,0:T(8,128)(2,1)} %collective-permute-done.14.refs_3_.g1_ref, ...), custom_call_target="tpu_custom_call" | custom-call | flops 1000 | bytes 1000 | tf_op jit(solution)/shard_map/weight_pass/pallas_call | solution.py:515
  370.9 12.3 %gates_pass.3 = (bf16[1024,1152]{1,0:T(8,128)(2,1)}, bf16[1024,1152]{1,0:T(8,128)(2,1)}) custom-call(bf16[512,2048]{1,0:T(8,128)(2,1)} %bitcast_convert_fusion.refs_2_.g0_ref, bf16[512,2048]{1,0:T(8,128)(2,1)} %collective-permute-done.14.refs_3_.g1_ref, bf16[1152,2048]{1,0:T(8,128)(2,1)} %bitcast.284, bf16[1024,1152]{1,0:T(8,128)(2,1)} %get-tuple-element.226.gate_ref, ...), custom_call_target="tpu_custom_call" | custom-call | flops 1000 | bytes 1000 | tf_op jit(solution)/shard_map/gates_pass/pallas_call | solution.py:442
  383.1 15.9 %weight_pass.4 = bf16[2048,1152]{1,0:T(8,128)(2,1)} custom-call(bf16[512,2048]{1,0:T(8,128)(2,1)S(1)} %multiply_convert_fusion.n0_ref.refs_0_, bf16[512,2048]{1,0:T(8,128)(2,1)} %collective-permute-done.18.n1_ref.refs_1_, bf16[512,2048]{1,0:T(8,128)(2,1)} %collective-permute-done.19.n0_ref.refs_2_, bf16[512,2048]{1,0:T(8,128)(2,1)} %collective-permute-done.21.n1_ref.refs_3_, ...), custom_call_target="tpu_custom_call" | custom-call | flops 1000 | bytes 1000 | tf_op jit(solution)/shard_map/weight_pass/pallas_call | solution.py:515
  399.1 14.9 %back_pass.5 = (f32[512,2048]{1,0:T(8,128)}, bf16[512,2048]{1,0:T(8,128)(2,1)}) custom-call(bf16[1024,1152]{1,0:T(8,128)(2,1)S(1)} %copy-done.13, bf16[1024,1152]{1,0:T(8,128)(2,1)} %get-tuple-element.234.refs_1_.refs_4_, bf16[2048,1152]{1,0:T(8,128)(2,1)} %bitcast.278, bf16[2048,1152]{1,0:T(8,128)(2,1)} %bitcast.282), custom_call_target="tpu_custom_call" | custom-call | flops 1000 | bytes 1000 | tf_op jit(solution)/shard_map/back_pass/pallas_call | solution.py:481
  414.0 16.2 %weight_pass.5 = bf16[2048,1152]{1,0:T(8,128)(2,1)} custom-call(bf16[512,2048]{1,0:T(8,128)(2,1)S(1)} %multiply_convert_fusion.n0_ref.refs_0_, bf16[512,2048]{1,0:T(8,128)(2,1)} %collective-permute-done.18.n1_ref.refs_1_, bf16[512,2048]{1,0:T(8,128)(2,1)} %collective-permute-done.19.n0_ref.refs_2_, bf16[512,2048]{1,0:T(8,128)(2,1)} %collective-permute-done.21.n1_ref.refs_3_, ...), custom_call_target="tpu_custom_call" | custom-call | flops 1000 | bytes 1000 | tf_op jit(solution)/shard_map/weight_pass/pallas_call | solution.py:515
  456.9 11.0 %attend_backward.2 = (bf16[512,512]{1,0:T(8,128)(2,1)S(1)}, bf16[2048,256]{1,0:T(8,128)(2,1)S(1)}) custom-call(s32[1]{0:T(128)} %bitcast.place_ref, bf16[512,1280]{1,0:T(8,128)(2,1)S(1)} %copy-done.8, bf16[2048,640]{1,0:T(8,128)(2,1)} %all-gather.14.cloned.1.call-done.k_ref.v_ref, bf16[2048,640]{1,0:T(8,128)(2,1)} %all-gather.14.cloned.1.call-done.k_ref.v_ref, ...), custom_call_target="tpu_custom_call" | custom-call | flops 1000 | bytes 1000 | tf_op jit(solution)/shard_map/attend_backward/pallas_call | solution.py:363
  470.0 13.3 %reduce-scatter.7.cloned.1.call-done = bf16[1,144,2048]{2,1,0:T(8,128)(2,1)} async-done(((bf16[4,144,2048]{2,1,0:T(8,128)(2,1)}), bf16[1,144,2048]{2,1,0:T(8,128)(2,1)}) %reduce-scatter.7.cloned.1.call-update) | async-done | bytes 589840 | tf_op jit(solution)/shard_map/reduce_scatter | solution.py:719
  518.1 16.9 %attend_backward.3 = (bf16[512,768]{1,0:T(8,128)(2,1)S(1)}, bf16[2048,384]{1,0:T(8,128)(2,1)}) custom-call(s32[1]{0:T(128)} %bitcast.place_ref, bf16[512,1280]{1,0:T(8,128)(2,1)S(1)} %copy-done.8, bf16[2048,640]{1,0:T(8,128)(2,1)} %all-gather.14.cloned.1.call-done.k_ref.v_ref, bf16[2048,640]{1,0:T(8,128)(2,1)} %all-gather.14.cloned.1.call-done.k_ref.v_ref, ...), custom_call_target="tpu_custom_call" | custom-call | flops 1000 | bytes 1000 | tf_op jit(solution)/shard_map/attend_backward/pallas_call | solution.py:363
  535.0 26.4 %collective-permute-done.30 = bf16[2,2,4,64,1152]{4,3,1,0,2:T(8,128)(2,1)} collective-permute-done((bf16[2,2,4,64,1152]{4,3,1,0,2:T(8,128)(2,1)S(1)}, bf16[2,2,4,64,1152]{4,3,1,0,2:T(8,128)(2,1)}, u32[]{:S(2)}, u32[]{:S(2)}) %collective-permute-start.30) | collective-permute-done | bytes 2359328 | tf_op jit(solution)/shard_map/ppermute | solution.py:618
  564.6 8.8 %reduce-scatter.11.cloned.1.call-done = bf16[1,2,2,64,1152]{4,3,2,1,0:T(8,128)(2,1)} async-done(((bf16[4,2,2,64,1152]{4,3,2,1,0:T(8,128)(2,1)}), bf16[1,2,2,64,1152]{4,3,2,1,0:T(8,128)(2,1)}) %reduce-scatter.11.cloned.1.call-update) | async-done | bytes 589840 | tf_op jit(solution)/shard_map/reduce_scatter | solution.py:719
  577.2 9.0 %heads_backward.2 = (bf16[512,1280]{1,0:T(8,128)(2,1)}, f32[8,1280]{1,0:T(8,128)}) custom-call(bf16[512,1280]{1,0:T(8,128)(2,1)} %pad_maximum_fusion.3.grad_ref, f32[512,1280]{1,0:T(8,128)} %get-tuple-element.261.joint_ref, f32[8,1280]{1,0:T(8,128)} %copy-done.30, f32[512,128]{1,0:T(8,128)} %copy-done.14, f32[512,128]{1,0:T(8,128)} %copy-done.15), custom_call_target="tpu_custom_call" | custom-call | flops 1000 | bytes 1000 | tf_op jit(solution)/shard_map/heads_backward/pallas_call | solution.py:158
  648.5 11.6 %collective-permute-done.33 = bf16[2,4,64,1280]{3,2,1,0:T(8,128)(2,1)} collective-permute-done((bf16[2,4,64,1280]{3,2,1,0:T(8,128)(2,1)}, bf16[2,4,64,1280]{3,2,1,0:T(8,128)(2,1)}, u32[]{:S(2)}, u32[]{:S(2)}) %collective-permute-start.33) | collective-permute-done | bytes 1310752 | tf_op jit(solution)/shard_map/ppermute | solution.py:618
  (424 shorter events, 354.1 us)
Async XLA Ops:
  9.8 130.4 %all-gather.16.cloned.1.call-start = ((), (), s32[]{:S(2)}) async-start(), calls=%async_computation.14 | async-start | bytes 2949120 | tf_op jit(solution)/shard_map/all_gather | solution.py:715
  53.2 119.9 %all-gather.14.cloned.1.call-start = ((), (), s32[]{:S(2)}) async-start(), calls=%async_computation.13 | async-start | bytes 3276800 | tf_op jit(solution)/shard_map/all_gather | solution.py:715
  53.4 48.3 %collective-permute-start.10 = (bf16[144,2048]{1,0:T(8,128)(2,1)}, bf16[144,2048]{1,0:T(8,128)(2,1)}, u32[]{:S(2)}, u32[]{:S(2)}) collective-permute-start(bf16[144,2048]{1,0:T(8,128)(2,1)} %param.20), channel_id=1, source_target_pairs={{0,16},{4,20},{8,24},{12,28},{16,0},{20,4},{24,8},{28,12},{1,17},{... | collective-permute-start | bytes 1769480 | tf_op jit(solution)/shard_map/ppermute | solution.py:618
  105.2 105.8 %all-gather.18.cloned.1.call-start = ((), (), s32[]{:S(2)}) async-start(), calls=%async_computation.15 | async-start | bytes 2949120 | tf_op jit(solution)/shard_map/all_gather | solution.py:715
  112.0 206.7 %all-gather.20.cloned.1.call-start = ((), (), s32[]{:S(2)}) async-start(), calls=%async_computation.16 | async-start | bytes 5898240 | tf_op jit(solution)/shard_map/all_gather | solution.py:715
  168.9 48.4 %collective-permute-start.16 = (bf16[2,2,4,64,1280]{4,3,2,1,0:T(8,128)(2,1)}, bf16[2,2,4,64,1280]{4,3,2,1,0:T(8,128)(2,1)}, u32[]{:S(2)}, u32[]{:S(2)}) collective-permute-start(bf16[2,2,4,64,1280]{4,3,2,1,0:T(8,128)(2,1)} %bitcast.63), channel_id=1, source_target_pairs={{0,4},{4,0},{8,12},{12,8},{16,20},{20,16},{24,28},{28,24},{1,5},{5... | collective-permute-start | bytes 7864328 | tf_op jit(solution)/shard_map/ppermute | solution.py:618
  169.4 47.9 %collective-permute-start.15 = (bf16[512,2048]{1,0:T(8,128)(2,1)}, bf16[512,2048]{1,0:T(8,128)(2,1)}, u32[]{:S(2)}, u32[]{:S(2)}) collective-permute-start(bf16[512,2048]{1,0:T(8,128)(2,1)} %bitcast_convert_fusion.refs_2_.g0_ref), channel_id=1, source_target_pairs={{0,8},{4,12},{8,0},{12,4},{16,24},{20,28},{24,16},{28,20},{1,9},{5... | collective-permute-start | bytes 6291464 | tf_op jit(solution)/shard_map/ppermute | solution.py:618
  170.8 46.5 %collective-permute-start.14 = (bf16[512,2048]{1,0:T(8,128)(2,1)}, bf16[512,2048]{1,0:T(8,128)(2,1)}, u32[]{:S(2)}, u32[]{:S(2)}) collective-permute-start(bf16[512,2048]{1,0:T(8,128)(2,1)} %bitcast_convert_fusion.refs_2_.g0_ref), channel_id=1, source_target_pairs={{0,4},{4,0},{8,12},{12,8},{16,20},{20,16},{24,28},{28,24},{1,5},{5... | collective-permute-start | bytes 6291464 | tf_op jit(solution)/shard_map/ppermute | solution.py:618
  173.1 310.2 %reduce-scatter.7.cloned.1.call-start = ((), (), s32[]{:S(2)}) async-start(), calls=%async_computation.6 | async-start | bytes 2949120 | tf_op jit(solution)/shard_map/reduce_scatter | solution.py:719
  173.6 58.8 %collective-permute-start.17 = (bf16[4,2,2,64,1152]{4,3,2,1,0:T(8,128)(2,1)}, bf16[4,2,2,64,1152]{4,3,2,1,0:T(8,128)(2,1)}, u32[]{:S(2)}, u32[]{:S(2)}) collective-permute-start(bf16[4,2,2,64,1152]{4,3,2,1,0:T(8,128)(2,1)} %bitcast.315), channel_id=1, source_target_pairs={{0,16},{4,20},{8,24},{12,28},{16,0},{20,4},{24,8},{28,12},{1,17},{... | collective-permute-start | bytes 7077896 | tf_op jit(solution)/shard_map/ppermute | solution.py:618
  217.3 62.0 %collective-permute-start.20 = (bf16[4,2,2,64,1152]{4,3,2,1,0:T(8,128)(2,1)}, bf16[4,2,2,64,1152]{4,3,2,1,0:T(8,128)(2,1)}, u32[]{:S(2)}, u32[]{:S(2)}) collective-permute-start(bf16[4,2,2,64,1152]{4,3,2,1,0:T(8,128)(2,1)} %bitcast.317), channel_id=1, source_target_pairs={{0,16},{4,20},{8,24},{12,28},{16,0},{20,4},{24,8},{28,12},{1,17},{... | collective-permute-start | bytes 7077896 | tf_op jit(solution)/shard_map/ppermute | solution.py:618
  232.4 46.9 %collective-permute-start.19 = (bf16[512,2048]{1,0:T(8,128)(2,1)S(1)}, bf16[512,2048]{1,0:T(8,128)(2,1)}, u32[]{:S(2)}, u32[]{:S(2)}) collective-permute-start(bf16[512,2048]{1,0:T(8,128)(2,1)S(1)} %multiply_convert_fusion.n0_ref.refs_0_), channel_id=1, source_target_pairs={{0,8},{4,12},{8,0},{12,4},{16,24},{20,28},{24,16},{28,20},{1,9},{5... | collective-permute-start | bytes 6291464 | tf_op jit(solution)/shard_map/ppermute | solution.py:618
  233.7 68.7 %collective-permute-start.22 = (bf16[512,2048]{1,0:T(8,128)(2,1)}, bf16[512,2048]{1,0:T(8,128)(2,1)}, u32[]{:S(2)}, u32[]{:S(2)}) collective-permute-start(bf16[512,2048]{1,0:T(8,128)(2,1)} %collective-permute-done.15.g0_ref.refs_4_), channel_id=1, source_target_pairs={{0,4},{4,0},{8,12},{12,8},{16,20},{20,16},{24,28},{28,24},{1,5},{5... | collective-permute-start | bytes 6291464 | tf_op jit(solution)/shard_map/ppermute | solution.py:618
  365.8 48.1 %collective-permute-start.24 = (bf16[512,2048]{1,0:T(8,128)(2,1)}, bf16[512,2048]{1,0:T(8,128)(2,1)}, u32[]{:S(2)}, u32[]{:S(2)}) collective-permute-start(bf16[512,2048]{1,0:T(8,128)(2,1)} %add_convert_fusion.2), channel_id=1, source_target_pairs={{0,8},{4,12},{8,0},{12,4},{16,24},{20,28},{24,16},{28,20},{1,9},{5... | collective-permute-start | bytes 6291464 | tf_op jit(solution)/shard_map/ppermute | solution.py:618
  370.5 59.7 %collective-permute-start.26 = (bf16[4,144,2048]{2,1,0:T(8,128)(2,1)}, bf16[4,144,2048]{2,1,0:T(8,128)(2,1)}, u32[]{:S(2)}, u32[]{:S(2)}) collective-permute-start(bf16[4,144,2048]{2,1,0:T(8,128)(2,1)} %dynamic-slice_bitcast_fusion.1), channel_id=1, source_target_pairs={{0,16},{4,20},{8,24},{12,28},{16,0},{20,4},{24,8},{28,12},{1,17},{... | collective-permute-start | bytes 7077896 | tf_op jit(solution)/shard_map/ppermute | solution.py:618
  435.1 126.3 %reduce-scatter.9.cloned.1.call-start = ((), (), s32[]{:S(2)}) async-start(), calls=%async_computation.7 | async-start | bytes 1310720 | tf_op jit(solution)/shard_map/reduce_scatter | solution.py:719
  443.3 57.6 %collective-permute-start.28 = (bf16[2,2,4,64,1152]{4,3,1,0,2:T(8,128)(2,1)}, bf16[2,2,4,64,1152]{4,3,1,0,2:T(8,128)(2,1)}, u32[]{:S(2)}, u32[]{:S(2)}) collective-permute-start(bf16[2,2,4,64,1152]{4,3,1,0,2:T(8,128)(2,1)} %copy_bitcast_fusion.2), channel_id=1, source_target_pairs={{0,16},{4,20},{8,24},{12,28},{16,0},{20,4},{24,8},{28,12},{1,17},{... | collective-permute-start | bytes 7077896 | tf_op jit(solution)/shard_map/ppermute | solution.py:618
  493.2 80.1 %reduce-scatter.11.cloned.1.call-start = ((), (), s32[]{:S(2)}) async-start(), calls=%async_computation.8 | async-start | bytes 2949120 | tf_op jit(solution)/shard_map/reduce_scatter | solution.py:719
  505.6 105.6 %reduce-scatter.13.cloned.1.call-start = ((), (), s32[]{:S(2)}) async-start(), calls=%async_computation.9 | async-start | bytes 1966080 | tf_op jit(solution)/shard_map/reduce_scatter | solution.py:719
  507.6 53.9 %collective-permute-start.30 = (bf16[2,2,4,64,1152]{4,3,1,0,2:T(8,128)(2,1)S(1)}, bf16[2,2,4,64,1152]{4,3,1,0,2:T(8,128)(2,1)}, u32[]{:S(2)}, u32[]{:S(2)}) collective-permute-start(bf16[2,2,4,64,1152]{4,3,1,0,2:T(8,128)(2,1)S(1)} %copy_bitcast_fusion.1), channel_id=1, source_target_pairs={{0,16},{4,20},{8,24},{12,28},{16,0},{20,4},{24,8},{28,12},{1,17},{... | collective-permute-start | bytes 7077896 | tf_op jit(solution)/shard_map/ppermute | solution.py:618
  512.5 52.1 %collective-permute-start.29 = (bf16[2,2,4,64,1280]{4,3,2,1,0:T(8,128)(2,1)}, bf16[2,2,4,64,1280]{4,3,2,1,0:T(8,128)(2,1)}, u32[]{:S(2)}, u32[]{:S(2)}) collective-permute-start(bf16[2,2,4,64,1280]{4,3,2,1,0:T(8,128)(2,1)} %dynamic-slice_bitcast_fusion), channel_id=1, source_target_pairs={{0,4},{4,0},{8,12},{12,8},{16,20},{20,16},{24,28},{28,24},{1,5},{5... | collective-permute-start | bytes 7864328 | tf_op jit(solution)/shard_map/ppermute | solution.py:618
  516.6 48.0 %collective-permute-start.31 = (bf16[512,2048]{1,0:T(8,128)(2,1)}, bf16[512,2048]{1,0:T(8,128)(2,1)}, u32[]{:S(2)}, u32[]{:S(2)}) collective-permute-start(bf16[512,2048]{1,0:T(8,128)(2,1)} %add_convert_fusion.1), channel_id=1, source_target_pairs={{0,8},{4,12},{8,0},{12,4},{16,24},{20,28},{24,16},{28,20},{1,9},{5... | collective-permute-start | bytes 6291464 | tf_op jit(solution)/shard_map/ppermute | solution.py:618
  576.0 109.0 %reduce-scatter.15.cloned.1.call-start = ((), (), s32[]{:S(2)}) async-start(), calls=%async_computation.10 | async-start | bytes 2949120 | tf_op jit(solution)/shard_map/reduce_scatter | solution.py:719
  615.8 122.8 %reduce-scatter.17.cloned.1.call-start = ((), (), s32[]{:S(2)}) async-start(), calls=%async_computation.11 | async-start | bytes 2129920 | tf_op jit(solution)/shard_map/reduce_scatter | solution.py:719
  (107 other events, 1133.8 us)
Sparse Core Ops, SparseCore 0:
  10.2 41.6 all-gather.11
  53.4 49.5 all-gather.15
  105.3 54.9 all-gather.13
  161.7 49.2 all-gather.17
  213.0 88.2 all-gather.19
  435.2 48.0 reduce-scatter.6
  493.3 30.8 reduce-scatter.8
  526.6 46.7 reduce-scatter.10
  576.3 34.7 reduce-scatter.12
  615.9 47.1 reduce-scatter.14
  703.6 34.9 reduce-scatter.16

commit v9 on v8

--- a/solution.py
+++ b/solution.py
@@ -60,11 +60,7 @@
     )
 
 
-def heads_forward_kernel(
-    norm_columns, normed_ref, weight_ref, gain_ref, cos_ref, sin_ref, joint_ref, out_ref
-):
-    joint = dot_nn(normed_ref[...], weight_ref[...])
-    joint_ref[...] = joint
+def heads_of(joint, norm_columns, gain_ref, cos_ref, sin_ref, out_ref):
     columns = joint.shape[1]
     for start in range(0, columns, LANES):
         chunk = slice(start, start + LANES)
@@ -74,6 +70,60 @@
         turned = normed * cos_ref[...] + partner(normed) * sin_ref[...]
         place = pl.program_id(0) * columns + start + lanes_of(values.shape)
         out_ref[:, chunk] = jnp.where(place < norm_columns, turned, values).astype(bf16)
+
+
+def heads_forward_kernel(
+    norm_columns, normed_ref, weight_ref, gain_ref, cos_ref, sin_ref, joint_ref, out_ref
+):
+    joint = dot_nn(normed_ref[...], weight_ref[...])
+    joint_ref[...] = joint
+    heads_of(joint, norm_columns, gain_ref, cos_ref, sin_ref, out_ref)
+
+
+def heads_halves_kernel(
+    side_ref, normed_ref, own_ref, other_ref, gain_ref, cos_ref, sin_ref, joint_ref, out_ref
+):
+    count, block, _ = own_ref.shape
+    joint = None
+    for index in range(count):
+        for weight_ref, side in ((own_ref, side_ref[0]), (other_ref, 1 - side_ref[0])):
+            rows = pl.ds(pl.multiple_of((2 * index + side) * block, block), block)
+            term = dot_nn(normed_ref[:, rows], weight_ref[index])
+            joint = term if joint is None else joint + term
+    joint_ref[...] = joint
+    heads_of(joint, QUERY_COLUMNS, gain_ref, cos_ref, sin_ref, out_ref)
+
+
+def heads_forward_halves(normed, own, other, side, gain, cos, sin):
+    tokens, width = normed.shape
+    count, block, columns = own.shape
+    tile = 2 * LANES
+    out = pl.BlockSpec((tokens, tile), lambda i, s: (0, i))
+    table = pl.BlockSpec((tokens, LANES), lambda i, s: (0, 0))
+    weight = pl.BlockSpec((count, block, tile), lambda i, s: (0, 0, i))
+    return pl.pallas_call(
+        heads_halves_kernel,
+        grid_spec=pltpu.PrefetchScalarGridSpec(
+            num_scalar_prefetch=1,
+            grid=(columns // tile,),
+            in_specs=[
+                pl.BlockSpec((tokens, width), lambda i, s: (0, 0)),
+                weight,
+                weight,
+                pl.BlockSpec((8, tile), lambda i, s: (0, i)),
+                table,
+                table,
+            ],
+            out_specs=[out, out],
+        ),
+        out_shape=[
+            jax.ShapeDtypeStruct((tokens, columns), f32),
+            jax.ShapeDtypeStruct((tokens, columns), bf16),
+        ],
+        compiler_params=pltpu.CompilerParams(vmem_limit_bytes=VMEM_LIMIT),
+        name="heads_forward_halves",
+        cost_estimate=LIGHT,
+    )(side.astype(jnp.int32).reshape(1), normed, own, other, gain, cos, sin)
 
 
 def heads_forward(normed, weight, gain, cos, sin, norm_columns):
@@ -104,27 +154,24 @@
 
 
 def project_kernel(side_ref, mixed_ref, own_ref, other_ref, inputs_ref, out_ref):
-    mine = pl.program_id(0) % 2 == side_ref[0]
-
-    @pl.when(mine)
-    def _():
-        out_ref[...] = inputs_ref[...].astype(f32) + dot_nt(mixed_ref[...], own_ref[0])
-
-    @pl.when(jnp.logical_not(mine))
-    def _():
-        out_ref[...] = inputs_ref[...].astype(f32) + dot_nt(mixed_ref[...], other_ref[0])
+    block = own_ref.shape[1]
+    for weight_ref, side in ((own_ref, side_ref[0]), (other_ref, 1 - side_ref[0])):
+        columns = pl.ds(pl.multiple_of(side * block, block), block)
+        out_ref[:, columns] = inputs_ref[:, columns].astype(f32) + dot_nt(
+            mixed_ref[...], weight_ref[0]
+        )
 
 
 def project(mixed, own, other, inputs, side):
     tokens, depth = mixed.shape
     count, block, _ = own.shape
-    weight = pl.BlockSpec((1, block, depth), lambda i, s: (i // 2, 0, 0))
-    out = pl.BlockSpec((tokens, block), lambda i, s: (0, i))
+    weight = pl.BlockSpec((1, block, depth), lambda i, s: (i, 0, 0))
+    out = pl.BlockSpec((tokens, 2 * block), lambda i, s: (0, i))
     return pl.pallas_call(
         project_kernel,
         grid_spec=pltpu.PrefetchScalarGridSpec(
             num_scalar_prefetch=1,
-            grid=(2 * count,),
+            grid=(count,),
             in_specs=[pl.BlockSpec((tokens, depth), lambda i, s: (0, 0)), weight, weight, out],
             out_specs=out,
         ),
@@ -530,34 +577,37 @@
 
     @pl.when(mine)
     def _():
-        out_ref[0, 0] = own_ref[:, 0]
+        for g in range(out_ref.shape[1]):
+            out_ref[0, g] = own_ref[:, g]
 
     @pl.when(jnp.logical_not(mine))
     def _():
-        out_ref[0, 0] = other_ref[:, 0]
+        for g in range(out_ref.shape[1]):
+            out_ref[0, g] = other_ref[:, g]
 
 
 def placed(own, other, side):
     seq, group, rows, columns = own.shape
 
     def entry(mine, e, g, s):
-        parked = jnp.where(e == 0, 0, group - 1)
+        parked = jnp.where(e == 0, 0, group // 2 - 1)
         return (0, jnp.where((e == s[0]) == mine, g, parked), 0, 0)
 
     return pl.pallas_call(
         placed_kernel,
         grid_spec=pltpu.PrefetchScalarGridSpec(
             num_scalar_prefetch=1,
-            grid=(2, group),
+            grid=(2, group // 2),
             in_specs=[
-                pl.BlockSpec((seq, 1, rows, columns), partial(entry, True)),
-                pl.BlockSpec((seq, 1, rows, columns), partial(entry, False)),
+                pl.BlockSpec((seq, 2, rows, columns), partial(entry, True)),
+                pl.BlockSpec((seq, 2, rows, columns), partial(entry, False)),
             ],
             out_specs=pl.BlockSpec(
-                (1, 1, seq, rows, columns), lambda e, g, s: (e, g, 0, 0, 0)
+                (1, 2, seq, rows, columns), lambda e, g, s: (e, g, 0, 0, 0)
             ),
         ),
         out_shape=jax.ShapeDtypeStruct((2, group, seq, rows, columns), own.dtype),
+        compiler_params=pltpu.CompilerParams(vmem_limit_bytes=VMEM_LIMIT),
         name="placed",
         cost_estimate=LIGHT,
     )(side.astype(jnp.int32).reshape(1), own, other)
@@ -853,19 +903,21 @@
     joint_kv, own_kv = heads_forward(
         normed, wkv, wide_k, cos_table, sin_table, KEY_COLUMNS
     )
-    own_kv, q_left_other, q_right_other, down_other, up_in = stage(
-        own_kv, q_left_other, q_right_other, send_outer(w_down), gate_up[:, :, 1]
+    own_kv, q_left_other, q_right_other, up_in = stage(
+        own_kv, q_left_other, q_right_other, gate_up[:, :, 1]
     )
     up_lines = gather_seq(up_in)
     keys_values = gather_seq(own_kv).reshape(-1, 2 * KEY_COLUMNS)
     q_left = join_outer(q_left, q_left_other, 0)
     q_right = joined(q_right, q_right_other, near, 0)
-    left_other, right_other, gate_lines = stage(
-        swap(q_left, 2), send_outer(q_right), gate_lines
+    left_other, right_other, gate_lines, w_down = stage(
+        swap(q_left, 2), send_outer(q_right), gate_lines, w_down
     )
     q_left = joined(q_left, left_other, near, 1)
     gate_other = send_outer(gate_lines)
-    wq = gather_bit(q_left, 1, 2).reshape(width, -1)
+    down_other = send_outer(w_down)
+    half_rows = (2 * outer, seq_devices * d_rows, QUERY_COLUMNS)
+    q_left_other = swap(q_left, 1)
 
     corpora = jnp.arange(CORPORA, dtype=jnp.int32)
     per_device = corpus_full.reshape(-1, d_rows)[:, 0].astype(jnp.int32)
@@ -877,10 +929,11 @@
     count_row = jnp.sum(own_corpus * counts)
     factor = weight_row / DENOM * (jnp.sum(counts) / (CORPORA * count_row))
     grad_full = upstream[0].astype(f32) * factor
-    grad_top, wq = stage(grad_full.astype(bf16), wq)
-
-    joint_q, queries = heads_forward(
-        normed, wq, wide_q, cos_table, sin_table, QUERY_COLUMNS
+    grad_top, q_left, q_left_other = stage(grad_full.astype(bf16), q_left, q_left_other)
+
+    q_halves = (q_left.reshape(half_rows), q_left_other.reshape(half_rows))
+    joint_q, queries = heads_forward_halves(
+        normed, *q_halves, core, wide_q, cos_table, sin_table
     )
     queries, q_right, right_other, down_other = stage(queries, q_right, right_other, down_other)
     q_right = join_outer(q_right, right_other, 0)
@@ -892,7 +945,6 @@
     mixed, grad_top1, grad_top2, up_lines, wout_other = stage(
         mixed, swap(grad_top, 1), swap(grad_top, 2), up_lines, swap(q_right, 1)
     )
-    half_rows = (2 * outer, seq_devices * d_rows, QUERY_COLUMNS)
     middle = project(
         mixed, q_right.reshape(half_rows), wout_other.reshape(half_rows), tokens_in[0], core
     )
@@ -900,9 +952,10 @@
     ffn_scale = norm_scale(middle)
     normed_ffn = (middle * ffn_scale * ffn_gain_full).astype(bf16)
     up_other = send_outer(up_lines)
-    normed_ffn, gate_other, q_right, wout_other = stage(
-        normed_ffn, gate_other, q_right, wout_other
-    )
+    normed_ffn, gate_other, q_right, wout_other, q_left, q_left_other = stage(
+        normed_ffn, gate_other, q_right, wout_other, q_left, q_left_other
+    )
+    wq = joined(q_left, q_left_other, core, 2).reshape(width, -1)
     wout_t = joined(q_right, wout_other, core, 2).reshape(width, -1)
     normed1, normed2, up_other, wgate = stage(
         swap(normed_ffn, 1),

time: 760 us -> 756 us (level)
  local copies, waits for them, and re-layouts: 68.3 us -> 78.5 us
  Pallas kernels: 271 us -> 261 us
    all_gather x5, waiting for transfers between devices: 25.1 us -> 40.8 us  [gather_seq(): return lax.all_gather(values, 'seq', axis=0, tiled=False)]
    ppermute x46, waiting for transfers between devices: 155 us -> 143 us  [swap(): return lax.ppermute(values, 'rows', pairs)]
    unnamed x139 -> x159, local copies, waits for them, and re-layouts: 17.2 us -> 26.5 us
    pallas_call x0 -> x1, Pallas kernels: none -> 8.8 us  [heads_forward_halves(): pl.pallas_call(heads_halves_kernel, grid_spec=pltpu.PrefetchScalarGridSpe...]
    pallas_call x2 -> x1, Pallas kernels: 15.6 us -> 7.3 us  [heads_forward(): pl.pallas_call(partial(heads_forward_kernel, norm_columns), grid=(columns...]
  transfers between devices with their start and end apart: 62 -> 62, of which waited for: 28 -> 28; matrix products, arithmetic and copies ran while one was open for 19% -> 19% of each run, Pallas kernels for 32% -> 31%
where the time goes in v9:
time: 756 us; the launch traced here: 746 us
  Pallas kernels  261 us (35%)
  waiting for transfers between devices  210 us (28%)
  other arithmetic  82.8 us (11%)
  local copies, waits for them, and re-layouts  78.5 us (10%)
  starting transfers between devices  42.1 us (6%)
  matrix products  33.2 us (4%)
  blocking collectives  19.9 us (3%)
  between operations  18.3 us (2%)
    ppermute x46, waiting for transfers between devices, swap(): return lax.ppermute(values, 'rows', pairs)  143 us
    pallas_call x3, Pallas kernels, weight_pass(): pl.pallas_call(partial(weight_kernel, len(lefts)), grid=(rows // tile,),...  47.8 us
    pallas_call x4, Pallas kernels, back_pass(): pl.pallas_call(partial(back_kernel, count, transposed), grid=(width // ti...  46.1 us
    all_gather x5, waiting for transfers between devices, gather_seq(): return lax.all_gather(values, 'seq', axis=0, tiled=False)  40.8 us
    ppermute x46, starting transfers between devices, swap(): return lax.ppermute(values, 'rows', pairs)  37.2 us
    pallas_call x2, Pallas kernels, hidden_pass(): pl.pallas_call(hidden_kernel, grid=(pl.cdiv(columns, tile),), in_specs=[w...  29.8 us
    pallas_call x2, Pallas kernels, attend_backward(): pl.pallas_call(partial(attend_backward_kernel, first, count), grid_spec=p...  27.9 us
    unnamed x159, local copies, waits for them, and re-layouts  26.5 us
  transfers between devices with their start and end apart: 62, of which 28 were waited for; matrix products, arithmetic and copies ran while one was open for 19% of the time, Pallas kernels for 31%

profile of v9, /device:TPU:0, one launch (start us, length us, event | category | flops | bytes accessed | tf_op | source)
XLA Modules:
  0.0 745.8 jit_solution(9236048421434440586)
XLA Ops:
  28.3 19.9 %all-gather = bf16[256,768]{1,0:T(8,128)(2,1)S(1)} all-gather(bf16[64,768]{1,0:T(8,128)(2,1)S(1)} %fusion.35), channel_id=2, replica_groups=mesh['rows'=8,'seq'=4] {'seq'}, dimensions={0}, use_global_device_ids=true | all-gather | bytes 491520 | tf_op jit(solution)/shard_map/all_gather | solution.py:765
  99.2 27.7 %collective-permute-done.11 = bf16[2,4,64,1280]{3,2,1,0:T(8,128)(2,1)} collective-permute-done((bf16[2,4,64,1280]{3,2,1,0:T(8,128)(2,1)}, bf16[2,4,64,1280]{3,2,1,0:T(8,128)(2,1)}, u32[]{:S(2)}, u32[]{:S(2)}) %collective-permute-start.11) | collective-permute-done | bytes 1310752 | tf_op jit(solution)/shard_map/ppermute | solution.py:668
  139.8 8.8 %heads_forward_halves.1 = (f32[512,1280]{1,0:T(8,128)}, bf16[512,1280]{1,0:T(8,128)(2,1)S(1)}) custom-call(s32[1]{0:T(128)} %bitcast.2.side_ref, bf16[512,2048]{1,0:T(8,128)(2,1)S(1)} %copy-done.3, bf16[4,256,1280]{2,1,0:T(8,128)(2,1)} %bitcast.54.own_ref, bf16[4,256,1280]{2,1,0:T(8,128)(2,1)} %bitcast.55.other_ref, ...), custom_call_target="tpu_custom_call" | custom-call | flops 1000 | bytes 1000 | tf_op jit(solution)/shard_map/heads_forward_halves/pallas_call | solution.py:104
  162.1 11.7 %attend_forward.1 = (bf16[512,1280]{1,0:T(8,128)(2,1)S(1)}, f32[512,1280]{1,0:T(8,128)S(1)}) custom-call(s32[1]{0:T(128)} %bitcast.place_ref, bf16[512,1280]{1,0:T(8,128)(2,1)S(1)} %copy-done.12, bf16[2048,640]{1,0:T(8,128)(2,1)} %all-gather.14.cloned.1.call-done.k_ref.v_ref, bf16[2048,640]{1,0:T(8,128)(2,1)} %all-gather.14.cloned.1.call-done.k_ref.v_ref), custom_call_target="tpu_custom_call" | custom-call | flops 1000 | bytes 1000 | tf_op jit(solution)/shard_map/attend_forward/pallas_call | solution.py:273
  175.3 34.2 %all-gather.18.cloned.1.call-done = bf16[8,2,64,1152]{3,2,1,0:T(8,128)(2,1)} async-done(((bf16[2,2,64,1152]{3,2,1,0:T(8,128)(2,1)}), bf16[8,2,64,1152]{3,2,1,0:T(8,128)(2,1)}) %all-gather.18.cloned.1.call-update) | async-done | bytes 2359312 | tf_op jit(solution)/shard_map/all_gather | solution.py:765
  229.9 39.8 %collective-permute-done.19.n0_ref.refs_2_ = bf16[512,2048]{1,0:T(8,128)(2,1)S(1)} collective-permute-done((bf16[512,2048]{1,0:T(8,128)(2,1)S(1)}, bf16[512,2048]{1,0:T(8,128)(2,1)S(1)}, u32[]{:S(2)}, u32[]{:S(2)}) %collective-permute-start.19) | collective-permute-done | bytes 2097184 | tf_op jit(solution)/shard_map/ppermute | solution.py:668
  278.2 14.9 %hidden_pass.2 = (bf16[1024,1152]{1,0:T(8,128)(2,1)}, bf16[1024,1152]{1,0:T(8,128)(2,1)}, bf16[1024,1152]{1,0:T(8,128)(2,1)}) custom-call(bf16[512,2048]{1,0:T(8,128)(2,1)S(1)} %multiply_convert_fusion.n0_ref.refs_0_, bf16[512,2048]{1,0:T(8,128)(2,1)S(1)} %collective-permute-done.18.n1_ref.refs_1_, bf16[2048,1152]{1,0:T(8,128)(2,1)} %bitcast.282, ...), custom_call_target="tpu_custom_call" | custom-call | flops 1000 | bytes 1000 | tf_op jit(solution)/shard_map/hidden_pass/pallas_call | solution.py:454
  294.4 14.9 %hidden_pass.3 = (bf16[1024,1152]{1,0:T(8,128)(2,1)}, bf16[1024,1152]{1,0:T(8,128)(2,1)}, bf16[1024,1152]{1,0:T(8,128)(2,1)}) custom-call(bf16[512,2048]{1,0:T(8,128)(2,1)S(1)} %collective-permute-done.19.n0_ref.refs_2_, bf16[512,2048]{1,0:T(8,128)(2,1)S(1)} %collective-permute-done.21.n1_ref.refs_3_, bf16[2048,1152]{1,0:T(8,128)(2,1)} %bitcast.283, ...), custom_call_target="tpu_custom_call" | custom-call | flops 1000 | bytes 1000 | tf_op jit(solution)/shard_map/hidden_pass/pallas_call | solution.py:454
  312.3 11.6 %gates_pass.2 = (bf16[1024,1152]{1,0:T(8,128)(2,1)}, bf16[1024,1152]{1,0:T(8,128)(2,1)}) custom-call(bf16[512,2048]{1,0:T(8,128)(2,1)} %collective-permute-done.15.g0_ref.refs_4_, bf16[512,2048]{1,0:T(8,128)(2,1)S(1)} %copy-done.20, bf16[1152,2048]{1,0:T(8,128)(2,1)} %bitcast.290, bf16[1024,1152]{1,0:T(8,128)(2,1)} %get-tuple-element.216.gate_ref, ...), custom_call_target="tpu_custom_call" | custom-call | flops 1000 | bytes 1000 | tf_op jit(solution)/shard_map/gates_pass/pallas_call | solution.py:489
  325.6 14.8 %back_pass.4 = (f32[512,2048]{1,0:T(8,128)}, bf16[512,2048]{1,0:T(8,128)(2,1)S(1)}) custom-call(bf16[1024,1152]{1,0:T(8,128)(2,1)S(1)} %copy-done.17, bf16[1024,1152]{1,0:T(8,128)(2,1)} %get-tuple-element.219.refs_1_.refs_5_, bf16[2048,1152]{1,0:T(8,128)(2,1)} %bitcast.284, bf16[2048,1152]{1,0:T(8,128)(2,1)} %bitcast.288), custom_call_target="tpu_custom_call" | custom-call | flops 1000 | bytes 1000 | tf_op jit(solution)/shard_map/back_pass/pallas_call | solution.py:528
  340.4 15.8 %weight_pass.3 = bf16[1152,2048]{1,0:T(8,128)(2,1)} custom-call(bf16[1024,1152]{1,0:T(8,128)(2,1)} %get-tuple-element.297.refs_0_, bf16[1024,1152]{1,0:T(8,128)(2,1)} %get-tuple-element.247.refs_1_.refs_0_, bf16[512,2048]{1,0:T(8,128)(2,1)} %bitcast_convert_fusion.refs_2_.g0_ref, bf16[512,2048]{1,0:T(8,128)(2,1)} %collective-permute-done.14.refs_3_.g1_ref, ...), custom_call_target="tpu_custom_call" | custom-call | flops 1000 | bytes 1000 | tf_op jit(solution)/shard_map/weight_pass/pallas_call | solution.py:562
  363.3 12.4 %gates_pass.3 = (bf16[1024,1152]{1,0:T(8,128)(2,1)}, bf16[1024,1152]{1,0:T(8,128)(2,1)}) custom-call(bf16[512,2048]{1,0:T(8,128)(2,1)} %bitcast_convert_fusion.refs_2_.g0_ref, bf16[512,2048]{1,0:T(8,128)(2,1)} %collective-permute-done.14.refs_3_.g1_ref, bf16[1152,2048]{1,0:T(8,128)(2,1)} %bitcast.291, bf16[1024,1152]{1,0:T(8,128)(2,1)} %get-tuple-element.230.gate_ref, ...), custom_call_target="tpu_custom_call" | custom-call | flops 1000 | bytes 1000 | tf_op jit(solution)/shard_map/gates_pass/pallas_call | solution.py:489
  375.7 15.9 %weight_pass.4 = bf16[2048,1152]{1,0:T(8,128)(2,1)} custom-call(bf16[512,2048]{1,0:T(8,128)(2,1)S(1)} %multiply_convert_fusion.n0_ref.refs_0_, bf16[512,2048]{1,0:T(8,128)(2,1)S(1)} %copy-done.8, bf16[512,2048]{1,0:T(8,128)(2,1)} %copy-done.6, bf16[512,2048]{1,0:T(8,128)(2,1)} %copy-done.10, bf16[1024,1152]{1,0:T(8,128)(2,1)} %get-tuple-element.232.refs_0_.refs_4_, ...), custom_call_target="tpu_custom_call" | custom-call | flops 1000 | bytes 1000 | tf_op jit(solution)/shard_map/weight_pass/pallas_call | solution.py:562
  391.6 14.9 %back_pass.5 = (f32[512,2048]{1,0:T(8,128)}, bf16[512,2048]{1,0:T(8,128)(2,1)}) custom-call(bf16[1024,1152]{1,0:T(8,128)(2,1)S(1)} %copy-done.18, bf16[1024,1152]{1,0:T(8,128)(2,1)} %get-tuple-element.238.refs_1_.refs_4_, bf16[2048,1152]{1,0:T(8,128)(2,1)} %bitcast.285, bf16[2048,1152]{1,0:T(8,128)(2,1)} %bitcast.289), custom_call_target="tpu_custom_call" | custom-call | flops 1000 | bytes 1000 | tf_op jit(solution)/shard_map/back_pass/pallas_call | solution.py:528
  408.3 16.1 %weight_pass.5 = bf16[2048,1152]{1,0:T(8,128)(2,1)} custom-call(bf16[512,2048]{1,0:T(8,128)(2,1)S(1)} %multiply_convert_fusion.n0_ref.refs_0_, bf16[512,2048]{1,0:T(8,128)(2,1)S(1)} %copy-done.9, bf16[512,2048]{1,0:T(8,128)(2,1)} %copy-done.6, bf16[512,2048]{1,0:T(8,128)(2,1)} %copy-done.10, bf16[1024,1152]{1,0:T(8,128)(2,1)} %get-tuple-element.238.refs_1_.refs_4_, ...), custom_call_target="tpu_custom_call" | custom-call | flops 1000 | bytes 1000 | tf_op jit(solution)/shard_map/weight_pass/pallas_call | solution.py:562
  451.4 11.0 %attend_backward.2 = (bf16[512,512]{1,0:T(8,128)(2,1)S(1)}, bf16[2048,256]{1,0:T(8,128)(2,1)S(1)}) custom-call(s32[1]{0:T(128)} %bitcast.place_ref, bf16[512,1280]{1,0:T(8,128)(2,1)S(1)} %copy-done.13, bf16[2048,640]{1,0:T(8,128)(2,1)} %all-gather.14.cloned.1.call-done.k_ref.v_ref, bf16[2048,640]{1,0:T(8,128)(2,1)} %all-gather.14.cloned.1.call-done.k_ref.v_ref, ...), custom_call_target="tpu_custom_call" | custom-call | flops 1000 | bytes 1000 | tf_op jit(solution)/shard_map/attend_backward/pallas_call | solution.py:410
  464.4 11.5 %reduce-scatter.7.cloned.1.call-done = bf16[1,144,2048]{2,1,0:T(8,128)(2,1)} async-done(((bf16[4,144,2048]{2,1,0:T(8,128)(2,1)}), bf16[1,144,2048]{2,1,0:T(8,128)(2,1)}) %reduce-scatter.7.cloned.1.call-update) | async-done | bytes 589840 | tf_op jit(solution)/shard_map/reduce_scatter | solution.py:769
  477.6 8.2 %back_pass.6 = (f32[512,2048]{1,0:T(8,128)}, bf16[512,2048]{1,0:T(8,128)(2,1)}) custom-call(bf16[1024,1152]{1,0:T(8,128)(2,1)S(1)} %copy-done.16, bf16[1152,2048]{1,0:T(8,128)(2,1)} %bitcast.292), custom_call_target="tpu_custom_call" | custom-call | flops 1000 | bytes 1000 | tf_op jit(solution)/shard_map/back_pass/pallas_call | solution.py:528
  510.6 16.9 %attend_backward.3 = (bf16[512,768]{1,0:T(8,128)(2,1)S(1)}, bf16[2048,384]{1,0:T(8,128)(2,1)}) custom-call(s32[1]{0:T(128)} %bitcast.place_ref, bf16[512,1280]{1,0:T(8,128)(2,1)S(1)} %copy-done.13, bf16[2048,640]{1,0:T(8,128)(2,1)} %all-gather.14.cloned.1.call-done.k_ref.v_ref, bf16[2048,640]{1,0:T(8,128)(2,1)} %all-gather.14.cloned.1.call-done.k_ref.v_ref, ...), custom_call_target="tpu_custom_call" | custom-call | flops 1000 | bytes 1000 | tf_op jit(solution)/shard_map/attend_backward/pallas_call | solution.py:410
  527.5 26.5 %collective-permute-done.30 = bf16[2,2,4,64,1152]{4,3,1,0,2:T(8,128)(2,1)} collective-permute-done((bf16[2,2,4,64,1152]{4,3,1,0,2:T(8,128)(2,1)S(1)}, bf16[2,2,4,64,1152]{4,3,1,0,2:T(8,128)(2,1)}, u32[]{:S(2)}, u32[]{:S(2)}) %collective-permute-start.30) | collective-permute-done | bytes 2359328 | tf_op jit(solution)/shard_map/ppermute | solution.py:668
  557.2 8.8 %reduce-scatter.11.cloned.1.call-done = bf16[1,2,2,64,1152]{4,3,2,1,0:T(8,128)(2,1)} async-done(((bf16[4,2,2,64,1152]{4,3,2,1,0:T(8,128)(2,1)}), bf16[1,2,2,64,1152]{4,3,2,1,0:T(8,128)(2,1)}) %reduce-scatter.11.cloned.1.call-update) | async-done | bytes 589840 | tf_op jit(solution)/shard_map/reduce_scatter | solution.py:769
  575.9 8.9 %heads_backward.2 = (bf16[512,1280]{1,0:T(8,128)(2,1)}, f32[8,1280]{1,0:T(8,128)}) custom-call(bf16[512,1280]{1,0:T(8,128)(2,1)} %pad_maximum_fusion.3.grad_ref, f32[512,1280]{1,0:T(8,128)} %get-tuple-element.265.joint_ref, f32[8,1280]{1,0:T(8,128)} %copy-done.40, f32[512,128]{1,0:T(8,128)} %copy-done.21, f32[512,128]{1,0:T(8,128)} %copy-done.22), custom_call_target="tpu_custom_call" | custom-call | flops 1000 | bytes 1000 | tf_op jit(solution)/shard_map/heads_backward/pallas_call | solution.py:205
  643.3 11.6 %collective-permute-done.33 = bf16[2,4,64,1280]{3,2,1,0:T(8,128)(2,1)} collective-permute-done((bf16[2,4,64,1280]{3,2,1,0:T(8,128)(2,1)}, bf16[2,4,64,1280]{3,2,1,0:T(8,128)(2,1)}, u32[]{:S(2)}, u32[]{:S(2)}) %collective-permute-start.33) | collective-permute-done | bytes 1310752 | tf_op jit(solution)/shard_map/ppermute | solution.py:668
  667.0 8.2 %back_pass.7 = (f32[512,2048]{1,0:T(8,128)}, bf16[512,2048]{1,0:T(8,128)(2,1)}) custom-call(bf16[1024,1152]{1,0:T(8,128)(2,1)S(1)} %copy-done.15, bf16[1152,2048]{1,0:T(8,128)(2,1)} %bitcast.293), custom_call_target="tpu_custom_call" | custom-call | flops 1000 | bytes 1000 | tf_op jit(solution)/shard_map/back_pass/pallas_call | solution.py:528
  (444 shorter events, 342.4 us)
Async XLA Ops:
  9.8 118.5 %all-gather.16.cloned.1.call-start = ((), (), s32[]{:S(2)}) async-start(), calls=%async_computation.14 | async-start | bytes 2949120 | tf_op jit(solution)/shard_map/all_gather | solution.py:765
  53.2 105.6 %all-gather.14.cloned.1.call-start = ((), (), s32[]{:S(2)}) async-start(), calls=%async_computation.13 | async-start | bytes 3276800 | tf_op jit(solution)/shard_map/all_gather | solution.py:765
  93.3 116.2 %all-gather.18.cloned.1.call-start = ((), (), s32[]{:S(2)}) async-start(), calls=%async_computation.15 | async-start | bytes 2949120 | tf_op jit(solution)/shard_map/all_gather | solution.py:765
  99.2 211.5 %all-gather.20.cloned.1.call-start = ((), (), s32[]{:S(2)}) async-start(), calls=%async_computation.16 | async-start | bytes 5898240 | tf_op jit(solution)/shard_map/all_gather | solution.py:765
  153.0 56.5 %collective-permute-start.16 = (bf16[2,2,4,64,1280]{4,3,2,1,0:T(8,128)(2,1)}, bf16[2,2,4,64,1280]{4,3,2,1,0:T(8,128)(2,1)}, u32[]{:S(2)}, u32[]{:S(2)}) collective-permute-start(bf16[2,2,4,64,1280]{4,3,2,1,0:T(8,128)(2,1)} %bitcast.62), channel_id=1, source_target_pairs={{0,4},{4,0},{8,12},{12,8},{16,20},{20,16},{24,28},{28,24},{1,5},{5... | collective-permute-start | bytes 7864328 | tf_op jit(solution)/shard_map/ppermute | solution.py:668
  153.2 56.3 %collective-permute-start.15 = (bf16[512,2048]{1,0:T(8,128)(2,1)}, bf16[512,2048]{1,0:T(8,128)(2,1)}, u32[]{:S(2)}, u32[]{:S(2)}) collective-permute-start(bf16[512,2048]{1,0:T(8,128)(2,1)} %bitcast_convert_fusion.refs_2_.g0_ref), channel_id=1, source_target_pairs={{0,8},{4,12},{8,0},{12,4},{16,24},{20,28},{24,16},{28,20},{1,9},{5... | collective-permute-start | bytes 6291464 | tf_op jit(solution)/shard_map/ppermute | solution.py:668
  153.7 55.8 %collective-permute-start.14 = (bf16[512,2048]{1,0:T(8,128)(2,1)}, bf16[512,2048]{1,0:T(8,128)(2,1)}, u32[]{:S(2)}, u32[]{:S(2)}) collective-permute-start(bf16[512,2048]{1,0:T(8,128)(2,1)} %bitcast_convert_fusion.refs_2_.g0_ref), channel_id=1, source_target_pairs={{0,4},{4,0},{8,12},{12,8},{16,20},{20,16},{24,28},{28,24},{1,5},{5... | collective-permute-start | bytes 6291464 | tf_op jit(solution)/shard_map/ppermute | solution.py:668
  158.8 317.2 %reduce-scatter.7.cloned.1.call-start = ((), (), s32[]{:S(2)}) async-start(), calls=%async_computation.6 | async-start | bytes 2949120 | tf_op jit(solution)/shard_map/reduce_scatter | solution.py:769
  159.3 63.1 %collective-permute-start.17 = (bf16[4,2,2,64,1152]{4,3,2,1,0:T(8,128)(2,1)}, bf16[4,2,2,64,1152]{4,3,2,1,0:T(8,128)(2,1)}, u32[]{:S(2)}, u32[]{:S(2)}) collective-permute-start(bf16[4,2,2,64,1152]{4,3,2,1,0:T(8,128)(2,1)} %bitcast.258), channel_id=1, source_target_pairs={{0,16},{4,20},{8,24},{12,28},{16,0},{20,4},{24,8},{28,12},{1,17},{... | collective-permute-start | bytes 7077896 | tf_op jit(solution)/shard_map/ppermute | solution.py:668
  209.5 60.1 %collective-permute-start.20 = (bf16[4,2,2,64,1152]{4,3,2,1,0:T(8,128)(2,1)}, bf16[4,2,2,64,1152]{4,3,2,1,0:T(8,128)(2,1)}, u32[]{:S(2)}, u32[]{:S(2)}) collective-permute-start(bf16[4,2,2,64,1152]{4,3,2,1,0:T(8,128)(2,1)} %bitcast.260), channel_id=1, source_target_pairs={{0,16},{4,20},{8,24},{12,28},{16,0},{20,4},{24,8},{28,12},{1,17},{... | collective-permute-start | bytes 7077896 | tf_op jit(solution)/shard_map/ppermute | solution.py:668
  222.4 47.2 %collective-permute-start.19 = (bf16[512,2048]{1,0:T(8,128)(2,1)S(1)}, bf16[512,2048]{1,0:T(8,128)(2,1)S(1)}, u32[]{:S(2)}, u32[]{:S(2)}) collective-permute-start(bf16[512,2048]{1,0:T(8,128)(2,1)S(1)} %multiply_convert_fusion.n0_ref.refs_0_), channel_id=1, source_target_pairs={{0,8},{4,12},{8,0},{12,4},{16,24},{20,28},{24,16},{28,20},{1,9},{5... | collective-permute-start | bytes 6291464 | tf_op jit(solution)/shard_map/ppermute | solution.py:668
  224.1 45.6 %collective-permute-start.18 = (bf16[512,2048]{1,0:T(8,128)(2,1)S(1)}, bf16[512,2048]{1,0:T(8,128)(2,1)S(1)}, u32[]{:S(2)}, u32[]{:S(2)}) collective-permute-start(bf16[512,2048]{1,0:T(8,128)(2,1)S(1)} %multiply_convert_fusion.n0_ref.refs_0_), channel_id=1, source_target_pairs={{0,4},{4,0},{8,12},{12,8},{16,20},{20,16},{24,28},{28,24},{1,5},{5... | collective-permute-start | bytes 6291464 | tf_op jit(solution)/shard_map/ppermute | solution.py:668
  224.1 69.1 %collective-permute-start.22 = (bf16[512,2048]{1,0:T(8,128)(2,1)}, bf16[512,2048]{1,0:T(8,128)(2,1)S(1)}, u32[]{:S(2)}, u32[]{:S(2)}) collective-permute-start(bf16[512,2048]{1,0:T(8,128)(2,1)} %collective-permute-done.15.g0_ref.refs_4_), channel_id=1, source_target_pairs={{0,4},{4,0},{8,12},{12,8},{16,20},{20,16},{24,28},{28,24},{1,5},{5... | collective-permute-start | bytes 6291464 | tf_op jit(solution)/shard_map/ppermute | solution.py:668
  358.3 48.3 %collective-permute-start.24 = (bf16[512,2048]{1,0:T(8,128)(2,1)}, bf16[512,2048]{1,0:T(8,128)(2,1)}, u32[]{:S(2)}, u32[]{:S(2)}) collective-permute-start(bf16[512,2048]{1,0:T(8,128)(2,1)} %add_convert_fusion.2), channel_id=1, source_target_pairs={{0,8},{4,12},{8,0},{12,4},{16,24},{20,28},{24,16},{28,20},{1,9},{5... | collective-permute-start | bytes 6291464 | tf_op jit(solution)/shard_map/ppermute | solution.py:668
  363.2 61.1 %collective-permute-start.26 = (bf16[4,144,2048]{2,1,0:T(8,128)(2,1)}, bf16[4,144,2048]{2,1,0:T(8,128)(2,1)}, u32[]{:S(2)}, u32[]{:S(2)}) collective-permute-start(bf16[4,144,2048]{2,1,0:T(8,128)(2,1)} %dynamic-slice_bitcast_fusion.1), channel_id=1, source_target_pairs={{0,16},{4,20},{8,24},{12,28},{16,0},{20,4},{24,8},{28,12},{1,17},{... | collective-permute-start | bytes 7077896 | tf_op jit(solution)/shard_map/ppermute | solution.py:668
  429.3 124.7 %reduce-scatter.9.cloned.1.call-start = ((), (), s32[]{:S(2)}) async-start(), calls=%async_computation.7 | async-start | bytes 1310720 | tf_op jit(solution)/shard_map/reduce_scatter | solution.py:769
  437.6 56.0 %collective-permute-start.28 = (bf16[2,2,4,64,1152]{4,3,1,0,2:T(8,128)(2,1)}, bf16[2,2,4,64,1152]{4,3,1,0,2:T(8,128)(2,1)}, u32[]{:S(2)}, u32[]{:S(2)}) collective-permute-start(bf16[2,2,4,64,1152]{4,3,1,0,2:T(8,128)(2,1)} %copy_bitcast_fusion.2), channel_id=1, source_target_pairs={{0,16},{4,20},{8,24},{12,28},{16,0},{20,4},{24,8},{28,12},{1,17},{... | collective-permute-start | bytes 7077896 | tf_op jit(solution)/shard_map/ppermute | solution.py:668
  485.9 80.1 %reduce-scatter.11.cloned.1.call-start = ((), (), s32[]{:S(2)}) async-start(), calls=%async_computation.8 | async-start | bytes 2949120 | tf_op jit(solution)/shard_map/reduce_scatter | solution.py:769
  498.1 106.9 %reduce-scatter.13.cloned.1.call-start = ((), (), s32[]{:S(2)}) async-start(), calls=%async_computation.9 | async-start | bytes 1966080 | tf_op jit(solution)/shard_map/reduce_scatter | solution.py:769
  500.1 53.9 %collective-permute-start.30 = (bf16[2,2,4,64,1152]{4,3,1,0,2:T(8,128)(2,1)S(1)}, bf16[2,2,4,64,1152]{4,3,1,0,2:T(8,128)(2,1)}, u32[]{:S(2)}, u32[]{:S(2)}) collective-permute-start(bf16[2,2,4,64,1152]{4,3,1,0,2:T(8,128)(2,1)S(1)} %copy_bitcast_fusion.1), channel_id=1, source_target_pairs={{0,16},{4,20},{8,24},{12,28},{16,0},{20,4},{24,8},{28,12},{1,17},{... | collective-permute-start | bytes 7077896 | tf_op jit(solution)/shard_map/ppermute | solution.py:668
  505.0 52.1 %collective-permute-start.29 = (bf16[2,2,4,64,1280]{4,3,2,1,0:T(8,128)(2,1)}, bf16[2,2,4,64,1280]{4,3,2,1,0:T(8,128)(2,1)}, u32[]{:S(2)}, u32[]{:S(2)}) collective-permute-start(bf16[2,2,4,64,1280]{4,3,2,1,0:T(8,128)(2,1)} %dynamic-slice_bitcast_fusion), channel_id=1, source_target_pairs={{0,4},{4,0},{8,12},{12,8},{16,20},{20,16},{24,28},{28,24},{1,5},{5... | collective-permute-start | bytes 7864328 | tf_op jit(solution)/shard_map/ppermute | solution.py:668
  509.2 48.0 %collective-permute-start.31 = (bf16[512,2048]{1,0:T(8,128)(2,1)}, bf16[512,2048]{1,0:T(8,128)(2,1)}, u32[]{:S(2)}, u32[]{:S(2)}) collective-permute-start(bf16[512,2048]{1,0:T(8,128)(2,1)} %add_convert_fusion.1), channel_id=1, source_target_pairs={{0,8},{4,12},{8,0},{12,4},{16,24},{20,28},{24,16},{28,20},{1,9},{5... | collective-permute-start | bytes 6291464 | tf_op jit(solution)/shard_map/ppermute | solution.py:668
  568.6 111.1 %reduce-scatter.15.cloned.1.call-start = ((), (), s32[]{:S(2)}) async-start(), calls=%async_computation.10 | async-start | bytes 2949120 | tf_op jit(solution)/shard_map/reduce_scatter | solution.py:769
  610.6 123.4 %reduce-scatter.17.cloned.1.call-start = ((), (), s32[]{:S(2)}) async-start(), calls=%async_computation.11 | async-start | bytes 2129920 | tf_op jit(solution)/shard_map/reduce_scatter | solution.py:769
  (117 other events, 1111.5 us)
Sparse Core Ops, SparseCore 0:
  10.2 41.6 all-gather.11
  53.4 49.5 all-gather.15
  105.1 53.6 all-gather.13
  160.2 49.2 all-gather.17
  211.5 88.2 all-gather.19
  429.4 46.5 reduce-scatter.6
  486.0 30.7 reduce-scatter.8
  519.2 46.7 reduce-scatter.10
  568.9 34.7 reduce-scatter.12
  610.7 47.7 reduce-scatter.14
  698.3 35.6 reduce-scatter.16

commit v10 on v9

--- a/solution.py
+++ b/solution.py
@@ -464,6 +464,56 @@
     )(*normed, wgate, wup)
 
 
+def gate_kernel(n0_ref, n1_ref, wg_ref, gate_ref):
+    tokens = n0_ref.shape[0]
+    gate_ref[:tokens] = dot_nn(n0_ref[...], wg_ref[...]).astype(bf16)
+    gate_ref[tokens:] = dot_nn(n1_ref[...], wg_ref[...]).astype(bf16)
+
+
+def gate_pass(normed, wgate):
+    tokens, width = normed[0].shape
+    columns = wgate.shape[1]
+    tile = min(256, columns)
+    whole = pl.BlockSpec((tokens, width), lambda i: (0, 0))
+    return pl.pallas_call(
+        gate_kernel,
+        grid=(pl.cdiv(columns, tile),),
+        in_specs=[whole] * 2 + [pl.BlockSpec((width, tile), lambda i: (0, i))],
+        out_specs=pl.BlockSpec((2 * tokens, tile), lambda i: (0, i)),
+        out_shape=jax.ShapeDtypeStruct((2 * tokens, columns), bf16),
+        compiler_params=pltpu.CompilerParams(vmem_limit_bytes=VMEM_LIMIT),
+        name="gate_pass",
+        cost_estimate=LIGHT,
+    )(*normed, wgate)
+
+
+def up_kernel(n0_ref, n1_ref, wu_ref, gate_ref, hidden_ref, up_ref):
+    tokens = n0_ref.shape[0]
+    for n_ref, rows in ((n0_ref, slice(0, tokens)), (n1_ref, slice(tokens, 2 * tokens))):
+        up = dot_nn(n_ref[...], wu_ref[...])
+        gate = gate_ref[rows].astype(f32)
+        hidden_ref[rows] = (gate / (1.0 + jnp.exp(-gate)) * up).astype(bf16)
+        up_ref[rows] = up.astype(bf16)
+
+
+def up_pass(normed, wup, gate):
+    tokens, width = normed[0].shape
+    columns = wup.shape[1]
+    tile = min(256, columns)
+    whole = pl.BlockSpec((tokens, width), lambda i: (0, 0))
+    out = pl.BlockSpec((2 * tokens, tile), lambda i: (0, i))
+    return pl.pallas_call(
+        up_kernel,
+        grid=(pl.cdiv(columns, tile),),
+        in_specs=[whole] * 2 + [pl.BlockSpec((width, tile), lambda i: (0, i)), out],
+        out_specs=[out] * 2,
+        out_shape=[jax.ShapeDtypeStruct((2 * tokens, columns), bf16)] * 2,
+        compiler_params=pltpu.CompilerParams(vmem_limit_bytes=VMEM_LIMIT),
+        name="up_pass",
+        cost_estimate=LIGHT,
+    )(*normed, wup, gate)
+
+
 def gates_kernel(g0_ref, g1_ref, wd_ref, gate_ref, up_ref, gate_out_ref, up_out_ref, g_all):
     tokens = g0_ref.shape[0]
 
@@ -955,16 +1005,18 @@
     normed_ffn, gate_other, q_right, wout_other, q_left, q_left_other = stage(
         normed_ffn, gate_other, q_right, wout_other, q_left, q_left_other
     )
-    wq = joined(q_left, q_left_other, core, 2).reshape(width, -1)
-    wout_t = joined(q_right, wout_other, core, 2).reshape(width, -1)
-    normed1, normed2, up_other, wgate = stage(
-        swap(normed_ffn, 1),
+    normed1 = swap(normed_ffn, 1)
+    wgate = spread_hidden(gate_lines, gate_other)
+    gate_near, normed2, up_other, wout_t, wq = stage(
+        gate_pass((normed_ffn, normed1), wgate),
         swap(normed_ffn, 2),
         up_other,
-        spread_hidden(gate_lines, gate_other),
-    )
+        joined(q_right, wout_other, core, 2),
+        joined(q_left, q_left_other, core, 2),
+    )
+    wout_t, wq = wout_t.reshape(width, -1), wq.reshape(width, -1)
     wup = spread_hidden(up_lines, up_other)
-    hidden_near, gate_near, up_near = hidden_pass((normed_ffn, normed1), wgate, wup)
+    hidden_near, up_near = up_pass((normed_ffn, normed1), wup, gate_near)
     normed3, hidden_near, grad_top3 = stage(
         swap(normed2, 1), hidden_near, swap(grad_top2, 1)
     )
@@ -1037,11 +1089,16 @@
     grad_wq = t_mm(normed, joint_grad_q).astype(bf16).reshape(*shape, QUERY_COLUMNS)
     grad_wout = add_bit(grad_wout, wout_other, 1, 2)
     grad_up = jnp.moveaxis(add_outer(grad_wup, up_other, 0), 2, 0)
-    grad_kv2, grad_normed, grad_wq, grad_wout, grad_up = stage(
-        grad_kv2, mm_t(joint_grad_q, wq), grad_wq, grad_wout, grad_up
+    grad_kv2, grad_normed, grad_wq, grad_wout, grad_up, wq_other = stage(
+        grad_kv2,
+        mm_t(joint_grad_q, wq),
+        grad_wq,
+        grad_wout,
+        grad_up,
+        pass_bit(grad_wq, 1, 2),
     )
     grad_up = reduce_seq(grad_up)
-    grad_wq, grad_kv2 = stage(reduce_bit(grad_wq, 1, 2), grad_kv2)
+    grad_wq, grad_kv2 = stage(add_bit(grad_wq, wq_other, 1, 2), grad_kv2)
     wq_other, wout_other = pass_bit(grad_wq, 2, 1), pass_outer(grad_wout, 0)
 
 

time: 756 us -> 736 us (0.974)
  waiting for transfers between devices: 210 us -> 188 us
    pallas_call x0 -> x2, Pallas kernels: none -> 19 us  [the longest x1 9.73 us: up_pass(): pl.pallas_call(up_kernel, grid=(pl.cdiv(columns, tile),), in_specs=[whole...]
    ppermute x46, waiting for transfers between devices: 143 us -> 124 us  [swap(): return lax.ppermute(values, 'rows', pairs)]
    pallas_call x2 -> x1, Pallas kernels: 29.8 us -> 14.9 us  [hidden_pass(): pl.pallas_call(hidden_kernel, grid=(pl.cdiv(columns, tile),), in_specs=[w...]
    unnamed x159 -> x163, local copies, waits for them, and re-layouts: 26.5 us -> 27.6 us
  transfers between devices with their start and end apart: 62 -> 62, of which waited for: 28 -> 26; matrix products, arithmetic and copies ran while one was open for 19% -> 19% of each run, Pallas kernels for 31% -> 33%
where the time goes in v10:
time: 736 us; the launch traced here: 726 us
  Pallas kernels  265 us (36%)
  waiting for transfers between devices  188 us (26%)
  other arithmetic  83.9 us (11%)
  local copies, waits for them, and re-layouts  76.9 us (10%)
  starting transfers between devices  41.4 us (6%)
  matrix products  32.4 us (4%)
  blocking collectives  19.9 us (3%)
  between operations  18.4 us (2%)
    ppermute x46, waiting for transfers between devices, swap(): return lax.ppermute(values, 'rows', pairs)  124 us
    pallas_call x3, Pallas kernels, weight_pass(): pl.pallas_call(partial(weight_kernel, len(lefts)), grid=(rows // tile,),...  47.1 us
    pallas_call x4, Pallas kernels, back_pass(): pl.pallas_call(partial(back_kernel, count, transposed), grid=(width // ti...  46.3 us
    all_gather x5, waiting for transfers between devices, gather_seq(): return lax.all_gather(values, 'seq', axis=0, tiled=False)  39 us
    ppermute x46, starting transfers between devices, swap(): return lax.ppermute(values, 'rows', pairs)  36.4 us
    pallas_call x2, Pallas kernels, attend_backward(): pl.pallas_call(partial(attend_backward_kernel, first, count), grid_spec=p...  28 us
    unnamed x163, local copies, waits for them, and re-layouts  27.6 us
    pallas_call x17, Pallas kernels, joined(): pl.pallas_call(joined_kernel, grid_spec=pltpu.PrefetchScalarGridSpec(num_...  25.3 us
  transfers between devices with their start and end apart: 62, of which 26 were waited for; matrix products, arithmetic and copies ran while one was open for 19% of the time, Pallas kernels for 33%

profile of v10, /device:TPU:0, one launch (start us, length us, event | category | flops | bytes accessed | tf_op | source)
XLA Modules:
  0.0 726.2 jit_solution(11657049970605575172)
XLA Ops:
  28.3 19.9 %all-gather = bf16[256,768]{1,0:T(8,128)(2,1)S(1)} all-gather(bf16[64,768]{1,0:T(8,128)(2,1)S(1)} %fusion.35), channel_id=2, replica_groups=mesh['rows'=8,'seq'=4] {'seq'}, dimensions={0}, use_global_device_ids=true | all-gather | bytes 491520 | tf_op jit(solution)/shard_map/all_gather | solution.py:815
  100.4 26.6 %collective-permute-done.11 = bf16[2,4,64,1280]{3,2,1,0:T(8,128)(2,1)} collective-permute-done((bf16[2,4,64,1280]{3,2,1,0:T(8,128)(2,1)}, bf16[2,4,64,1280]{3,2,1,0:T(8,128)(2,1)}, u32[]{:S(2)}, u32[]{:S(2)}) %collective-permute-start.11) | collective-permute-done | bytes 1310752 | tf_op jit(solution)/shard_map/ppermute | solution.py:718
  141.0 8.8 %heads_forward_halves.1 = (f32[512,1280]{1,0:T(8,128)}, bf16[512,1280]{1,0:T(8,128)(2,1)S(1)}) custom-call(s32[1]{0:T(128)} %bitcast.2.side_ref, bf16[512,2048]{1,0:T(8,128)(2,1)S(1)} %copy-done.6, bf16[4,256,1280]{2,1,0:T(8,128)(2,1)} %bitcast.54.own_ref, bf16[4,256,1280]{2,1,0:T(8,128)(2,1)} %bitcast.55.other_ref, ...), custom_call_target="tpu_custom_call" | custom-call | flops 1000 | bytes 1000 | tf_op jit(solution)/shard_map/heads_forward_halves/pallas_call | solution.py:104
  161.5 11.7 %attend_forward.1 = (bf16[512,1280]{1,0:T(8,128)(2,1)S(1)}, f32[512,1280]{1,0:T(8,128)S(1)}) custom-call(s32[1]{0:T(128)} %bitcast.place_ref, bf16[512,1280]{1,0:T(8,128)(2,1)S(1)} %copy-done.12, bf16[2048,640]{1,0:T(8,128)(2,1)} %all-gather.14.cloned.1.call-done.k_ref.v_ref, bf16[2048,640]{1,0:T(8,128)(2,1)} %all-gather.14.cloned.1.call-done.k_ref.v_ref), custom_call_target="tpu_custom_call" | custom-call | flops 1000 | bytes 1000 | tf_op jit(solution)/shard_map/attend_forward/pallas_call | solution.py:273
  174.8 34.1 %all-gather.18.cloned.1.call-done = bf16[8,2,64,1152]{3,2,1,0:T(8,128)(2,1)} async-done(((bf16[2,2,64,1152]{3,2,1,0:T(8,128)(2,1)}), bf16[8,2,64,1152]{3,2,1,0:T(8,128)(2,1)}) %all-gather.18.cloned.1.call-update) | async-done | bytes 2359312 | tf_op jit(solution)/shard_map/all_gather | solution.py:815
  241.3 9.3 %gate_pass.1.gate_ref = bf16[1024,1152]{1,0:T(8,128)(2,1)} custom-call(bf16[512,2048]{1,0:T(8,128)(2,1)S(1)} %multiply_convert_fusion.n0_ref.refs_0_, bf16[512,2048]{1,0:T(8,128)(2,1)S(1)} %collective-permute-done.18.n1_ref.refs_1_, bf16[2048,1152]{1,0:T(8,128)(2,1)} %bitcast.284), custom_call_target="tpu_custom_call" | custom-call | flops 1000 | bytes 1000 | tf_op jit(solution)/shard_map/gate_pass/pallas_call | solution.py:478
  250.6 19.4 %collective-permute-done.19.n0_ref.refs_2_ = bf16[512,2048]{1,0:T(8,128)(2,1)S(1)} collective-permute-done((bf16[512,2048]{1,0:T(8,128)(2,1)S(1)}, bf16[512,2048]{1,0:T(8,128)(2,1)S(1)}, u32[]{:S(2)}, u32[]{:S(2)}) %collective-permute-start.19) | collective-permute-done | bytes 2097184 | tf_op jit(solution)/shard_map/ppermute | solution.py:718
  275.9 9.7 %up_pass.1 = (bf16[1024,1152]{1,0:T(8,128)(2,1)}, bf16[1024,1152]{1,0:T(8,128)(2,1)}) custom-call(bf16[512,2048]{1,0:T(8,128)(2,1)S(1)} %multiply_convert_fusion.n0_ref.refs_0_, bf16[512,2048]{1,0:T(8,128)(2,1)S(1)} %collective-permute-done.18.n1_ref.refs_1_, bf16[2048,1152]{1,0:T(8,128)(2,1)} %bitcast.288, bf16[1024,1152]{1,0:T(8,128)(2,1)} %gate_pass.1.gate_ref), custom_call_target="tpu_custom_call" | custom-call | flops 1000 | bytes 1000 | tf_op jit(solution)/shard_map/up_pass/pallas_call | solution.py:505
  285.7 14.9 %hidden_pass.1 = (bf16[1024,1152]{1,0:T(8,128)(2,1)}, bf16[1024,1152]{1,0:T(8,128)(2,1)}, bf16[1024,1152]{1,0:T(8,128)(2,1)}) custom-call(bf16[512,2048]{1,0:T(8,128)(2,1)S(1)} %collective-permute-done.19.n0_ref.refs_2_, bf16[512,2048]{1,0:T(8,128)(2,1)S(1)} %collective-permute-done.21.n1_ref.refs_3_, bf16[2048,1152]{1,0:T(8,128)(2,1)} %bitcast.285, ...), custom_call_target="tpu_custom_call" | custom-call | flops 1000 | bytes 1000 | tf_op jit(solution)/shard_map/hidden_pass/pallas_call | solution.py:454
  301.9 12.3 %gates_pass.2 = (bf16[1024,1152]{1,0:T(8,128)(2,1)}, bf16[1024,1152]{1,0:T(8,128)(2,1)}) custom-call(bf16[512,2048]{1,0:T(8,128)(2,1)} %collective-permute-done.15.g0_ref.refs_4_, bf16[512,2048]{1,0:T(8,128)(2,1)} %collective-permute-done.22.g1_ref.refs_5_, bf16[1152,2048]{1,0:T(8,128)(2,1)} %bitcast.292, bf16[1024,1152]{1,0:T(8,128)(2,1)} %get-tuple-element.220.gate_ref, ...), custom_call_target="tpu_custom_call" | custom-call | flops 1000 | bytes 1000 | tf_op jit(solution)/shard_map/gates_pass/pallas_call | solution.py:539
  315.9 14.9 %back_pass.4 = (f32[512,2048]{1,0:T(8,128)}, bf16[512,2048]{1,0:T(8,128)(2,1)S(1)}) custom-call(bf16[1024,1152]{1,0:T(8,128)(2,1)S(1)} %copy-done.17, bf16[1024,1152]{1,0:T(8,128)(2,1)} %get-tuple-element.223.refs_1_.refs_5_, bf16[2048,1152]{1,0:T(8,128)(2,1)} %bitcast.286, bf16[2048,1152]{1,0:T(8,128)(2,1)} %bitcast.290), custom_call_target="tpu_custom_call" | custom-call | flops 1000 | bytes 1000 | tf_op jit(solution)/shard_map/back_pass/pallas_call | solution.py:578
  330.7 15.7 %weight_pass.3 = bf16[1152,2048]{1,0:T(8,128)(2,1)} custom-call(bf16[1024,1152]{1,0:T(8,128)(2,1)} %get-tuple-element.299.refs_0_, bf16[1024,1152]{1,0:T(8,128)(2,1)} %get-tuple-element.249.refs_1_.refs_0_, bf16[512,2048]{1,0:T(8,128)(2,1)} %bitcast_convert_fusion.refs_2_.g0_ref, bf16[512,2048]{1,0:T(8,128)(2,1)} %collective-permute-done.14.refs_3_.g1_ref, ...), custom_call_target="tpu_custom_call" | custom-call | flops 1000 | bytes 1000 | tf_op jit(solution)/shard_map/weight_pass/pallas_call | solution.py:612
  353.4 12.4 %gates_pass.3 = (bf16[1024,1152]{1,0:T(8,128)(2,1)}, bf16[1024,1152]{1,0:T(8,128)(2,1)}) custom-call(bf16[512,2048]{1,0:T(8,128)(2,1)} %bitcast_convert_fusion.refs_2_.g0_ref, bf16[512,2048]{1,0:T(8,128)(2,1)} %collective-permute-done.14.refs_3_.g1_ref, bf16[1152,2048]{1,0:T(8,128)(2,1)} %bitcast.293, bf16[1024,1152]{1,0:T(8,128)(2,1)} %gate_pass.1.gate_ref, ...), custom_call_target="tpu_custom_call" | custom-call | flops 1000 | bytes 1000 | tf_op jit(solution)/shard_map/gates_pass/pallas_call | solution.py:539
  367.4 15.0 %back_pass.5 = (f32[512,2048]{1,0:T(8,128)}, bf16[512,2048]{1,0:T(8,128)(2,1)}) custom-call(bf16[1024,1152]{1,0:T(8,128)(2,1)S(1)} %copy-done.18, bf16[1024,1152]{1,0:T(8,128)(2,1)} %get-tuple-element.241.refs_1_.refs_4_, bf16[2048,1152]{1,0:T(8,128)(2,1)} %bitcast.287, bf16[2048,1152]{1,0:T(8,128)(2,1)} %bitcast.291), custom_call_target="tpu_custom_call" | custom-call | flops 1000 | bytes 1000 | tf_op jit(solution)/shard_map/back_pass/pallas_call | solution.py:578
  382.5 15.7 %weight_pass.4 = bf16[2048,1152]{1,0:T(8,128)(2,1)} custom-call(bf16[512,2048]{1,0:T(8,128)(2,1)S(1)} %multiply_convert_fusion.n0_ref.refs_0_, bf16[512,2048]{1,0:T(8,128)(2,1)S(1)} %copy-done.3, bf16[512,2048]{1,0:T(8,128)(2,1)} %copy-done.9, bf16[512,2048]{1,0:T(8,128)(2,1)} %copy-done.10, bf16[1024,1152]{1,0:T(8,128)(2,1)} %get-tuple-element.235.refs_0_.refs_4_, ...), custom_call_target="tpu_custom_call" | custom-call | flops 1000 | bytes 1000 | tf_op jit(solution)/shard_map/weight_pass/pallas_call | solution.py:612
  400.0 15.7 %weight_pass.5 = bf16[2048,1152]{1,0:T(8,128)(2,1)} custom-call(bf16[512,2048]{1,0:T(8,128)(2,1)S(1)} %multiply_convert_fusion.n0_ref.refs_0_, bf16[512,2048]{1,0:T(8,128)(2,1)S(1)} %copy-done.4, bf16[512,2048]{1,0:T(8,128)(2,1)} %copy-done.9, bf16[512,2048]{1,0:T(8,128)(2,1)} %copy-done.10, bf16[1024,1152]{1,0:T(8,128)(2,1)} %get-tuple-element.241.refs_1_.refs_4_, ...), custom_call_target="tpu_custom_call" | custom-call | flops 1000 | bytes 1000 | tf_op jit(solution)/shard_map/weight_pass/pallas_call | solution.py:612
  438.2 11.0 %attend_backward.2 = (bf16[512,512]{1,0:T(8,128)(2,1)S(1)}, bf16[2048,256]{1,0:T(8,128)(2,1)S(1)}) custom-call(s32[1]{0:T(128)} %bitcast.place_ref, bf16[512,1280]{1,0:T(8,128)(2,1)S(1)} %copy-done.13, bf16[2048,640]{1,0:T(8,128)(2,1)} %all-gather.14.cloned.1.call-done.k_ref.v_ref, bf16[2048,640]{1,0:T(8,128)(2,1)} %all-gather.14.cloned.1.call-done.k_ref.v_ref, ...), custom_call_target="tpu_custom_call" | custom-call | flops 1000 | bytes 1000 | tf_op jit(solution)/shard_map/attend_backward/pallas_call | solution.py:410
  452.1 15.1 %reduce-scatter.7.cloned.1.call-done = bf16[1,144,2048]{2,1,0:T(8,128)(2,1)} async-done(((bf16[4,144,2048]{2,1,0:T(8,128)(2,1)}), bf16[1,144,2048]{2,1,0:T(8,128)(2,1)}) %reduce-scatter.7.cloned.1.call-update) | async-done | bytes 589840 | tf_op jit(solution)/shard_map/reduce_scatter | solution.py:819
  468.9 8.2 %back_pass.6 = (f32[512,2048]{1,0:T(8,128)}, bf16[512,2048]{1,0:T(8,128)(2,1)}) custom-call(bf16[1024,1152]{1,0:T(8,128)(2,1)S(1)} %copy-done.16, bf16[1152,2048]{1,0:T(8,128)(2,1)} %bitcast.294), custom_call_target="tpu_custom_call" | custom-call | flops 1000 | bytes 1000 | tf_op jit(solution)/shard_map/back_pass/pallas_call | solution.py:578
  501.7 16.9 %attend_backward.3 = (bf16[512,768]{1,0:T(8,128)(2,1)S(1)}, bf16[2048,384]{1,0:T(8,128)(2,1)}) custom-call(s32[1]{0:T(128)} %bitcast.place_ref, bf16[512,1280]{1,0:T(8,128)(2,1)S(1)} %copy-done.13, bf16[2048,640]{1,0:T(8,128)(2,1)} %all-gather.14.cloned.1.call-done.k_ref.v_ref, bf16[2048,640]{1,0:T(8,128)(2,1)} %all-gather.14.cloned.1.call-done.k_ref.v_ref, ...), custom_call_target="tpu_custom_call" | custom-call | flops 1000 | bytes 1000 | tf_op jit(solution)/shard_map/attend_backward/pallas_call | solution.py:410
  518.7 26.4 %collective-permute-done.30 = bf16[2,2,4,64,1152]{4,3,1,0,2:T(8,128)(2,1)} collective-permute-done((bf16[2,2,4,64,1152]{4,3,1,0,2:T(8,128)(2,1)S(1)}, bf16[2,2,4,64,1152]{4,3,1,0,2:T(8,128)(2,1)}, u32[]{:S(2)}, u32[]{:S(2)}) %collective-permute-start.30) | collective-permute-done | bytes 2359328 | tf_op jit(solution)/shard_map/ppermute | solution.py:718
  557.0 9.0 %heads_backward.2 = (bf16[512,1280]{1,0:T(8,128)(2,1)}, f32[8,1280]{1,0:T(8,128)}) custom-call(bf16[512,1280]{1,0:T(8,128)(2,1)} %pad_maximum_fusion.3.grad_ref, f32[512,1280]{1,0:T(8,128)} %get-tuple-element.267.joint_ref, f32[8,1280]{1,0:T(8,128)} %copy-done.40, f32[512,128]{1,0:T(8,128)} %copy-done.19, f32[512,128]{1,0:T(8,128)} %copy-done.20), custom_call_target="tpu_custom_call" | custom-call | flops 1000 | bytes 1000 | tf_op jit(solution)/shard_map/heads_backward/pallas_call | solution.py:205
  621.6 12.9 %collective-permute-done.34 = bf16[2,4,64,1280]{3,2,1,0:T(8,128)(2,1)} collective-permute-done((bf16[2,4,64,1280]{3,2,1,0:T(8,128)(2,1)}, bf16[2,4,64,1280]{3,2,1,0:T(8,128)(2,1)}, u32[]{:S(2)}, u32[]{:S(2)}) %collective-permute-start.34) | collective-permute-done | bytes 1310752 | tf_op jit(solution)/shard_map/ppermute | solution.py:718
  646.9 8.2 %back_pass.7 = (f32[512,2048]{1,0:T(8,128)}, bf16[512,2048]{1,0:T(8,128)(2,1)}) custom-call(bf16[1024,1152]{1,0:T(8,128)(2,1)S(1)} %copy-done.15, bf16[1152,2048]{1,0:T(8,128)(2,1)} %bitcast.295), custom_call_target="tpu_custom_call" | custom-call | flops 1000 | bytes 1000 | tf_op jit(solution)/shard_map/back_pass/pallas_call | solution.py:578
  (448 shorter events, 344.0 us)
Async XLA Ops:
  7.2 44.7 %all-gather.12.cloned.1.call-start = ((), (), s32[]{:S(2)}) async-start(), calls=%async_computation.12 | async-start | bytes 1638400 | tf_op jit(solution)/shard_map/all_gather | solution.py:815
  9.8 119.7 %all-gather.16.cloned.1.call-start = ((), (), s32[]{:S(2)}) async-start(), calls=%async_computation.14 | async-start | bytes 2949120 | tf_op jit(solution)/shard_map/all_gather | solution.py:815
  53.2 105.0 %all-gather.14.cloned.1.call-start = ((), (), s32[]{:S(2)}) async-start(), calls=%async_computation.13 | async-start | bytes 3276800 | tf_op jit(solution)/shard_map/all_gather | solution.py:815
  93.3 115.6 %all-gather.18.cloned.1.call-start = ((), (), s32[]{:S(2)}) async-start(), calls=%async_computation.15 | async-start | bytes 2949120 | tf_op jit(solution)/shard_map/all_gather | solution.py:815
  100.3 201.6 %all-gather.20.cloned.1.call-start = ((), (), s32[]{:S(2)}) async-start(), calls=%async_computation.16 | async-start | bytes 5898240 | tf_op jit(solution)/shard_map/all_gather | solution.py:815
  154.1 54.8 %collective-permute-start.16 = (bf16[2,2,4,64,1280]{4,3,2,1,0:T(8,128)(2,1)}, bf16[2,2,4,64,1280]{4,3,2,1,0:T(8,128)(2,1)}, u32[]{:S(2)}, u32[]{:S(2)}) collective-permute-start(bf16[2,2,4,64,1280]{4,3,2,1,0:T(8,128)(2,1)} %bitcast.62), channel_id=1, source_target_pairs={{0,4},{4,0},{8,12},{12,8},{16,20},{20,16},{24,28},{28,24},{1,5},{5... | collective-permute-start | bytes 7864328 | tf_op jit(solution)/shard_map/ppermute | solution.py:718
  154.3 54.6 %collective-permute-start.15 = (bf16[512,2048]{1,0:T(8,128)(2,1)}, bf16[512,2048]{1,0:T(8,128)(2,1)}, u32[]{:S(2)}, u32[]{:S(2)}) collective-permute-start(bf16[512,2048]{1,0:T(8,128)(2,1)} %bitcast_convert_fusion.refs_2_.g0_ref), channel_id=1, source_target_pairs={{0,8},{4,12},{8,0},{12,4},{16,24},{20,28},{24,16},{28,20},{1,9},{5... | collective-permute-start | bytes 6291464 | tf_op jit(solution)/shard_map/ppermute | solution.py:718
  154.9 54.0 %collective-permute-start.14 = (bf16[512,2048]{1,0:T(8,128)(2,1)}, bf16[512,2048]{1,0:T(8,128)(2,1)}, u32[]{:S(2)}, u32[]{:S(2)}) collective-permute-start(bf16[512,2048]{1,0:T(8,128)(2,1)} %bitcast_convert_fusion.refs_2_.g0_ref), channel_id=1, source_target_pairs={{0,4},{4,0},{8,12},{12,8},{16,20},{20,16},{24,28},{28,24},{1,5},{5... | collective-permute-start | bytes 6291464 | tf_op jit(solution)/shard_map/ppermute | solution.py:718
  158.2 309.0 %reduce-scatter.7.cloned.1.call-start = ((), (), s32[]{:S(2)}) async-start(), calls=%async_computation.6 | async-start | bytes 2949120 | tf_op jit(solution)/shard_map/reduce_scatter | solution.py:819
  158.7 63.2 %collective-permute-start.17 = (bf16[4,2,2,64,1152]{4,3,2,1,0:T(8,128)(2,1)}, bf16[4,2,2,64,1152]{4,3,2,1,0:T(8,128)(2,1)}, u32[]{:S(2)}, u32[]{:S(2)}) collective-permute-start(bf16[4,2,2,64,1152]{4,3,2,1,0:T(8,128)(2,1)} %bitcast.260), channel_id=1, source_target_pairs={{0,16},{4,20},{8,24},{12,28},{16,0},{20,4},{24,8},{28,12},{1,17},{... | collective-permute-start | bytes 7077896 | tf_op jit(solution)/shard_map/ppermute | solution.py:718
  208.9 61.1 %collective-permute-start.20 = (bf16[4,2,2,64,1152]{4,3,2,1,0:T(8,128)(2,1)}, bf16[4,2,2,64,1152]{4,3,2,1,0:T(8,128)(2,1)}, u32[]{:S(2)}, u32[]{:S(2)}) collective-permute-start(bf16[4,2,2,64,1152]{4,3,2,1,0:T(8,128)(2,1)} %bitcast.262), channel_id=1, source_target_pairs={{0,16},{4,20},{8,24},{12,28},{16,0},{20,4},{24,8},{28,12},{1,17},{... | collective-permute-start | bytes 7077896 | tf_op jit(solution)/shard_map/ppermute | solution.py:718
  221.9 48.0 %collective-permute-start.19 = (bf16[512,2048]{1,0:T(8,128)(2,1)S(1)}, bf16[512,2048]{1,0:T(8,128)(2,1)S(1)}, u32[]{:S(2)}, u32[]{:S(2)}) collective-permute-start(bf16[512,2048]{1,0:T(8,128)(2,1)S(1)} %multiply_convert_fusion.n0_ref.refs_0_), channel_id=1, source_target_pairs={{0,8},{4,12},{8,0},{12,4},{16,24},{20,28},{24,16},{28,20},{1,9},{5... | collective-permute-start | bytes 6291464 | tf_op jit(solution)/shard_map/ppermute | solution.py:718
  223.6 62.1 %collective-permute-start.22 = (bf16[512,2048]{1,0:T(8,128)(2,1)}, bf16[512,2048]{1,0:T(8,128)(2,1)}, u32[]{:S(2)}, u32[]{:S(2)}) collective-permute-start(bf16[512,2048]{1,0:T(8,128)(2,1)} %collective-permute-done.15.g0_ref.refs_4_), channel_id=1, source_target_pairs={{0,4},{4,0},{8,12},{12,8},{16,20},{20,16},{24,28},{28,24},{1,5},{5... | collective-permute-start | bytes 6291464 | tf_op jit(solution)/shard_map/ppermute | solution.py:718
  348.4 49.8 %collective-permute-start.24 = (bf16[512,2048]{1,0:T(8,128)(2,1)}, bf16[512,2048]{1,0:T(8,128)(2,1)}, u32[]{:S(2)}, u32[]{:S(2)}) collective-permute-start(bf16[512,2048]{1,0:T(8,128)(2,1)} %add_convert_fusion.2), channel_id=1, source_target_pairs={{0,8},{4,12},{8,0},{12,4},{16,24},{20,28},{24,16},{28,20},{1,9},{5... | collective-permute-start | bytes 6291464 | tf_op jit(solution)/shard_map/ppermute | solution.py:718
  353.4 62.4 %collective-permute-start.26 = (bf16[4,144,2048]{2,1,0:T(8,128)(2,1)}, bf16[4,144,2048]{2,1,0:T(8,128)(2,1)}, u32[]{:S(2)}, u32[]{:S(2)}) collective-permute-start(bf16[4,144,2048]{2,1,0:T(8,128)(2,1)} %dynamic-slice_bitcast_fusion.1), channel_id=1, source_target_pairs={{0,16},{4,20},{8,24},{12,28},{16,0},{20,4},{24,8},{28,12},{1,17},{... | collective-permute-start | bytes 7077896 | tf_op jit(solution)/shard_map/ppermute | solution.py:718
  420.6 124.4 %reduce-scatter.9.cloned.1.call-start = ((), (), s32[]{:S(2)}) async-start(), calls=%async_computation.7 | async-start | bytes 1310720 | tf_op jit(solution)/shard_map/reduce_scatter | solution.py:819
  424.1 60.4 %collective-permute-start.28 = (bf16[2,2,4,64,1152]{4,3,1,0,2:T(8,128)(2,1)}, bf16[2,2,4,64,1152]{4,3,1,0,2:T(8,128)(2,1)}, u32[]{:S(2)}, u32[]{:S(2)}) collective-permute-start(bf16[2,2,4,64,1152]{4,3,1,0,2:T(8,128)(2,1)} %copy_bitcast_fusion.2), channel_id=1, source_target_pairs={{0,16},{4,20},{8,24},{12,28},{16,0},{20,4},{24,8},{28,12},{1,17},{... | collective-permute-start | bytes 7077896 | tf_op jit(solution)/shard_map/ppermute | solution.py:718
  477.1 76.1 %reduce-scatter.11.cloned.1.call-start = ((), (), s32[]{:S(2)}) async-start(), calls=%async_computation.8 | async-start | bytes 2949120 | tf_op jit(solution)/shard_map/reduce_scatter | solution.py:819
  489.1 103.6 %reduce-scatter.13.cloned.1.call-start = ((), (), s32[]{:S(2)}) async-start(), calls=%async_computation.9 | async-start | bytes 1966080 | tf_op jit(solution)/shard_map/reduce_scatter | solution.py:819
  491.2 53.8 %collective-permute-start.30 = (bf16[2,2,4,64,1152]{4,3,1,0,2:T(8,128)(2,1)S(1)}, bf16[2,2,4,64,1152]{4,3,1,0,2:T(8,128)(2,1)}, u32[]{:S(2)}, u32[]{:S(2)}) collective-permute-start(bf16[2,2,4,64,1152]{4,3,1,0,2:T(8,128)(2,1)S(1)} %copy_bitcast_fusion.1), channel_id=1, source_target_pairs={{0,16},{4,20},{8,24},{12,28},{16,0},{20,4},{24,8},{28,12},{1,17},{... | collective-permute-start | bytes 7077896 | tf_op jit(solution)/shard_map/ppermute | solution.py:718
  496.2 52.1 %collective-permute-start.29 = (bf16[2,2,4,64,1280]{4,3,2,1,0:T(8,128)(2,1)}, bf16[2,2,4,64,1280]{4,3,2,1,0:T(8,128)(2,1)}, u32[]{:S(2)}, u32[]{:S(2)}) collective-permute-start(bf16[2,2,4,64,1280]{4,3,2,1,0:T(8,128)(2,1)} %dynamic-slice_bitcast_fusion), channel_id=1, source_target_pairs={{0,4},{4,0},{8,12},{12,8},{16,20},{20,16},{24,28},{28,24},{1,5},{5... | collective-permute-start | bytes 7864328 | tf_op jit(solution)/shard_map/ppermute | solution.py:718
  500.2 48.1 %collective-permute-start.31 = (bf16[512,2048]{1,0:T(8,128)(2,1)}, bf16[512,2048]{1,0:T(8,128)(2,1)}, u32[]{:S(2)}, u32[]{:S(2)}) collective-permute-start(bf16[512,2048]{1,0:T(8,128)(2,1)} %add_convert_fusion.1), channel_id=1, source_target_pairs={{0,8},{4,12},{8,0},{12,4},{16,24},{20,28},{24,16},{28,20},{1,9},{5... | collective-permute-start | bytes 6291464 | tf_op jit(solution)/shard_map/ppermute | solution.py:718
  555.8 111.4 %reduce-scatter.15.cloned.1.call-start = ((), (), s32[]{:S(2)}) async-start(), calls=%async_computation.10 | async-start | bytes 2949120 | tf_op jit(solution)/shard_map/reduce_scatter | solution.py:819
  599.0 115.4 %reduce-scatter.17.cloned.1.call-start = ((), (), s32[]{:S(2)}) async-start(), calls=%async_computation.11 | async-start | bytes 2129920 | tf_op jit(solution)/shard_map/reduce_scatter | solution.py:819
  (119 other events, 1154.0 us)
Sparse Core Ops, SparseCore 0:
  10.2 41.6 all-gather.11
  53.4 49.5 all-gather.15
  104.6 53.6 all-gather.13
  159.6 49.2 all-gather.17
  210.9 88.2 all-gather.19
  420.7 46.4 reduce-scatter.6
  477.2 26.7 reduce-scatter.8
  506.4 46.7 reduce-scatter.10
  556.2 34.7 reduce-scatter.12
  599.1 47.5 reduce-scatter.14
  679.3 35.0 reduce-scatter.16

commit v11 on v10

--- a/solution.py
+++ b/solution.py
@@ -1089,18 +1089,10 @@
     grad_wq = t_mm(normed, joint_grad_q).astype(bf16).reshape(*shape, QUERY_COLUMNS)
     grad_wout = add_bit(grad_wout, wout_other, 1, 2)
     grad_up = jnp.moveaxis(add_outer(grad_wup, up_other, 0), 2, 0)
-    grad_kv2, grad_normed, grad_wq, grad_wout, grad_up, wq_other = stage(
-        grad_kv2,
-        mm_t(joint_grad_q, wq),
-        grad_wq,
-        grad_wout,
-        grad_up,
-        pass_bit(grad_wq, 1, 2),
-    )
+    grad_wq = reduce_bit(grad_wq, 1, 2)
+    wq_other, wout_other = pass_bit(grad_wq, 2, 1), pass_outer(grad_wout, 0)
+    grad_kv2, grad_normed, grad_up = stage(grad_kv2, mm_t(joint_grad_q, wq), grad_up)
     grad_up = reduce_seq(grad_up)
-    grad_wq, grad_kv2 = stage(add_bit(grad_wq, wq_other, 1, 2), grad_kv2)
-    wq_other, wout_other = pass_bit(grad_wq, 2, 1), pass_outer(grad_wout, 0)
-
 
     grad_kv1, grad_kv2 = (
         part_.reshape(shard_length, 2, -1) for part_ in (grad_kv1, grad_kv2)
@@ -1109,6 +1101,7 @@
     joint_grad_kv, gain_k = heads_backward(
         grad_kv, joint_kv, wide_k, cos_table, sin_table, KEY_COLUMNS
     )
+    joint_grad_kv, wq_other, wout_other = stage(joint_grad_kv, wq_other, wout_other)
     grad_wkv = t_mm(normed, joint_grad_kv).astype(bf16)
     grad_normed = grad_normed + mm_t(joint_grad_kv, wkv)
     grad_input_part, grad_attn_gain = norm_backward(
@@ -1118,9 +1111,7 @@
 
     gain_rows = jnp.stack([grad_attn_gain, grad_ffn_gain]).astype(bf16)
     gain_columns = t_mm(gain_rows, jnp.eye(2, LANES, dtype=bf16)).astype(bf16)
-    grad_wkv, gain_columns, wq_other, wout_other, hidden_near = stage(
-        grad_wkv, gain_columns, wq_other, wout_other, hidden_near
-    )
+    grad_wkv, gain_columns, hidden_near = stage(grad_wkv, gain_columns, hidden_near)
     own_near, send_near = back_pass((hidden_near,), (wdown,), False)
     grad_wq = add_bit(grad_wq, wq_other, 2, 1)
     grad_wout = add_outer(grad_wout, wout_other, 0)

time: 736 us -> 730 us (level)
    reduce_scatter x6, waiting for transfers between devices: 22.6 us -> 36.3 us  [reduce_seq(): return lax.psum_scatter(values, 'seq', scatter_dimension=0, tiled=False)]
    ppermute x46, waiting for transfers between devices: 124 us -> 111 us  [swap(): return lax.ppermute(values, 'rows', pairs)]
    squeeze x16 -> x15, local copies, waits for them, and re-layouts: 18.3 us -> 15.2 us  [part(): return lax.dynamic_index_in_dim(values, index, axis, keepdims=False)]
    unnamed x163 -> x155, local copies, waits for them, and re-layouts: 27.6 us -> 24.9 us
  transfers between devices with their start and end apart: 62 -> 62, of which waited for: 26 -> 25; matrix products, arithmetic and copies ran while one was open for 19% -> 19% of each run, Pallas kernels for 33% -> 32%
where the time goes in v11:
time: 730 us; the launch traced here: 719 us
  Pallas kernels  266 us (36%)
  waiting for transfers between devices  188 us (26%)
  other arithmetic  83.2 us (11%)
  local copies, waits for them, and re-layouts  72.2 us (10%)
  starting transfers between devices  43 us (6%)
  matrix products  29 us (4%)
  blocking collectives  19.9 us (3%)
  between operations  18.3 us (3%)
    ppermute x46, waiting for transfers between devices, swap(): return lax.ppermute(values, 'rows', pairs)  111 us
    pallas_call x3, Pallas kernels, weight_pass(): pl.pallas_call(partial(weight_kernel, len(lefts)), grid=(rows // tile,),...  47.2 us
    pallas_call x4, Pallas kernels, back_pass(): pl.pallas_call(partial(back_kernel, count, transposed), grid=(width // ti...  46.3 us
    all_gather x5, waiting for transfers between devices, gather_seq(): return lax.all_gather(values, 'seq', axis=0, tiled=False)  38.9 us
    ppermute x46, starting transfers between devices, swap(): return lax.ppermute(values, 'rows', pairs)  37.4 us
    reduce_scatter x6, waiting for transfers between devices, reduce_seq(): return lax.psum_scatter(values, 'seq', scatter_dimension=0, tiled=False)  36.3 us
    pallas_call x2, Pallas kernels, attend_backward(): pl.pallas_call(partial(attend_backward_kernel, first, count), grid_spec=p...  28 us
    pallas_call x17, Pallas kernels, joined(): pl.pallas_call(joined_kernel, grid_spec=pltpu.PrefetchScalarGridSpec(num_...  25.3 us
  transfers between devices with their start and end apart: 62, of which 25 were waited for; matrix products, arithmetic and copies ran while one was open for 19% of the time, Pallas kernels for 32%

profile of v11, /device:TPU:0, one launch (start us, length us, event | category | flops | bytes accessed | tf_op | source)
XLA Modules:
  0.0 719.4 jit_solution(7780285837232621076)
XLA Ops:
  28.3 19.9 %all-gather = bf16[256,768]{1,0:T(8,128)(2,1)S(1)} all-gather(bf16[64,768]{1,0:T(8,128)(2,1)S(1)} %fusion.35), channel_id=2, replica_groups=mesh['rows'=8,'seq'=4] {'seq'}, dimensions={0}, use_global_device_ids=true | all-gather | bytes 491520 | tf_op jit(solution)/shard_map/all_gather | solution.py:815
  100.4 26.6 %collective-permute-done.11 = bf16[2,4,64,1280]{3,2,1,0:T(8,128)(2,1)} collective-permute-done((bf16[2,4,64,1280]{3,2,1,0:T(8,128)(2,1)}, bf16[2,4,64,1280]{3,2,1,0:T(8,128)(2,1)}, u32[]{:S(2)}, u32[]{:S(2)}) %collective-permute-start.11) | collective-permute-done | bytes 1310752 | tf_op jit(solution)/shard_map/ppermute | solution.py:718
  141.0 8.8 %heads_forward_halves.1 = (f32[512,1280]{1,0:T(8,128)}, bf16[512,1280]{1,0:T(8,128)(2,1)S(1)}) custom-call(s32[1]{0:T(128)} %bitcast.1.side_ref, bf16[512,2048]{1,0:T(8,128)(2,1)S(1)} %copy-done.6, bf16[4,256,1280]{2,1,0:T(8,128)(2,1)} %bitcast.54.own_ref, bf16[4,256,1280]{2,1,0:T(8,128)(2,1)} %bitcast.55.other_ref, ...), custom_call_target="tpu_custom_call" | custom-call | flops 1000 | bytes 1000 | tf_op jit(solution)/shard_map/heads_forward_halves/pallas_call | solution.py:104
  161.5 11.7 %attend_forward.1 = (bf16[512,1280]{1,0:T(8,128)(2,1)S(1)}, f32[512,1280]{1,0:T(8,128)S(1)}) custom-call(s32[1]{0:T(128)} %bitcast.33.place_ref, bf16[512,1280]{1,0:T(8,128)(2,1)S(1)} %copy-done.12, bf16[2048,640]{1,0:T(8,128)(2,1)} %all-gather.14.cloned.1.call-done.k_ref.v_ref, bf16[2048,640]{1,0:T(8,128)(2,1)} %all-gather.14.cloned.1.call-done.k_ref.v_ref), custom_call_target="tpu_custom_call" | custom-call | flops 1000 | bytes 1000 | tf_op jit(solution)/shard_map/attend_forward/pallas_call | solution.py:273
  174.8 34.1 %all-gather.18.cloned.1.call-done = bf16[8,2,64,1152]{3,2,1,0:T(8,128)(2,1)} async-done(((bf16[2,2,64,1152]{3,2,1,0:T(8,128)(2,1)}), bf16[8,2,64,1152]{3,2,1,0:T(8,128)(2,1)}) %all-gather.18.cloned.1.call-update) | async-done | bytes 2359312 | tf_op jit(solution)/shard_map/all_gather | solution.py:815
  241.2 9.3 %gate_pass.1.gate_ref = bf16[1024,1152]{1,0:T(8,128)(2,1)} custom-call(bf16[512,2048]{1,0:T(8,128)(2,1)S(1)} %multiply_convert_fusion.n0_ref.refs_0_, bf16[512,2048]{1,0:T(8,128)(2,1)S(1)} %collective-permute-done.18.n1_ref.refs_1_, bf16[2048,1152]{1,0:T(8,128)(2,1)} %bitcast.287), custom_call_target="tpu_custom_call" | custom-call | flops 1000 | bytes 1000 | tf_op jit(solution)/shard_map/gate_pass/pallas_call | solution.py:478
  250.5 19.5 %collective-permute-done.19.n0_ref.refs_2_ = bf16[512,2048]{1,0:T(8,128)(2,1)S(1)} collective-permute-done((bf16[512,2048]{1,0:T(8,128)(2,1)S(1)}, bf16[512,2048]{1,0:T(8,128)(2,1)S(1)}, u32[]{:S(2)}, u32[]{:S(2)}) %collective-permute-start.19) | collective-permute-done | bytes 2097184 | tf_op jit(solution)/shard_map/ppermute | solution.py:718
  276.1 9.7 %up_pass.1 = (bf16[1024,1152]{1,0:T(8,128)(2,1)}, bf16[1024,1152]{1,0:T(8,128)(2,1)}) custom-call(bf16[512,2048]{1,0:T(8,128)(2,1)S(1)} %multiply_convert_fusion.n0_ref.refs_0_, bf16[512,2048]{1,0:T(8,128)(2,1)S(1)} %collective-permute-done.18.n1_ref.refs_1_, bf16[2048,1152]{1,0:T(8,128)(2,1)} %bitcast.291, bf16[1024,1152]{1,0:T(8,128)(2,1)} %gate_pass.1.gate_ref), custom_call_target="tpu_custom_call" | custom-call | flops 1000 | bytes 1000 | tf_op jit(solution)/shard_map/up_pass/pallas_call | solution.py:505
  285.8 14.9 %hidden_pass.1 = (bf16[1024,1152]{1,0:T(8,128)(2,1)}, bf16[1024,1152]{1,0:T(8,128)(2,1)}, bf16[1024,1152]{1,0:T(8,128)(2,1)}) custom-call(bf16[512,2048]{1,0:T(8,128)(2,1)S(1)} %collective-permute-done.19.n0_ref.refs_2_, bf16[512,2048]{1,0:T(8,128)(2,1)S(1)} %collective-permute-done.21.n1_ref.refs_3_, bf16[2048,1152]{1,0:T(8,128)(2,1)} %bitcast.288, ...), custom_call_target="tpu_custom_call" | custom-call | flops 1000 | bytes 1000 | tf_op jit(solution)/shard_map/hidden_pass/pallas_call | solution.py:454
  302.0 12.3 %gates_pass.2 = (bf16[1024,1152]{1,0:T(8,128)(2,1)}, bf16[1024,1152]{1,0:T(8,128)(2,1)}) custom-call(bf16[512,2048]{1,0:T(8,128)(2,1)} %collective-permute-done.15.g0_ref.refs_4_, bf16[512,2048]{1,0:T(8,128)(2,1)} %collective-permute-done.22.g1_ref.refs_5_, bf16[1152,2048]{1,0:T(8,128)(2,1)} %bitcast.295, bf16[1024,1152]{1,0:T(8,128)(2,1)} %get-tuple-element.216.gate_ref, ...), custom_call_target="tpu_custom_call" | custom-call | flops 1000 | bytes 1000 | tf_op jit(solution)/shard_map/gates_pass/pallas_call | solution.py:539
  316.0 14.9 %back_pass.4 = (f32[512,2048]{1,0:T(8,128)}, bf16[512,2048]{1,0:T(8,128)(2,1)S(1)}) custom-call(bf16[1024,1152]{1,0:T(8,128)(2,1)S(1)} %copy-done.17, bf16[1024,1152]{1,0:T(8,128)(2,1)} %get-tuple-element.219.refs_1_.refs_5_, bf16[2048,1152]{1,0:T(8,128)(2,1)} %bitcast.289, bf16[2048,1152]{1,0:T(8,128)(2,1)} %bitcast.293), custom_call_target="tpu_custom_call" | custom-call | flops 1000 | bytes 1000 | tf_op jit(solution)/shard_map/back_pass/pallas_call | solution.py:578
  331.0 15.6 %weight_pass.3 = bf16[1152,2048]{1,0:T(8,128)(2,1)} custom-call(bf16[1024,1152]{1,0:T(8,128)(2,1)} %get-tuple-element.291.refs_0_, bf16[1024,1152]{1,0:T(8,128)(2,1)} %get-tuple-element.246.refs_1_.refs_0_, bf16[512,2048]{1,0:T(8,128)(2,1)} %bitcast_convert_fusion.refs_2_.g0_ref, bf16[512,2048]{1,0:T(8,128)(2,1)} %collective-permute-done.14.refs_3_.g1_ref, ...), custom_call_target="tpu_custom_call" | custom-call | flops 1000 | bytes 1000 | tf_op jit(solution)/shard_map/weight_pass/pallas_call | solution.py:612
  353.6 12.3 %gates_pass.3 = (bf16[1024,1152]{1,0:T(8,128)(2,1)}, bf16[1024,1152]{1,0:T(8,128)(2,1)}) custom-call(bf16[512,2048]{1,0:T(8,128)(2,1)} %bitcast_convert_fusion.refs_2_.g0_ref, bf16[512,2048]{1,0:T(8,128)(2,1)} %collective-permute-done.14.refs_3_.g1_ref, bf16[1152,2048]{1,0:T(8,128)(2,1)} %bitcast.296, bf16[1024,1152]{1,0:T(8,128)(2,1)} %gate_pass.1.gate_ref, ...), custom_call_target="tpu_custom_call" | custom-call | flops 1000 | bytes 1000 | tf_op jit(solution)/shard_map/gates_pass/pallas_call | solution.py:539
  367.6 15.0 %back_pass.5 = (f32[512,2048]{1,0:T(8,128)}, bf16[512,2048]{1,0:T(8,128)(2,1)}) custom-call(bf16[1024,1152]{1,0:T(8,128)(2,1)S(1)} %copy-done.18, bf16[1024,1152]{1,0:T(8,128)(2,1)} %get-tuple-element.237.refs_1_.refs_4_, bf16[2048,1152]{1,0:T(8,128)(2,1)} %bitcast.290, bf16[2048,1152]{1,0:T(8,128)(2,1)} %bitcast.294), custom_call_target="tpu_custom_call" | custom-call | flops 1000 | bytes 1000 | tf_op jit(solution)/shard_map/back_pass/pallas_call | solution.py:578
  382.6 15.8 %weight_pass.4 = bf16[2048,1152]{1,0:T(8,128)(2,1)} custom-call(bf16[512,2048]{1,0:T(8,128)(2,1)S(1)} %multiply_convert_fusion.n0_ref.refs_0_, bf16[512,2048]{1,0:T(8,128)(2,1)S(1)} %copy-done.3, bf16[512,2048]{1,0:T(8,128)(2,1)} %copy-done.9, bf16[512,2048]{1,0:T(8,128)(2,1)} %copy-done.10, bf16[1024,1152]{1,0:T(8,128)(2,1)} %get-tuple-element.231.refs_0_.refs_4_, ...), custom_call_target="tpu_custom_call" | custom-call | flops 1000 | bytes 1000 | tf_op jit(solution)/shard_map/weight_pass/pallas_call | solution.py:612
  400.2 15.7 %weight_pass.5 = bf16[2048,1152]{1,0:T(8,128)(2,1)} custom-call(bf16[512,2048]{1,0:T(8,128)(2,1)S(1)} %multiply_convert_fusion.n0_ref.refs_0_, bf16[512,2048]{1,0:T(8,128)(2,1)S(1)} %copy-done.4, bf16[512,2048]{1,0:T(8,128)(2,1)} %copy-done.9, bf16[512,2048]{1,0:T(8,128)(2,1)} %copy-done.10, bf16[1024,1152]{1,0:T(8,128)(2,1)} %get-tuple-element.237.refs_1_.refs_4_, ...), custom_call_target="tpu_custom_call" | custom-call | flops 1000 | bytes 1000 | tf_op jit(solution)/shard_map/weight_pass/pallas_call | solution.py:612
  438.5 11.0 %attend_backward.2 = (bf16[512,512]{1,0:T(8,128)(2,1)S(1)}, bf16[2048,256]{1,0:T(8,128)(2,1)S(1)}) custom-call(s32[1]{0:T(128)} %bitcast.33.place_ref, bf16[512,1280]{1,0:T(8,128)(2,1)S(1)} %copy-done.13, bf16[2048,640]{1,0:T(8,128)(2,1)} %all-gather.14.cloned.1.call-done.k_ref.v_ref, bf16[2048,640]{1,0:T(8,128)(2,1)} %all-gather.14.cloned.1.call-done.k_ref.v_ref, ...), custom_call_target="tpu_custom_call" | custom-call | flops 1000 | bytes 1000 | tf_op jit(solution)/shard_map/attend_backward/pallas_call | solution.py:410
  452.4 15.0 %reduce-scatter.7.cloned.1.call-done = bf16[1,144,2048]{2,1,0:T(8,128)(2,1)} async-done(((bf16[4,144,2048]{2,1,0:T(8,128)(2,1)}), bf16[1,144,2048]{2,1,0:T(8,128)(2,1)}) %reduce-scatter.7.cloned.1.call-update) | async-done | bytes 589840 | tf_op jit(solution)/shard_map/reduce_scatter | solution.py:819
  469.1 8.2 %back_pass.6 = (f32[512,2048]{1,0:T(8,128)}, bf16[512,2048]{1,0:T(8,128)(2,1)}) custom-call(bf16[1024,1152]{1,0:T(8,128)(2,1)S(1)} %copy-done.16, bf16[1152,2048]{1,0:T(8,128)(2,1)} %bitcast.297), custom_call_target="tpu_custom_call" | custom-call | flops 1000 | bytes 1000 | tf_op jit(solution)/shard_map/back_pass/pallas_call | solution.py:578
  501.9 17.0 %attend_backward.3 = (bf16[512,768]{1,0:T(8,128)(2,1)S(1)}, bf16[2048,384]{1,0:T(8,128)(2,1)}) custom-call(s32[1]{0:T(128)} %bitcast.33.place_ref, bf16[512,1280]{1,0:T(8,128)(2,1)S(1)} %copy-done.13, bf16[2048,640]{1,0:T(8,128)(2,1)} %all-gather.14.cloned.1.call-done.k_ref.v_ref, bf16[2048,640]{1,0:T(8,128)(2,1)} %all-gather.14.cloned.1.call-done.k_ref.v_ref, ...), custom_call_target="tpu_custom_call" | custom-call | flops 1000 | bytes 1000 | tf_op jit(solution)/shard_map/attend_backward/pallas_call | solution.py:410
  518.9 26.3 %collective-permute-done.30 = bf16[2,2,4,64,1152]{4,3,1,0,2:T(8,128)(2,1)} collective-permute-done((bf16[2,2,4,64,1152]{4,3,1,0,2:T(8,128)(2,1)S(1)}, bf16[2,2,4,64,1152]{4,3,1,0,2:T(8,128)(2,1)}, u32[]{:S(2)}, u32[]{:S(2)}) %collective-permute-start.30) | collective-permute-done | bytes 2359328 | tf_op jit(solution)/shard_map/ppermute | solution.py:718
  555.6 8.9 %heads_backward.2 = (bf16[512,1280]{1,0:T(8,128)(2,1)}, f32[8,1280]{1,0:T(8,128)}) custom-call(bf16[512,1280]{1,0:T(8,128)(2,1)} %pad_maximum_fusion.3.grad_ref, f32[512,1280]{1,0:T(8,128)} %get-tuple-element.262.joint_ref, f32[8,1280]{1,0:T(8,128)} %copy-done.39, f32[512,128]{1,0:T(8,128)} %copy-done.19, f32[512,128]{1,0:T(8,128)} %copy-done.20), custom_call_target="tpu_custom_call" | custom-call | flops 1000 | bytes 1000 | tf_op jit(solution)/shard_map/heads_backward/pallas_call | solution.py:205
  595.4 13.6 %reduce-scatter.13.cloned.1.call-done = bf16[1,512,384]{1,2,0:T(8,128)(2,1)} async-done(((bf16[4,512,384]{1,2,0:T(8,128)(2,1)}), bf16[1,512,384]{1,2,0:T(8,128)(2,1)}) %reduce-scatter.13.cloned.1.call-update) | async-done | bytes 393232 | tf_op jit(solution)/shard_map/reduce_scatter | solution.py:819
  638.5 8.2 %back_pass.7 = (f32[512,2048]{1,0:T(8,128)}, bf16[512,2048]{1,0:T(8,128)(2,1)}) custom-call(bf16[1024,1152]{1,0:T(8,128)(2,1)S(1)} %copy-done.15, bf16[1152,2048]{1,0:T(8,128)(2,1)} %bitcast.298), custom_call_target="tpu_custom_call" | custom-call | flops 1000 | bytes 1000 | tf_op jit(solution)/shard_map/back_pass/pallas_call | solution.py:578
  (441 shorter events, 336.6 us)
Async XLA Ops:
  7.2 44.7 %all-gather.12.cloned.1.call-start = ((), (), s32[]{:S(2)}) async-start(), calls=%async_computation.12 | async-start | bytes 1638400 | tf_op jit(solution)/shard_map/all_gather | solution.py:815
  9.8 119.7 %all-gather.16.cloned.1.call-start = ((), (), s32[]{:S(2)}) async-start(), calls=%async_computation.14 | async-start | bytes 2949120 | tf_op jit(solution)/shard_map/all_gather | solution.py:815
  53.2 105.0 %all-gather.14.cloned.1.call-start = ((), (), s32[]{:S(2)}) async-start(), calls=%async_computation.13 | async-start | bytes 3276800 | tf_op jit(solution)/shard_map/all_gather | solution.py:815
  93.3 115.6 %all-gather.18.cloned.1.call-start = ((), (), s32[]{:S(2)}) async-start(), calls=%async_computation.15 | async-start | bytes 2949120 | tf_op jit(solution)/shard_map/all_gather | solution.py:815
  100.3 201.7 %all-gather.20.cloned.1.call-start = ((), (), s32[]{:S(2)}) async-start(), calls=%async_computation.16 | async-start | bytes 5898240 | tf_op jit(solution)/shard_map/all_gather | solution.py:815
  154.2 54.8 %collective-permute-start.16 = (bf16[2,2,4,64,1280]{4,3,2,1,0:T(8,128)(2,1)}, bf16[2,2,4,64,1280]{4,3,2,1,0:T(8,128)(2,1)}, u32[]{:S(2)}, u32[]{:S(2)}) collective-permute-start(bf16[2,2,4,64,1280]{4,3,2,1,0:T(8,128)(2,1)} %bitcast.62), channel_id=1, source_target_pairs={{0,4},{4,0},{8,12},{12,8},{16,20},{20,16},{24,28},{28,24},{1,5},{5... | collective-permute-start | bytes 7864328 | tf_op jit(solution)/shard_map/ppermute | solution.py:718
  154.3 54.6 %collective-permute-start.15 = (bf16[512,2048]{1,0:T(8,128)(2,1)}, bf16[512,2048]{1,0:T(8,128)(2,1)}, u32[]{:S(2)}, u32[]{:S(2)}) collective-permute-start(bf16[512,2048]{1,0:T(8,128)(2,1)} %bitcast_convert_fusion.refs_2_.g0_ref), channel_id=1, source_target_pairs={{0,8},{4,12},{8,0},{12,4},{16,24},{20,28},{24,16},{28,20},{1,9},{5... | collective-permute-start | bytes 6291464 | tf_op jit(solution)/shard_map/ppermute | solution.py:718
  155.0 54.0 %collective-permute-start.14 = (bf16[512,2048]{1,0:T(8,128)(2,1)}, bf16[512,2048]{1,0:T(8,128)(2,1)}, u32[]{:S(2)}, u32[]{:S(2)}) collective-permute-start(bf16[512,2048]{1,0:T(8,128)(2,1)} %bitcast_convert_fusion.refs_2_.g0_ref), channel_id=1, source_target_pairs={{0,4},{4,0},{8,12},{12,8},{16,20},{20,16},{24,28},{28,24},{1,5},{5... | collective-permute-start | bytes 6291464 | tf_op jit(solution)/shard_map/ppermute | solution.py:718
  158.2 309.2 %reduce-scatter.7.cloned.1.call-start = ((), (), s32[]{:S(2)}) async-start(), calls=%async_computation.6 | async-start | bytes 2949120 | tf_op jit(solution)/shard_map/reduce_scatter | solution.py:819
  158.7 63.2 %collective-permute-start.17 = (bf16[4,2,2,64,1152]{4,3,2,1,0:T(8,128)(2,1)}, bf16[4,2,2,64,1152]{4,3,2,1,0:T(8,128)(2,1)}, u32[]{:S(2)}, u32[]{:S(2)}) collective-permute-start(bf16[4,2,2,64,1152]{4,3,2,1,0:T(8,128)(2,1)} %bitcast.263), channel_id=1, source_target_pairs={{0,16},{4,20},{8,24},{12,28},{16,0},{20,4},{24,8},{28,12},{1,17},{... | collective-permute-start | bytes 7077896 | tf_op jit(solution)/shard_map/ppermute | solution.py:718
  208.9 61.1 %collective-permute-start.20 = (bf16[4,2,2,64,1152]{4,3,2,1,0:T(8,128)(2,1)}, bf16[4,2,2,64,1152]{4,3,2,1,0:T(8,128)(2,1)}, u32[]{:S(2)}, u32[]{:S(2)}) collective-permute-start(bf16[4,2,2,64,1152]{4,3,2,1,0:T(8,128)(2,1)} %bitcast.265), channel_id=1, source_target_pairs={{0,16},{4,20},{8,24},{12,28},{16,0},{20,4},{24,8},{28,12},{1,17},{... | collective-permute-start | bytes 7077896 | tf_op jit(solution)/shard_map/ppermute | solution.py:718
  222.0 48.0 %collective-permute-start.19 = (bf16[512,2048]{1,0:T(8,128)(2,1)S(1)}, bf16[512,2048]{1,0:T(8,128)(2,1)S(1)}, u32[]{:S(2)}, u32[]{:S(2)}) collective-permute-start(bf16[512,2048]{1,0:T(8,128)(2,1)S(1)} %multiply_convert_fusion.n0_ref.refs_0_), channel_id=1, source_target_pairs={{0,8},{4,12},{8,0},{12,4},{16,24},{20,28},{24,16},{28,20},{1,9},{5... | collective-permute-start | bytes 6291464 | tf_op jit(solution)/shard_map/ppermute | solution.py:718
  223.6 62.1 %collective-permute-start.22 = (bf16[512,2048]{1,0:T(8,128)(2,1)}, bf16[512,2048]{1,0:T(8,128)(2,1)}, u32[]{:S(2)}, u32[]{:S(2)}) collective-permute-start(bf16[512,2048]{1,0:T(8,128)(2,1)} %collective-permute-done.15.g0_ref.refs_4_), channel_id=1, source_target_pairs={{0,4},{4,0},{8,12},{12,8},{16,20},{20,16},{24,28},{28,24},{1,5},{5... | collective-permute-start | bytes 6291464 | tf_op jit(solution)/shard_map/ppermute | solution.py:718
  348.6 49.8 %collective-permute-start.24 = (bf16[512,2048]{1,0:T(8,128)(2,1)}, bf16[512,2048]{1,0:T(8,128)(2,1)}, u32[]{:S(2)}, u32[]{:S(2)}) collective-permute-start(bf16[512,2048]{1,0:T(8,128)(2,1)} %add_convert_fusion.2), channel_id=1, source_target_pairs={{0,8},{4,12},{8,0},{12,4},{16,24},{20,28},{24,16},{28,20},{1,9},{5... | collective-permute-start | bytes 6291464 | tf_op jit(solution)/shard_map/ppermute | solution.py:718
  353.6 62.3 %collective-permute-start.26 = (bf16[4,144,2048]{2,1,0:T(8,128)(2,1)}, bf16[4,144,2048]{2,1,0:T(8,128)(2,1)}, u32[]{:S(2)}, u32[]{:S(2)}) collective-permute-start(bf16[4,144,2048]{2,1,0:T(8,128)(2,1)} %dynamic-slice_bitcast_fusion.1), channel_id=1, source_target_pairs={{0,16},{4,20},{8,24},{12,28},{16,0},{20,4},{24,8},{28,12},{1,17},{... | collective-permute-start | bytes 7077896 | tf_op jit(solution)/shard_map/ppermute | solution.py:718
  420.8 124.4 %reduce-scatter.9.cloned.1.call-start = ((), (), s32[]{:S(2)}) async-start(), calls=%async_computation.7 | async-start | bytes 1310720 | tf_op jit(solution)/shard_map/reduce_scatter | solution.py:819
  424.4 60.4 %collective-permute-start.28 = (bf16[2,2,4,64,1152]{4,3,1,0,2:T(8,128)(2,1)}, bf16[2,2,4,64,1152]{4,3,1,0,2:T(8,128)(2,1)}, u32[]{:S(2)}, u32[]{:S(2)}) collective-permute-start(bf16[2,2,4,64,1152]{4,3,1,0,2:T(8,128)(2,1)} %copy_bitcast_fusion.3), channel_id=1, source_target_pairs={{0,16},{4,20},{8,24},{12,28},{16,0},{20,4},{24,8},{28,12},{1,17},{... | collective-permute-start | bytes 7077896 | tf_op jit(solution)/shard_map/ppermute | solution.py:718
  477.3 76.1 %reduce-scatter.11.cloned.1.call-start = ((), (), s32[]{:S(2)}) async-start(), calls=%async_computation.8 | async-start | bytes 2949120 | tf_op jit(solution)/shard_map/reduce_scatter | solution.py:819
  489.3 119.7 %reduce-scatter.13.cloned.1.call-start = ((), (), s32[]{:S(2)}) async-start(), calls=%async_computation.9 | async-start | bytes 1966080 | tf_op jit(solution)/shard_map/reduce_scatter | solution.py:819
  491.4 53.8 %collective-permute-start.30 = (bf16[2,2,4,64,1152]{4,3,1,0,2:T(8,128)(2,1)S(1)}, bf16[2,2,4,64,1152]{4,3,1,0,2:T(8,128)(2,1)}, u32[]{:S(2)}, u32[]{:S(2)}) collective-permute-start(bf16[2,2,4,64,1152]{4,3,1,0,2:T(8,128)(2,1)S(1)} %copy_bitcast_fusion.2), channel_id=1, source_target_pairs={{0,16},{4,20},{8,24},{12,28},{16,0},{20,4},{24,8},{28,12},{1,17},{... | collective-permute-start | bytes 7077896 | tf_op jit(solution)/shard_map/ppermute | solution.py:718
  496.4 52.1 %collective-permute-start.29 = (bf16[2,2,4,64,1280]{4,3,2,1,0:T(8,128)(2,1)}, bf16[2,2,4,64,1280]{4,3,2,1,0:T(8,128)(2,1)}, u32[]{:S(2)}, u32[]{:S(2)}) collective-permute-start(bf16[2,2,4,64,1280]{4,3,2,1,0:T(8,128)(2,1)} %dynamic-slice_bitcast_fusion), channel_id=1, source_target_pairs={{0,4},{4,0},{8,12},{12,8},{16,20},{20,16},{24,28},{28,24},{1,5},{5... | collective-permute-start | bytes 7864328 | tf_op jit(solution)/shard_map/ppermute | solution.py:718
  500.5 48.1 %collective-permute-start.31 = (bf16[512,2048]{1,0:T(8,128)(2,1)}, bf16[512,2048]{1,0:T(8,128)(2,1)}, u32[]{:S(2)}, u32[]{:S(2)}) collective-permute-start(bf16[512,2048]{1,0:T(8,128)(2,1)} %add_convert_fusion.1), channel_id=1, source_target_pairs={{0,8},{4,12},{8,0},{12,4},{16,24},{20,28},{24,16},{28,20},{1,9},{5... | collective-permute-start | bytes 6291464 | tf_op jit(solution)/shard_map/ppermute | solution.py:718
  573.9 85.9 %reduce-scatter.15.cloned.1.call-start = ((), (), s32[]{:S(2)}) async-start(), calls=%async_computation.10 | async-start | bytes 2949120 | tf_op jit(solution)/shard_map/reduce_scatter | solution.py:819
  611.1 96.5 %reduce-scatter.17.cloned.1.call-start = ((), (), s32[]{:S(2)}) async-start(), calls=%async_computation.11 | async-start | bytes 2129920 | tf_op jit(solution)/shard_map/reduce_scatter | solution.py:819
  (115 other events, 1080.8 us)
Sparse Core Ops, SparseCore 0:
  10.2 41.6 all-gather.11
  53.4 49.5 all-gather.15
  104.6 53.6 all-gather.13
  159.6 49.2 all-gather.17
  210.9 88.2 all-gather.19
  421.0 46.4 reduce-scatter.6
  477.4 26.7 reduce-scatter.8
  506.7 46.7 reduce-scatter.10
  574.0 34.9 reduce-scatter.12
  611.3 47.0 reduce-scatter.14
  671.8 35.7 reduce-scatter.16

commit v12 on v11

--- a/solution.py
+++ b/solution.py
@@ -1070,12 +1070,11 @@
     across = (own_far + far_other.astype(f32)).astype(bf16)
     across, grad_mixed = stage(across, grad_mixed)
     grad_q2, grad_kv2 = attend_backward(2, 3, *attend, grad_mixed)
-    grad_q2, grad_kv2, hidden_near, grad_kv1, grad_gate, wout_other, up_other, across = stage(
+    grad_q2, grad_kv2, hidden_near, grad_kv1, wout_other, up_other, across = stage(
         grad_q2,
         grad_kv2,
         hidden_near,
         grad_kv1,
-        grad_gate,
         pass_bit(grad_wout, 1, 2),
         pass_outer(grad_wup, 0),
         swap(across, 2),
@@ -1091,7 +1090,9 @@
     grad_up = jnp.moveaxis(add_outer(grad_wup, up_other, 0), 2, 0)
     grad_wq = reduce_bit(grad_wq, 1, 2)
     wq_other, wout_other = pass_bit(grad_wq, 2, 1), pass_outer(grad_wout, 0)
-    grad_kv2, grad_normed, grad_up = stage(grad_kv2, mm_t(joint_grad_q, wq), grad_up)
+    grad_kv2, grad_normed, grad_up, grad_gate = stage(
+        grad_kv2, mm_t(joint_grad_q, wq), grad_up, grad_gate
+    )
     grad_up = reduce_seq(grad_up)
 
     grad_kv1, grad_kv2 = (

time: 730 us -> 721 us (0.988)
  waiting for transfers between devices: 188 us -> 179 us
    unnamed x155 -> x161, local copies, waits for them, and re-layouts: 24.9 us -> 29.1 us
  transfers between devices with their start and end apart: 62 -> 62, of which waited for: 25 -> 24; matrix products, arithmetic and copies ran while one was open for 19% -> 20% of each run, Pallas kernels for 32% -> 34%
where the time goes in v12:
time: 721 us; the launch traced here: 711 us
  Pallas kernels  266 us (37%)
  waiting for transfers between devices  179 us (25%)
  other arithmetic  82.6 us (11%)
  local copies, waits for them, and re-layouts  76.2 us (11%)
  starting transfers between devices  42 us (6%)
  matrix products  26.7 us (4%)
  blocking collectives  19.9 us (3%)
  between operations  18.4 us (3%)
    ppermute x46, waiting for transfers between devices, swap(): return lax.ppermute(values, 'rows', pairs)  105 us
    pallas_call x3, Pallas kernels, weight_pass(): pl.pallas_call(partial(weight_kernel, len(lefts)), grid=(rows // tile,),...  47.6 us
    pallas_call x4, Pallas kernels, back_pass(): pl.pallas_call(partial(back_kernel, count, transposed), grid=(width // ti...  46.3 us
    all_gather x5, waiting for transfers between devices, gather_seq(): return lax.all_gather(values, 'seq', axis=0, tiled=False)  38.9 us
    ppermute x46, starting transfers between devices, swap(): return lax.ppermute(values, 'rows', pairs)  36.4 us
    reduce_scatter x6, waiting for transfers between devices, reduce_seq(): return lax.psum_scatter(values, 'seq', scatter_dimension=0, tiled=False)  32.5 us
    unnamed x161, local copies, waits for them, and re-layouts  29.1 us
    pallas_call x2, Pallas kernels, attend_backward(): pl.pallas_call(partial(attend_backward_kernel, first, count), grid_spec=p...  28 us
  transfers between devices with their start and end apart: 62, of which 24 were waited for; matrix products, arithmetic and copies ran while one was open for 20% of the time, Pallas kernels for 34%

profile of v12, /device:TPU:0, one launch (start us, length us, event | category | flops | bytes accessed | tf_op | source)
XLA Modules:
  0.0 710.9 jit_solution(9960939473838239823)
XLA Ops:
  28.3 19.9 %all-gather = bf16[256,768]{1,0:T(8,128)(2,1)S(1)} all-gather(bf16[64,768]{1,0:T(8,128)(2,1)S(1)} %fusion.35), channel_id=2, replica_groups=mesh['rows'=8,'seq'=4] {'seq'}, dimensions={0}, use_global_device_ids=true | all-gather | bytes 491520 | tf_op jit(solution)/shard_map/all_gather | solution.py:815
  100.4 26.6 %collective-permute-done.11 = bf16[2,4,64,1280]{3,2,1,0:T(8,128)(2,1)} collective-permute-done((bf16[2,4,64,1280]{3,2,1,0:T(8,128)(2,1)}, bf16[2,4,64,1280]{3,2,1,0:T(8,128)(2,1)}, u32[]{:S(2)}, u32[]{:S(2)}) %collective-permute-start.11) | collective-permute-done | bytes 1310752 | tf_op jit(solution)/shard_map/ppermute | solution.py:718
  141.0 8.8 %heads_forward_halves.1 = (f32[512,1280]{1,0:T(8,128)}, bf16[512,1280]{1,0:T(8,128)(2,1)S(1)}) custom-call(s32[1]{0:T(128)} %bitcast.1.side_ref, bf16[512,2048]{1,0:T(8,128)(2,1)S(1)} %copy-done.6, bf16[4,256,1280]{2,1,0:T(8,128)(2,1)} %bitcast.54.own_ref, bf16[4,256,1280]{2,1,0:T(8,128)(2,1)} %bitcast.55.other_ref, ...), custom_call_target="tpu_custom_call" | custom-call | flops 1000 | bytes 1000 | tf_op jit(solution)/shard_map/heads_forward_halves/pallas_call | solution.py:104
  161.5 11.7 %attend_forward.1 = (bf16[512,1280]{1,0:T(8,128)(2,1)S(1)}, f32[512,1280]{1,0:T(8,128)S(1)}) custom-call(s32[1]{0:T(128)} %bitcast.33.place_ref, bf16[512,1280]{1,0:T(8,128)(2,1)S(1)} %copy-done.12, bf16[2048,640]{1,0:T(8,128)(2,1)} %all-gather.14.cloned.1.call-done.k_ref.v_ref, bf16[2048,640]{1,0:T(8,128)(2,1)} %all-gather.14.cloned.1.call-done.k_ref.v_ref), custom_call_target="tpu_custom_call" | custom-call | flops 1000 | bytes 1000 | tf_op jit(solution)/shard_map/attend_forward/pallas_call | solution.py:273
  174.8 34.1 %all-gather.18.cloned.1.call-done = bf16[8,2,64,1152]{3,2,1,0:T(8,128)(2,1)} async-done(((bf16[2,2,64,1152]{3,2,1,0:T(8,128)(2,1)}), bf16[8,2,64,1152]{3,2,1,0:T(8,128)(2,1)}) %all-gather.18.cloned.1.call-update) | async-done | bytes 2359312 | tf_op jit(solution)/shard_map/all_gather | solution.py:815
  241.2 9.3 %gate_pass.1.gate_ref = bf16[1024,1152]{1,0:T(8,128)(2,1)} custom-call(bf16[512,2048]{1,0:T(8,128)(2,1)S(1)} %multiply_convert_fusion.n0_ref.refs_0_, bf16[512,2048]{1,0:T(8,128)(2,1)S(1)} %collective-permute-done.18.n1_ref.refs_1_, bf16[2048,1152]{1,0:T(8,128)(2,1)} %bitcast.287), custom_call_target="tpu_custom_call" | custom-call | flops 1000 | bytes 1000 | tf_op jit(solution)/shard_map/gate_pass/pallas_call | solution.py:478
  250.5 19.5 %collective-permute-done.19.n0_ref.refs_2_ = bf16[512,2048]{1,0:T(8,128)(2,1)S(1)} collective-permute-done((bf16[512,2048]{1,0:T(8,128)(2,1)S(1)}, bf16[512,2048]{1,0:T(8,128)(2,1)S(1)}, u32[]{:S(2)}, u32[]{:S(2)}) %collective-permute-start.19) | collective-permute-done | bytes 2097184 | tf_op jit(solution)/shard_map/ppermute | solution.py:718
  276.0 9.7 %up_pass.1 = (bf16[1024,1152]{1,0:T(8,128)(2,1)}, bf16[1024,1152]{1,0:T(8,128)(2,1)}) custom-call(bf16[512,2048]{1,0:T(8,128)(2,1)S(1)} %multiply_convert_fusion.n0_ref.refs_0_, bf16[512,2048]{1,0:T(8,128)(2,1)S(1)} %collective-permute-done.18.n1_ref.refs_1_, bf16[2048,1152]{1,0:T(8,128)(2,1)} %bitcast.291, bf16[1024,1152]{1,0:T(8,128)(2,1)} %gate_pass.1.gate_ref), custom_call_target="tpu_custom_call" | custom-call | flops 1000 | bytes 1000 | tf_op jit(solution)/shard_map/up_pass/pallas_call | solution.py:505
  285.7 14.9 %hidden_pass.1 = (bf16[1024,1152]{1,0:T(8,128)(2,1)}, bf16[1024,1152]{1,0:T(8,128)(2,1)}, bf16[1024,1152]{1,0:T(8,128)(2,1)}) custom-call(bf16[512,2048]{1,0:T(8,128)(2,1)S(1)} %collective-permute-done.19.n0_ref.refs_2_, bf16[512,2048]{1,0:T(8,128)(2,1)S(1)} %collective-permute-done.21.n1_ref.refs_3_, bf16[2048,1152]{1,0:T(8,128)(2,1)} %bitcast.288, ...), custom_call_target="tpu_custom_call" | custom-call | flops 1000 | bytes 1000 | tf_op jit(solution)/shard_map/hidden_pass/pallas_call | solution.py:454
  302.0 12.3 %gates_pass.2 = (bf16[1024,1152]{1,0:T(8,128)(2,1)}, bf16[1024,1152]{1,0:T(8,128)(2,1)}) custom-call(bf16[512,2048]{1,0:T(8,128)(2,1)} %collective-permute-done.15.g0_ref.refs_4_, bf16[512,2048]{1,0:T(8,128)(2,1)} %collective-permute-done.22.g1_ref.refs_5_, bf16[1152,2048]{1,0:T(8,128)(2,1)} %bitcast.295, bf16[1024,1152]{1,0:T(8,128)(2,1)} %get-tuple-element.216.gate_ref, ...), custom_call_target="tpu_custom_call" | custom-call | flops 1000 | bytes 1000 | tf_op jit(solution)/shard_map/gates_pass/pallas_call | solution.py:539
  315.9 14.9 %back_pass.4 = (f32[512,2048]{1,0:T(8,128)}, bf16[512,2048]{1,0:T(8,128)(2,1)S(1)}) custom-call(bf16[1024,1152]{1,0:T(8,128)(2,1)S(1)} %copy-done.17, bf16[1024,1152]{1,0:T(8,128)(2,1)} %get-tuple-element.219.refs_1_.refs_5_, bf16[2048,1152]{1,0:T(8,128)(2,1)} %bitcast.289, bf16[2048,1152]{1,0:T(8,128)(2,1)} %bitcast.293), custom_call_target="tpu_custom_call" | custom-call | flops 1000 | bytes 1000 | tf_op jit(solution)/shard_map/back_pass/pallas_call | solution.py:578
  330.8 15.7 %weight_pass.3 = bf16[1152,2048]{1,0:T(8,128)(2,1)} custom-call(bf16[1024,1152]{1,0:T(8,128)(2,1)} %get-tuple-element.291.refs_0_, bf16[1024,1152]{1,0:T(8,128)(2,1)} %get-tuple-element.246.refs_1_.refs_0_, bf16[512,2048]{1,0:T(8,128)(2,1)} %bitcast_convert_fusion.refs_2_.g0_ref, bf16[512,2048]{1,0:T(8,128)(2,1)} %collective-permute-done.14.refs_3_.g1_ref, ...), custom_call_target="tpu_custom_call" | custom-call | flops 1000 | bytes 1000 | tf_op jit(solution)/shard_map/weight_pass/pallas_call | solution.py:612
  353.7 12.3 %gates_pass.3 = (bf16[1024,1152]{1,0:T(8,128)(2,1)}, bf16[1024,1152]{1,0:T(8,128)(2,1)}) custom-call(bf16[512,2048]{1,0:T(8,128)(2,1)} %bitcast_convert_fusion.refs_2_.g0_ref, bf16[512,2048]{1,0:T(8,128)(2,1)} %collective-permute-done.14.refs_3_.g1_ref, bf16[1152,2048]{1,0:T(8,128)(2,1)} %bitcast.296, bf16[1024,1152]{1,0:T(8,128)(2,1)} %gate_pass.1.gate_ref, ...), custom_call_target="tpu_custom_call" | custom-call | flops 1000 | bytes 1000 | tf_op jit(solution)/shard_map/gates_pass/pallas_call | solution.py:539
  367.7 15.0 %back_pass.5 = (f32[512,2048]{1,0:T(8,128)}, bf16[512,2048]{1,0:T(8,128)(2,1)}) custom-call(bf16[1024,1152]{1,0:T(8,128)(2,1)S(1)} %copy-done.18, bf16[1024,1152]{1,0:T(8,128)(2,1)} %get-tuple-element.237.refs_1_.refs_4_, bf16[2048,1152]{1,0:T(8,128)(2,1)} %bitcast.290, bf16[2048,1152]{1,0:T(8,128)(2,1)} %bitcast.294), custom_call_target="tpu_custom_call" | custom-call | flops 1000 | bytes 1000 | tf_op jit(solution)/shard_map/back_pass/pallas_call | solution.py:578
  382.7 15.8 %weight_pass.4 = bf16[2048,1152]{1,0:T(8,128)(2,1)} custom-call(bf16[512,2048]{1,0:T(8,128)(2,1)S(1)} %multiply_convert_fusion.n0_ref.refs_0_, bf16[512,2048]{1,0:T(8,128)(2,1)S(1)} %copy-done.3, bf16[512,2048]{1,0:T(8,128)(2,1)} %copy-done.9, bf16[512,2048]{1,0:T(8,128)(2,1)} %copy-done.10, bf16[1024,1152]{1,0:T(8,128)(2,1)} %get-tuple-element.231.refs_0_.refs_4_, ...), custom_call_target="tpu_custom_call" | custom-call | flops 1000 | bytes 1000 | tf_op jit(solution)/shard_map/weight_pass/pallas_call | solution.py:612
  400.2 16.1 %weight_pass.5 = bf16[2048,1152]{1,0:T(8,128)(2,1)} custom-call(bf16[512,2048]{1,0:T(8,128)(2,1)S(1)} %multiply_convert_fusion.n0_ref.refs_0_, bf16[512,2048]{1,0:T(8,128)(2,1)S(1)} %copy-done.4, bf16[512,2048]{1,0:T(8,128)(2,1)} %copy-done.9, bf16[512,2048]{1,0:T(8,128)(2,1)} %copy-done.10, bf16[1024,1152]{1,0:T(8,128)(2,1)} %get-tuple-element.237.refs_1_.refs_4_, ...), custom_call_target="tpu_custom_call" | custom-call | flops 1000 | bytes 1000 | tf_op jit(solution)/shard_map/weight_pass/pallas_call | solution.py:612
  438.6 11.0 %attend_backward.2 = (bf16[512,512]{1,0:T(8,128)(2,1)S(1)}, bf16[2048,256]{1,0:T(8,128)(2,1)S(1)}) custom-call(s32[1]{0:T(128)} %bitcast.33.place_ref, bf16[512,1280]{1,0:T(8,128)(2,1)S(1)} %copy-done.13, bf16[2048,640]{1,0:T(8,128)(2,1)} %all-gather.14.cloned.1.call-done.k_ref.v_ref, bf16[2048,640]{1,0:T(8,128)(2,1)} %all-gather.14.cloned.1.call-done.k_ref.v_ref, ...), custom_call_target="tpu_custom_call" | custom-call | flops 1000 | bytes 1000 | tf_op jit(solution)/shard_map/attend_backward/pallas_call | solution.py:410
  452.5 15.4 %reduce-scatter.7.cloned.1.call-done = bf16[1,144,2048]{2,1,0:T(8,128)(2,1)} async-done(((bf16[4,144,2048]{2,1,0:T(8,128)(2,1)}), bf16[1,144,2048]{2,1,0:T(8,128)(2,1)}) %reduce-scatter.7.cloned.1.call-update) | async-done | bytes 589840 | tf_op jit(solution)/shard_map/reduce_scatter | solution.py:819
  503.6 16.9 %attend_backward.3 = (bf16[512,768]{1,0:T(8,128)(2,1)S(1)}, bf16[2048,384]{1,0:T(8,128)(2,1)}) custom-call(s32[1]{0:T(128)} %bitcast.33.place_ref, bf16[512,1280]{1,0:T(8,128)(2,1)S(1)} %copy-done.13, bf16[2048,640]{1,0:T(8,128)(2,1)} %all-gather.14.cloned.1.call-done.k_ref.v_ref, bf16[2048,640]{1,0:T(8,128)(2,1)} %all-gather.14.cloned.1.call-done.k_ref.v_ref, ...), custom_call_target="tpu_custom_call" | custom-call | flops 1000 | bytes 1000 | tf_op jit(solution)/shard_map/attend_backward/pallas_call | solution.py:410
  520.5 14.5 %collective-permute-done.30 = bf16[2,2,4,64,1152]{4,3,1,0,2:T(8,128)(2,1)} collective-permute-done((bf16[2,2,4,64,1152]{4,3,1,0,2:T(8,128)(2,1)}, bf16[2,2,4,64,1152]{4,3,1,0,2:T(8,128)(2,1)}, u32[]{:S(2)}, u32[]{:S(2)}) %collective-permute-start.30) | collective-permute-done | bytes 2359328 | tf_op jit(solution)/shard_map/ppermute | solution.py:718
  535.1 9.9 %collective-permute-done.31 = bf16[512,2048]{1,0:T(8,128)(2,1)} collective-permute-done((bf16[512,2048]{1,0:T(8,128)(2,1)}, bf16[512,2048]{1,0:T(8,128)(2,1)}, u32[]{:S(2)}, u32[]{:S(2)}) %collective-permute-start.31) | collective-permute-done | bytes 2097184 | tf_op jit(solution)/shard_map/ppermute | solution.py:718
  547.2 8.9 %heads_backward.2 = (bf16[512,1280]{1,0:T(8,128)(2,1)}, f32[8,1280]{1,0:T(8,128)}) custom-call(bf16[512,1280]{1,0:T(8,128)(2,1)} %pad_maximum_fusion.3.grad_ref, f32[512,1280]{1,0:T(8,128)} %get-tuple-element.261.joint_ref, f32[8,1280]{1,0:T(8,128)} %copy-done.39, f32[512,128]{1,0:T(8,128)} %copy-done.19, f32[512,128]{1,0:T(8,128)} %copy-done.20), custom_call_target="tpu_custom_call" | custom-call | flops 1000 | bytes 1000 | tf_op jit(solution)/shard_map/heads_backward/pallas_call | solution.py:205
  586.4 14.1 %reduce-scatter.11.cloned.1.call-done = bf16[1,512,384]{1,2,0:T(8,128)(2,1)} async-done(((bf16[4,512,384]{1,2,0:T(8,128)(2,1)}), bf16[1,512,384]{1,2,0:T(8,128)(2,1)}) %reduce-scatter.11.cloned.1.call-update) | async-done | bytes 393232 | tf_op jit(solution)/shard_map/reduce_scatter | solution.py:819
  629.9 8.2 %back_pass.7 = (f32[512,2048]{1,0:T(8,128)}, bf16[512,2048]{1,0:T(8,128)(2,1)}) custom-call(bf16[1024,1152]{1,0:T(8,128)(2,1)S(1)} %copy-done.15, bf16[1152,2048]{1,0:T(8,128)(2,1)} %bitcast.298), custom_call_target="tpu_custom_call" | custom-call | flops 1000 | bytes 1000 | tf_op jit(solution)/shard_map/back_pass/pallas_call | solution.py:578
  (448 shorter events, 336.7 us)
Async XLA Ops:
  7.2 44.7 %all-gather.12.cloned.1.call-start = ((), (), s32[]{:S(2)}) async-start(), calls=%async_computation.12 | async-start | bytes 1638400 | tf_op jit(solution)/shard_map/all_gather | solution.py:815
  9.8 119.7 %all-gather.16.cloned.1.call-start = ((), (), s32[]{:S(2)}) async-start(), calls=%async_computation.14 | async-start | bytes 2949120 | tf_op jit(solution)/shard_map/all_gather | solution.py:815
  53.2 105.0 %all-gather.14.cloned.1.call-start = ((), (), s32[]{:S(2)}) async-start(), calls=%async_computation.13 | async-start | bytes 3276800 | tf_op jit(solution)/shard_map/all_gather | solution.py:815
  93.3 115.6 %all-gather.18.cloned.1.call-start = ((), (), s32[]{:S(2)}) async-start(), calls=%async_computation.15 | async-start | bytes 2949120 | tf_op jit(solution)/shard_map/all_gather | solution.py:815
  100.4 201.6 %all-gather.20.cloned.1.call-start = ((), (), s32[]{:S(2)}) async-start(), calls=%async_computation.16 | async-start | bytes 5898240 | tf_op jit(solution)/shard_map/all_gather | solution.py:815
  154.3 54.6 %collective-permute-start.16 = (bf16[2,2,4,64,1280]{4,3,2,1,0:T(8,128)(2,1)}, bf16[2,2,4,64,1280]{4,3,2,1,0:T(8,128)(2,1)}, u32[]{:S(2)}, u32[]{:S(2)}) collective-permute-start(bf16[2,2,4,64,1280]{4,3,2,1,0:T(8,128)(2,1)} %bitcast.62), channel_id=1, source_target_pairs={{0,4},{4,0},{8,12},{12,8},{16,20},{20,16},{24,28},{28,24},{1,5},{5... | collective-permute-start | bytes 7864328 | tf_op jit(solution)/shard_map/ppermute | solution.py:718
  154.5 54.5 %collective-permute-start.15 = (bf16[512,2048]{1,0:T(8,128)(2,1)}, bf16[512,2048]{1,0:T(8,128)(2,1)}, u32[]{:S(2)}, u32[]{:S(2)}) collective-permute-start(bf16[512,2048]{1,0:T(8,128)(2,1)} %bitcast_convert_fusion.refs_2_.g0_ref), channel_id=1, source_target_pairs={{0,8},{4,12},{8,0},{12,4},{16,24},{20,28},{24,16},{28,20},{1,9},{5... | collective-permute-start | bytes 6291464 | tf_op jit(solution)/shard_map/ppermute | solution.py:718
  155.1 53.8 %collective-permute-start.14 = (bf16[512,2048]{1,0:T(8,128)(2,1)}, bf16[512,2048]{1,0:T(8,128)(2,1)}, u32[]{:S(2)}, u32[]{:S(2)}) collective-permute-start(bf16[512,2048]{1,0:T(8,128)(2,1)} %bitcast_convert_fusion.refs_2_.g0_ref), channel_id=1, source_target_pairs={{0,4},{4,0},{8,12},{12,8},{16,20},{20,16},{24,28},{28,24},{1,5},{5... | collective-permute-start | bytes 6291464 | tf_op jit(solution)/shard_map/ppermute | solution.py:718
  158.2 309.7 %reduce-scatter.7.cloned.1.call-start = ((), (), s32[]{:S(2)}) async-start(), calls=%async_computation.6 | async-start | bytes 2949120 | tf_op jit(solution)/shard_map/reduce_scatter | solution.py:819
  158.7 63.2 %collective-permute-start.17 = (bf16[4,2,2,64,1152]{4,3,2,1,0:T(8,128)(2,1)}, bf16[4,2,2,64,1152]{4,3,2,1,0:T(8,128)(2,1)}, u32[]{:S(2)}, u32[]{:S(2)}) collective-permute-start(bf16[4,2,2,64,1152]{4,3,2,1,0:T(8,128)(2,1)} %bitcast.263), channel_id=1, source_target_pairs={{0,16},{4,20},{8,24},{12,28},{16,0},{20,4},{24,8},{28,12},{1,17},{... | collective-permute-start | bytes 7077896 | tf_op jit(solution)/shard_map/ppermute | solution.py:718
  208.9 61.1 %collective-permute-start.20 = (bf16[4,2,2,64,1152]{4,3,2,1,0:T(8,128)(2,1)}, bf16[4,2,2,64,1152]{4,3,2,1,0:T(8,128)(2,1)}, u32[]{:S(2)}, u32[]{:S(2)}) collective-permute-start(bf16[4,2,2,64,1152]{4,3,2,1,0:T(8,128)(2,1)} %bitcast.265), channel_id=1, source_target_pairs={{0,16},{4,20},{8,24},{12,28},{16,0},{20,4},{24,8},{28,12},{1,17},{... | collective-permute-start | bytes 7077896 | tf_op jit(solution)/shard_map/ppermute | solution.py:718
  222.0 48.0 %collective-permute-start.19 = (bf16[512,2048]{1,0:T(8,128)(2,1)S(1)}, bf16[512,2048]{1,0:T(8,128)(2,1)S(1)}, u32[]{:S(2)}, u32[]{:S(2)}) collective-permute-start(bf16[512,2048]{1,0:T(8,128)(2,1)S(1)} %multiply_convert_fusion.n0_ref.refs_0_), channel_id=1, source_target_pairs={{0,8},{4,12},{8,0},{12,4},{16,24},{20,28},{24,16},{28,20},{1,9},{5... | collective-permute-start | bytes 6291464 | tf_op jit(solution)/shard_map/ppermute | solution.py:718
  223.6 62.1 %collective-permute-start.22 = (bf16[512,2048]{1,0:T(8,128)(2,1)}, bf16[512,2048]{1,0:T(8,128)(2,1)}, u32[]{:S(2)}, u32[]{:S(2)}) collective-permute-start(bf16[512,2048]{1,0:T(8,128)(2,1)} %collective-permute-done.15.g0_ref.refs_4_), channel_id=1, source_target_pairs={{0,4},{4,0},{8,12},{12,8},{16,20},{20,16},{24,28},{28,24},{1,5},{5... | collective-permute-start | bytes 6291464 | tf_op jit(solution)/shard_map/ppermute | solution.py:718
  348.5 49.9 %collective-permute-start.24 = (bf16[512,2048]{1,0:T(8,128)(2,1)}, bf16[512,2048]{1,0:T(8,128)(2,1)}, u32[]{:S(2)}, u32[]{:S(2)}) collective-permute-start(bf16[512,2048]{1,0:T(8,128)(2,1)} %add_convert_fusion.2), channel_id=1, source_target_pairs={{0,8},{4,12},{8,0},{12,4},{16,24},{20,28},{24,16},{28,20},{1,9},{5... | collective-permute-start | bytes 6291464 | tf_op jit(solution)/shard_map/ppermute | solution.py:718
  353.7 62.7 %collective-permute-start.26 = (bf16[4,144,2048]{2,1,0:T(8,128)(2,1)}, bf16[4,144,2048]{2,1,0:T(8,128)(2,1)}, u32[]{:S(2)}, u32[]{:S(2)}) collective-permute-start(bf16[4,144,2048]{2,1,0:T(8,128)(2,1)} %dynamic-slice_bitcast_fusion.1), channel_id=1, source_target_pairs={{0,16},{4,20},{8,24},{12,28},{16,0},{20,4},{24,8},{28,12},{1,17},{... | collective-permute-start | bytes 7077896 | tf_op jit(solution)/shard_map/ppermute | solution.py:718
  421.3 113.8 %reduce-scatter.9.cloned.1.call-start = ((), (), s32[]{:S(2)}) async-start(), calls=%async_computation.7 | async-start | bytes 1310720 | tf_op jit(solution)/shard_map/reduce_scatter | solution.py:819
  424.8 63.1 %collective-permute-start.28 = (bf16[2,2,4,64,1152]{4,3,1,0,2:T(8,128)(2,1)}, bf16[2,2,4,64,1152]{4,3,1,0,2:T(8,128)(2,1)}, u32[]{:S(2)}, u32[]{:S(2)}) collective-permute-start(bf16[2,2,4,64,1152]{4,3,1,0,2:T(8,128)(2,1)} %copy_bitcast_fusion.3), channel_id=1, source_target_pairs={{0,16},{4,20},{8,24},{12,28},{16,0},{20,4},{24,8},{28,12},{1,17},{... | collective-permute-start | bytes 7077896 | tf_op jit(solution)/shard_map/ppermute | solution.py:718
  481.1 54.0 %collective-permute-start.30 = (bf16[2,2,4,64,1152]{4,3,1,0,2:T(8,128)(2,1)}, bf16[2,2,4,64,1152]{4,3,1,0,2:T(8,128)(2,1)}, u32[]{:S(2)}, u32[]{:S(2)}) collective-permute-start(bf16[2,2,4,64,1152]{4,3,1,0,2:T(8,128)(2,1)} %copy_bitcast_fusion.2), channel_id=1, source_target_pairs={{0,16},{4,20},{8,24},{12,28},{16,0},{20,4},{24,8},{28,12},{1,17},{... | collective-permute-start | bytes 7077896 | tf_op jit(solution)/shard_map/ppermute | solution.py:718
  482.6 103.8 %reduce-scatter.13.cloned.1.call-start = ((), (), s32[]{:S(2)}) async-start(), calls=%async_computation.9 | async-start | bytes 2949120 | tf_op jit(solution)/shard_map/reduce_scatter | solution.py:819
  491.8 53.1 %collective-permute-start.29 = (bf16[2,2,4,64,1280]{4,3,2,1,0:T(8,128)(2,1)}, bf16[2,2,4,64,1280]{4,3,2,1,0:T(8,128)(2,1)}, u32[]{:S(2)}, u32[]{:S(2)}) collective-permute-start(bf16[2,2,4,64,1280]{4,3,2,1,0:T(8,128)(2,1)} %dynamic-slice_bitcast_fusion), channel_id=1, source_target_pairs={{0,4},{4,0},{8,12},{12,8},{16,20},{20,16},{24,28},{28,24},{1,5},{5... | collective-permute-start | bytes 7864328 | tf_op jit(solution)/shard_map/ppermute | solution.py:718
  496.9 48.1 %collective-permute-start.31 = (bf16[512,2048]{1,0:T(8,128)(2,1)}, bf16[512,2048]{1,0:T(8,128)(2,1)}, u32[]{:S(2)}, u32[]{:S(2)}) collective-permute-start(bf16[512,2048]{1,0:T(8,128)(2,1)} %add_convert_fusion.1), channel_id=1, source_target_pairs={{0,8},{4,12},{8,0},{12,4},{16,24},{20,28},{24,16},{28,20},{1,9},{5... | collective-permute-start | bytes 6291464 | tf_op jit(solution)/shard_map/ppermute | solution.py:718
  502.2 98.3 %reduce-scatter.11.cloned.1.call-start = ((), (), s32[]{:S(2)}) async-start(), calls=%async_computation.8 | async-start | bytes 1966080 | tf_op jit(solution)/shard_map/reduce_scatter | solution.py:819
  565.4 85.8 %reduce-scatter.15.cloned.1.call-start = ((), (), s32[]{:S(2)}) async-start(), calls=%async_computation.10 | async-start | bytes 2949120 | tf_op jit(solution)/shard_map/reduce_scatter | solution.py:819
  602.7 96.4 %reduce-scatter.17.cloned.1.call-start = ((), (), s32[]{:S(2)}) async-start(), calls=%async_computation.11 | async-start | bytes 2129920 | tf_op jit(solution)/shard_map/reduce_scatter | solution.py:819
  (118 other events, 1095.6 us)
Sparse Core Ops, SparseCore 0:
  10.2 41.6 all-gather.11
  53.4 49.5 all-gather.15
  104.6 53.6 all-gather.13
  159.6 49.2 all-gather.17
  210.9 88.2 all-gather.19
  421.4 46.4 reduce-scatter.6
  482.7 26.0 reduce-scatter.8
  511.2 46.7 reduce-scatter.12
  565.6 34.9 reduce-scatter.10
  602.8 47.0 reduce-scatter.14
  663.2 35.8 reduce-scatter.16

commit v13 on v12

--- a/solution.py
+++ b/solution.py
@@ -992,12 +992,13 @@
     keys_values, queries, down_in = stage(keys_values, queries, down_pair)
     down_lines = gather_seq(down_in)
     mixed, logs = attend_forward(place_array, queries, keys_values)
-    mixed, grad_top1, grad_top2, up_lines, wout_other = stage(
-        mixed, swap(grad_top, 1), swap(grad_top, 2), up_lines, swap(q_right, 1)
+    mixed, grad_top1, grad_top2, wout_other = stage(
+        mixed, swap(grad_top, 1), swap(grad_top, 2), swap(q_right, 1)
     )
     middle = project(
         mixed, q_right.reshape(half_rows), wout_other.reshape(half_rows), tokens_in[0], core
     )
+    middle, up_lines = stage(middle, up_lines)
 
     ffn_scale = norm_scale(middle)
     normed_ffn = (middle * ffn_scale * ffn_gain_full).astype(bf16)

time: 721 us -> 718 us (level)
    all_gather x5, waiting for transfers between devices: 38.9 us -> 9.96 us  [gather_seq(): return lax.all_gather(values, 'seq', axis=0, tiled=False)]
    ppermute x46, waiting for transfers between devices: 105 us -> 134 us  [swap(): return lax.ppermute(values, 'rows', pairs)]
  transfers between devices with their start and end apart: 62 -> 62, of which waited for: 24 -> 26; matrix products, arithmetic and copies ran while one was open for 20% -> 20% of each run, Pallas kernels for 34% -> 34%
where the time goes in v13:
time: 718 us; the launch traced here: 708 us
  Pallas kernels  266 us (37%)
  waiting for transfers between devices  178 us (25%)
  other arithmetic  82.6 us (12%)
  local copies, waits for them, and re-layouts  75.1 us (10%)
  starting transfers between devices  40.9 us (6%)
  matrix products  26.7 us (4%)
  blocking collectives  19.9 us (3%)
  between operations  18.4 us (3%)
    ppermute x46, waiting for transfers between devices, swap(): return lax.ppermute(values, 'rows', pairs)  134 us
    pallas_call x3, Pallas kernels, weight_pass(): pl.pallas_call(partial(weight_kernel, len(lefts)), grid=(rows // tile,),...  47.6 us
    pallas_call x4, Pallas kernels, back_pass(): pl.pallas_call(partial(back_kernel, count, transposed), grid=(width // ti...  46.3 us
    ppermute x46, starting transfers between devices, swap(): return lax.ppermute(values, 'rows', pairs)  35.2 us
    reduce_scatter x6, waiting for transfers between devices, reduce_seq(): return lax.psum_scatter(values, 'seq', scatter_dimension=0, tiled=False)  32 us
    unnamed x161, local copies, waits for them, and re-layouts  28 us
    pallas_call x2, Pallas kernels, attend_backward(): pl.pallas_call(partial(attend_backward_kernel, first, count), grid_spec=p...  28 us
    pallas_call x17, Pallas kernels, joined(): pl.pallas_call(joined_kernel, grid_spec=pltpu.PrefetchScalarGridSpec(num_...  25.3 us
  transfers between devices with their start and end apart: 62, of which 26 were waited for; matrix products, arithmetic and copies ran while one was open for 20% of the time, Pallas kernels for 34%

profile of v13, /device:TPU:0, one launch (start us, length us, event | category | flops | bytes accessed | tf_op | source)
XLA Modules:
  0.0 707.6 jit_solution(14039611028647773039)
XLA Ops:
  28.3 19.9 %all-gather = bf16[256,768]{1,0:T(8,128)(2,1)S(1)} all-gather(bf16[64,768]{1,0:T(8,128)(2,1)S(1)} %fusion.35), channel_id=2, replica_groups=mesh['rows'=8,'seq'=4] {'seq'}, dimensions={0}, use_global_device_ids=true | all-gather | bytes 491520 | tf_op jit(solution)/shard_map/all_gather | solution.py:815
  100.4 26.6 %collective-permute-done.11 = bf16[2,4,64,1280]{3,2,1,0:T(8,128)(2,1)} collective-permute-done((bf16[2,4,64,1280]{3,2,1,0:T(8,128)(2,1)}, bf16[2,4,64,1280]{3,2,1,0:T(8,128)(2,1)}, u32[]{:S(2)}, u32[]{:S(2)}) %collective-permute-start.11) | collective-permute-done | bytes 1310752 | tf_op jit(solution)/shard_map/ppermute | solution.py:718
  141.0 8.8 %heads_forward_halves.1 = (f32[512,1280]{1,0:T(8,128)}, bf16[512,1280]{1,0:T(8,128)(2,1)S(1)}) custom-call(s32[1]{0:T(128)} %bitcast.1.side_ref, bf16[512,2048]{1,0:T(8,128)(2,1)S(1)} %copy-done.6, bf16[4,256,1280]{2,1,0:T(8,128)(2,1)} %bitcast.54.own_ref, bf16[4,256,1280]{2,1,0:T(8,128)(2,1)} %bitcast.55.other_ref, ...), custom_call_target="tpu_custom_call" | custom-call | flops 1000 | bytes 1000 | tf_op jit(solution)/shard_map/heads_forward_halves/pallas_call | solution.py:104
  161.5 11.7 %attend_forward.1 = (bf16[512,1280]{1,0:T(8,128)(2,1)S(1)}, f32[512,1280]{1,0:T(8,128)S(1)}) custom-call(s32[1]{0:T(128)} %bitcast.33.place_ref, bf16[512,1280]{1,0:T(8,128)(2,1)S(1)} %copy-done.12, bf16[2048,640]{1,0:T(8,128)(2,1)} %all-gather.14.cloned.1.call-done.k_ref.v_ref, bf16[2048,640]{1,0:T(8,128)(2,1)} %all-gather.14.cloned.1.call-done.k_ref.v_ref), custom_call_target="tpu_custom_call" | custom-call | flops 1000 | bytes 1000 | tf_op jit(solution)/shard_map/attend_forward/pallas_call | solution.py:273
  174.8 27.9 %collective-permute-done.15.g0_ref.refs_4_ = bf16[512,2048]{1,0:T(8,128)(2,1)} collective-permute-done((bf16[512,2048]{1,0:T(8,128)(2,1)}, bf16[512,2048]{1,0:T(8,128)(2,1)}, u32[]{:S(2)}, u32[]{:S(2)}) %collective-permute-start.15) | collective-permute-done | bytes 2097184 | tf_op jit(solution)/shard_map/ppermute | solution.py:718
  232.9 9.3 %gate_pass.1.gate_ref = bf16[1024,1152]{1,0:T(8,128)(2,1)} custom-call(bf16[512,2048]{1,0:T(8,128)(2,1)S(1)} %multiply_convert_fusion.n0_ref.refs_0_, bf16[512,2048]{1,0:T(8,128)(2,1)S(1)} %collective-permute-done.18.n1_ref.refs_1_, bf16[2048,1152]{1,0:T(8,128)(2,1)} %bitcast.287), custom_call_target="tpu_custom_call" | custom-call | flops 1000 | bytes 1000 | tf_op jit(solution)/shard_map/gate_pass/pallas_call | solution.py:478
  242.2 19.7 %collective-permute-done.19.n0_ref.refs_2_ = bf16[512,2048]{1,0:T(8,128)(2,1)S(1)} collective-permute-done((bf16[512,2048]{1,0:T(8,128)(2,1)S(1)}, bf16[512,2048]{1,0:T(8,128)(2,1)S(1)}, u32[]{:S(2)}, u32[]{:S(2)}) %collective-permute-start.19) | collective-permute-done | bytes 2097184 | tf_op jit(solution)/shard_map/ppermute | solution.py:718
  267.9 9.7 %up_pass.1 = (bf16[1024,1152]{1,0:T(8,128)(2,1)}, bf16[1024,1152]{1,0:T(8,128)(2,1)}) custom-call(bf16[512,2048]{1,0:T(8,128)(2,1)S(1)} %multiply_convert_fusion.n0_ref.refs_0_, bf16[512,2048]{1,0:T(8,128)(2,1)S(1)} %collective-permute-done.18.n1_ref.refs_1_, bf16[2048,1152]{1,0:T(8,128)(2,1)} %bitcast.291, bf16[1024,1152]{1,0:T(8,128)(2,1)} %gate_pass.1.gate_ref), custom_call_target="tpu_custom_call" | custom-call | flops 1000 | bytes 1000 | tf_op jit(solution)/shard_map/up_pass/pallas_call | solution.py:505
  277.7 14.9 %hidden_pass.1 = (bf16[1024,1152]{1,0:T(8,128)(2,1)}, bf16[1024,1152]{1,0:T(8,128)(2,1)}, bf16[1024,1152]{1,0:T(8,128)(2,1)}) custom-call(bf16[512,2048]{1,0:T(8,128)(2,1)S(1)} %collective-permute-done.19.n0_ref.refs_2_, bf16[512,2048]{1,0:T(8,128)(2,1)S(1)} %collective-permute-done.21.n1_ref.refs_3_, bf16[2048,1152]{1,0:T(8,128)(2,1)} %bitcast.288, ...), custom_call_target="tpu_custom_call" | custom-call | flops 1000 | bytes 1000 | tf_op jit(solution)/shard_map/hidden_pass/pallas_call | solution.py:454
  299.2 12.3 %gates_pass.2 = (bf16[1024,1152]{1,0:T(8,128)(2,1)}, bf16[1024,1152]{1,0:T(8,128)(2,1)}) custom-call(bf16[512,2048]{1,0:T(8,128)(2,1)} %collective-permute-done.15.g0_ref.refs_4_, bf16[512,2048]{1,0:T(8,128)(2,1)} %collective-permute-done.22.g1_ref.refs_5_, bf16[1152,2048]{1,0:T(8,128)(2,1)} %bitcast.295, bf16[1024,1152]{1,0:T(8,128)(2,1)} %get-tuple-element.218.gate_ref, ...), custom_call_target="tpu_custom_call" | custom-call | flops 1000 | bytes 1000 | tf_op jit(solution)/shard_map/gates_pass/pallas_call | solution.py:539
  313.1 14.9 %back_pass.4 = (f32[512,2048]{1,0:T(8,128)}, bf16[512,2048]{1,0:T(8,128)(2,1)S(1)}) custom-call(bf16[1024,1152]{1,0:T(8,128)(2,1)S(1)} %copy-done.17, bf16[1024,1152]{1,0:T(8,128)(2,1)} %get-tuple-element.221.refs_1_.refs_5_, bf16[2048,1152]{1,0:T(8,128)(2,1)} %bitcast.289, bf16[2048,1152]{1,0:T(8,128)(2,1)} %bitcast.293), custom_call_target="tpu_custom_call" | custom-call | flops 1000 | bytes 1000 | tf_op jit(solution)/shard_map/back_pass/pallas_call | solution.py:578
  328.0 15.7 %weight_pass.3 = bf16[1152,2048]{1,0:T(8,128)(2,1)} custom-call(bf16[1024,1152]{1,0:T(8,128)(2,1)} %get-tuple-element.293.refs_0_, bf16[1024,1152]{1,0:T(8,128)(2,1)} %get-tuple-element.248.refs_1_.refs_0_, bf16[512,2048]{1,0:T(8,128)(2,1)} %bitcast_convert_fusion.refs_2_.g0_ref, bf16[512,2048]{1,0:T(8,128)(2,1)} %collective-permute-done.14.refs_3_.g1_ref, ...), custom_call_target="tpu_custom_call" | custom-call | flops 1000 | bytes 1000 | tf_op jit(solution)/shard_map/weight_pass/pallas_call | solution.py:612
  352.3 12.3 %gates_pass.3 = (bf16[1024,1152]{1,0:T(8,128)(2,1)}, bf16[1024,1152]{1,0:T(8,128)(2,1)}) custom-call(bf16[512,2048]{1,0:T(8,128)(2,1)} %bitcast_convert_fusion.refs_2_.g0_ref, bf16[512,2048]{1,0:T(8,128)(2,1)} %collective-permute-done.14.refs_3_.g1_ref, bf16[1152,2048]{1,0:T(8,128)(2,1)} %bitcast.296, bf16[1024,1152]{1,0:T(8,128)(2,1)} %gate_pass.1.gate_ref, ...), custom_call_target="tpu_custom_call" | custom-call | flops 1000 | bytes 1000 | tf_op jit(solution)/shard_map/gates_pass/pallas_call | solution.py:539
  366.3 15.0 %back_pass.5 = (f32[512,2048]{1,0:T(8,128)}, bf16[512,2048]{1,0:T(8,128)(2,1)}) custom-call(bf16[1024,1152]{1,0:T(8,128)(2,1)S(1)} %copy-done.18, bf16[1024,1152]{1,0:T(8,128)(2,1)} %get-tuple-element.239.refs_1_.refs_4_, bf16[2048,1152]{1,0:T(8,128)(2,1)} %bitcast.290, bf16[2048,1152]{1,0:T(8,128)(2,1)} %bitcast.294), custom_call_target="tpu_custom_call" | custom-call | flops 1000 | bytes 1000 | tf_op jit(solution)/shard_map/back_pass/pallas_call | solution.py:578
  381.3 15.8 %weight_pass.4 = bf16[2048,1152]{1,0:T(8,128)(2,1)} custom-call(bf16[512,2048]{1,0:T(8,128)(2,1)S(1)} %multiply_convert_fusion.n0_ref.refs_0_, bf16[512,2048]{1,0:T(8,128)(2,1)S(1)} %copy-done.3, bf16[512,2048]{1,0:T(8,128)(2,1)} %copy-done.9, bf16[512,2048]{1,0:T(8,128)(2,1)} %copy-done.10, bf16[1024,1152]{1,0:T(8,128)(2,1)} %get-tuple-element.233.refs_0_.refs_4_, ...), custom_call_target="tpu_custom_call" | custom-call | flops 1000 | bytes 1000 | tf_op jit(solution)/shard_map/weight_pass/pallas_call | solution.py:612
  398.7 16.1 %weight_pass.5 = bf16[2048,1152]{1,0:T(8,128)(2,1)} custom-call(bf16[512,2048]{1,0:T(8,128)(2,1)S(1)} %multiply_convert_fusion.n0_ref.refs_0_, bf16[512,2048]{1,0:T(8,128)(2,1)S(1)} %copy-done.4, bf16[512,2048]{1,0:T(8,128)(2,1)} %copy-done.9, bf16[512,2048]{1,0:T(8,128)(2,1)} %copy-done.10, bf16[1024,1152]{1,0:T(8,128)(2,1)} %get-tuple-element.239.refs_1_.refs_4_, ...), custom_call_target="tpu_custom_call" | custom-call | flops 1000 | bytes 1000 | tf_op jit(solution)/shard_map/weight_pass/pallas_call | solution.py:612
  435.7 11.0 %attend_backward.2 = (bf16[512,512]{1,0:T(8,128)(2,1)S(1)}, bf16[2048,256]{1,0:T(8,128)(2,1)S(1)}) custom-call(s32[1]{0:T(128)} %bitcast.33.place_ref, bf16[512,1280]{1,0:T(8,128)(2,1)S(1)} %copy-done.13, bf16[2048,640]{1,0:T(8,128)(2,1)} %all-gather.14.cloned.1.call-done.k_ref.v_ref, bf16[2048,640]{1,0:T(8,128)(2,1)} %all-gather.14.cloned.1.call-done.k_ref.v_ref, ...), custom_call_target="tpu_custom_call" | custom-call | flops 1000 | bytes 1000 | tf_op jit(solution)/shard_map/attend_backward/pallas_call | solution.py:410
  449.6 15.0 %reduce-scatter.7.cloned.1.call-done = bf16[1,144,2048]{2,1,0:T(8,128)(2,1)} async-done(((bf16[4,144,2048]{2,1,0:T(8,128)(2,1)}), bf16[1,144,2048]{2,1,0:T(8,128)(2,1)}) %reduce-scatter.7.cloned.1.call-update) | async-done | bytes 589840 | tf_op jit(solution)/shard_map/reduce_scatter | solution.py:819
  500.3 16.9 %attend_backward.3 = (bf16[512,768]{1,0:T(8,128)(2,1)S(1)}, bf16[2048,384]{1,0:T(8,128)(2,1)}) custom-call(s32[1]{0:T(128)} %bitcast.33.place_ref, bf16[512,1280]{1,0:T(8,128)(2,1)S(1)} %copy-done.13, bf16[2048,640]{1,0:T(8,128)(2,1)} %all-gather.14.cloned.1.call-done.k_ref.v_ref, bf16[2048,640]{1,0:T(8,128)(2,1)} %all-gather.14.cloned.1.call-done.k_ref.v_ref, ...), custom_call_target="tpu_custom_call" | custom-call | flops 1000 | bytes 1000 | tf_op jit(solution)/shard_map/attend_backward/pallas_call | solution.py:410
  517.2 14.5 %collective-permute-done.30 = bf16[2,2,4,64,1152]{4,3,1,0,2:T(8,128)(2,1)} collective-permute-done((bf16[2,2,4,64,1152]{4,3,1,0,2:T(8,128)(2,1)}, bf16[2,2,4,64,1152]{4,3,1,0,2:T(8,128)(2,1)}, u32[]{:S(2)}, u32[]{:S(2)}) %collective-permute-start.30) | collective-permute-done | bytes 2359328 | tf_op jit(solution)/shard_map/ppermute | solution.py:718
  531.8 9.9 %collective-permute-done.31 = bf16[512,2048]{1,0:T(8,128)(2,1)} collective-permute-done((bf16[512,2048]{1,0:T(8,128)(2,1)}, bf16[512,2048]{1,0:T(8,128)(2,1)}, u32[]{:S(2)}, u32[]{:S(2)}) %collective-permute-start.31) | collective-permute-done | bytes 2097184 | tf_op jit(solution)/shard_map/ppermute | solution.py:718
  543.9 8.9 %heads_backward.2 = (bf16[512,1280]{1,0:T(8,128)(2,1)}, f32[8,1280]{1,0:T(8,128)}) custom-call(bf16[512,1280]{1,0:T(8,128)(2,1)} %pad_maximum_fusion.3.grad_ref, f32[512,1280]{1,0:T(8,128)} %get-tuple-element.263.joint_ref, f32[8,1280]{1,0:T(8,128)} %copy-done.39, f32[512,128]{1,0:T(8,128)} %copy-done.19, f32[512,128]{1,0:T(8,128)} %copy-done.20), custom_call_target="tpu_custom_call" | custom-call | flops 1000 | bytes 1000 | tf_op jit(solution)/shard_map/heads_backward/pallas_call | solution.py:205
  583.1 14.1 %reduce-scatter.11.cloned.1.call-done = bf16[1,512,384]{1,2,0:T(8,128)(2,1)} async-done(((bf16[4,512,384]{1,2,0:T(8,128)(2,1)}), bf16[1,512,384]{1,2,0:T(8,128)(2,1)}) %reduce-scatter.11.cloned.1.call-update) | async-done | bytes 393232 | tf_op jit(solution)/shard_map/reduce_scatter | solution.py:819
  626.6 8.2 %back_pass.7 = (f32[512,2048]{1,0:T(8,128)}, bf16[512,2048]{1,0:T(8,128)(2,1)}) custom-call(bf16[1024,1152]{1,0:T(8,128)(2,1)S(1)} %copy-done.15, bf16[1152,2048]{1,0:T(8,128)(2,1)} %bitcast.298), custom_call_target="tpu_custom_call" | custom-call | flops 1000 | bytes 1000 | tf_op jit(solution)/shard_map/back_pass/pallas_call | solution.py:578
  (448 shorter events, 339.9 us)
Async XLA Ops:
  7.2 44.7 %all-gather.12.cloned.1.call-start = ((), (), s32[]{:S(2)}) async-start(), calls=%async_computation.12 | async-start | bytes 1638400 | tf_op jit(solution)/shard_map/all_gather | solution.py:815
  9.8 119.7 %all-gather.16.cloned.1.call-start = ((), (), s32[]{:S(2)}) async-start(), calls=%async_computation.14 | async-start | bytes 2949120 | tf_op jit(solution)/shard_map/all_gather | solution.py:815
  53.2 105.0 %all-gather.14.cloned.1.call-start = ((), (), s32[]{:S(2)}) async-start(), calls=%async_computation.13 | async-start | bytes 3276800 | tf_op jit(solution)/shard_map/all_gather | solution.py:815
  93.3 116.2 %all-gather.18.cloned.1.call-start = ((), (), s32[]{:S(2)}) async-start(), calls=%async_computation.15 | async-start | bytes 2949120 | tf_op jit(solution)/shard_map/all_gather | solution.py:815
  100.4 198.8 %all-gather.20.cloned.1.call-start = ((), (), s32[]{:S(2)}) async-start(), calls=%async_computation.16 | async-start | bytes 5898240 | tf_op jit(solution)/shard_map/all_gather | solution.py:815
  154.3 48.4 %collective-permute-start.16 = (bf16[2,2,4,64,1280]{4,3,2,1,0:T(8,128)(2,1)}, bf16[2,2,4,64,1280]{4,3,2,1,0:T(8,128)(2,1)}, u32[]{:S(2)}, u32[]{:S(2)}) collective-permute-start(bf16[2,2,4,64,1280]{4,3,2,1,0:T(8,128)(2,1)} %bitcast.61), channel_id=1, source_target_pairs={{0,4},{4,0},{8,12},{12,8},{16,20},{20,16},{24,28},{28,24},{1,5},{5... | collective-permute-start | bytes 7864328 | tf_op jit(solution)/shard_map/ppermute | solution.py:718
  154.5 48.2 %collective-permute-start.15 = (bf16[512,2048]{1,0:T(8,128)(2,1)}, bf16[512,2048]{1,0:T(8,128)(2,1)}, u32[]{:S(2)}, u32[]{:S(2)}) collective-permute-start(bf16[512,2048]{1,0:T(8,128)(2,1)} %bitcast_convert_fusion.refs_2_.g0_ref), channel_id=1, source_target_pairs={{0,8},{4,12},{8,0},{12,4},{16,24},{20,28},{24,16},{28,20},{1,9},{5... | collective-permute-start | bytes 6291464 | tf_op jit(solution)/shard_map/ppermute | solution.py:718
  155.1 47.6 %collective-permute-start.14 = (bf16[512,2048]{1,0:T(8,128)(2,1)}, bf16[512,2048]{1,0:T(8,128)(2,1)}, u32[]{:S(2)}, u32[]{:S(2)}) collective-permute-start(bf16[512,2048]{1,0:T(8,128)(2,1)} %bitcast_convert_fusion.refs_2_.g0_ref), channel_id=1, source_target_pairs={{0,4},{4,0},{8,12},{12,8},{16,20},{20,16},{24,28},{28,24},{1,5},{5... | collective-permute-start | bytes 6291464 | tf_op jit(solution)/shard_map/ppermute | solution.py:718
  158.2 306.4 %reduce-scatter.7.cloned.1.call-start = ((), (), s32[]{:S(2)}) async-start(), calls=%async_computation.6 | async-start | bytes 2949120 | tf_op jit(solution)/shard_map/reduce_scatter | solution.py:819
  158.7 55.1 %collective-permute-start.17 = (bf16[4,2,2,64,1152]{4,3,2,1,0:T(8,128)(2,1)}, bf16[4,2,2,64,1152]{4,3,2,1,0:T(8,128)(2,1)}, u32[]{:S(2)}, u32[]{:S(2)}) collective-permute-start(bf16[4,2,2,64,1152]{4,3,2,1,0:T(8,128)(2,1)} %bitcast.263), channel_id=1, source_target_pairs={{0,16},{4,20},{8,24},{12,28},{16,0},{20,4},{24,8},{28,12},{1,17},{... | collective-permute-start | bytes 7077896 | tf_op jit(solution)/shard_map/ppermute | solution.py:718
  209.5 53.0 %collective-permute-start.20 = (bf16[4,2,2,64,1152]{4,3,2,1,0:T(8,128)(2,1)}, bf16[4,2,2,64,1152]{4,3,2,1,0:T(8,128)(2,1)}, u32[]{:S(2)}, u32[]{:S(2)}) collective-permute-start(bf16[4,2,2,64,1152]{4,3,2,1,0:T(8,128)(2,1)} %bitcast.265), channel_id=1, source_target_pairs={{0,16},{4,20},{8,24},{12,28},{16,0},{20,4},{24,8},{28,12},{1,17},{... | collective-permute-start | bytes 7077896 | tf_op jit(solution)/shard_map/ppermute | solution.py:718
  213.9 48.0 %collective-permute-start.19 = (bf16[512,2048]{1,0:T(8,128)(2,1)S(1)}, bf16[512,2048]{1,0:T(8,128)(2,1)S(1)}, u32[]{:S(2)}, u32[]{:S(2)}) collective-permute-start(bf16[512,2048]{1,0:T(8,128)(2,1)S(1)} %multiply_convert_fusion.n0_ref.refs_0_), channel_id=1, source_target_pairs={{0,8},{4,12},{8,0},{12,4},{16,24},{20,28},{24,16},{28,20},{1,9},{5... | collective-permute-start | bytes 6291464 | tf_op jit(solution)/shard_map/ppermute | solution.py:718
  215.0 62.6 %collective-permute-start.22 = (bf16[512,2048]{1,0:T(8,128)(2,1)}, bf16[512,2048]{1,0:T(8,128)(2,1)}, u32[]{:S(2)}, u32[]{:S(2)}) collective-permute-start(bf16[512,2048]{1,0:T(8,128)(2,1)} %collective-permute-done.15.g0_ref.refs_4_), channel_id=1, source_target_pairs={{0,4},{4,0},{8,12},{12,8},{16,20},{20,16},{24,28},{28,24},{1,5},{5... | collective-permute-start | bytes 6291464 | tf_op jit(solution)/shard_map/ppermute | solution.py:718
  345.8 51.3 %collective-permute-start.24 = (bf16[512,2048]{1,0:T(8,128)(2,1)}, bf16[512,2048]{1,0:T(8,128)(2,1)}, u32[]{:S(2)}, u32[]{:S(2)}) collective-permute-start(bf16[512,2048]{1,0:T(8,128)(2,1)} %add_convert_fusion.2), channel_id=1, source_target_pairs={{0,8},{4,12},{8,0},{12,4},{16,24},{20,28},{24,16},{28,20},{1,9},{5... | collective-permute-start | bytes 6291464 | tf_op jit(solution)/shard_map/ppermute | solution.py:718
  350.8 64.0 %collective-permute-start.26 = (bf16[4,144,2048]{2,1,0:T(8,128)(2,1)}, bf16[4,144,2048]{2,1,0:T(8,128)(2,1)}, u32[]{:S(2)}, u32[]{:S(2)}) collective-permute-start(bf16[4,144,2048]{2,1,0:T(8,128)(2,1)} %dynamic-slice_bitcast_fusion.1), channel_id=1, source_target_pairs={{0,16},{4,20},{8,24},{12,28},{16,0},{20,4},{24,8},{28,12},{1,17},{... | collective-permute-start | bytes 7077896 | tf_op jit(solution)/shard_map/ppermute | solution.py:718
  419.7 112.1 %reduce-scatter.9.cloned.1.call-start = ((), (), s32[]{:S(2)}) async-start(), calls=%async_computation.7 | async-start | bytes 1310720 | tf_op jit(solution)/shard_map/reduce_scatter | solution.py:819
  423.2 61.4 %collective-permute-start.28 = (bf16[2,2,4,64,1152]{4,3,1,0,2:T(8,128)(2,1)}, bf16[2,2,4,64,1152]{4,3,1,0,2:T(8,128)(2,1)}, u32[]{:S(2)}, u32[]{:S(2)}) collective-permute-start(bf16[2,2,4,64,1152]{4,3,1,0,2:T(8,128)(2,1)} %copy_bitcast_fusion.3), channel_id=1, source_target_pairs={{0,16},{4,20},{8,24},{12,28},{16,0},{20,4},{24,8},{28,12},{1,17},{... | collective-permute-start | bytes 7077896 | tf_op jit(solution)/shard_map/ppermute | solution.py:718
  477.8 54.0 %collective-permute-start.30 = (bf16[2,2,4,64,1152]{4,3,1,0,2:T(8,128)(2,1)}, bf16[2,2,4,64,1152]{4,3,1,0,2:T(8,128)(2,1)}, u32[]{:S(2)}, u32[]{:S(2)}) collective-permute-start(bf16[2,2,4,64,1152]{4,3,1,0,2:T(8,128)(2,1)} %copy_bitcast_fusion.2), channel_id=1, source_target_pairs={{0,16},{4,20},{8,24},{12,28},{16,0},{20,4},{24,8},{28,12},{1,17},{... | collective-permute-start | bytes 7077896 | tf_op jit(solution)/shard_map/ppermute | solution.py:718
  479.3 103.8 %reduce-scatter.13.cloned.1.call-start = ((), (), s32[]{:S(2)}) async-start(), calls=%async_computation.9 | async-start | bytes 2949120 | tf_op jit(solution)/shard_map/reduce_scatter | solution.py:819
  488.5 53.1 %collective-permute-start.29 = (bf16[2,2,4,64,1280]{4,3,2,1,0:T(8,128)(2,1)}, bf16[2,2,4,64,1280]{4,3,2,1,0:T(8,128)(2,1)}, u32[]{:S(2)}, u32[]{:S(2)}) collective-permute-start(bf16[2,2,4,64,1280]{4,3,2,1,0:T(8,128)(2,1)} %dynamic-slice_bitcast_fusion), channel_id=1, source_target_pairs={{0,4},{4,0},{8,12},{12,8},{16,20},{20,16},{24,28},{28,24},{1,5},{5... | collective-permute-start | bytes 7864328 | tf_op jit(solution)/shard_map/ppermute | solution.py:718
  493.6 48.1 %collective-permute-start.31 = (bf16[512,2048]{1,0:T(8,128)(2,1)}, bf16[512,2048]{1,0:T(8,128)(2,1)}, u32[]{:S(2)}, u32[]{:S(2)}) collective-permute-start(bf16[512,2048]{1,0:T(8,128)(2,1)} %add_convert_fusion.1), channel_id=1, source_target_pairs={{0,8},{4,12},{8,0},{12,4},{16,24},{20,28},{24,16},{28,20},{1,9},{5... | collective-permute-start | bytes 6291464 | tf_op jit(solution)/shard_map/ppermute | solution.py:718
  498.9 98.3 %reduce-scatter.11.cloned.1.call-start = ((), (), s32[]{:S(2)}) async-start(), calls=%async_computation.8 | async-start | bytes 1966080 | tf_op jit(solution)/shard_map/reduce_scatter | solution.py:819
  562.1 85.8 %reduce-scatter.15.cloned.1.call-start = ((), (), s32[]{:S(2)}) async-start(), calls=%async_computation.10 | async-start | bytes 2949120 | tf_op jit(solution)/shard_map/reduce_scatter | solution.py:819
  599.4 96.4 %reduce-scatter.17.cloned.1.call-start = ((), (), s32[]{:S(2)}) async-start(), calls=%async_computation.11 | async-start | bytes 2129920 | tf_op jit(solution)/shard_map/reduce_scatter | solution.py:819
  (118 other events, 1092.6 us)
Sparse Core Ops, SparseCore 0:
  10.2 41.6 all-gather.11
  53.4 49.5 all-gather.15
  104.6 53.6 all-gather.13
  159.6 49.2 all-gather.17
  210.9 88.2 all-gather.19
  419.8 44.7 reduce-scatter.6
  479.4 26.0 reduce-scatter.8
  507.9 46.6 reduce-scatter.12
  562.3 34.9 reduce-scatter.10
  599.5 47.0 reduce-scatter.14
  659.9 35.8 reduce-scatter.16
